TPU v7x, 32 devices: a whole 2x2x4 slice. The times are simulated.
32 devices in a mesh: dp: 16 (over z, y, x), tensor: 2 (over core).
Axes of the slice: x: 2, y: 2, z: 4, core: 2. Of those that a mesh axis runs over, the one named last changes fastest.
Arguments:
- tokens: bfloat16 [8192, 2048], P('dp'), may hold values from -24 to 24
- segments: int32 [16, 512], P('dp'), may hold values from 0 to 3, never falling along the last dimension, each value on 1 to 320 neighbouring positions
- cotangent: float32 [8192, 2048], P('dp'), may hold values from -6 to 6
- attn_gain: float32 [2048], replicated, may hold values from 0.5 to 1.5
- ffn_gain: float32 [2048], replicated, may hold values from 0.5 to 1.5
- query_gain: float32 [64], replicated, may hold values from 0.5 to 1.5
- key_gain: float32 [64], replicated, may hold values from 0.5 to 1.5
- w_query: bfloat16 [2048, 2048], P('dp', 'tensor'), may hold values from -0.125 to 0.125
- key_weight: bfloat16 [2048, 512], P('dp', 'tensor'), may hold values from -0.125 to 0.125
- value_weight: bfloat16 [2048, 512], P('dp', 'tensor'), may hold values from -0.125 to 0.125
- w_out: bfloat16 [2048, 2048], P('dp', 'tensor'), may hold values from -0.375 to 0.375
- w_gate: bfloat16 [2048, 8192], P('dp', 'tensor'), may hold values from -0.125 to 0.125
- w_up: bfloat16 [2048, 8192], P('dp', 'tensor'), may hold values from -0.125 to 0.125
- w_down: bfloat16 [2048, 8192], P('dp', 'tensor'), may hold values from -0.0625 to 0.0625
Outputs:
- mixed: float32 [8192, 2048], P('dp')
- input_grad: float32 [8192, 2048], P('dp')
- attn_gain_grad: float32 [2048], replicated
- ffn_gain_grad: float32 [2048], replicated
- query_gain_grad: float32 [64], replicated
- key_gain_grad: float32 [64], replicated
- w_query_grad: float32 [2048, 2048], P('dp', 'tensor')
- w_key_grad: float32 [2048, 512], P('dp', 'tensor')
- w_value_grad: float32 [2048, 512], P('dp', 'tensor')
- w_out_grad: float32 [2048, 2048], P('dp', 'tensor')
- w_gate_grad: float32 [2048, 8192], P('dp', 'tensor')
- w_up_grad: float32 [2048, 8192], P('dp', 'tensor')
- w_down_grad: float32 [2048, 8192], P('dp', 'tensor')
Inputs may be any that keep to these rules, and one draw needn't show every extreme that they name: `segments`: within each sequence the numbers never fall; each document holds 1 to 320 tokens and one holds exactly 320.
All inputs are finite; a program needn't handle non-finite values.
Results may differ from a plain program's by a relative error of at most 0.014.
Values may be sent and summed in bfloat16 or wider, within the bound.
No kernel may reach another device: no remote copies, remote signals or barrier semaphores. Data moves between devices by JAX's collectives and lax.ppermute only.
A program may use at most 320 MiB of HBM per device.

v0:
```python
import jax
import jax.numpy as jnp
from jax import lax
from jax.sharding import PartitionSpec as P

eps = 1e-05
rope_base = 1000000.0


def norm_rows(values, gain):
    scale = lax.rsqrt(jnp.mean(values * values, axis=-1, keepdims=True) + eps)
    return (values * scale * gain, scale)


def norm_back(values, scale, gain, incoming):
    weighted = incoming * gain
    return scale * weighted - values * (scale * scale * scale) * jnp.mean(
        weighted * values, axis=-1, keepdims=True
    )


def positions_of(segment_row):
    row_index = jnp.arange(segment_row.shape[0], dtype=jnp.int32)
    earlier = jnp.concatenate([segment_row[:1] - 1, segment_row[:-1]])
    starts = jnp.where(segment_row != earlier, row_index, jnp.zeros_like(row_index))
    return row_index - lax.cummax(starts, axis=0)


def angles(positions, width):
    frequency = rope_base ** (-jnp.arange(0, width, 2, dtype=jnp.float32) / width)
    phases = positions.astype(jnp.float32)[:, None] * frequency[None, :]
    phases = jnp.concatenate([phases, phases], axis=-1)
    return (jnp.cos(phases)[:, None, :], jnp.sin(phases)[:, None, :])


def head_prepare(raw_heads, gain, cosine_table, sine_table):
    scaled = (
        raw_heads * lax.rsqrt(jnp.mean(raw_heads * raw_heads, axis=-1, keepdims=True) + eps) * gain
    )
    half_width = scaled.shape[-1] // 2
    turned = jnp.concatenate([-scaled[..., half_width:], scaled[..., :half_width]], axis=-1)
    return scaled * cosine_table + turned * sine_table


def rows_product(left, right):
    return lax.dot_general(
        left, right, (((0,), (0,)), ((), ())), preferred_element_type=jnp.float32
    )


def cols_product(left, right):
    return lax.dot_general(
        left, right, (((1,), (1,)), ((), ())), preferred_element_type=jnp.float32
    )


def local(
    tokens,
    segments,
    cotangent,
    attn_gain,
    ffn_gain,
    query_gain,
    key_gain,
    w_query,
    key_weight,
    value_weight,
    w_out,
    w_gate,
    w_up,
    w_down,
):
    token_length = tokens.shape[0]
    head_dim = query_gain.shape[0]
    query_heads = w_query.shape[1] // head_dim
    value_heads = key_weight.shape[1] // head_dim
    query_group_count = query_heads // value_heads
    segment_row = segments.reshape(token_length)
    row_index = jnp.arange(token_length, dtype=jnp.int32)
    allowed = (segment_row[:, None] == segment_row[None, :]) & (
        row_index[:, None] >= row_index[None, :]
    )
    cosine_table, sine_table = angles(positions_of(segment_row), head_dim)
    attn_full = (
        lax.all_gather(w_query, "dp", axis=0, tiled=True),
        lax.all_gather(key_weight, "dp", axis=0, tiled=True),
        lax.all_gather(value_weight, "dp", axis=0, tiled=True),
        lax.all_gather(w_out, "dp", axis=0, tiled=True),
    )
    ffn_full = (
        lax.all_gather(w_gate, "dp", axis=0, tiled=True),
        lax.all_gather(w_up, "dp", axis=0, tiled=True),
        lax.all_gather(w_down, "dp", axis=0, tiled=True),
    )
    query_full, key_full, value_full, out_full = attn_full
    gate_full, up_full, down_full = ffn_full
    source = tokens.astype(jnp.float32)
    normed_f, scale_first = norm_rows(source, attn_gain)
    normalized_input = normed_f.astype(jnp.bfloat16)
    query_raw = jnp.dot(normalized_input, query_full, preferred_element_type=jnp.float32).reshape(
        token_length, query_heads, head_dim
    )
    key_unrotated = jnp.dot(normalized_input, key_full, preferred_element_type=jnp.float32).reshape(
        token_length, value_heads, head_dim
    )
    value_rows = (
        jnp.dot(normalized_input, value_full, preferred_element_type=jnp.float32)
        .astype(jnp.bfloat16)
        .reshape(token_length, value_heads, head_dim)
    )
    query_turned, query_pull = jax.vjp(
        lambda raw_in, gain_in: head_prepare(raw_in, gain_in, cosine_table, sine_table),
        query_raw,
        query_gain,
    )
    key_turned, key_pull = jax.vjp(
        lambda raw_in, gain_in: head_prepare(raw_in, gain_in, cosine_table, sine_table),
        key_unrotated,
        key_gain,
    )
    query_rows = query_turned.astype(jnp.bfloat16).reshape(
        token_length, value_heads, query_group_count, head_dim
    )
    key = key_turned.astype(jnp.bfloat16)
    attention_logits = 0.125 * jnp.einsum(
        "hcfw,kcw->cfhk", query_rows, key, preferred_element_type=jnp.float32
    )
    attention_logits = jnp.where(allowed, attention_logits, -1000000000.0)
    probs_f = jax.nn.softmax(attention_logits, axis=-1)
    attention_probabilities = probs_f.astype(jnp.bfloat16)
    head_outputs = jnp.einsum(
        "ljxe,elv->xljv", attention_probabilities, value_rows, preferred_element_type=jnp.float32
    )
    head_outputs = head_outputs.astype(jnp.bfloat16).reshape(token_length, query_heads * head_dim)
    attended = lax.psum(cols_product(head_outputs, out_full), "tensor")
    state = source + attended
    normed2_f, scale_second = norm_rows(state, ffn_gain)
    normed2 = normed2_f.astype(jnp.bfloat16)
    gate_proj = jnp.dot(normed2, gate_full, preferred_element_type=jnp.float32)
    up_proj = jnp.dot(normed2, up_full, preferred_element_type=jnp.float32)
    sigmoid_gate = jax.nn.sigmoid(gate_proj)
    silu_gate = gate_proj * sigmoid_gate
    inner = (silu_gate * up_proj).astype(jnp.bfloat16)
    branch = lax.psum(cols_product(inner, down_full).astype(jnp.bfloat16), "tensor").astype(
        jnp.float32
    )
    mixed = state + branch
    gate_back, up_back, down_back = (gate_full, up_full, down_full)
    out_b = cotangent.astype(jnp.bfloat16)
    w_down_grad = rows_product(out_b, inner)
    inner_grad = jnp.dot(out_b, down_back, preferred_element_type=jnp.float32)
    gate_grad = (
        inner_grad * up_proj * sigmoid_gate * (1.0 + gate_proj * (1.0 - sigmoid_gate))
    ).astype(jnp.bfloat16)
    up_grad = (inner_grad * silu_gate).astype(jnp.bfloat16)
    w_gate_grad = rows_product(normed2, gate_grad)
    w_up_grad = rows_product(normed2, up_grad)
    normed2_part = cols_product(gate_grad, gate_back) + cols_product(up_grad, up_back)
    ffn_gain_part = jnp.sum(normed2_part * state * scale_second, axis=0)
    normed2_grad = lax.psum(normed2_part, "tensor")
    state_grad = cotangent + norm_back(state, scale_second, ffn_gain, normed2_grad)
    query_back, key_back, value_back, out_back = (query_full, key_full, value_full, out_full)
    attended_b = state_grad.astype(jnp.bfloat16)
    w_out_grad = rows_product(attended_b, head_outputs)
    head_output_grad = jnp.dot(attended_b, out_back, preferred_element_type=jnp.float32).astype(
        jnp.bfloat16
    )
    head_output_grad = head_output_grad.reshape(
        token_length, value_heads, query_group_count, head_dim
    )
    probability_grad = jnp.einsum(
        "hcfw,kcw->cfhk", head_output_grad, value_rows, preferred_element_type=jnp.float32
    )
    value_rows_grad = jnp.einsum(
        "ilac,ailz->ciz",
        attention_probabilities,
        head_output_grad,
        preferred_element_type=jnp.float32,
    )
    value_rows_grad = value_rows_grad.astype(jnp.bfloat16).reshape(
        token_length, value_heads * head_dim
    )
    logit_grad = probs_f * (
        probability_grad - jnp.sum(probs_f * probability_grad, axis=-1, keepdims=True)
    )
    logit_grad = logit_grad.astype(jnp.bfloat16)
    query_grad = 0.125 * jnp.einsum(
        "ljxe,elv->xljv", logit_grad, key, preferred_element_type=jnp.float32
    )
    key_grad = 0.125 * jnp.einsum(
        "ilac,ailz->ciz", logit_grad, query_rows, preferred_element_type=jnp.float32
    )
    query_raw_grad, query_gain_part = query_pull(
        query_grad.reshape(token_length, query_heads, head_dim)
    )
    key_raw_grad, key_gain_part = key_pull(key_grad)
    query_raw_b = query_raw_grad.astype(jnp.bfloat16).reshape(token_length, query_heads * head_dim)
    key_raw_b = key_raw_grad.astype(jnp.bfloat16).reshape(token_length, value_heads * head_dim)
    w_query_grad = rows_product(normalized_input, query_raw_b)
    w_key_grad = rows_product(normalized_input, key_raw_b)
    w_value_grad = rows_product(normalized_input, value_rows_grad)
    normed_part = (
        cols_product(query_raw_b, query_back)
        + cols_product(key_raw_b, key_back)
        + cols_product(value_rows_grad, value_back)
    )
    attn_gain_part = jnp.sum(normed_part * source * scale_first, axis=0)
    normed_grad = lax.psum(normed_part, "tensor")
    summed = (
        lax.psum_scatter(w_query_grad, "dp", scatter_dimension=0, tiled=True),
        lax.psum_scatter(w_key_grad, "dp", scatter_dimension=0, tiled=True),
        lax.psum_scatter(w_value_grad, "dp", scatter_dimension=0, tiled=True),
        lax.psum_scatter(w_out_grad, "dp", scatter_dimension=0, tiled=True),
        lax.psum_scatter(w_gate_grad, "dp", scatter_dimension=0, tiled=True),
        lax.psum_scatter(w_up_grad, "dp", scatter_dimension=0, tiled=True),
        lax.psum_scatter(w_down_grad, "dp", scatter_dimension=0, tiled=True),
    )
    attn_sums = (summed[0], summed[1], summed[2], summed[3])
    ffn_sums = (summed[4], summed[5], summed[6])
    input_grad = state_grad + norm_back(source, scale_first, attn_gain, normed_grad)
    gain_totals = lax.psum(
        (attn_gain_part, ffn_gain_part, query_gain_part, key_gain_part), ("dp", "tensor")
    )
    return (
        mixed,
        input_grad,
        gain_totals[0],
        gain_totals[1],
        gain_totals[2],
        gain_totals[3],
        attn_sums[0],
        attn_sums[1],
        attn_sums[2],
        attn_sums[3],
        ffn_sums[0],
        ffn_sums[1],
        ffn_sums[2],
    )


def solution(mesh):
    placed = (
        P("dp", None),
        P("dp", None),
        P("dp", None),
        P(),
        P(),
        P(),
        P(),
        P("dp", "tensor"),
        P("dp", "tensor"),
        P("dp", "tensor"),
        P("dp", "tensor"),
        P("dp", "tensor"),
        P("dp", "tensor"),
        P("dp", "tensor"),
    )
    return jax.shard_map(
        local,
        mesh=mesh,
        in_specs=placed,
        out_specs=(
            P("dp", None),
            P("dp", None),
            P(),
            P(),
            P(),
            P(),
            P("dp", "tensor"),
            P("dp", "tensor"),
            P("dp", "tensor"),
            P("dp", "tensor"),
            P("dp", "tensor"),
            P("dp", "tensor"),
            P("dp", "tensor"),
        ),
        check_vma=False,
    )
```

profile of v0, /device:TPU:1, one launch (start us, length us, event | category | flops | bytes accessed | tf_op | source)
XLA Modules:
  0.0 3694.5 jit_solution(6172145689824093899)
XLA Ops:
  18.8 48.1 %all-gather.10.cloned.1.call-done = bf16[2048,256]{1,0:T(8,128)(2,1)} async-done(((bf16[128,256]{1,0:T(8,128)(2,1)}), bf16[2048,256]{1,0:T(8,128)(2,1)}) %all-gather.10.cloned.1.call-update) | async-done | bytes 1048592 | tf_op jit(solution)/shard_map/all_gather | solution.py:86
  66.9 3.0 multiply_reduce_fusion.8
  71.9 51.8 %all-gather.8.cloned.1.call-done = bf16[2048,256]{1,0:T(8,128)(2,1)} async-done(((bf16[128,256]{1,0:T(8,128)(2,1)}), bf16[2048,256]{1,0:T(8,128)(2,1)}) %all-gather.8.cloned.1.call-update) | async-done | bytes 1048592 | tf_op jit(solution)/shard_map/all_gather | solution.py:87
  123.7 2.9 convolution_convert_fusion.2
  126.6 74.9 %all-gather.12.cloned.1.call-done = bf16[2048,1024]{1,0:T(8,128)(2,1)} async-done(((bf16[128,1024]{1,0:T(8,128)(2,1)}), bf16[2048,1024]{1,0:T(8,128)(2,1)}) %all-gather.12.cloned.1.call-update) | async-done | bytes 4194320 | tf_op jit(solution)/shard_map/all_gather | solution.py:85
  201.5 5.3 multiply_reduce_fusion.5
  208.9 10.8 fusion.71
  219.8 7.4 fusion.29
  227.2 51.7 %all-gather.14.cloned.1.call-done = bf16[2048,1024]{1,0:T(8,128)(2,1)} async-done(((bf16[128,1024]{1,0:T(8,128)(2,1)}), bf16[2048,1024]{1,0:T(8,128)(2,1)}) %all-gather.14.cloned.1.call-update) | async-done | bytes 4194320 | tf_op jit(solution)/shard_map/all_gather | solution.py:88
  278.9 6.6 fusion.72
  287.6 26.6 all-reduce.10.cloned.1.call-done
  314.2 2.8 multiply_reduce_fusion.2
  319.5 189.8 %all-gather.18.cloned.1.call-done = bf16[2048,4096]{1,0:T(8,128)(2,1)} async-done(((bf16[128,4096]{1,0:T(8,128)(2,1)}), bf16[2048,4096]{1,0:T(8,128)(2,1)}) %all-gather.18.cloned.1.call-update) | async-done | bytes 16777232 | tf_op jit(solution)/shard_map/all_gather | solution.py:92
  509.3 14.6 fusion.74
  523.9 178.4 %all-gather.16.cloned.1.call-done = bf16[2048,4096]{1,0:T(8,128)(2,1)} async-done(((bf16[128,4096]{1,0:T(8,128)(2,1)}), bf16[2048,4096]{1,0:T(8,128)(2,1)}) %all-gather.16.cloned.1.call-update) | async-done | bytes 16777232 | tf_op jit(solution)/shard_map/all_gather | solution.py:91
  702.3 14.4 fusion.73
  716.7 178.6 %all-gather.20.cloned.1.call-done = bf16[2048,4096]{1,0:T(8,128)(2,1)} async-done(((bf16[128,4096]{1,0:T(8,128)(2,1)}), bf16[2048,4096]{1,0:T(8,128)(2,1)}) %all-gather.20.cloned.1.call-update) | async-done | bytes 16777232 | tf_op jit(solution)/shard_map/all_gather | solution.py:93
  895.3 22.8 multiply_convert_fusion
  918.0 13.3 fusion.75
  931.4 13.8 convolution_add_fusion
  945.2 14.6 convolution_convert_fusion
  959.9 12.8 all-reduce.14.cloned.1.call-done
  972.7 6.3 multiply_reduce_fusion
  979.1 18.9 all-reduce.12.cloned.1.call-done
  997.9 8.6 subtract_add_fusion
  1011.5 8.6 fusion.35
  1020.1 13.0 fusion.1
  1034.0 8.4 fusion.3
  1044.1 2.6 broadcast_multiply_fusion
  1052.5 2.4 fusion.76
  1056.1 2.7 add_add_fusion
  1058.9 19.8 convolution_bitcast_fusion
  1080.5 2.4 fusion.57
  1085.4 8.2 fusion.38
  1094.9 6.0 fusion.61
  1100.9 18.2 fusion.79
  1119.2 18.0 fusion.78
  1137.3 4.8 fusion.17
  1142.0 48.8 %all-reduce.4 = (f32[2048]{0:T(1024)}, f32[2048]{0:T(1024)}, f32[64]{0:T(128)}, f32[64]{0:T(128)}) all-reduce(f32[2048]{0:T(1024)S(1)} %get-tuple-element.43, f32[2048]{0:T(1024)S(1)} %copy-done.38, f32[64]{0:T(128)S(1)} %get-tuple-element.41, f32[64]{0:T(128)S(1)} %get-tuple-element.45), channel_id=1, replica_groups=mesh['dp'=16,'tensor'=2] {'dp','tensor'}, use_global_device_ids=true, to_apply=%region_18.19 | all-reduce | flops 4224 | bytes 33792 | tf_op jit(solution)/shard_map/psum | solution.py:221
  1190.8 6.6 fusion.14
  1197.5 579.1 %reduce-scatter.20.cloned.1.call-done = f32[128,4096]{0,1:T(8,128)} async-done(((f32[2048,4096]{0,1:T(8,128)}), f32[128,4096]{0,1:T(8,128)}) %reduce-scatter.20.cloned.1.call-update) | async-done | bytes 2097168 | tf_op jit(solution)/shard_map/reduce_scatter | solution.py:216
  1776.6 2.9 copy.49
  1779.4 75.6 %reduce-scatter.12.cloned.1.call-done = f32[128,256]{1,0:T(8,128)} async-done(((f32[2048,256]{1,0:T(8,128)}), f32[128,256]{1,0:T(8,128)}) %reduce-scatter.12.cloned.1.call-update) | async-done | bytes 131088 | tf_op jit(solution)/shard_map/reduce_scatter | solution.py:212
  1855.1 80.5 %reduce-scatter.10.cloned.1.call-done = f32[128,256]{1,0:T(8,128)} async-done(((f32[2048,256]{1,0:T(8,128)}), f32[128,256]{1,0:T(8,128)}) %reduce-scatter.10.cloned.1.call-update) | async-done | bytes 131088 | tf_op jit(solution)/shard_map/reduce_scatter | solution.py:211
  1935.6 187.8 %reduce-scatter.14.cloned.1.call-done = f32[128,1024]{1,0:T(8,128)} async-done(((f32[2048,1024]{1,0:T(8,128)}), f32[128,1024]{1,0:T(8,128)}) %reduce-scatter.14.cloned.1.call-update) | async-done | bytes 524304 | tf_op jit(solution)/shard_map/reduce_scatter | solution.py:213
  2123.4 183.0 %reduce-scatter.8.cloned.1.call-done = f32[128,1024]{1,0:T(8,128)} async-done(((f32[2048,1024]{1,0:T(8,128)}), f32[128,1024]{1,0:T(8,128)}) %reduce-scatter.8.cloned.1.call-update) | async-done | bytes 524304 | tf_op jit(solution)/shard_map/reduce_scatter | solution.py:210
  2306.4 688.9 %reduce-scatter.18.cloned.1.call-done = f32[128,4096]{1,0:T(8,128)} async-done(((f32[2048,4096]{1,0:T(8,128)}), f32[128,4096]{1,0:T(8,128)}) %reduce-scatter.18.cloned.1.call-update) | async-done | bytes 2097168 | tf_op jit(solution)/shard_map/reduce_scatter | solution.py:215
  2995.4 691.9 %reduce-scatter.16.cloned.1.call-done = f32[128,4096]{1,0:T(8,128)} async-done(((f32[2048,4096]{1,0:T(8,128)}), f32[128,4096]{1,0:T(8,128)}) %reduce-scatter.16.cloned.1.call-update) | async-done | bytes 2097168 | tf_op jit(solution)/shard_map/reduce_scatter | solution.py:214
  (190 shorter events, 39.5 us)
Async XLA Ops:
  7.2 59.7 %all-gather.10.cloned.1.call-start = ((), (), s32[]{:S(2)}) async-start(), calls=%async_computation.8 | async-start | bytes 1114112 | tf_op jit(solution)/shard_map/all_gather | solution.py:86
  7.9 115.8 %all-gather.8.cloned.1.call-start = ((), (), s32[]{:S(2)}) async-start(), calls=%async_computation.7 | async-start | bytes 1114112 | tf_op jit(solution)/shard_map/all_gather | solution.py:87
  8.7 192.9 %all-gather.12.cloned.1.call-start = ((), (), s32[]{:S(2)}) async-start(), calls=%async_computation.9 | async-start | bytes 4456448 | tf_op jit(solution)/shard_map/all_gather | solution.py:85
  9.4 269.5 %all-gather.14.cloned.1.call-start = ((), (), s32[]{:S(2)}) async-start(), calls=%async_computation.10 | async-start | bytes 4456448 | tf_op jit(solution)/shard_map/all_gather | solution.py:88
  10.0 304.3 %all-reduce.10.cloned.1.call-start = ((), (), s32[]{:S(2)}) async-start(), calls=%async_computation.11 | async-start | bytes 8388608 | tf_op jit(solution)/shard_map/psum | solution.py:135
  13.4 57.1 %copy-start.41 = (f32[64]{0:T(128)S(1)}, f32[64]{0:T(128)}, u32[]{:S(2)}) copy-start(f32[64]{0:T(128)} %param.20) | copy-start | bytes 772
  14.3 193.7 %copy-start.12 = (f32[512,64]{0,1:T(8,128)}, f32[512,64]{0,1:T(8,128)S(1)}, u32[]{:S(2)}) copy-start(f32[512,64]{0,1:T(8,128)S(1)} %get-tuple-element.71) | copy-start | bytes 393220
  14.3 193.7 %copy-start.15 = (f32[512,64]{0,1:T(8,128)}, f32[512,64]{0,1:T(8,128)S(1)}, u32[]{:S(2)}) copy-start(f32[512,64]{0,1:T(8,128)S(1)} %get-tuple-element.70) | copy-start | bytes 393220
  17.1 184.4 %copy-start.39 = (f32[512]{0:T(512)}, f32[512]{0:T(512)S(1)}, u32[]{:S(2)}) copy-start(f32[512]{0:T(512)S(1)} %get-tuple-element.73) | copy-start | bytes 6148
  66.9 56.9 %copy-start.4 = (bf16[512,2048]{1,0:T(8,128)(2,1)S(1)}, bf16[512,2048]{1,0:T(8,128)(2,1)}, u32[]{:S(2)}) copy-start(bf16[512,2048]{1,0:T(8,128)(2,1)} %param.14) | copy-start | bytes 6291460
  66.9 56.9 %copy-start.34 = (f32[2048]{0:T(1024)S(1)}, f32[2048]{0:T(1024)}, u32[]{:S(2)}) copy-start(f32[2048]{0:T(1024)} %param.17) | copy-start | bytes 24580
  126.6 80.3 %copy-start.43 = (f32[64]{0:T(128)S(1)}, f32[64]{0:T(128)}, u32[]{:S(2)}) copy-start(f32[64]{0:T(128)} %param.19) | copy-start | bytes 772
  208.9 10.8 copy-start.9
  208.9 10.8 copy-start.49
  219.7 7.4 copy-start.32
  227.1 51.7 %copy-start.17 = (bf16[4,64,4,512]{3,1,2,0:T(8,128)(2,1)}, bf16[4,64,4,512]{3,1,2,0:T(8,128)(2,1)S(1)}, u32[]{:S(2)}) copy-start(bf16[4,64,4,512]{3,1,2,0:T(8,128)(2,1)S(1)} %fusion.29) | copy-start | bytes 3145732
  285.5 28.8 copy-start.5
  285.5 223.8 %all-gather.18.cloned.1.call-start = ((), (), s32[]{:S(2)}) async-start(), calls=%async_computation.13 | async-start | bytes 17825792 | tf_op jit(solution)/shard_map/all_gather | solution.py:92
  286.1 416.2 %all-gather.16.cloned.1.call-start = ((), (), s32[]{:S(2)}) async-start(), calls=%async_computation.12 | async-start | bytes 17825792 | tf_op jit(solution)/shard_map/all_gather | solution.py:91
  286.8 608.4 %all-gather.20.cloned.1.call-start = ((), (), s32[]{:S(2)}) async-start(), calls=%async_computation.14 | async-start | bytes 17825792 | tf_op jit(solution)/shard_map/all_gather | solution.py:93
  287.6 31.5 copy-start.31
  287.6 685.2 %all-reduce.14.cloned.1.call-start = ((), (), s32[]{:S(2)}) async-start(), calls=%async_computation.16 | async-start | bytes 8388608 | tf_op jit(solution)/shard_map/psum | solution.py:160
  319.5 382.8 %copy-start.14 = (bf16[512,2048]{1,0:T(8,128)(2,1)}, bf16[512,2048]{1,0:T(8,128)(2,1)S(1)}, u32[]{:S(2)}) copy-start(bf16[512,2048]{1,0:T(8,128)(2,1)S(1)} %multiply_convert_fusion.3) | copy-start | bytes 6291460
  918.0 13.3 copy-start.51
  945.2 52.8 %all-reduce.12.cloned.1.call-start = ((), (), s32[]{:S(2)}) async-start(), calls=%async_computation.15 | async-start | bytes 4194304 | tf_op jit(solution)/shard_map/psum | solution.py:144
  959.9 38.1 %copy-start.46 = (f32[512]{0:T(512)S(1)}, f32[512]{0:T(512)}, u32[]{:S(2)}) copy-start(f32[512]{0:T(512)} %get-tuple-element.74) | copy-start | bytes 6148
  959.9 177.4 %all-reduce.16.cloned.1.call-start = ((), (), s32[]{:S(2)}) async-start(), calls=%async_computation.17 | async-start | bytes 8388608 | tf_op jit(solution)/shard_map/psum | solution.py:208
  997.9 10.6 copy-start.48
  1008.5 2.9 copy-start.33
  1011.5 8.6 copy-start.50
  1011.5 21.7 slice-start
  1011.5 21.7 slice-start.1
  1020.1 13.1 slice-start.2
  1020.1 13.9 slice-start.3
  1034.0 8.4 copy-start.23
  1044.0 2.8 copy-start.8
  1044.1 3.0 copy-start.37
  1044.1 3.0 copy-start.16
  1050.8 4.1 copy-start.19
  1058.9 717.7 %reduce-scatter.20.cloned.1.call-start = ((), (), s32[]{:S(2)}) async-start(), calls=%async_computation.24 | async-start | bytes 35651584 | tf_op jit(solution)/shard_map/reduce_scatter | solution.py:216
  1078.8 776.3 %reduce-scatter.12.cloned.1.call-start = ((), (), s32[]{:S(2)}) async-start(), calls=%async_computation.20 | async-start | bytes 2228224 | tf_op jit(solution)/shard_map/reduce_scatter | solution.py:212
  1082.9 852.7 %reduce-scatter.10.cloned.1.call-start = ((), (), s32[]{:S(2)}) async-start(), calls=%async_computation.19 | async-start | bytes 2228224 | tf_op jit(solution)/shard_map/reduce_scatter | solution.py:211
  1085.4 1038.1 %reduce-scatter.14.cloned.1.call-start = ((), (), s32[]{:S(2)}) async-start(), calls=%async_computation.21 | async-start | bytes 8912896 | tf_op jit(solution)/shard_map/reduce_scatter | solution.py:213
  1093.7 1212.8 %reduce-scatter.8.cloned.1.call-start = ((), (), s32[]{:S(2)}) async-start(), calls=%async_computation.18 | async-start | bytes 8912896 | tf_op jit(solution)/shard_map/reduce_scatter | solution.py:210
  1100.9 1894.5 %reduce-scatter.18.cloned.1.call-start = ((), (), s32[]{:S(2)}) async-start(), calls=%async_computation.23 | async-start | bytes 35651584 | tf_op jit(solution)/shard_map/reduce_scatter | solution.py:215
  1119.1 2568.1 %reduce-scatter.16.cloned.1.call-start = ((), (), s32[]{:S(2)}) async-start(), calls=%async_computation.22 | async-start | bytes 35651584 | tf_op jit(solution)/shard_map/reduce_scatter | solution.py:214
  1137.2 4.8 copy-start.38
  1137.2 53.6 %copy-start.45 = (f32[512]{0:T(512)S(1)}, f32[512]{0:T(512)}, u32[]{:S(2)}) copy-start(f32[512]{0:T(512)} %get-tuple-element.72) | copy-start | bytes 6148
  (26 other events, 43.5 us)
Sparse Core Ops, SparseCore 0:
  10.8 56.0 all-gather.9
  69.6 54.0 all-gather.7
  126.5 74.9 all-gather.11
  204.2 74.6 all-gather.13
  285.6 28.5 all-reduce.9
  317.2 191.9 all-gather.17
  512.4 189.7 all-gather.15
  705.4 189.7 all-gather.19
  945.3 27.3 all-reduce.13
  975.5 22.3 all-reduce.11
  1059.0 29.5 all-reduce.15
  1090.8 685.6 reduce-scatter.19
  1779.4 75.6 reduce-scatter.11
  1857.8 77.7 reduce-scatter.9
  1938.3 185.0 reduce-scatter.13
  2126.2 180.2 reduce-scatter.7
  2309.2 686.1 reduce-scatter.17
  2998.1 689.0 reduce-scatter.15
where the time goes:
time: 3710 us; the launch traced here: 3690 us
  waiting for transfers between devices  3320 us (89%)
  matrix products  238 us (6%)
  other arithmetic  50.7 us (1%)
  blocking collectives  48.8 us (1%)
    reduce_scatter x1, waiting for transfers between devices, local(): lax.psum_scatter(w_gate_grad, 'dp', scatter_dimension=0, tiled=True)  692 us
    reduce_scatter x1, waiting for transfers between devices, local(): lax.psum_scatter(w_up_grad, 'dp', scatter_dimension=0, tiled=True)  689 us
    reduce_scatter x1, waiting for transfers between devices, local(): lax.psum_scatter(w_down_grad, 'dp', scatter_dimension=0, tiled=True)  579 us
    all_gather x1, waiting for transfers between devices, local(): lax.all_gather(w_up, 'dp', axis=0, tiled=True)  190 us
    reduce_scatter x1, waiting for transfers between devices, local(): lax.psum_scatter(w_out_grad, 'dp', scatter_dimension=0, tiled=True)  188 us
    reduce_scatter x1, waiting for transfers between devices, local(): lax.psum_scatter(w_query_grad, 'dp', scatter_dimension=0, tiled=True)  183 us
    all_gather x1, waiting for transfers between devices, local(): lax.all_gather(w_down, 'dp', axis=0, tiled=True)  179 us
    all_gather x1, waiting for transfers between devices, local(): lax.all_gather(w_gate, 'dp', axis=0, tiled=True)  178 us
  transfers between devices with their start and end apart: 18, of which 17 were waited for; matrix products, arithmetic and copies ran while one was open for 5% of the time, Pallas kernels for 0%

commit v1 on v0

v1 whole, which is shorter than its diff:
```python
import jax
import jax.numpy as jnp
from jax import lax
from jax.sharding import PartitionSpec as P

eps = 1e-05
rope_base = 1000000.0
group = 4
sub_count = 2


def norm_rows(values, gain):
    scale = lax.rsqrt(jnp.mean(values * values, axis=-1, keepdims=True) + eps)
    return (values * scale * gain, scale)


def norm_back(values, scale, gain, incoming):
    weighted = incoming * gain
    return scale * weighted - values * (scale * scale * scale) * jnp.mean(
        weighted * values, axis=-1, keepdims=True
    )


def positions_of(segment_row):
    row_index = jnp.arange(segment_row.shape[0], dtype=jnp.int32)
    earlier = jnp.concatenate([segment_row[:1] - 1, segment_row[:-1]])
    starts = jnp.where(segment_row != earlier, row_index, jnp.zeros_like(row_index))
    return row_index - lax.cummax(starts, axis=0)


def angles(positions, width):
    frequency = rope_base ** (-jnp.arange(0, width, 2, dtype=jnp.float32) / width)
    phases = positions.astype(jnp.float32)[..., None] * frequency
    phases = jnp.concatenate([phases, phases], axis=-1)
    return (jnp.cos(phases)[..., None, :], jnp.sin(phases)[..., None, :])


def head_prepare(raw_heads, gain, cosine_table, sine_table):
    scaled = (
        raw_heads * lax.rsqrt(jnp.mean(raw_heads * raw_heads, axis=-1, keepdims=True) + eps) * gain
    )
    half_width = scaled.shape[-1] // 2
    turned = jnp.concatenate([-scaled[..., half_width:], scaled[..., :half_width]], axis=-1)
    return scaled * cosine_table + turned * sine_table


def rows_product(left, right):
    return lax.dot_general(
        left, right, (((0,), (0,)), ((), ())), preferred_element_type=jnp.float32
    )


def cols_product(left, right):
    return lax.dot_general(
        left, right, (((1,), (1,)), ((), ())), preferred_element_type=jnp.float32
    )


def swap_cores(values):
    return lax.ppermute(values, "tensor", [(0, 1), (1, 0)])


class Lines:
    def __init__(self, dp):
        self.dp = dp
        self.length = dp // group
        index = lax.axis_index("dp")
        self.place = index % group
        self.spot = index // group

    def flip(self, values, relation):
        return lax.ppermute(values, "dp", [(i, i ^ relation) for i in range(self.dp)])

    def hop(self, values, first, last, step):
        pairs = [
            (spot * group + place, (spot + step) * group + place)
            for spot in range(first, last + 1)
            for place in range(group)
        ]
        return lax.ppermute(values, "dp", pairs)

    def turn(self, values, step):
        pairs = [
            (spot * group + place, ((spot + step) % self.length) * group + place)
            for spot in range(self.length)
            for place in range(group)
        ]
        return lax.ppermute(values, "dp", pairs)

    def by_place(self, related):
        odd = self.place % 2 == 1
        high = self.place // 2 == 1
        own, one, two, three = related
        pairs = (
            (jnp.where(odd, one, own), jnp.where(odd, own, one)),
            (jnp.where(odd, three, two), jnp.where(odd, two, three)),
        )
        return [
            jnp.where(high, pairs[1][0], pairs[0][0]),
            jnp.where(high, pairs[1][1], pairs[0][1]),
            jnp.where(high, pairs[0][0], pairs[1][0]),
            jnp.where(high, pairs[0][1], pairs[1][1]),
        ]

    def share_columns(self, piece_of):
        pieces = [piece_of(self.place ^ relation) for relation in range(group)]
        related = [pieces[0]] + [self.flip(pieces[r], r) for r in range(1, group)]
        return jnp.concatenate(self.by_place(related), axis=0)

    def gather_line(self, block):
        length = self.length
        if length != 4:
            return [block] + [self.turn(block, -k) for k in range(1, length)]
        ups, downs = [block], [block]
        for k in range(1, length):
            ups.append(self.hop(ups[-1], k - 1, length - 2, 1))
            downs.append(self.hop(downs[-1], 1, length - k, -1))
        return [block] + [
            jnp.where(self.spot + k < length, downs[k], ups[length - k])
            for k in range(1, length)
        ]

    def scatter_line(self, blocks):
        length = self.length
        total = blocks[0].astype(jnp.float32)
        if length != 4:
            for k in range(1, length):
                total = total + self.turn(blocks[k], k).astype(jnp.float32)
            return total
        up = down = None
        for s in range(1, length):
            send_up, send_down = blocks[length - s], blocks[s]
            if up is not None:
                send_up = (send_up.astype(jnp.float32) + up.astype(jnp.float32)).astype(jnp.bfloat16)
                send_down = (send_down.astype(jnp.float32) + down.astype(jnp.float32)).astype(
                    jnp.bfloat16
                )
            up = self.hop(send_up, 0, min(s - 1, length - 2), 1)
            down = self.hop(send_down, max(length - s, 1), length - 1, -1)
        return total + up.astype(jnp.float32) + down.astype(jnp.float32)

    def share_rows(self, total):
        rows = total.shape[0] // group
        parts = total.astype(jnp.bfloat16)
        related = [lax.dynamic_slice_in_dim(total, self.place * rows, rows)]
        for r in range(1, group):
            piece = lax.dynamic_slice_in_dim(parts, (self.place ^ r) * rows, rows)
            related.append(self.flip(piece, r).astype(jnp.float32))
        return self.by_place(related)

    def gather_tokens(self, mine):
        kept = [mine] + [self.flip(mine, r) for r in range(1, group)]
        return jnp.stack([jnp.stack([one, swap_cores(one)]) for one in kept])

    def scatter_tokens(self, part):
        total = None
        for r in range(1, group):
            both = part[r, 0].astype(jnp.float32) + swap_cores(part[r, 1]).astype(jnp.float32)
            term = self.flip(both.astype(jnp.bfloat16), r).astype(jnp.float32)
            total = term if total is None else total + term
        return total + part[0, 0].astype(jnp.float32) + swap_cores(part[0, 1]).astype(jnp.float32)


def sum_all(values, dp):
    bit = 1
    while bit < dp:
        values = values + lax.ppermute(values, "dp", [(i, i ^ bit) for i in range(dp)])
        bit *= 2
    return values + swap_cores(values)


def local(
    dp,
    tokens,
    segments,
    cotangent,
    attn_gain,
    ffn_gain,
    query_gain,
    key_gain,
    w_query,
    key_weight,
    value_weight,
    w_out,
    w_gate,
    w_up,
    w_down,
):
    lines = Lines(dp)
    core = lax.axis_index("tensor")
    length, width = tokens.shape
    half = length // 2
    head_dim = query_gain.shape[0]
    rows = w_query.shape[0]
    block_rows = rows * group
    query_width = w_query.shape[1] // group
    key_width = key_weight.shape[1] // group
    query_heads = query_width // head_dim
    value_heads = key_width // head_dim
    query_group_count = query_heads // value_heads
    ff = w_gate.shape[1] // group
    ff_sub = ff // sub_count
    all_tokens = group * length

    def around(values):
        return jnp.roll(values, -lines.spot * block_rows, axis=-1)

    def back_around(values):
        return jnp.roll(values, lines.spot * block_rows, axis=-1)

    def halves(values, axis=0):
        return jnp.roll(values, -core * half, axis=axis)

    attn_gain_r, ffn_gain_r = around(attn_gain), around(ffn_gain)

    def columns(weight, start, size):
        return lax.dynamic_slice_in_dim(weight, start, size, axis=1)

    qkv_block = lines.share_columns(
        lambda j: jnp.concatenate(
            [
                columns(w_query, j * query_width, query_width),
                columns(key_weight, j * key_width, key_width),
                columns(value_weight, j * key_width, key_width),
            ],
            axis=1,
        )
    )
    out_block = lines.share_columns(lambda j: columns(w_out, j * query_width, query_width))
    qkv_w = jnp.concatenate(lines.gather_line(qkv_block), axis=0)
    out_w = jnp.concatenate(lines.gather_line(out_block), axis=0)
    gate_up_w, down_w = [], []
    for s in range(sub_count):
        ffn_block = lines.share_columns(
            lambda j: jnp.concatenate(
                [
                    columns(weight, s * group * ff_sub + j * ff_sub, ff_sub)
                    for weight in (w_gate, w_up, w_down)
                ],
                axis=1,
            )
        )
        got = lines.gather_line(ffn_block)
        gate_up_w.append(jnp.concatenate([b[:, : 2 * ff_sub] for b in got], axis=0))
        down_w.append(jnp.concatenate([b[:, 2 * ff_sub :] for b in got], axis=0))

    seg_all = jnp.stack([segments[0]] + [lines.flip(segments, r)[0] for r in range(1, group)])
    positions = halves(jax.vmap(positions_of)(seg_all), axis=1)
    seg_all = halves(seg_all, axis=1)
    row_index = halves(jnp.arange(length, dtype=jnp.int32))
    allowed = (seg_all[:, :, None] == seg_all[:, None, :]) & (
        row_index[:, None] >= row_index[None, :]
    )
    cosine_table, sine_table = angles(positions, head_dim)

    source = around(lax.dynamic_slice_in_dim(tokens, core * half, half)).astype(jnp.float32)
    normed_f, scale_first = norm_rows(source, attn_gain_r)
    normed = lines.gather_tokens(normed_f.astype(jnp.bfloat16)).reshape(all_tokens, width)
    cot_half = around(lax.dynamic_slice_in_dim(cotangent, core * half, half))
    out_b = lines.gather_tokens(cot_half.astype(jnp.bfloat16)).reshape(all_tokens, width)

    qkv = jnp.dot(normed, qkv_w, preferred_element_type=jnp.float32)
    query_raw = qkv[:, :query_width].reshape(group, length, query_heads, head_dim)
    key_raw = qkv[:, query_width : query_width + key_width].reshape(
        group, length, value_heads, head_dim
    )
    value = (
        qkv[:, query_width + key_width :]
        .astype(jnp.bfloat16)
        .reshape(group, length, value_heads, head_dim)
    )
    query_turned, query_pull = jax.vjp(
        lambda raw_in, gain_in: head_prepare(raw_in, gain_in, cosine_table, sine_table),
        query_raw,
        query_gain,
    )
    key_turned, key_pull = jax.vjp(
        lambda raw_in, gain_in: head_prepare(raw_in, gain_in, cosine_table, sine_table),
        key_raw,
        key_gain,
    )
    query = query_turned.astype(jnp.bfloat16).reshape(
        group, length, value_heads, query_group_count, head_dim
    )
    key = key_turned.astype(jnp.bfloat16)
    scores = 0.125 * jnp.einsum("shcfw,skcw->scfhk", query, key, preferred_element_type=jnp.float32)
    scores = jnp.where(allowed[:, None, None], scores, -1000000000.0)
    probs_f = jax.nn.softmax(scores, axis=-1)
    probs = probs_f.astype(jnp.bfloat16)
    heads_out = jnp.einsum("scfhk,skcw->shcfw", probs, value, preferred_element_type=jnp.float32)
    heads_out = heads_out.astype(jnp.bfloat16).reshape(all_tokens, query_width)
    attended_part = cols_product(heads_out, out_w).astype(jnp.bfloat16)
    attended = lines.scatter_tokens(attended_part.reshape(group, 2, half, width))

    state = source + attended
    normed2_f, scale_second = norm_rows(state, ffn_gain_r)
    normed2 = lines.gather_tokens(normed2_f.astype(jnp.bfloat16)).reshape(all_tokens, width)
    branch_part = normed2_part = None
    ffn_grads = []
    for s in range(sub_count):
        gate_up = jnp.dot(normed2, gate_up_w[s], preferred_element_type=jnp.float32)
        gate, up = gate_up[:, :ff_sub], gate_up[:, ff_sub:]
        sigmoid_gate = jax.nn.sigmoid(gate)
        silu_gate = gate * sigmoid_gate
        inner = (silu_gate * up).astype(jnp.bfloat16)
        inner_grad = jnp.dot(out_b, down_w[s], preferred_element_type=jnp.float32)
        gate_grad = (inner_grad * up * sigmoid_gate * (1.0 + gate * (1.0 - sigmoid_gate))).astype(
            jnp.bfloat16
        )
        up_grad = (inner_grad * silu_gate).astype(jnp.bfloat16)
        both_grad = jnp.concatenate([gate_grad, up_grad], axis=1)
        gate_up_g = rows_product(normed2, both_grad).astype(jnp.bfloat16)
        down_g = rows_product(out_b, inner).astype(jnp.bfloat16)
        blocks = [
            jnp.concatenate(
                [
                    gate_up_g[k * block_rows : (k + 1) * block_rows],
                    down_g[k * block_rows : (k + 1) * block_rows],
                ],
                axis=1,
            )
            for k in range(lines.length)
        ]
        ffn_grads.append(lines.share_rows(lines.scatter_line(blocks)))
        more = cols_product(both_grad, gate_up_w[s])
        normed2_part = more if normed2_part is None else normed2_part + more
        more = cols_product(inner, down_w[s])
        branch_part = more if branch_part is None else branch_part + more
    normed2_grad = lines.scatter_tokens(
        normed2_part.astype(jnp.bfloat16).reshape(group, 2, half, width)
    )
    ffn_gain_part = jnp.sum(normed2_grad * state * scale_second, axis=0)
    state_grad = cot_half + norm_back(state, scale_second, ffn_gain_r, normed2_grad)

    attended_b = lines.gather_tokens(state_grad.astype(jnp.bfloat16)).reshape(all_tokens, width)
    heads_grad = jnp.dot(attended_b, out_w, preferred_element_type=jnp.float32).astype(jnp.bfloat16)
    heads_grad = heads_grad.reshape(group, length, value_heads, query_group_count, head_dim)

    def attention_grads(product):
        return lines.share_rows(
            lines.scatter_line(
                [product[k * block_rows : (k + 1) * block_rows] for k in range(lines.length)]
            )
        )

    out_grads = attention_grads(rows_product(attended_b, heads_out).astype(jnp.bfloat16))
    probs_grad = jnp.einsum(
        "shcfw,skcw->scfhk", heads_grad, value, preferred_element_type=jnp.float32
    )
    value_grad = jnp.einsum("scfhk,shcfw->skcw", probs, heads_grad, preferred_element_type=jnp.float32)
    value_grad = value_grad.astype(jnp.bfloat16).reshape(all_tokens, key_width)
    score_grad = probs_f * (probs_grad - jnp.sum(probs_f * probs_grad, axis=-1, keepdims=True))
    score_grad = score_grad.astype(jnp.bfloat16)
    query_grad = 0.125 * jnp.einsum(
        "scfhk,skcw->shcfw", score_grad, key, preferred_element_type=jnp.float32
    )
    key_grad = 0.125 * jnp.einsum(
        "scfhk,shcfw->skcw", score_grad, query, preferred_element_type=jnp.float32
    )
    query_raw_grad, query_gain_part = query_pull(
        query_grad.reshape(group, length, query_heads, head_dim)
    )
    key_raw_grad, key_gain_part = key_pull(key_grad)
    qkv_grad = jnp.concatenate(
        [
            query_raw_grad.astype(jnp.bfloat16).reshape(all_tokens, query_width),
            key_raw_grad.astype(jnp.bfloat16).reshape(all_tokens, key_width),
            value_grad,
        ],
        axis=1,
    )
    qkv_grads = attention_grads(rows_product(normed, qkv_grad).astype(jnp.bfloat16))
    normed_part = cols_product(qkv_grad, qkv_w).astype(jnp.bfloat16)
    normed_grad = lines.scatter_tokens(normed_part.reshape(group, 2, half, width))
    attn_gain_part = jnp.sum(normed_grad * source * scale_first, axis=0)
    input_grad = state_grad + norm_back(source, scale_first, attn_gain_r, normed_grad)
    mixed = state + lines.scatter_tokens(
        branch_part.astype(jnp.bfloat16).reshape(group, 2, half, width)
    )

    def whole_rows(mine):
        mine = back_around(mine)
        return jnp.roll(jnp.concatenate([mine, swap_cores(mine)], axis=0), core * half, axis=0)

    gains = sum_all(
        jnp.concatenate(
            [
                back_around(attn_gain_part),
                back_around(ffn_gain_part),
                query_gain_part,
                key_gain_part,
            ]
        ),
        dp,
    )

    def columns_of(blocks, start, stop):
        return jnp.concatenate([b[:, start:stop] for b in blocks], axis=1)

    def ffn_columns(which):
        return jnp.concatenate(
            [columns_of(blocks, which * ff_sub, (which + 1) * ff_sub) for blocks in ffn_grads],
            axis=1,
        )

    return (
        whole_rows(mixed),
        whole_rows(input_grad),
        gains[:width],
        gains[width : 2 * width],
        gains[2 * width : 2 * width + head_dim],
        gains[2 * width + head_dim :],
        columns_of(qkv_grads, 0, query_width),
        columns_of(qkv_grads, query_width, query_width + key_width),
        columns_of(qkv_grads, query_width + key_width, query_width + 2 * key_width),
        columns_of(out_grads, 0, query_width),
        ffn_columns(0),
        ffn_columns(1),
        ffn_columns(2),
    )


def solution(mesh):
    dp = mesh.shape["dp"]
    weight = P("dp", "tensor")
    rows = P("dp", None)
    return jax.shard_map(
        lambda *arrays: local(dp, *arrays),
        mesh=mesh,
        in_specs=(rows, rows, rows, P(), P(), P(), P()) + (weight,) * 7,
        out_specs=(rows, rows, P(), P(), P(), P()) + (weight,) * 7,
        check_vma=False,
    )
```

time: 3710 us -> 1100 us (0.30)
  waiting for transfers between devices: 3320 us -> 371 us
  starting transfers between devices: 0.72 us -> 240 us
  local copies, waits for them, and re-layouts: 16.7 us -> 123 us
  other arithmetic: 50.7 us -> 155 us
  blocking collectives: 48.8 us -> 0 us
  matrix products: 238 us -> 196 us
    reduce_scatter x7 -> x0, waiting for transfers between devices: 2490 us -> none  [the longest x1 692 us: local(): lax.psum_scatter(w_gate_grad, 'dp', scatter_dimension=0, tiled=True)]
    all_gather x7 -> x0, waiting for transfers between devices: 773 us -> none  [the longest x1 190 us: local(): lax.all_gather(w_up, 'dp', axis=0, tiled=True)]
    ppermute x0 -> x138, waiting for transfers between devices: none -> 371 us  [the longest x48 198 us: hop(): return lax.ppermute(values, 'dp', pairs)]
    ppermute x0 -> x138, starting transfers between devices: none -> 240 us  [the longest x48 108 us: hop(): return lax.ppermute(values, 'dp', pairs)]
    psum x4 -> x0, waiting for transfers between devices: 58.3 us -> none  [the longest x1 26.6 us: local(): attended = lax.psum(cols_product(head_outputs, out_full), 'tensor')]
    psum x1 -> x0, blocking collectives: 48.8 us -> none  [local(): lax.psum((attn_gain_part, ffn_gain_part, query_gain_part, key_gain_part),...]
    unnamed x113 -> x412, local copies, waits for them, and re-layouts: 14.8 us -> 63.4 us
    convert_element_type x5 -> x25, other arithmetic: 9.69 us -> 47.8 us  [the longest x4 15.4 us: scatter_tokens(): term = self.flip(both.astype(jnp.bfloat16), r).astype(jnp.float32)]
  transfers between devices with their start and end apart: 18 -> 138, of which waited for: 17 -> 36; matrix products, arithmetic and copies ran while one was open for 5% -> 30% of each run, Pallas kernels for 0% -> 0%
where the time goes in v1:
time: 1100 us; the launch traced here: 1090 us
  waiting for transfers between devices  371 us (34%)
  starting transfers between devices  240 us (22%)
  matrix products  196 us (18%)
  other arithmetic  155 us (14%)
  local copies, waits for them, and re-layouts  123 us (11%)
    ppermute x48, waiting for transfers between devices, hop(): return lax.ppermute(values, 'dp', pairs)  198 us
    ppermute x51, waiting for transfers between devices, flip(): lax.ppermute(values, 'dp', [(i, i ^ relation) for i in range(self.dp)])  166 us
    ppermute x48, starting transfers between devices, hop(): return lax.ppermute(values, 'dp', pairs)  108 us
    ppermute x35, starting transfers between devices, swap_cores(): return lax.ppermute(values, 'tensor', [(0, 1), (1, 0)])  82.4 us
    unnamed x412, local copies, waits for them, and re-layouts  63.4 us
    dot_general x6, matrix products, cols_product(): lax.dot_general(left, right, (((1,), (1,)), ((), ())), preferred_element_...  61.7 us
    ppermute x51, starting transfers between devices, flip(): lax.ppermute(values, 'dp', [(i, i ^ relation) for i in range(self.dp)])  46.1 us
    dot_general x6, matrix products, rows_product(): lax.dot_general(left, right, (((0,), (0,)), ((), ())), preferred_element_...  43.5 us
  transfers between devices with their start and end apart: 138, of which 36 were waited for; matrix products, arithmetic and copies ran while one was open for 30% of the time, Pallas kernels for 0%

profile of v1, /device:TPU:1, one launch (start us, length us, event | category | flops | bytes accessed | tf_op | source)
XLA Modules:
  0.0 1089.3 jit_solution(13584845837007484688)
XLA Ops:
  91.0 5.6 collective-permute-start
  113.3 6.2 collective-permute-done.26
  123.7 6.1 collective-permute-done.27
  133.0 7.1 collective-permute-start.2
  140.2 14.4 %collective-permute-start.4 = (bf16[256,2048]{1,0:T(8,128)(2,1)S(1)}, bf16[256,2048]{1,0:T(8,128)(2,1)S(1)}, u32[]{:S(2)}, u32[]{:S(2)}) collective-permute-start(bf16[256,2048]{1,0:T(8,128)(2,1)S(1)} %collective-permute-done.3), channel_id=1, source_target_pairs={{0,1},{1,0},{2,3},{3,2},{4,5},{5,4},{6,7},{7,6},{8,9},{9,8},{10,11... | collective-permute-start | bytes 3145736 | tf_op jit(solution)/shard_map/ppermute | solution.py:60
  158.3 11.2 %collective-permute-done.15 = bf16[512,384]{0,1:T(8,128)(2,1)S(1)} collective-permute-done((bf16[512,384]{0,1:T(8,128)(2,1)S(1)}, bf16[512,384]{0,1:T(8,128)(2,1)S(1)}, u32[]{:S(2)}, u32[]{:S(2)}) %collective-permute-start.15) | collective-permute-done | bytes 393248 | tf_op jit(solution)/shard_map/ppermute | solution.py:80
  211.2 5.6 fusion.62
  223.9 19.7 %collective-permute-done.54 = bf16[512,1536]{0,1:T(8,128)(2,1)S(1)} collective-permute-done((bf16[512,1536]{0,1:T(8,128)(2,1)}, bf16[512,1536]{0,1:T(8,128)(2,1)S(1)}, u32[]{:S(2)}, u32[]{:S(2)}) %collective-permute-start.54) | collective-permute-done | bytes 1572896 | tf_op jit(solution)/shard_map/ppermute | solution.py:80
  257.6 19.7 %collective-permute-done.45 = bf16[512,1536]{0,1:T(8,128)(2,1)S(1)} collective-permute-done((bf16[512,1536]{0,1:T(8,128)(2,1)S(1)}, bf16[512,1536]{0,1:T(8,128)(2,1)S(1)}, u32[]{:S(2)}, u32[]{:S(2)}) %collective-permute-start.45) | collective-permute-done | bytes 1572896 | tf_op jit(solution)/shard_map/ppermute | solution.py:80
  291.5 24.5 %collective-permute-done.58 = bf16[512,1536]{0,1:T(8,128)(2,1)} collective-permute-done((bf16[512,1536]{0,1:T(8,128)(2,1)S(1)}, bf16[512,1536]{0,1:T(8,128)(2,1)}, u32[]{:S(2)}, u32[]{:S(2)}) %collective-permute-start.58) | collective-permute-done | bytes 1572896 | tf_op jit(solution)/shard_map/ppermute | solution.py:80
  320.7 28.8 %collective-permute-done.49 = bf16[512,1536]{0,1:T(8,128)(2,1)S(1)} collective-permute-done((bf16[512,1536]{0,1:T(8,128)(2,1)S(1)}, bf16[512,1536]{0,1:T(8,128)(2,1)S(1)}, u32[]{:S(2)}, u32[]{:S(2)}) %collective-permute-start.49) | collective-permute-done | bytes 1572896 | tf_op jit(solution)/shard_map/ppermute | solution.py:80
  354.6 7.4 collective-permute-done.31
  370.3 17.5 %collective-permute-done.59 = bf16[512,1536]{0,1:T(8,128)(2,1)S(1)} collective-permute-done((bf16[512,1536]{0,1:T(8,128)(2,1)}, bf16[512,1536]{0,1:T(8,128)(2,1)S(1)}, u32[]{:S(2)}, u32[]{:S(2)}) %collective-permute-start.59) | collective-permute-done | bytes 1572896 | tf_op jit(solution)/shard_map/ppermute | solution.py:80
  389.3 7.0 collective-permute-start.35
  396.5 20.1 %collective-permute-start.39 = (bf16[256,2048]{1,0:T(8,128)(2,1)S(1)}, bf16[256,2048]{1,0:T(8,128)(2,1)S(1)}, u32[]{:S(2)}, u32[]{:S(2)}) collective-permute-start(bf16[256,2048]{1,0:T(8,128)(2,1)S(1)} %collective-permute-done.38), channel_id=1, source_target_pairs={{0,1},{1,0},{2,3},{3,2},{4,5},{5,4},{6,7},{7,6},{8,9},{9,8},{10,11... | collective-permute-start | bytes 3145736 | tf_op jit(solution)/shard_map/ppermute | solution.py:60
  430.0 13.6 %fusion.87 = f32[2048,1024]{0,1:T(8,128)} fusion(bf16[2048,2048]{1,0:T(8,128)(2,1)} %bitcast.396, bf16[512,1024]{0,1:T(8,128)(2,1)S(1)} %slice.538, bf16[512,1024]{0,1:T(8,128)(2,1)S(1)} %copy-done.69, bf16[512,1024]{0,1:T(8,128)(2,1)S(1)} %slice.536, bf16[512,1024]{0,1:T(8,128)(2,1)S(1)} %copy-done.67), kind=kOutput, calls=%fused_computation.251 | convolution fusion | flops 8606711808 | bytes 20971520 | tf_op jit(solution)/shard_map/dot_general | solution.py:301
  443.6 10.5 multiply_convert_fusion.1
  454.1 6.5 convolution_convert_fusion.4
  460.7 8.5 fusion.105
  469.1 12.4 %convolution_convert_fusion.2 = bf16[2048,1024]{0,1:T(8,128)(2,1)} fusion(bf16[2048,2048]{1,0:T(8,128)(2,1)S(1)} %bitcast.401, bf16[2048,512]{0,1:T(8,128)(2,1)} %get-tuple-element.114, bf16[2048,512]{0,1:T(8,128)(2,1)} %get-tuple-element.113), kind=kOutput, calls=%fused_computation.69 | convolution fusion | flops 8600420352 | bytes 16777216 | tf_op jit(solution)/shard_map/dot_general | solution.py:48
  481.5 15.0 %fusion.24 = f32[2048,2048]{1,0:T(8,128)} fusion(bf16[2048,512]{0,1:T(8,128)(2,1)} %get-tuple-element.114, bf16[2048,512]{0,1:T(8,128)(2,1)} %get-tuple-element.113, bf16[512,1024]{0,1:T(8,128)(2,1)} %copy-done.72, bf16[512,1024]{0,1:T(8,128)(2,1)S(1)} %copy-done.69, bf16[512,1024]{0,1:T(8,128)(2,1)} %copy-done.71, bf16[512,1024]{0,1:T(8,128)(2,1)S(1)} %copy-done.67), kind=kOutput, calls=%fused_computation.85 | convolution fusion | flops 8615100416 | bytes 25165824 | tf_op jit(solution)/shard_map/dot_general | solution.py:54
  496.6 13.9 %fusion.88 = f32[2048,1024]{0,1:T(8,128)} fusion(bf16[2048,2048]{1,0:T(8,128)(2,1)} %bitcast.397, bf16[512,1024]{0,1:T(8,128)(2,1)} %slice.528, bf16[512,1024]{0,1:T(8,128)(2,1)S(1)} %copy-done.68, bf16[512,1024]{0,1:T(8,128)(2,1)S(1)} %slice.526, bf16[512,1024]{0,1:T(8,128)(2,1)S(1)} %copy-done.66), kind=kOutput, calls=%fused_computation.252 | convolution fusion | flops 8606711808 | bytes 20971520 | tf_op jit(solution)/shard_map/dot_general | solution.py:301
  510.5 10.2 multiply_convert_fusion.3
  522.0 5.8 convolution_convert_fusion.5
  527.8 14.5 %add_convert_fusion.1 = bf16[2048,2048]{1,0:T(8,128)(2,1)} fusion(f32[2048,2048]{1,0:T(8,128)} %fusion.105, bf16[2048,512]{0,1:T(8,128)(2,1)} %copy-done.163, bf16[512,512]{0,1:T(8,128)(2,1)} %slice.534, bf16[512,512]{0,1:T(8,128)(2,1)S(1)} %copy-done.91, bf16[512,512]{0,1:T(8,128)(2,1)S(1)} %copy-done.94, bf16[512,512]{0,1:T(8,128)(2,1)S(1)} %copy-done.89), kind=kOutput, calls=%fused_computation.7 | convolution fusion | flops 4311744512 | bytes 29360128 | tf_op jit(solution)/shard_map/dot_general | solution.py:54
  550.3 13.0 %convolution_convert_fusion.3 = bf16[2048,1024]{0,1:T(8,128)(2,1)} fusion(bf16[2048,2048]{1,0:T(8,128)(2,1)} %bitcast.398, bf16[2048,512]{0,1:T(8,128)(2,1)S(1)} %copy-done.165, bf16[2048,512]{0,1:T(8,128)(2,1)S(1)} %copy-done.164), kind=kOutput, calls=%fused_computation.70 | convolution fusion | flops 8600420352 | bytes 16777216 | tf_op jit(solution)/shard_map/dot_general | solution.py:48
  563.3 16.6 %add_convert_fusion = bf16[2048,2048]{1,0:T(8,128)(2,1)} fusion(f32[2048,2048]{1,0:T(8,128)} %fusion.24, bf16[2048,512]{0,1:T(8,128)(2,1)} %get-tuple-element.112, bf16[2048,512]{0,1:T(8,128)(2,1)} %get-tuple-element.111, bf16[512,1024]{0,1:T(8,128)(2,1)} %slice.528, bf16[512,1024]{0,1:T(8,128)(2,1)} %slice.527, bf16[512,1024]{0,1:T(8,128)(2,1)} %copy-done.70, ...), kind=kOutput, calls=%fused_computation.6 | convolution fusion | flops 8623489024 | bytes 33554432 | tf_op jit(solution)/shard_map/dot_general | solution.py:54
  611.9 17.4 %collective-permute-done.129 = bf16[512,1536]{0,1:T(8,128)(2,1)} collective-permute-done((bf16[512,1536]{0,1:T(8,128)(2,1)S(1)}, bf16[512,1536]{0,1:T(8,128)(2,1)}, u32[]{:S(2)}, u32[]{:S(2)}) %collective-permute-start.129) | collective-permute-done | bytes 1572896 | tf_op jit(solution)/shard_map/ppermute | solution.py:80
  636.3 12.4 %collective-permute-done.80 = bf16[256,2048]{1,0:T(8,128)(2,1)} collective-permute-done((bf16[256,2048]{1,0:T(8,128)(2,1)}, bf16[256,2048]{1,0:T(8,128)(2,1)}, u32[]{:S(2)}, u32[]{:S(2)}) %collective-permute-start.80) | collective-permute-done | bytes 1048608 | tf_op jit(solution)/shard_map/ppermute | solution.py:72
  657.8 13.2 %collective-permute-done.61 = bf16[256,2048]{1,0:T(8,128)(2,1)} collective-permute-done((bf16[256,2048]{1,0:T(8,128)(2,1)}, bf16[256,2048]{1,0:T(8,128)(2,1)}, u32[]{:S(2)}, u32[]{:S(2)}) %collective-permute-start.61) | collective-permute-done | bytes 1048608 | tf_op jit(solution)/shard_map/ppermute | solution.py:72
  673.2 20.5 %collective-permute-done.65 = bf16[256,2048]{1,0:T(8,128)(2,1)} collective-permute-done((bf16[256,2048]{1,0:T(8,128)(2,1)}, bf16[256,2048]{1,0:T(8,128)(2,1)}, u32[]{:S(2)}, u32[]{:S(2)}) %collective-permute-start.65) | collective-permute-done | bytes 1048608 | tf_op jit(solution)/shard_map/ppermute | solution.py:72
  714.0 17.7 %collective-permute-done.83 = bf16[256,2048]{1,0:T(8,128)(2,1)S(1)} collective-permute-done((bf16[256,2048]{1,0:T(8,128)(2,1)S(1)}, bf16[256,2048]{1,0:T(8,128)(2,1)S(1)}, u32[]{:S(2)}, u32[]{:S(2)}) %collective-permute-start.83) | collective-permute-done | bytes 1048608 | tf_op jit(solution)/shard_map/ppermute | solution.py:72
  732.9 21.4 %collective-permute-done.85 = bf16[256,2048]{1,0:T(8,128)(2,1)S(1)} collective-permute-done((bf16[256,2048]{1,0:T(8,128)(2,1)S(1)}, bf16[256,2048]{1,0:T(8,128)(2,1)S(1)}, u32[]{:S(2)}, u32[]{:S(2)}) %collective-permute-start.85) | collective-permute-done | bytes 1048608 | tf_op jit(solution)/shard_map/ppermute | solution.py:72
  758.5 17.2 %collective-permute-start.131 = (bf16[512,1536]{0,1:T(8,128)(2,1)}, bf16[512,1536]{0,1:T(8,128)(2,1)}, u32[]{:S(2)}, u32[]{:S(2)}) collective-permute-start(bf16[512,1536]{0,1:T(8,128)(2,1)} %add_convert_fusion.3), channel_id=1, source_target_pairs={{0,8},{2,10},{4,12},{6,14},{8,16},{10,18},{12,20},{14,22},{16,24},... | collective-permute-start | bytes 4718600 | tf_op jit(solution)/shard_map/ppermute | solution.py:80
  795.1 8.8 fusion.73
  803.9 12.4 %fusion = (f32[4,4,512]{2,1,0:T(4,128)S(1)}, f32[4,512,512,4]{2,1,3,0:T(8,128)}) fusion(f32[4,4,512]{2,1,0:T(4,128)S(1)} %copy-done.130, f32[4,4,512]{2,1,0:T(4,128)S(1)} %copy-done.106, f32[4,512,512,4]{2,1,3,0:T(8,128)} %copy-done.2, pred[4,512,512]{1,2,0:T(8,128)(4,1)S(1)} %copy-done.13, bf16[4,512,4,64]{1,3,2,0:T(8,128)(2,1)S(1)} %copy-done.64, ...), kind=kOutput, calls=%fused_computation.3 | convolution fusion | flops 562028544 | bytes 36012032 | tf_op jit(solution)/shard_map/shcfw,skcw->scfhk/dot_general | solution.py:347
  821.4 12.3 %fusion.6 = bf16[4,4,512,512]{2,3,1,0:T(8,128)(2,1)S(1)} fusion(f32[4,512,512,4]{2,1,3,0:T(8,128)} %get-tuple-element.312, f32[4,4,512]{2,1,0:T(4,128)S(1)} %get-tuple-element.311, f32[4,4,512]{2,1,0:T(4,128)S(1)} %copy-done.130, f32[4,4,512]{2,1,0:T(4,128)S(1)} %copy-done.106, f32[4,512,512,4]{2,1,3,0:T(8,128)} %copy-done.2, ...), kind=kLoop, calls=%fused_computation.12 | loop fusion | flops 29360128 | bytes 43089920 | tf_op jit(solution)/shard_map/reshape.19
  872.9 6.7 fusion.16
  879.7 26.3 %collective-permute-done.112 = bf16[512,256]{0,1:T(8,128)(2,1)S(1)} collective-permute-done((bf16[512,256]{0,1:T(8,128)(2,1)S(1)}, bf16[512,256]{0,1:T(8,128)(2,1)S(1)}, u32[]{:S(2)}, u32[]{:S(2)}) %collective-permute-start.112) | collective-permute-done | bytes 262176 | tf_op jit(solution)/shard_map/ppermute | solution.py:80
  906.9 11.4 %collective-permute-start.103 = (bf16[512,384]{0,1:T(8,128)(2,1)S(1)}, bf16[512,384]{0,1:T(8,128)(2,1)S(1)}, u32[]{:S(2)}, u32[]{:S(2)}) collective-permute-start(bf16[512,384]{0,1:T(8,128)(2,1)S(1)} %get-tuple-element.188), channel_id=1, source_target_pairs={{0,8},{2,10},{4,12},{6,14},{8,16},{10,18},{12,20},{14,22},{1,9},{3... | collective-permute-start | bytes 1179656 | tf_op jit(solution)/shard_map/ppermute | solution.py:80
  941.5 17.4 %collective-permute-done.118 = bf16[128,256]{0,1:T(8,128)(2,1)S(1)} collective-permute-done((bf16[128,256]{0,1:T(8,128)(2,1)S(1)}, bf16[128,256]{0,1:T(8,128)(2,1)S(1)}, u32[]{:S(2)}, u32[]{:S(2)}) %collective-permute-start.118) | collective-permute-done | bytes 65568 | tf_op jit(solution)/shard_map/ppermute | solution.py:72
  964.4 8.4 collective-permute-done.135
  973.0 8.6 collective-permute-done.136
  994.6 8.6 collective-permute-done.107
  1005.8 6.9 collective-permute-done.90
  1012.7 22.6 %collective-permute-done.94 = bf16[256,2048]{1,0:T(8,128)(2,1)S(1)} collective-permute-done((bf16[256,2048]{1,0:T(8,128)(2,1)S(1)}, bf16[256,2048]{1,0:T(8,128)(2,1)S(1)}, u32[]{:S(2)}, u32[]{:S(2)}) %collective-permute-start.94) | collective-permute-done | bytes 1048608 | tf_op jit(solution)/shard_map/ppermute | solution.py:72
  1038.1 5.5 collective-permute-start.96
  1081.9 6.9 fusion.13
  (887 shorter events, 460.6 us)
Async XLA Ops:
  0.7 62.5 %collective-permute-start.16 = (s32[1,512]{1,0:T(1,128)}, s32[1,512]{1,0:T(1,128)S(1)}, u32[]{:S(2)}, u32[]{:S(2)}) collective-permute-start(s32[1,512]{1,0:T(1,128)} %param.23), channel_id=1, source_target_pairs={{0,2},{2,0},{4,6},{6,4},{8,10},{10,8},{12,14},{14,12},{16,18},{18,... | collective-permute-start | bytes 6152 | tf_op jit(solution)/shard_map/ppermute | solution.py:72
  2.8 61.6 %collective-permute-start.17 = (s32[1,512]{1,0:T(1,128)}, s32[1,512]{1,0:T(1,128)S(1)}, u32[]{:S(2)}, u32[]{:S(2)}) collective-permute-start(s32[1,512]{1,0:T(1,128)} %param.23), channel_id=1, source_target_pairs={{0,4},{2,6},{4,0},{6,2},{8,12},{10,14},{12,8},{14,10},{16,20},{18,... | collective-permute-start | bytes 6152 | tf_op jit(solution)/shard_map/ppermute | solution.py:72
  4.0 60.5 %collective-permute-start.18 = (s32[1,512]{1,0:T(1,128)}, s32[1,512]{1,0:T(1,128)}, u32[]{:S(2)}, u32[]{:S(2)}) collective-permute-start(s32[1,512]{1,0:T(1,128)} %param.23), channel_id=1, source_target_pairs={{0,6},{2,4},{4,2},{6,0},{8,14},{10,12},{12,10},{14,8},{16,22},{18,... | collective-permute-start | bytes 6152 | tf_op jit(solution)/shard_map/ppermute | solution.py:72
  14.0 66.6 %collective-permute-start.51 = (bf16[128,1536]{0,1:T(8,128)(2,1)}, bf16[128,1536]{0,1:T(8,128)(2,1)}, u32[]{:S(2)}, u32[]{:S(2)}) collective-permute-start(bf16[128,1536]{0,1:T(8,128)(2,1)} %pad_maximum_fusion.35), channel_id=1, source_target_pairs={{0,6},{2,4},{4,2},{6,0},{8,14},{10,12},{12,10},{14,8},{16,22},{18,... | collective-permute-start | bytes 1179656 | tf_op jit(solution)/shard_map/ppermute | solution.py:72
  20.2 61.5 %collective-permute-start.52 = (bf16[128,1536]{0,1:T(8,128)(2,1)}, bf16[128,1536]{0,1:T(8,128)(2,1)}, u32[]{:S(2)}, u32[]{:S(2)}) collective-permute-start(bf16[128,1536]{0,1:T(8,128)(2,1)} %pad_maximum_fusion.36), channel_id=1, source_target_pairs={{0,4},{2,6},{4,0},{6,2},{8,12},{10,14},{12,8},{14,10},{16,20},{18,... | collective-permute-start | bytes 1179656 | tf_op jit(solution)/shard_map/ppermute | solution.py:72
  91.0 41.0 %collective-permute-start = (bf16[256,2048]{1,0:T(8,128)(2,1)S(1)}, bf16[256,2048]{1,0:T(8,128)(2,1)S(1)}, u32[]{:S(2)}, u32[]{:S(2)}) collective-permute-start(bf16[256,2048]{1,0:T(8,128)(2,1)S(1)} %copy-done.73), channel_id=1, source_target_pairs={{0,1},{1,0},{2,3},{3,2},{4,5},{5,4},{6,7},{7,6},{8,9},{9,8},{10,11... | collective-permute-start | bytes 3145736 | tf_op jit(solution)/shard_map/ppermute | solution.py:60
  133.0 37.5 %collective-permute-start.2 = (bf16[256,2048]{1,0:T(8,128)(2,1)S(1)}, bf16[256,2048]{1,0:T(8,128)(2,1)S(1)}, u32[]{:S(2)}, u32[]{:S(2)}) collective-permute-start(bf16[256,2048]{1,0:T(8,128)(2,1)S(1)} %collective-permute-done.1), channel_id=1, source_target_pairs={{0,1},{1,0},{2,3},{3,2},{4,5},{5,4},{6,7},{7,6},{8,9},{9,8},{10,11... | collective-permute-start | bytes 3145736 | tf_op jit(solution)/shard_map/ppermute | solution.py:60
  154.9 50.8 %collective-permute-start.71 = (bf16[256,2048]{1,0:T(8,128)(2,1)}, bf16[256,2048]{1,0:T(8,128)(2,1)}, u32[]{:S(2)}, u32[]{:S(2)}) collective-permute-start(bf16[256,2048]{1,0:T(8,128)(2,1)} %fusion.119), channel_id=1, source_target_pairs={{0,4},{2,6},{4,0},{6,2},{8,12},{10,14},{12,8},{14,10},{16,20},{18,... | collective-permute-start | bytes 3145736 | tf_op jit(solution)/shard_map/ppermute | solution.py:72
  169.4 37.5 %collective-permute-start.73 = (bf16[256,2048]{1,0:T(8,128)(2,1)}, bf16[256,2048]{1,0:T(8,128)(2,1)}, u32[]{:S(2)}, u32[]{:S(2)}) collective-permute-start(bf16[256,2048]{1,0:T(8,128)(2,1)} %fusion.119), channel_id=1, source_target_pairs={{0,6},{2,4},{4,2},{6,0},{8,14},{10,12},{12,10},{14,8},{16,22},{18,... | collective-permute-start | bytes 3145736 | tf_op jit(solution)/shard_map/ppermute | solution.py:72
  170.5 47.5 %collective-permute-start.69 = (bf16[256,2048]{1,0:T(8,128)(2,1)}, bf16[256,2048]{1,0:T(8,128)(2,1)}, u32[]{:S(2)}, u32[]{:S(2)}) collective-permute-start(bf16[256,2048]{1,0:T(8,128)(2,1)} %fusion.119), channel_id=1, source_target_pairs={{0,2},{2,0},{4,6},{6,4},{8,10},{10,8},{12,14},{14,12},{16,18},{18,... | collective-permute-start | bytes 3145736 | tf_op jit(solution)/shard_map/ppermute | solution.py:72
  172.1 49.1 %collective-permute-start.68 = (bf16[256,2048]{1,0:T(8,128)(2,1)}, bf16[256,2048]{1,0:T(8,128)(2,1)}, u32[]{:S(2)}, u32[]{:S(2)}) collective-permute-start(bf16[256,2048]{1,0:T(8,128)(2,1)} %fusion.119), channel_id=1, source_target_pairs={{0,1},{1,0},{2,3},{3,2},{4,5},{5,4},{6,7},{7,6},{8,9},{9,8},{10,11... | collective-permute-start | bytes 3145736 | tf_op jit(solution)/shard_map/ppermute | solution.py:60
  173.6 48.9 %collective-permute-start.55 = (bf16[512,1536]{0,1:T(8,128)(2,1)}, bf16[512,1536]{0,1:T(8,128)(2,1)}, u32[]{:S(2)}, u32[]{:S(2)}) collective-permute-start(bf16[512,1536]{0,1:T(8,128)(2,1)} %pad_maximum_fusion.15), channel_id=1, source_target_pairs={{0,8},{2,10},{4,12},{6,14},{8,16},{10,18},{12,20},{14,22},{16,24},... | collective-permute-start | bytes 4718600 | tf_op jit(solution)/shard_map/ppermute | solution.py:80
  205.6 37.9 %collective-permute-start.54 = (bf16[512,1536]{0,1:T(8,128)(2,1)}, bf16[512,1536]{0,1:T(8,128)(2,1)S(1)}, u32[]{:S(2)}, u32[]{:S(2)}) collective-permute-start(bf16[512,1536]{0,1:T(8,128)(2,1)} %pad_maximum_fusion.15), channel_id=1, source_target_pairs={{8,0},{10,2},{12,4},{14,6},{16,8},{18,10},{20,12},{22,14},{24,16},... | collective-permute-start | bytes 4718600 | tf_op jit(solution)/shard_map/ppermute | solution.py:80
  206.9 38.2 %collective-permute-start.46 = (bf16[512,1536]{0,1:T(8,128)(2,1)S(1)}, bf16[512,1536]{0,1:T(8,128)(2,1)S(1)}, u32[]{:S(2)}, u32[]{:S(2)}) collective-permute-start(bf16[512,1536]{0,1:T(8,128)(2,1)S(1)} %copy-done.22), channel_id=1, source_target_pairs={{0,8},{2,10},{4,12},{6,14},{8,16},{10,18},{12,20},{14,22},{16,24},... | collective-permute-start | bytes 4718600 | tf_op jit(solution)/shard_map/ppermute | solution.py:80
  221.2 56.1 %collective-permute-start.45 = (bf16[512,1536]{0,1:T(8,128)(2,1)S(1)}, bf16[512,1536]{0,1:T(8,128)(2,1)S(1)}, u32[]{:S(2)}, u32[]{:S(2)}) collective-permute-start(bf16[512,1536]{0,1:T(8,128)(2,1)S(1)} %copy-done.22), channel_id=1, source_target_pairs={{8,0},{10,2},{12,4},{14,6},{16,8},{18,10},{20,12},{22,14},{24,16},... | collective-permute-start | bytes 4718600 | tf_op jit(solution)/shard_map/ppermute | solution.py:80
  279.1 36.9 %collective-permute-start.58 = (bf16[512,1536]{0,1:T(8,128)(2,1)S(1)}, bf16[512,1536]{0,1:T(8,128)(2,1)}, u32[]{:S(2)}, u32[]{:S(2)}) collective-permute-start(bf16[512,1536]{0,1:T(8,128)(2,1)S(1)} %copy-done.51), channel_id=1, source_target_pairs={{8,0},{10,2},{12,4},{14,6},{16,8},{18,10},{20,12},{22,14},{9,1},{1... | collective-permute-start | bytes 4718600 | tf_op jit(solution)/shard_map/ppermute | solution.py:80
  282.8 66.8 %collective-permute-start.49 = (bf16[512,1536]{0,1:T(8,128)(2,1)S(1)}, bf16[512,1536]{0,1:T(8,128)(2,1)S(1)}, u32[]{:S(2)}, u32[]{:S(2)}) collective-permute-start(bf16[512,1536]{0,1:T(8,128)(2,1)S(1)} %collective-permute-done.45), channel_id=1, source_target_pairs={{8,0},{10,2},{12,4},{14,6},{16,8},{18,10},{20,12},{22,14},{9,1},{1... | collective-permute-start | bytes 4718600 | tf_op jit(solution)/shard_map/ppermute | solution.py:80
  286.2 66.2 %collective-permute-start.34 = (bf16[256,2048]{1,0:T(8,128)(2,1)}, bf16[256,2048]{1,0:T(8,128)(2,1)S(1)}, u32[]{:S(2)}, u32[]{:S(2)}) collective-permute-start(bf16[256,2048]{1,0:T(8,128)(2,1)} %get-tuple-element.142), channel_id=1, source_target_pairs={{0,1},{1,0},{2,3},{3,2},{4,5},{5,4},{6,7},{7,6},{8,9},{9,8},{10,11... | collective-permute-start | bytes 3145736 | tf_op jit(solution)/shard_map/ppermute | solution.py:60
  291.3 62.4 %collective-permute-start.29 = (bf16[256,2048]{1,0:T(8,128)(2,1)}, bf16[256,2048]{1,0:T(8,128)(2,1)S(1)}, u32[]{:S(2)}, u32[]{:S(2)}) collective-permute-start(bf16[256,2048]{1,0:T(8,128)(2,1)} %get-tuple-element.138), channel_id=1, source_target_pairs={{0,2},{2,0},{4,6},{6,4},{8,10},{10,8},{12,14},{14,12},{16,18},{18,... | collective-permute-start | bytes 3145736 | tf_op jit(solution)/shard_map/ppermute | solution.py:72
  315.9 46.1 %collective-permute-start.31 = (bf16[256,2048]{1,0:T(8,128)(2,1)S(1)}, bf16[256,2048]{1,0:T(8,128)(2,1)S(1)}, u32[]{:S(2)}, u32[]{:S(2)}) collective-permute-start(bf16[256,2048]{1,0:T(8,128)(2,1)S(1)} %get-tuple-element.140), channel_id=1, source_target_pairs={{0,4},{2,6},{4,0},{6,2},{8,12},{10,14},{12,8},{14,10},{16,20},{18,... | collective-permute-start | bytes 3145736 | tf_op jit(solution)/shard_map/ppermute | solution.py:72
  316.4 47.4 %collective-permute-start.33 = (bf16[256,2048]{1,0:T(8,128)(2,1)S(1)}, bf16[256,2048]{1,0:T(8,128)(2,1)}, u32[]{:S(2)}, u32[]{:S(2)}) collective-permute-start(bf16[256,2048]{1,0:T(8,128)(2,1)S(1)} %get-tuple-element.139), channel_id=1, source_target_pairs={{0,6},{2,4},{4,2},{6,0},{8,14},{10,12},{12,10},{14,8},{16,22},{18,... | collective-permute-start | bytes 3145736 | tf_op jit(solution)/shard_map/ppermute | solution.py:72
  362.1 59.4 %collective-permute-start.50 = (bf16[512,1536]{0,1:T(8,128)(2,1)S(1)}, bf16[512,1536]{0,1:T(8,128)(2,1)S(1)}, u32[]{:S(2)}, u32[]{:S(2)}) collective-permute-start(bf16[512,1536]{0,1:T(8,128)(2,1)S(1)} %collective-permute-done.49), channel_id=1, source_target_pairs={{8,0},{10,2},{12,4},{14,6},{9,1},{11,3},{13,5},{15,7}} | collective-permute-start | bytes 4718600 | tf_op jit(solution)/shard_map/ppermute | solution.py:80
  546.7 42.3 %collective-permute-start.60 = (bf16[256,2048]{1,0:T(8,128)(2,1)}, bf16[256,2048]{1,0:T(8,128)(2,1)}, u32[]{:S(2)}, u32[]{:S(2)}) collective-permute-start(bf16[256,2048]{1,0:T(8,128)(2,1)} %get-tuple-element.134), channel_id=1, source_target_pairs={{0,1},{1,0},{2,3},{3,2},{4,5},{5,4},{6,7},{7,6},{8,9},{9,8},{10,11... | collective-permute-start | bytes 3145736 | tf_op jit(solution)/shard_map/ppermute | solution.py:60
  550.3 39.2 %collective-permute-start.62 = (bf16[256,2048]{1,0:T(8,128)(2,1)}, bf16[256,2048]{1,0:T(8,128)(2,1)}, u32[]{:S(2)}, u32[]{:S(2)}) collective-permute-start(bf16[256,2048]{1,0:T(8,128)(2,1)} %get-tuple-element.137), channel_id=1, source_target_pairs={{0,1},{1,0},{2,3},{3,2},{4,5},{5,4},{6,7},{7,6},{8,9},{9,8},{10,11... | collective-permute-start | bytes 3145736 | tf_op jit(solution)/shard_map/ppermute | solution.py:60
  603.3 45.4 %collective-permute-start.80 = (bf16[256,2048]{1,0:T(8,128)(2,1)}, bf16[256,2048]{1,0:T(8,128)(2,1)}, u32[]{:S(2)}, u32[]{:S(2)}) collective-permute-start(bf16[256,2048]{1,0:T(8,128)(2,1)} %get-tuple-element.123), channel_id=1, source_target_pairs={{0,6},{2,4},{4,2},{6,0},{8,14},{10,12},{12,10},{14,8},{16,22},{18,... | collective-permute-start | bytes 3145736 | tf_op jit(solution)/shard_map/ppermute | solution.py:72
  610.0 89.6 %collective-permute-start.123 = (bf16[512,1536]{0,1:T(8,128)(2,1)}, bf16[512,1536]{0,1:T(8,128)(2,1)}, u32[]{:S(2)}, u32[]{:S(2)}) collective-permute-start(bf16[512,1536]{0,1:T(8,128)(2,1)} %pad_maximum_fusion.16), channel_id=1, source_target_pairs={{24,16},{26,18},{28,20},{30,22},{25,17},{27,19},{29,21},{31,23}} | collective-permute-start | bytes 4718600 | tf_op jit(solution)/shard_map/ppermute | solution.py:80
  629.3 70.4 %collective-permute-start.120 = (bf16[512,1536]{0,1:T(8,128)(2,1)S(1)}, bf16[512,1536]{0,1:T(8,128)(2,1)}, u32[]{:S(2)}, u32[]{:S(2)}) collective-permute-start(bf16[512,1536]{0,1:T(8,128)(2,1)S(1)} %pad_maximum_fusion.18), channel_id=1, source_target_pairs={{0,8},{2,10},{4,12},{6,14},{1,9},{3,11},{5,13},{7,15}} | collective-permute-start | bytes 4718600 | tf_op jit(solution)/shard_map/ppermute | solution.py:80
  634.8 37.6 %collective-permute-start.63 = (bf16[256,2048]{1,0:T(8,128)(2,1)}, bf16[256,2048]{1,0:T(8,128)(2,1)}, u32[]{:S(2)}, u32[]{:S(2)}) collective-permute-start(bf16[256,2048]{1,0:T(8,128)(2,1)} %get-tuple-element.133), channel_id=1, source_target_pairs={{0,4},{2,6},{4,0},{6,2},{8,12},{10,14},{12,8},{14,10},{16,20},{18,... | collective-permute-start | bytes 3145736 | tf_op jit(solution)/shard_map/ppermute | solution.py:72
  648.7 44.9 %collective-permute-start.65 = (bf16[256,2048]{1,0:T(8,128)(2,1)}, bf16[256,2048]{1,0:T(8,128)(2,1)}, u32[]{:S(2)}, u32[]{:S(2)}) collective-permute-start(bf16[256,2048]{1,0:T(8,128)(2,1)} %get-tuple-element.132), channel_id=1, source_target_pairs={{0,6},{2,4},{4,2},{6,0},{8,14},{10,12},{12,10},{14,8},{16,22},{18,... | collective-permute-start | bytes 3145736 | tf_op jit(solution)/shard_map/ppermute | solution.py:72
  671.0 37.3 %collective-permute-start.130 = (bf16[512,1536]{0,1:T(8,128)(2,1)}, bf16[512,1536]{0,1:T(8,128)(2,1)S(1)}, u32[]{:S(2)}, u32[]{:S(2)}) collective-permute-start(bf16[512,1536]{0,1:T(8,128)(2,1)} %get-tuple-element.179), channel_id=1, source_target_pairs={{0,8},{2,10},{4,12},{6,14},{8,16},{10,18},{12,20},{14,22},{1,9},{3... | collective-permute-start | bytes 4718600 | tf_op jit(solution)/shard_map/ppermute | solution.py:80
  672.4 37.3 %collective-permute-start.133 = (bf16[512,1536]{0,1:T(8,128)(2,1)}, bf16[512,1536]{0,1:T(8,128)(2,1)S(1)}, u32[]{:S(2)}, u32[]{:S(2)}) collective-permute-start(bf16[512,1536]{0,1:T(8,128)(2,1)} %get-tuple-element.180), channel_id=1, source_target_pairs={{16,8},{18,10},{20,12},{22,14},{24,16},{26,18},{28,20},{30,22},{17... | collective-permute-start | bytes 4718600 | tf_op jit(solution)/shard_map/ppermute | solution.py:80
  702.4 54.5 %collective-permute-start.121 = (bf16[512,1536]{0,1:T(8,128)(2,1)S(1)}, bf16[512,1536]{0,1:T(8,128)(2,1)S(1)}, u32[]{:S(2)}, u32[]{:S(2)}) collective-permute-start(bf16[512,1536]{0,1:T(8,128)(2,1)S(1)} %get-tuple-element.184), channel_id=1, source_target_pairs={{0,8},{2,10},{4,12},{6,14},{8,16},{10,18},{12,20},{14,22},{1,9},{3... | collective-permute-start | bytes 4718600 | tf_op jit(solution)/shard_map/ppermute | solution.py:80
  703.8 54.7 %collective-permute-start.124 = (bf16[512,1536]{0,1:T(8,128)(2,1)S(1)}, bf16[512,1536]{0,1:T(8,128)(2,1)S(1)}, u32[]{:S(2)}, u32[]{:S(2)}) collective-permute-start(bf16[512,1536]{0,1:T(8,128)(2,1)S(1)} %get-tuple-element.185), channel_id=1, source_target_pairs={{16,8},{18,10},{20,12},{22,14},{24,16},{26,18},{28,20},{30,22},{17... | collective-permute-start | bytes 4718600 | tf_op jit(solution)/shard_map/ppermute | solution.py:80
  708.3 45.9 %collective-permute-start.85 = (bf16[256,2048]{1,0:T(8,128)(2,1)S(1)}, bf16[256,2048]{1,0:T(8,128)(2,1)S(1)}, u32[]{:S(2)}, u32[]{:S(2)}) collective-permute-start(bf16[256,2048]{1,0:T(8,128)(2,1)S(1)} %get-tuple-element.88), channel_id=1, source_target_pairs={{0,4},{2,6},{4,0},{6,2},{8,12},{10,14},{12,8},{14,10},{16,20},{18,... | collective-permute-start | bytes 3145736 | tf_op jit(solution)/shard_map/ppermute | solution.py:72
  709.7 46.4 %collective-permute-start.87 = (bf16[256,2048]{1,0:T(8,128)(2,1)S(1)}, bf16[256,2048]{1,0:T(8,128)(2,1)S(1)}, u32[]{:S(2)}, u32[]{:S(2)}) collective-permute-start(bf16[256,2048]{1,0:T(8,128)(2,1)S(1)} %get-tuple-element.88), channel_id=1, source_target_pairs={{0,6},{2,4},{4,2},{6,0},{8,14},{10,12},{12,10},{14,8},{16,22},{18,... | collective-permute-start | bytes 3145736 | tf_op jit(solution)/shard_map/ppermute | solution.py:72
  731.7 131.0 %collective-permute-start.67 = (f32[256,2048]{1,0:T(8,128)}, f32[256,2048]{1,0:T(8,128)}, u32[]{:S(2)}, u32[]{:S(2)}) collective-permute-start(f32[256,2048]{1,0:T(8,128)} %fusion.28), channel_id=1, source_target_pairs={{0,1},{1,0},{2,3},{3,2},{4,5},{5,4},{6,7},{7,6},{8,9},{9,8},{10,11... | collective-permute-start | bytes 6291464 | tf_op jit(solution)/shard_map/ppermute | solution.py:60
  758.5 159.9 %collective-permute-start.131 = (bf16[512,1536]{0,1:T(8,128)(2,1)}, bf16[512,1536]{0,1:T(8,128)(2,1)}, u32[]{:S(2)}, u32[]{:S(2)}) collective-permute-start(bf16[512,1536]{0,1:T(8,128)(2,1)} %add_convert_fusion.3), channel_id=1, source_target_pairs={{0,8},{2,10},{4,12},{6,14},{8,16},{10,18},{12,20},{14,22},{16,24},... | collective-permute-start | bytes 4718600 | tf_op jit(solution)/shard_map/ppermute | solution.py:80
  777.4 141.8 %collective-permute-start.134 = (bf16[512,1536]{0,1:T(8,128)(2,1)}, bf16[512,1536]{0,1:T(8,128)(2,1)}, u32[]{:S(2)}, u32[]{:S(2)}) collective-permute-start(bf16[512,1536]{0,1:T(8,128)(2,1)} %add_convert_fusion.2), channel_id=1, source_target_pairs={{8,0},{10,2},{12,4},{14,6},{16,8},{18,10},{20,12},{22,14},{24,16},... | collective-permute-start | bytes 4718600 | tf_op jit(solution)/shard_map/ppermute | solution.py:80
  816.4 41.1 %collective-permute-start.111 = (bf16[512,256]{0,1:T(8,128)(2,1)S(1)}, bf16[512,256]{0,1:T(8,128)(2,1)S(1)}, u32[]{:S(2)}, u32[]{:S(2)}) collective-permute-start(bf16[512,256]{0,1:T(8,128)(2,1)S(1)} %get-tuple-element.208), channel_id=1, source_target_pairs={{0,8},{2,10},{4,12},{6,14},{1,9},{3,11},{5,13},{7,15}} | collective-permute-start | bytes 786440 | tf_op jit(solution)/shard_map/ppermute | solution.py:80
  820.4 38.5 %collective-permute-start.114 = (bf16[512,256]{0,1:T(8,128)(2,1)S(1)}, bf16[512,256]{0,1:T(8,128)(2,1)S(1)}, u32[]{:S(2)}, u32[]{:S(2)}) collective-permute-start(bf16[512,256]{0,1:T(8,128)(2,1)S(1)} %get-tuple-element.209), channel_id=1, source_target_pairs={{24,16},{26,18},{28,20},{30,22},{25,17},{27,19},{29,21},{31,23}} | collective-permute-start | bytes 786440 | tf_op jit(solution)/shard_map/ppermute | solution.py:80
  863.2 62.9 %collective-permute-start.122 = (bf16[512,1536]{0,1:T(8,128)(2,1)S(1)}, bf16[512,1536]{0,1:T(8,128)(2,1)S(1)}, u32[]{:S(2)}, u32[]{:S(2)}) collective-permute-start(bf16[512,1536]{0,1:T(8,128)(2,1)S(1)} %copy-done.52), channel_id=1, source_target_pairs={{0,8},{2,10},{4,12},{6,14},{8,16},{10,18},{12,20},{14,22},{16,24},... | collective-permute-start | bytes 4718600 | tf_op jit(solution)/shard_map/ppermute | solution.py:80
  866.7 60.7 %collective-permute-start.125 = (bf16[512,1536]{0,1:T(8,128)(2,1)S(1)}, bf16[512,1536]{0,1:T(8,128)(2,1)S(1)}, u32[]{:S(2)}, u32[]{:S(2)}) collective-permute-start(bf16[512,1536]{0,1:T(8,128)(2,1)S(1)} %copy-done.53), channel_id=1, source_target_pairs={{8,0},{10,2},{12,4},{14,6},{16,8},{18,10},{20,12},{22,14},{24,16},... | collective-permute-start | bytes 4718600 | tf_op jit(solution)/shard_map/ppermute | solution.py:80
  868.0 38.0 %collective-permute-start.112 = (bf16[512,256]{0,1:T(8,128)(2,1)S(1)}, bf16[512,256]{0,1:T(8,128)(2,1)S(1)}, u32[]{:S(2)}, u32[]{:S(2)}) collective-permute-start(bf16[512,256]{0,1:T(8,128)(2,1)S(1)} %get-tuple-element.206), channel_id=1, source_target_pairs={{0,8},{2,10},{4,12},{6,14},{8,16},{10,18},{12,20},{14,22},{1,9},{3... | collective-permute-start | bytes 786440 | tf_op jit(solution)/shard_map/ppermute | solution.py:80
  991.7 43.6 %collective-permute-start.94 = (bf16[256,2048]{1,0:T(8,128)(2,1)S(1)}, bf16[256,2048]{1,0:T(8,128)(2,1)S(1)}, u32[]{:S(2)}, u32[]{:S(2)}) collective-permute-start(bf16[256,2048]{1,0:T(8,128)(2,1)S(1)} %get-tuple-element.116), channel_id=1, source_target_pairs={{0,6},{2,4},{4,2},{6,0},{8,14},{10,12},{12,10},{14,8},{16,22},{18,... | collective-permute-start | bytes 3145736 | tf_op jit(solution)/shard_map/ppermute | solution.py:72
  1004.4 51.9 %collective-permute-start.108 = (bf16[128,384]{0,1:T(8,128)(2,1)S(1)}, bf16[128,384]{0,1:T(8,128)(2,1)S(1)}, u32[]{:S(2)}, u32[]{:S(2)}) collective-permute-start(bf16[128,384]{0,1:T(8,128)(2,1)S(1)} %get-tuple-element.268), channel_id=1, source_target_pairs={{0,6},{2,4},{4,2},{6,0},{8,14},{10,12},{12,10},{14,8},{16,22},{18,... | collective-permute-start | bytes 294920 | tf_op jit(solution)/shard_map/ppermute | solution.py:72
  1005.8 50.5 %collective-permute-start.109 = (bf16[128,384]{0,1:T(8,128)(2,1)S(1)}, bf16[128,384]{0,1:T(8,128)(2,1)S(1)}, u32[]{:S(2)}, u32[]{:S(2)}) collective-permute-start(bf16[128,384]{0,1:T(8,128)(2,1)S(1)} %get-tuple-element.267), channel_id=1, source_target_pairs={{0,4},{2,6},{4,0},{6,2},{8,12},{10,14},{12,8},{14,10},{16,20},{18,... | collective-permute-start | bytes 294920 | tf_op jit(solution)/shard_map/ppermute | solution.py:72
  1012.7 43.6 %collective-permute-start.110 = (bf16[128,384]{0,1:T(8,128)(2,1)S(1)}, bf16[128,384]{0,1:T(8,128)(2,1)S(1)}, u32[]{:S(2)}, u32[]{:S(2)}) collective-permute-start(bf16[128,384]{0,1:T(8,128)(2,1)S(1)} %get-tuple-element.266), channel_id=1, source_target_pairs={{0,2},{2,0},{4,6},{6,4},{8,10},{10,8},{12,14},{14,12},{16,18},{18,... | collective-permute-start | bytes 294920 | tf_op jit(solution)/shard_map/ppermute | solution.py:72
  1038.1 43.8 %collective-permute-start.96 = (f32[256,2048]{1,0:T(8,128)S(1)}, f32[256,2048]{1,0:T(8,128)}, u32[]{:S(2)}, u32[]{:S(2)}) collective-permute-start(f32[256,2048]{1,0:T(8,128)S(1)} %fusion.26), channel_id=1, source_target_pairs={{0,1},{1,0},{2,3},{3,2},{4,5},{5,4},{6,7},{7,6},{8,9},{9,8},{10,11... | collective-permute-start | bytes 6291464 | tf_op jit(solution)/shard_map/ppermute | solution.py:60
  (266 other events, 4040.4 us)

commit v2 on v1

v2 whole, which is shorter than its diff:
```python
import functools

import jax
import jax.numpy as jnp
from jax import lax
from jax.experimental import pallas as pl
from jax.experimental.pallas import tpu as pltpu
from jax.sharding import PartitionSpec as P

eps = 1e-05
rope_base = 1000000.0
group = 4
sub_count = 2
vmem_limit = 52 * 1024 * 1024


def norm_rows(values, gain):
    scale = lax.rsqrt(jnp.mean(values * values, axis=-1, keepdims=True) + eps)
    return (values * scale * gain, scale)


def norm_back(values, scale, gain, incoming):
    weighted = incoming * gain
    return scale * weighted - values * (scale * scale * scale) * jnp.mean(
        weighted * values, axis=-1, keepdims=True
    )


def positions_of(segment_row):
    row_index = jnp.arange(segment_row.shape[0], dtype=jnp.int32)
    earlier = jnp.concatenate([segment_row[:1] - 1, segment_row[:-1]])
    starts = jnp.where(segment_row != earlier, row_index, jnp.zeros_like(row_index))
    return row_index - lax.cummax(starts, axis=0)


def angles(positions, width, lanes):
    frequency = rope_base ** (-jnp.arange(0, width, 2, dtype=jnp.float32) / width)
    frequency = jnp.tile(frequency, 2 * lanes // width)
    phases = positions.astype(jnp.float32)[..., None] * frequency
    return (jnp.cos(phases), jnp.sin(phases))


def dot_nn(left, right):
    return jnp.dot(left, right, preferred_element_type=jnp.float32)


def dot_nt(left, right):
    return lax.dot_general(
        left, right, (((1,), (1,)), ((), ())), preferred_element_type=jnp.float32
    )


def dot_tn(left, right):
    return lax.dot_general(
        left, right, (((0,), (0,)), ((), ())), preferred_element_type=jnp.float32
    )


def exact_dot(left, right):
    return jnp.dot(
        left, right, preferred_element_type=jnp.float32, precision=lax.Precision.HIGHEST
    )


def kernel_call(body, grid, in_specs, out_specs, out_shape, flops, moved):
    return pl.pallas_call(
        body,
        grid=grid,
        in_specs=in_specs,
        out_specs=out_specs,
        out_shape=out_shape,
        compiler_params=pltpu.CompilerParams(vmem_limit_bytes=vmem_limit),
        cost_estimate=pl.CostEstimate(flops=flops, bytes_accessed=moved, transcendentals=0),
    )


def whole(array):
    rank = len(array.shape)
    return pl.BlockSpec(array.shape, lambda *_: (0,) * rank)


def shape_of(shape, kind):
    return jax.ShapeDtypeStruct(shape, kind)


def turn_heads(values, head_dim):
    lanes = values.shape[-1]
    middle = head_dim // 2
    lane = lax.broadcasted_iota(jnp.int32, values.shape, 1) % head_dim
    ahead = pltpu.roll(values, lanes - middle, 1)
    behind = pltpu.roll(values, middle, 1)
    return jnp.where(lane < middle, -ahead, behind)


def index_pair(rows, columns):
    return (
        lax.broadcasted_iota(jnp.int32, (rows, columns), 0),
        lax.broadcasted_iota(jnp.int32, (rows, columns), 1),
    )


def spread(values, offset, columns, head_dim):
    row, column = index_pair(values.shape[1], columns)
    return exact_dot(values, (row - offset == column % head_dim).astype(jnp.float32))


def fold(values, head_dim):
    row, column = index_pair(values.shape[1], values.shape[1])
    return exact_dot(values, (row % head_dim == column % head_dim).astype(jnp.float32))


def head_mean(values, head_dim):
    row, column = index_pair(values.shape[1], values.shape[1])
    same = (row // head_dim == column // head_dim).astype(jnp.float32)
    return exact_dot(values, same) * (1.0 / head_dim)


def prepare_heads(raw, gain, cosine, sine, head_dim):
    scale = lax.rsqrt(head_mean(raw * raw, head_dim) + eps)
    scaled = raw * scale * gain
    return scaled * cosine + turn_heads(scaled, head_dim) * sine, scale


def prepare_back(raw, scale, gain, cosine, sine, incoming, head_dim):
    turned = incoming * cosine - turn_heads(incoming * sine, head_dim)
    weighted = turned * gain
    grad = scale * weighted - raw * (scale * scale * scale) * head_mean(weighted * raw, head_dim)
    return grad, jnp.sum(turned * raw * scale, axis=0, keepdims=True)


def head_inputs(raw, gains, cosine, sine, head_dim, width):
    query, query_scale = prepare_heads(raw[:, :width], gains[0:1], cosine, sine, head_dim)
    rest = raw[:, width:]
    key_raw = spread(rest, 0, width, head_dim)
    key, key_scale = prepare_heads(key_raw, gains[1:2], cosine, sine, head_dim)
    value = spread(rest, head_dim, width, head_dim).astype(jnp.bfloat16)
    return (
        query.astype(jnp.bfloat16),
        query_scale,
        key_raw,
        key.astype(jnp.bfloat16),
        key_scale,
        value,
    )


def only_head(values, head, head_dim):
    lane = lax.broadcasted_iota(jnp.int32, values.shape, 1)
    return jnp.where(lane // head_dim == head, values, jnp.zeros_like(values))


def softmax_of(query_h, key, allowed):
    scores = 0.125 * dot_nt(query_h, key)
    scores = jnp.where(allowed, scores, -1000000000.0)
    exps = jnp.exp(scores - jnp.max(scores, axis=-1, keepdims=True))
    return exps * (1.0 / jnp.sum(exps, axis=-1, keepdims=True))


def block_product(kept, other, blocks, start, stop):
    rows = blocks[0].shape[0]
    total = None
    for k, block in enumerate(blocks):
        left = jnp.concatenate(
            [kept[:, k * rows : (k + 1) * rows], other[:, k * rows : (k + 1) * rows]], axis=0
        )
        more = dot_nn(left, block[:, start:stop])
        total = more if total is None else total + more
    return total


def allowed_of(start_ref, index_column, index_row):
    key_index = index_row[...]
    return (key_index <= index_column[...]) & (key_index >= start_ref[0])


def attention_forward(count, head_dim, width, *refs):
    kept, other, cosine_ref, sine_ref, start_ref, index_column, index_row, gains = refs[:8]
    blocks = refs[8 : 8 + count]
    raw_ref, heads_ref, part_kept, part_other = refs[8 + count :]
    half = kept.shape[0]
    attn_width = raw_ref.shape[-1]
    raw = block_product(kept, other, blocks, 0, attn_width)
    raw_ref[0, 0] = raw[:half]
    raw_ref[1, 0] = raw[half:]
    repeat = width // cosine_ref.shape[-1]
    cosine = jnp.concatenate([cosine_ref[0]] * repeat, axis=1)
    sine = jnp.concatenate([sine_ref[0]] * repeat, axis=1)
    query, _, _, key, _, value = head_inputs(raw, gains[...], cosine, sine, head_dim, width)
    allowed = allowed_of(start_ref, index_column, index_row)
    heads = jnp.zeros((2 * half, width), jnp.float32)
    for head in range(width // head_dim):
        probs = softmax_of(only_head(query, head, head_dim), key, allowed).astype(jnp.bfloat16)
        heads = heads + only_head(dot_nn(probs, value), head, head_dim)
    heads = heads.astype(jnp.bfloat16)
    heads_ref[0, 0] = heads[:half]
    heads_ref[1, 0] = heads[half:]
    rows = blocks[0].shape[0]
    for k, block in enumerate(blocks):
        out = dot_nt(heads, block[:, attn_width : attn_width + width]).astype(jnp.bfloat16)
        part_kept[:, k * rows : (k + 1) * rows] = out[:half]
        part_other[:, k * rows : (k + 1) * rows] = out[half:]


def attention_backward(count, head_dim, width, *refs):
    kept, other, raw_ref, cosine_ref, sine_ref, start_ref, index_column, index_row, gains = refs[:9]
    blocks = refs[9 : 9 + count]
    grad_ref, gain_ref = refs[9 + count :]
    half = kept.shape[0]
    attn_width = raw_ref.shape[-1]
    heads_grad = block_product(kept, other, blocks, attn_width, attn_width + width)
    heads_grad = heads_grad.astype(jnp.bfloat16)
    raw = jnp.concatenate([raw_ref[0, 0], raw_ref[1, 0]], axis=0)
    repeat = width // cosine_ref.shape[-1]
    cosine = jnp.concatenate([cosine_ref[0]] * repeat, axis=1)
    sine = jnp.concatenate([sine_ref[0]] * repeat, axis=1)
    query, query_scale, key_raw, key, key_scale, value = head_inputs(
        raw, gains[...], cosine, sine, head_dim, width
    )
    allowed = allowed_of(start_ref, index_column, index_row)
    zero = jnp.zeros((2 * half, width), jnp.float32)
    query_grad, key_grad, value_grad = zero, zero, zero
    for head in range(width // head_dim):
        query_h = only_head(query, head, head_dim)
        grad_h = only_head(heads_grad, head, head_dim)
        probs_f = softmax_of(query_h, key, allowed)
        value_grad = value_grad + dot_tn(probs_f.astype(jnp.bfloat16), grad_h)
        probs_grad = dot_nt(grad_h, value)
        inner = jnp.sum(probs_f * probs_grad, axis=-1, keepdims=True)
        score_grad = (probs_f * (probs_grad - inner)).astype(jnp.bfloat16)
        query_grad = query_grad + only_head(dot_nn(score_grad, key), head, head_dim)
        key_grad = key_grad + dot_tn(score_grad, query_h)
    query_grad, query_gain_part = prepare_back(
        raw[:, :width], query_scale, gains[0:1], cosine, sine, 0.125 * query_grad, head_dim
    )
    key_grad, key_gain_part = prepare_back(
        key_raw, key_scale, gains[1:2], cosine, sine, 0.125 * fold(key_grad, head_dim), head_dim
    )
    value_grad = fold(value_grad, head_dim)
    rest = attn_width - width
    lane = lax.broadcasted_iota(jnp.int32, (2 * half, rest), 1)
    rest_grad = jnp.where(lane < head_dim, key_grad[:, :rest], value_grad[:, :rest])
    query_grad = query_grad.astype(jnp.bfloat16)
    rest_grad = rest_grad.astype(jnp.bfloat16)
    for side in range(2):
        rows = slice(side * half, (side + 1) * half)
        grad_ref[side, 0, :, :width] = query_grad[rows]
        grad_ref[side, 0, :, width:] = rest_grad[rows]
    parts = jnp.concatenate([query_gain_part, key_gain_part], axis=0)

    @pl.when(pl.program_id(0) == 0)
    def _():
        gain_ref[...] = parts

    @pl.when(pl.program_id(0) != 0)
    def _():
        gain_ref[...] = gain_ref[...] + parts


def run_attention(forward, pair, blocks, tables, gains, head_dim, width, attn_width, raw=None):
    half = pair[0].shape[0] // group
    model = pair[0].shape[1]
    cosine, sine, starts, index = tables
    rows = pl.BlockSpec((half, model), lambda s: (s, 0))
    halves = lambda n: pl.BlockSpec((2, 1, half, n), lambda s: (0, s, 0, 0))
    per_sequence = lambda a: pl.BlockSpec((1,) + a.shape[1:], lambda s: (s, 0, 0))
    column, row = index[:, None], index[None, :]
    common = [cosine, sine, starts, column, row, gains]
    common_specs = [per_sequence(cosine), per_sequence(sine), per_sequence(starts)]
    common_specs += [whole(column), whole(row), whole(gains)]
    flops = 2 * 2 * group * half * model * attn_width
    if forward:
        return kernel_call(
            functools.partial(attention_forward, len(blocks), head_dim, width),
            (group,),
            [rows, rows] + common_specs + [whole(b) for b in blocks],
            [halves(attn_width), halves(width), rows, rows],
            [
                shape_of((2, group, half, attn_width), jnp.float32),
                shape_of((2, group, half, width), jnp.bfloat16),
                shape_of((group * half, model), jnp.bfloat16),
                shape_of((group * half, model), jnp.bfloat16),
            ],
            flops,
            16 * group * half * model,
        )(*pair, *common, *blocks)
    return kernel_call(
        functools.partial(attention_backward, len(blocks), head_dim, width),
        (group,),
        [rows, rows, halves(attn_width)] + common_specs + [whole(b) for b in blocks],
        [halves(attn_width), pl.BlockSpec((2, width), lambda s: (0, 0))],
        [
            shape_of((2, group, half, attn_width), jnp.bfloat16),
            shape_of((2, width), jnp.float32),
        ],
        flops,
        16 * group * half * model,
    )(*pair, raw, *common, *blocks)


def ffn_units(count, ff_sub, *refs):
    normed, out = refs[0:2], refs[2:4]
    blocks = refs[4 : 4 + count]
    inner_refs, grad_refs = refs[4 + count : 6 + count], refs[6 + count :]
    tile = normed[0].shape[0]
    gate_up = block_product(normed[0], normed[1], blocks, 0, 2 * ff_sub)
    inner_grad = block_product(out[0], out[1], blocks, 2 * ff_sub, 3 * ff_sub)
    gate, up = gate_up[:, :ff_sub], gate_up[:, ff_sub:]
    sigmoid = 1.0 / (1.0 + jnp.exp(-gate))
    silu = gate * sigmoid
    inner = (silu * up).astype(jnp.bfloat16)
    gate_grad = (inner_grad * up * sigmoid * (1.0 + gate * (1.0 - sigmoid))).astype(jnp.bfloat16)
    up_grad = (inner_grad * silu).astype(jnp.bfloat16)
    for side in range(2):
        rows = slice(side * tile, (side + 1) * tile)
        inner_refs[side][...] = inner[rows]
        grad_refs[side][:, :ff_sub] = gate_grad[rows]
        grad_refs[side][:, ff_sub:] = up_grad[rows]


def run_ffn_units(normed, out, blocks, ff_sub):
    tokens, model = normed[0].shape
    tile = min(256, tokens)
    rows = lambda n: pl.BlockSpec((tile, n), lambda i: (i, 0))
    return kernel_call(
        functools.partial(ffn_units, len(blocks), ff_sub),
        (tokens // tile,),
        [rows(model)] * 4 + [whole(b) for b in blocks],
        [rows(ff_sub)] * 2 + [rows(2 * ff_sub)] * 2,
        [shape_of((tokens, ff_sub), jnp.bfloat16)] * 2
        + [shape_of((tokens, 2 * ff_sub), jnp.bfloat16)] * 2,
        12 * tokens * model * ff_sub,
        8 * tokens * model,
    )(*normed, *out, *blocks)


def weight_gradients(count, per, *refs):
    first, second = refs[0:2], refs[2:4]
    first_grad, second_grad = refs[4:6], refs[6:8]
    outs = refs[8:]
    one = dot_tn(first[0][...], first_grad[0][...]) + dot_tn(first[1][...], first_grad[1][...])
    two = dot_tn(second[0][...], second_grad[0][...]) + dot_tn(second[1][...], second_grad[1][...])
    width = one.shape[1]
    for k in range(count):

        @pl.when(pl.program_id(0) // per == k)
        def _(k=k):
            outs[k][:, :width] = one.astype(jnp.bfloat16)
            outs[k][:, width:] = two.astype(jnp.bfloat16)


def run_weight_gradients(first, first_grad, second, second_grad, count):
    tokens, model = first[0].shape
    block_rows = model // count
    tile = min(256, block_rows)
    per = block_rows // tile
    width = first_grad[0].shape[1] + second_grad[0].shape[1]
    columns = pl.BlockSpec((tokens, tile), lambda i: (0, i))
    out_spec = lambda k: pl.BlockSpec(
        (tile, width), lambda i: (jnp.clip(i - per * k, 0, per - 1), 0)
    )
    return kernel_call(
        functools.partial(weight_gradients, count, per),
        (model // tile,),
        [columns] * 4 + [whole(a) for a in (*first_grad, *second_grad)],
        [out_spec(k) for k in range(count)],
        [shape_of((block_rows, width), jnp.bfloat16)] * count,
        4 * tokens * model * width,
        8 * tokens * model,
    )(*first, *second, *first_grad, *second_grad)


def transposed_product(parts, count, *refs):
    lefts = refs[: 2 * parts]
    blocks = refs[2 * parts : 2 * parts + parts * count]
    outs = refs[2 * parts + parts * count :]
    tile = lefts[0].shape[0]
    rows = blocks[0].shape[0]
    for k in range(count):
        total = None
        for p in range(parts):
            left = jnp.concatenate([lefts[2 * p][...], lefts[2 * p + 1][...]], axis=0)
            more = dot_nt(left, blocks[p * count + k][...])
            total = more if total is None else total + more
        total = total.astype(jnp.bfloat16)
        outs[0][:, k * rows : (k + 1) * rows] = total[:tile]
        outs[1][:, k * rows : (k + 1) * rows] = total[tile:]


def run_transposed_product(pairs, blocks, column, columns):
    count = len(blocks[0])
    tokens = pairs[0][0].shape[0]
    model = count * blocks[0][0].shape[0]
    tile = min(256, tokens)
    rows = lambda n: pl.BlockSpec((tile, n), lambda i: (i, 0))
    lefts = [a for pair in pairs for a in pair]
    flat = [b for one in blocks for b in one]
    return kernel_call(
        functools.partial(transposed_product, len(pairs), count),
        (tokens // tile,),
        [rows(a.shape[1]) for a in lefts]
        + [pl.BlockSpec((b.shape[0], columns), lambda i: (0, column)) for b in flat],
        [rows(model)] * 2,
        [shape_of((tokens, model), jnp.bfloat16)] * 2,
        4 * tokens * model * columns * len(pairs),
        8 * tokens * model,
    )(*lefts, *flat)


def place_halves(place, mine, other, out):
    half = mine.shape[0]
    core = place[0]
    out[pl.ds(core * half, half), :] = mine[...]
    out[pl.ds((1 - core) * half, half), :] = other[...]


def run_place_halves(core, spot, count, mine, other):
    half, model = mine.shape
    block = model // count
    source = pl.BlockSpec((half, block), lambda k, place: (0, k))
    return pl.pallas_call(
        place_halves,
        grid_spec=pltpu.PrefetchScalarGridSpec(
            num_scalar_prefetch=1,
            grid=(count,),
            in_specs=[source, source],
            out_specs=pl.BlockSpec((2 * half, block), lambda k, place: (0, (k + place[1]) % count)),
        ),
        out_shape=shape_of((2 * half, model), jnp.float32),
        compiler_params=pltpu.CompilerParams(vmem_limit_bytes=vmem_limit),
        cost_estimate=pl.CostEstimate(flops=1, bytes_accessed=16 * half * model, transcendentals=0),
    )(jnp.stack([core, spot]).astype(jnp.int32), mine, other)


def swap_cores(values):
    return lax.ppermute(values, "tensor", [(0, 1), (1, 0)])


class Lines:
    def __init__(self, dp):
        self.dp = dp
        self.length = dp // group
        index = lax.axis_index("dp")
        self.place = index % group
        self.spot = index // group

    def flip(self, values, relation):
        return lax.ppermute(values, "dp", [(i, i ^ relation) for i in range(self.dp)])

    def hop(self, values, first, last, step):
        pairs = [
            (spot * group + place, (spot + step) * group + place)
            for spot in range(first, last + 1)
            for place in range(group)
        ]
        return lax.ppermute(values, "dp", pairs)

    def turn(self, values, step):
        pairs = [
            (spot * group + place, ((spot + step) % self.length) * group + place)
            for spot in range(self.length)
            for place in range(group)
        ]
        return lax.ppermute(values, "dp", pairs)

    def by_place(self, related):
        odd = self.place % 2 == 1
        high = self.place // 2 == 1
        own, one, two, three = related
        pairs = (
            (jnp.where(odd, one, own), jnp.where(odd, own, one)),
            (jnp.where(odd, three, two), jnp.where(odd, two, three)),
        )
        return [
            jnp.where(high, pairs[1][0], pairs[0][0]),
            jnp.where(high, pairs[1][1], pairs[0][1]),
            jnp.where(high, pairs[0][0], pairs[1][0]),
            jnp.where(high, pairs[0][1], pairs[1][1]),
        ]

    def pieces(self, piece_of):
        return [piece_of(self.place ^ relation) for relation in range(group)]

    def flip_pieces(self, pieces):
        return [pieces[0]] + [self.flip(pieces[r], r) for r in range(1, group)]

    def row_pieces(self, total):
        rows = total.shape[0] // group
        return [
            lax.dynamic_slice_in_dim(total, (self.place ^ r) * rows, rows) for r in range(group)
        ]

    def gather_near(self, mine):
        return [self.flip(mine, 1), self.flip(mine, 2)]

    def gather_across(self, near):
        middle = near[0].shape[0] // 2
        return [self.flip(near[0][:middle], 2), self.flip(near[1][middle:], 1)]

    def scatter_across(self, across):
        middle = across.shape[0] // 2
        return [self.flip(across[:middle], 1), self.flip(across[middle:], 2)]

    def gather_far(self, mine):
        near = self.gather_near(mine)
        return near, self.gather_across(near)

    def gather_tokens(self, mine):
        return self.both_cores(mine, *self.gather_far(mine))

    def both_cores(self, mine, near, across):
        kept = jnp.concatenate([mine] + near + across)
        return kept, swap_cores(kept)

    def terms(self, kept, other, relation):
        rows = kept.shape[0] // group
        span = slice(relation * rows, (relation + 1) * rows)
        return kept[span].astype(jnp.float32) + other[span].astype(jnp.float32)

    def across_terms(self, kept, other):
        return self.scatter_across(self.terms(kept, other, 3).astype(jnp.bfloat16))

    def near_terms(self, kept, other, got):
        one, two = self.terms(kept, other, 1), self.terms(kept, other, 2)
        middle = one.shape[0] // 2
        one = jnp.concatenate([one[:middle], one[middle:] + got[1].astype(jnp.float32)])
        two = jnp.concatenate([two[:middle] + got[0].astype(jnp.float32), two[middle:]])
        one = self.flip(one.astype(jnp.bfloat16), 1)
        two = self.flip(two.astype(jnp.bfloat16), 2)
        return self.terms(kept, other, 0) + one.astype(jnp.float32) + two.astype(jnp.float32)

    def scatter_tokens(self, kept, other):
        return self.near_terms(kept, other, self.across_terms(kept, other))


class LineGather:
    def __init__(self, lines, block):
        self.lines, self.block, self.got = lines, block, []

    def hop(self):
        lines, step = self.lines, len(self.got) + 1
        if lines.length != 4:
            turns = range(1, lines.length) if step == 1 else ()
            self.got.append([lines.turn(self.block, -k) for k in turns])
            return
        up, down = self.got[-1] if self.got else (self.block, self.block)
        self.got.append(
            [
                lines.hop(up, step - 1, lines.length - 2, 1),
                lines.hop(down, 1, lines.length - step, -1),
            ]
        )

    def blocks(self):
        lines = self.lines
        if lines.length != 4:
            return [self.block] + self.got[0]
        return [self.block] + [
            jnp.where(
                lines.spot + k < lines.length,
                self.got[k - 1][1],
                self.got[lines.length - k - 1][0],
            )
            for k in range(1, lines.length)
        ]


class LineScatter:
    def __init__(self, lines, blocks):
        self.lines, self.blocks, self.got = lines, blocks, []

    def hop(self):
        lines, step = self.lines, len(self.got) + 1
        if lines.length != 4:
            turns = range(1, lines.length) if step == 1 else ()
            self.got.append([lines.turn(self.blocks[k], k) for k in turns])
            return
        up, down = self.blocks[lines.length - step], self.blocks[step]
        if self.got:
            up, down = add(up, self.got[-1][0]), add(down, self.got[-1][1])
        self.got.append(
            [
                lines.hop(up, 0, min(step - 1, lines.length - 2), 1),
                lines.hop(down, max(lines.length - step, 1), lines.length - 1, -1),
            ]
        )

    def total(self):
        last = self.got[-1] if self.lines.length == 4 else self.got[0]
        result = self.blocks[0].astype(jnp.float32)
        for one in last:
            result = result + one.astype(jnp.float32)
        return result.astype(jnp.bfloat16)


def add(left, right):
    return (left.astype(jnp.float32) + right.astype(jnp.float32)).astype(jnp.bfloat16)


def tie(*values):
    return lax.optimization_barrier(values)


def sum_all(values, dp):
    bit = 1
    while bit < dp:
        values = values + lax.ppermute(values, "dp", [(i, i ^ bit) for i in range(dp)])
        bit *= 2
    return values + swap_cores(values)


def local(
    dp,
    tokens,
    segments,
    cotangent,
    attn_gain,
    ffn_gain,
    query_gain,
    key_gain,
    w_query,
    key_weight,
    value_weight,
    w_out,
    w_gate,
    w_up,
    w_down,
):
    lines = Lines(dp)
    core = lax.axis_index("tensor")
    length, width = tokens.shape
    half = length // 2
    head_dim = query_gain.shape[0]
    rows = w_query.shape[0]
    block_rows = rows * group
    query_width = w_query.shape[1] // group
    key_width = key_weight.shape[1] // group
    attn_width = query_width + 2 * key_width
    ff_sub = w_gate.shape[1] // group // sub_count

    def around(values):
        return jnp.roll(values, -lines.spot * block_rows, axis=-1)

    def back_around(values):
        return jnp.roll(values, lines.spot * block_rows, axis=-1)

    def halves(values, axis=0):
        return jnp.roll(values, -core * half, axis=axis)

    attn_gain_r, ffn_gain_r = around(attn_gain), around(ffn_gain)

    def columns(weight, start, size):
        return lax.dynamic_slice_in_dim(weight, start, size, axis=1)

    attn_pieces = lines.pieces(
        lambda j: jnp.concatenate(
            [
                columns(w_query, j * query_width, query_width),
                columns(key_weight, j * key_width, key_width),
                columns(value_weight, j * key_width, key_width),
                columns(w_out, j * query_width, query_width),
            ],
            axis=1,
        )
    )
    attn_shared = lines.flip_pieces(attn_pieces)
    source = around(lax.dynamic_slice_in_dim(tokens, core * half, half)).astype(jnp.float32)
    normed_f, scale_first = norm_rows(source, attn_gain_r)
    normed_mine = normed_f.astype(jnp.bfloat16)

    seg_all = jnp.stack([segments[0]] + [lines.flip(segments, r)[0] for r in range(1, group)])
    positions = halves(jax.vmap(positions_of)(seg_all), axis=1)
    index = halves(jnp.arange(length, dtype=jnp.int32))
    cosine, sine = angles(positions, head_dim, 2 * head_dim)
    tables = (cosine, sine, (index[None] - positions)[..., None], index)
    gains_two = jnp.stack(
        [
            jnp.tile(query_gain, query_width // head_dim),
            jnp.tile(key_gain, query_width // head_dim),
        ]
    )

    def ffn_piece(s):
        return lines.pieces(
            lambda j: jnp.concatenate(
                [
                    columns(weight, s * group * ff_sub + j * ff_sub, ff_sub)
                    for weight in (w_gate, w_up, w_down)
                ],
                axis=1,
            )
        )

    pieces_0, pieces_1 = ffn_piece(0), ffn_piece(1)
    cot_half = around(lax.dynamic_slice_in_dim(cotangent, core * half, half))
    out_mine = cot_half.astype(jnp.bfloat16)
    attn_shared, normed_mine, pieces_0, out_mine = tie(attn_shared, normed_mine, pieces_0, out_mine)

    attn_line = LineGather(lines, jnp.concatenate(lines.by_place(attn_shared), axis=0))
    attn_line.hop()
    near = lines.gather_near(normed_mine)
    near, attn_line.got[0], pieces_0 = tie(near, attn_line.got[0], pieces_0)
    attn_line.hop()
    across = lines.gather_across(near)
    across, attn_line.got[1], pieces_0, tables = tie(across, attn_line.got[1], pieces_0, tables)
    attn_line.hop()
    normed = lines.both_cores(normed_mine, near, across)
    shared_0 = lines.flip_pieces(pieces_0)
    normed, attn_line.got[2], shared_0, pieces_1, out_mine = tie(
        normed, attn_line.got[2], shared_0, pieces_1, out_mine
    )
    attn_w = attn_line.blocks()

    line_0 = LineGather(lines, jnp.concatenate(lines.by_place(shared_0), axis=0))
    line_0.hop()
    out_near, out_across = lines.gather_far(out_mine)
    qkv_raw, heads_out, attended_kept, attended_other = run_attention(
        True, normed, attn_w, tables, gains_two, head_dim, query_width, attn_width
    )
    attended_other, line_0.got[0], out_near, out_across, pieces_1 = tie(
        attended_other, line_0.got[0], out_near, out_across, pieces_1
    )

    line_0.hop()
    shared_1 = lines.flip_pieces(pieces_1)
    attended_other = swap_cores(attended_other)
    attended_other, shared_1 = tie(attended_other, shared_1)
    out_b = lines.both_cores(out_mine, out_near, out_across)
    attended = lines.scatter_tokens(attended_kept, attended_other)
    attended, line_0.got[1], out_b, shared_1 = tie(attended, line_0.got[1], out_b, shared_1)

    line_0.hop()
    line_1 = LineGather(lines, jnp.concatenate(lines.by_place(shared_1), axis=0))
    state = source + attended
    normed2_f, scale_second = norm_rows(state, ffn_gain_r)
    near, across = lines.gather_far(normed2_f.astype(jnp.bfloat16))
    near, across, line_0.got[2], line_1.block = tie(near, across, line_0.got[2], line_1.block)

    line_1.hop()
    normed2 = lines.both_cores(normed2_f.astype(jnp.bfloat16), near, across)
    ffn_w = [line_0.blocks()]
    units_0 = run_ffn_units(normed2, out_b, ffn_w[0], ff_sub)
    units_0, line_1.got[0] = tie(units_0, line_1.got[0])
    line_1.hop()
    ffn_g = run_weight_gradients(normed2, units_0[2:], out_b, units_0[:2], lines.length)
    ffn_g, line_1.got[1], units_0 = tie(ffn_g, line_1.got[1], units_0)
    line_1.hop()
    sum_0 = LineScatter(lines, ffn_g)
    line_1.got[2], sum_0.blocks = tie(line_1.got[2], sum_0.blocks)
    ffn_w.append(line_1.blocks())

    sum_0.hop()
    units_1 = run_ffn_units(normed2, out_b, ffn_w[1], ff_sub)
    kept, other = run_transposed_product([units_0[2:], units_1[2:]], ffn_w, 0, 2 * ff_sub)
    kept, other, sum_0.got[0], units_1 = tie(kept, other, sum_0.got[0], units_1)

    sum_0.hop()
    other = swap_cores(other)
    got = lines.across_terms(kept, other)
    got, units_1 = tie(got, units_1)
    sum_1 = LineScatter(
        lines, run_weight_gradients(normed2, units_1[2:], out_b, units_1[:2], lines.length)
    )
    normed2_grad = lines.near_terms(kept, other, got)
    normed2_grad, sum_0.got[1], sum_1.blocks, units_0, units_1 = tie(
        normed2_grad, sum_0.got[1], sum_1.blocks, units_0, units_1
    )

    sum_0.hop()
    ffn_gain_part = jnp.sum(normed2_grad * state * scale_second, axis=0)
    state_grad = cot_half + norm_back(state, scale_second, ffn_gain_r, normed2_grad)
    grad_mine = state_grad.astype(jnp.bfloat16)
    near = lines.gather_near(grad_mine)
    branch_kept, branch_other = run_transposed_product(
        [units_0[:2], units_1[:2]], ffn_w, 2, ff_sub
    )
    near, branch_kept, branch_other = tie(near, branch_kept, branch_other)
    across = lines.gather_across(near)
    across, sum_0.got[2], branch_kept, branch_other = tie(
        across, sum_0.got[2], branch_kept, branch_other
    )

    sum_1.hop()
    attended_b = lines.both_cores(grad_mine, near, across)

    def owners_rows(total):
        return lines.flip_pieces(lines.row_pieces(total))

    branch = lines.scatter_tokens(branch_kept, swap_cores(branch_other))
    ffn_grads = [owners_rows(sum_0.total())]
    qkv_grad, gain_parts = run_attention(
        False, attended_b, attn_w, tables, gains_two, head_dim, query_width, attn_width, qkv_raw
    )
    qkv_grad, ffn_grads[0], branch, sum_1.got[0] = tie(
        qkv_grad, ffn_grads[0], branch, sum_1.got[0]
    )

    sum_1.hop()
    qkv_grad = tuple(qkv_grad.reshape(2, group * half, attn_width))
    heads_out = tuple(heads_out.reshape(2, group * half, query_width))
    kept, other = run_transposed_product([qkv_grad], [attn_w], 0, attn_width)
    other = swap_cores(other)
    got = lines.across_terms(kept, other)
    attn_sum = LineScatter(
        lines, run_weight_gradients(normed, qkv_grad, attended_b, heads_out, lines.length)
    )
    got, sum_1.got[1], attn_sum.blocks = tie(got, sum_1.got[1], attn_sum.blocks)
    attn_sum.hop()
    sum_1.hop()
    normed_grad = lines.near_terms(kept, other, got)
    normed_grad, attn_sum.got[0], sum_1.got[2] = tie(normed_grad, attn_sum.got[0], sum_1.got[2])
    attn_sum.hop()
    attn_sum.hop()
    ffn_grads.append(owners_rows(sum_1.total()))
    attn_grads = owners_rows(attn_sum.total())
    mixed = state + branch
    attn_gain_part = jnp.sum(normed_grad * source * scale_first, axis=0)
    input_grad = state_grad + norm_back(source, scale_first, attn_gain_r, normed_grad)

    def whole_rows(mine):
        return run_place_halves(core, lines.spot, lines.length, mine, swap_cores(mine))

    gains = sum_all(
        jnp.concatenate(
            [
                back_around(attn_gain_part),
                back_around(ffn_gain_part),
                jnp.sum(gain_parts[0].reshape(-1, head_dim), axis=0),
                gain_parts[1][:head_dim],
            ]
        ),
        dp,
    )

    def columns_of(related, start, stop):
        blocks = lines.by_place([b[:, start:stop] for b in related])
        return jnp.concatenate(blocks, axis=1).astype(jnp.float32)

    def ffn_columns(which):
        return jnp.concatenate(
            [columns_of(blocks, which * ff_sub, (which + 1) * ff_sub) for blocks in ffn_grads],
            axis=1,
        )

    return (
        whole_rows(mixed),
        whole_rows(input_grad),
        gains[:width],
        gains[width : 2 * width],
        gains[2 * width : 2 * width + head_dim],
        gains[2 * width + head_dim :],
        columns_of(attn_grads, 0, query_width),
        columns_of(attn_grads, query_width, query_width + key_width),
        columns_of(attn_grads, query_width + key_width, attn_width),
        columns_of(attn_grads, attn_width, attn_width + query_width),
        ffn_columns(0),
        ffn_columns(1),
        ffn_columns(2),
    )


def solution(mesh):
    dp = mesh.shape["dp"]
    weight = P("dp", "tensor")
    rows = P("dp", None)
    return jax.shard_map(
        lambda *arrays: local(dp, *arrays),
        mesh=mesh,
        in_specs=(rows, rows, rows, P(), P(), P(), P()) + (weight,) * 7,
        out_specs=(rows, rows, P(), P(), P(), P()) + (weight,) * 7,
        check_vma=False,
    )
```

time: 1100 us -> 873 us (0.79)
  Pallas kernels: 0 us -> 221 us
  matrix products: 196 us -> 0 us
  starting transfers between devices: 240 us -> 150 us
  local copies, waits for them, and re-layouts: 123 us -> 43.7 us
  other arithmetic: 155 us -> 108 us
  waiting for transfers between devices: 371 us -> 336 us
    pallas_call x0 -> x12, Pallas kernels: none -> 221 us  [the longest x3 55.5 us: run_weight_gradients(): kernel_call(functools.partial(weight_gradients, count, per), (model // ti...]
    dot_general x24 -> x0, matrix products: 196 us -> none  [the longest x6 61.7 us: cols_product(): lax.dot_general(left, right, (((1,), (1,)), ((), ())), preferred_element_...]
    ppermute x48 -> x36, waiting for transfers between devices: 198 us -> 146 us  [hop(): return lax.ppermute(values, 'dp', pairs)]
    ppermute x35 -> x11, starting transfers between devices: 82.4 us -> 30.7 us  [swap_cores(): return lax.ppermute(values, 'tensor', [(0, 1), (1, 0)])]
    unnamed x412 -> x242, local copies, waits for them, and re-layouts: 63.4 us -> 20.4 us
    ppermute x48 -> x36, starting transfers between devices: 108 us -> 69.5 us  [hop(): return lax.ppermute(values, 'dp', pairs)]
    convert_element_type x27 -> x18, other arithmetic: 52.5 us -> 21.3 us  [the longest x9 13 us: add(): (left.astype(jnp.float32) + right.astype(jnp.float32)).astype(jnp.bfloat16)]
    another operation x26 -> x12, other arithmetic: 31.7 us -> 4.49 us  [the longest x23 17.9 us: gather_tokens(): return jnp.stack([jnp.stack([one, swap_cores(one)]) for one in kept])]
  transfers between devices with their start and end apart: 138 -> 104, of which waited for: 36 -> 45; matrix products, arithmetic and copies ran while one was open for 30% -> 14% of each run, Pallas kernels for 0% -> 24%
where the time goes in v2:
time: 873 us; the launch traced here: 861 us
  waiting for transfers between devices  336 us (38%)
  Pallas kernels  221 us (25%)
  starting transfers between devices  150 us (17%)
  other arithmetic  108 us (12%)
  local copies, waits for them, and re-layouts  43.7 us (5%)
    ppermute x53, waiting for transfers between devices, flip(): lax.ppermute(values, 'dp', [(i, i ^ relation) for i in range(self.dp)])  165 us
    ppermute x36, waiting for transfers between devices, hop(): return lax.ppermute(values, 'dp', pairs)  146 us
    ppermute x36, starting transfers between devices, hop(): return lax.ppermute(values, 'dp', pairs)  69.5 us
    pallas_call x3, Pallas kernels, run_weight_gradients(): kernel_call(functools.partial(weight_gradients, count, per), (model // ti...  55.5 us
    pallas_call x3, Pallas kernels, run_transposed_product(): kernel_call(functools.partial(transposed_product, len(pairs), count), (to...  45.1 us
    ppermute x53, starting transfers between devices, flip(): lax.ppermute(values, 'dp', [(i, i ^ relation) for i in range(self.dp)])  44.7 us
    pallas_call x1, Pallas kernels, run_attention(): kernel_call(functools.partial(attention_backward, len(blocks), head_dim,...  42.1 us
    pallas_call x2, Pallas kernels, run_ffn_units(): kernel_call(functools.partial(ffn_units, len(blocks), ff_sub), (tokens //...  39.1 us
  transfers between devices with their start and end apart: 104, of which 45 were waited for; matrix products, arithmetic and copies ran while one was open for 14% of the time, Pallas kernels for 24%

profile of v2, /device:TPU:1, one launch (start us, length us, event | category | flops | bytes accessed | tf_op | source)
XLA Modules:
  0.0 861.4 jit_solution(14492093268344926217)
XLA Ops:
  37.3 5.5 multiply_sine_fusion
  56.6 6.2 collective-permute-done.7
  62.8 6.4 collective-permute-done.10
  71.3 7.0 collective-permute-start.14
  83.4 5.7 collective-permute-done.17
  91.9 9.6 %collective-permute-done.18 = bf16[128,1536]{1,0:T(8,128)(2,1)S(1)} collective-permute-done((bf16[128,1536]{1,0:T(8,128)(2,1)S(1)}, bf16[128,1536]{1,0:T(8,128)(2,1)S(1)}, u32[]{:S(2)}, u32[]{:S(2)}) %collective-permute-start.18) | collective-permute-done | bytes 393248 | tf_op jit(solution)/shard_map/ppermute | solution.py:447
  104.1 4.9 collective-permute-start.20
  115.8 9.7 %collective-permute-done.22 = bf16[256,2048]{1,0:T(8,128)(2,1)} collective-permute-done((bf16[256,2048]{1,0:T(8,128)(2,1)}, bf16[256,2048]{1,0:T(8,128)(2,1)}, u32[]{:S(2)}, u32[]{:S(2)}) %collective-permute-start.22) | collective-permute-done | bytes 1048608 | tf_op jit(solution)/shard_map/ppermute | solution.py:447
  130.7 28.6 %shard_map.237 = (f32[2,4,256,384]{3,2,1,0:T(8,128)}, bf16[2,4,256,256]{3,2,1,0:T(8,128)(2,1)}, bf16[1024,2048]{1,0:T(8,128)(2,1)}, bf16[1024,2048]{1,0:T(8,128)(2,1)}) custom-call(bf16[1024,2048]{1,0:T(8,128)(2,1)} %copy-done.14, bf16[1024,2048]{1,0:T(8,128)(2,1)} %copy-done.24, f32[4,512,128]{2,1,0:T(8,128)} %get-tuple-element.227.refs_2_.refs_3_, ...), custom_call_target="tpu_custom_call" | custom-call | flops 3221225472 | bytes 33554432 | tf_op jit(solution)/shard_map/pallas_call | solution.py:272
  169.9 4.2 collective-permute-done.27
  174.1 8.5 collective-permute-done.29
  185.4 11.2 %collective-permute-done.32 = bf16[128,2048]{1,0:T(8,128)(2,1)S(1)} collective-permute-done((bf16[128,2048]{1,0:T(8,128)(2,1)S(1)}, bf16[128,2048]{1,0:T(8,128)(2,1)S(1)}, u32[]{:S(2)}, u32[]{:S(2)}) %collective-permute-start.32) | collective-permute-done | bytes 524320 | tf_op jit(solution)/shard_map/ppermute | solution.py:447
  200.5 19.3 %collective-permute-done.33 = bf16[256,2048]{1,0:T(8,128)(2,1)S(1)} collective-permute-done((bf16[256,2048]{1,0:T(8,128)(2,1)S(1)}, bf16[256,2048]{1,0:T(8,128)(2,1)S(1)}, u32[]{:S(2)}, u32[]{:S(2)}) %collective-permute-start.33) | collective-permute-done | bytes 1048608 | tf_op jit(solution)/shard_map/ppermute | solution.py:447
  221.6 13.8 %collective-permute-done.35 = bf16[512,1536]{1,0:T(8,128)(2,1)S(1)} collective-permute-done((bf16[512,1536]{1,0:T(8,128)(2,1)}, bf16[512,1536]{1,0:T(8,128)(2,1)S(1)}, u32[]{:S(2)}, u32[]{:S(2)}) %collective-permute-start.35) | collective-permute-done | bytes 1572896 | tf_op jit(solution)/shard_map/ppermute | solution.py:455
  240.2 17.7 %collective-permute-done.37 = bf16[256,2048]{1,0:T(8,128)(2,1)S(1)} collective-permute-done((bf16[256,2048]{1,0:T(8,128)(2,1)S(1)}, bf16[256,2048]{1,0:T(8,128)(2,1)S(1)}, u32[]{:S(2)}, u32[]{:S(2)}) %collective-permute-start.37) | collective-permute-done | bytes 1048608 | tf_op jit(solution)/shard_map/ppermute | solution.py:447
  261.0 11.0 %collective-permute-done.39 = bf16[128,2048]{1,0:T(8,128)(2,1)S(1)} collective-permute-done((bf16[128,2048]{1,0:T(8,128)(2,1)S(1)}, bf16[128,2048]{1,0:T(8,128)(2,1)S(1)}, u32[]{:S(2)}, u32[]{:S(2)}) %collective-permute-start.39) | collective-permute-done | bytes 524320 | tf_op jit(solution)/shard_map/ppermute | solution.py:447
  272.8 4.9 collective-permute-start.43
  286.1 19.5 %shard_map.238 = (bf16[1024,512]{1,0:T(8,128)(2,1)S(1)}, bf16[1024,512]{1,0:T(8,128)(2,1)}, bf16[1024,1024]{1,0:T(8,128)(2,1)}, bf16[1024,1024]{1,0:T(8,128)(2,1)}) custom-call(bf16[1024,2048]{1,0:T(8,128)(2,1)} %copy-done.91, bf16[1024,2048]{1,0:T(8,128)(2,1)} %collective-permute-done.43.refs_1_, bf16[1024,2048]{1,0:T(8,128)(2,1)} %copy-done.92, ...), custom_call_target="tpu_custom_call" | custom-call | flops 12884901888 | bytes 16777216 | tf_op jit(solution)/shard_map/pallas_call | solution.py:324
  305.6 7.9 collective-permute-done.44
  319.4 21.0 %shard_map.239 = (bf16[512,1536]{1,0:T(8,128)(2,1)}, bf16[512,1536]{1,0:T(8,128)(2,1)}, bf16[512,1536]{1,0:T(8,128)(2,1)}, bf16[512,1536]{1,0:T(8,128)(2,1)}) custom-call(bf16[1024,2048]{1,0:T(8,128)(2,1)} %copy-done.91, bf16[1024,2048]{1,0:T(8,128)(2,1)} %collective-permute-done.43.refs_1_, bf16[1024,2048]{1,0:T(8,128)(2,1)} %copy-done.92, ...), custom_call_target="tpu_custom_call" | custom-call | flops 12884901888 | bytes 16777216 | tf_op jit(solution)/shard_map/pallas_call | solution.py:361
  340.4 13.5 %collective-permute-done.47 = bf16[512,1536]{1,0:T(8,128)(2,1)} collective-permute-done((bf16[512,1536]{1,0:T(8,128)(2,1)S(1)}, bf16[512,1536]{1,0:T(8,128)(2,1)}, u32[]{:S(2)}, u32[]{:S(2)}) %collective-permute-start.47) | collective-permute-done | bytes 1572896 | tf_op jit(solution)/shard_map/ppermute | solution.py:455
  358.7 30.9 %collective-permute-done.49 = bf16[512,1536]{1,0:T(8,128)(2,1)S(1)} collective-permute-done((bf16[512,1536]{1,0:T(8,128)(2,1)}, bf16[512,1536]{1,0:T(8,128)(2,1)S(1)}, u32[]{:S(2)}, u32[]{:S(2)}) %collective-permute-start.49) | collective-permute-done | bytes 1572896 | tf_op jit(solution)/shard_map/ppermute | solution.py:455
  397.6 19.6 %shard_map.240 = (bf16[1024,512]{1,0:T(8,128)(2,1)S(1)}, bf16[1024,512]{1,0:T(8,128)(2,1)}, bf16[1024,1024]{1,0:T(8,128)(2,1)}, bf16[1024,1024]{1,0:T(8,128)(2,1)}) custom-call(bf16[1024,2048]{1,0:T(8,128)(2,1)} %copy-done.91, bf16[1024,2048]{1,0:T(8,128)(2,1)} %collective-permute-done.43.refs_1_, bf16[1024,2048]{1,0:T(8,128)(2,1)} %copy-done.92, ...), custom_call_target="tpu_custom_call" | custom-call | flops 12884901888 | bytes 16777216 | tf_op jit(solution)/shard_map/pallas_call | solution.py:324
  417.1 23.6 %shard_map.241 = (bf16[1024,2048]{1,0:T(8,128)(2,1)}, bf16[1024,2048]{1,0:T(8,128)(2,1)}) custom-call(bf16[1024,1024]{1,0:T(8,128)(2,1)} %get-tuple-element.290.refs_4_.refs_0_, bf16[1024,1024]{1,0:T(8,128)(2,1)} %get-tuple-element.291.refs_5_.refs_1_, bf16[1024,1024]{1,0:T(8,128)(2,1)} %get-tuple-element.319.refs_2_.refs_4_, ...), custom_call_target="tpu_custom_call" | custom-call | flops 17179869184 | bytes 16777216 | tf_op jit(solution)/shard_map/pallas_call | solution.py:397
  440.8 4.3 collective-permute-start.52
  445.0 7.0 collective-permute-done.52
  452.0 4.6 convert_add_fusion.13
  458.4 4.3 fusion.1
  473.2 21.0 %shard_map.242 = (bf16[512,1536]{1,0:T(8,128)(2,1)}, bf16[512,1536]{1,0:T(8,128)(2,1)}, bf16[512,1536]{1,0:T(8,128)(2,1)}, bf16[512,1536]{1,0:T(8,128)(2,1)}) custom-call(bf16[1024,2048]{1,0:T(8,128)(2,1)} %copy-done.91, bf16[1024,2048]{1,0:T(8,128)(2,1)} %collective-permute-done.43.refs_1_, bf16[1024,2048]{1,0:T(8,128)(2,1)} %copy-done.92, ...), custom_call_target="tpu_custom_call" | custom-call | flops 12884901888 | bytes 16777216 | tf_op jit(solution)/shard_map/pallas_call | solution.py:361
  512.6 13.4 %shard_map.243 = (bf16[1024,2048]{1,0:T(8,128)(2,1)}, bf16[1024,2048]{1,0:T(8,128)(2,1)}) custom-call(bf16[1024,512]{1,0:T(8,128)(2,1)S(1)} %get-tuple-element.330.refs_6_.refs_0_, bf16[1024,512]{1,0:T(8,128)(2,1)} %get-tuple-element.331.refs_7_.refs_1_, bf16[1024,512]{1,0:T(8,128)(2,1)} %copy-done.5, bf16[1024,512]{1,0:T(8,128)(2,1)} %get-tuple-element.333.refs_7_.refs_3_, ...), custom_call_target="tpu_custom_call" | custom-call | flops 8589934592 | bytes 16777216 | tf_op jit(solution)/shard_map/pallas_call | solution.py:397
  527.7 8.9 %collective-permute-done.61 = bf16[128,2048]{1,0:T(8,128)(2,1)S(1)} collective-permute-done((bf16[128,2048]{1,0:T(8,128)(2,1)S(1)}, bf16[128,2048]{1,0:T(8,128)(2,1)S(1)}, u32[]{:S(2)}, u32[]{:S(2)}) %collective-permute-start.61) | collective-permute-done | bytes 524320 | tf_op jit(solution)/shard_map/ppermute | solution.py:447
  540.7 5.7 collective-permute-done.64
  568.2 6.3 collective-permute-done.72
  582.1 42.1 %shard_map.244 = (bf16[2,4,256,384]{3,2,1,0:T(8,128)(2,1)}, f32[2,256]{1,0:T(2,128)S(1)}) custom-call(bf16[1024,2048]{1,0:T(8,128)(2,1)} %constant_dynamic-update-slice_fusion.15.refs_0_.refs_2_, bf16[1024,2048]{1,0:T(8,128)(2,1)} %collective-permute-done.65.refs_1_.refs_3_, f32[2,4,256,384]{3,2,1,0:T(8,128)} %get-tuple-element.344.refs_2_, ...), custom_call_target="tpu_custom_call" | custom-call | flops 3221225472 | bytes 33554432 | tf_op jit(solution)/shard_map/pallas_call | solution.py:286
  629.2 13.6 %collective-permute-done.67 = bf16[128,1536]{1,0:T(8,128)(2,1)S(1)} collective-permute-done((bf16[128,1536]{1,0:T(8,128)(2,1)S(1)}, bf16[128,1536]{1,0:T(8,128)(2,1)S(1)}, u32[]{:S(2)}, u32[]{:S(2)}) %collective-permute-start.67) | collective-permute-done | bytes 393248 | tf_op jit(solution)/shard_map/ppermute | solution.py:447
  644.1 8.1 shard_map.246
  673.6 13.6 %shard_map.247 = (bf16[512,640]{1,0:T(8,128)(2,1)S(1)}, bf16[512,640]{1,0:T(8,128)(2,1)}, bf16[512,640]{1,0:T(8,128)(2,1)}, bf16[512,640]{1,0:T(8,128)(2,1)}) custom-call(bf16[1024,2048]{1,0:T(8,128)(2,1)} %copy-done.14, bf16[1024,2048]{1,0:T(8,128)(2,1)} %copy-done.24, bf16[1024,2048]{1,0:T(8,128)(2,1)} %constant_dynamic-update-slice_fusion.15.refs_0_.refs_2_, ...), custom_call_target="tpu_custom_call" | custom-call | flops 5368709120 | bytes 16777216 | tf_op jit(solution)/shard_map/pallas_call | solution.py:361
  687.3 9.9 %collective-permute-done.80 = bf16[512,1536]{1,0:T(8,128)(2,1)} collective-permute-done((bf16[512,1536]{1,0:T(8,128)(2,1)}, bf16[512,1536]{1,0:T(8,128)(2,1)}, u32[]{:S(2)}, u32[]{:S(2)}) %collective-permute-start.80) | collective-permute-done | bytes 1572896 | tf_op jit(solution)/shard_map/ppermute | solution.py:455
  703.6 7.1 collective-permute-start.86
  719.0 4.2 collective-permute-done.83
  725.7 5.3 shard_map.245
  734.9 21.0 %collective-permute-done.84 = bf16[512,640]{1,0:T(8,128)(2,1)S(1)} collective-permute-done((bf16[512,640]{1,0:T(8,128)(2,1)S(1)}, bf16[512,640]{1,0:T(8,128)(2,1)S(1)}, u32[]{:S(2)}, u32[]{:S(2)}) %collective-permute-start.84) | collective-permute-done | bytes 655392 | tf_op jit(solution)/shard_map/ppermute | solution.py:455
  777.0 12.0 %collective-permute-done.92 = f32[4224]{0:T(1024)S(1)} collective-permute-done((f32[4224]{0:T(1024)S(1)}, f32[4224]{0:T(1024)S(1)}, u32[]{:S(2)}, u32[]{:S(2)}) %collective-permute-start.92) | collective-permute-done | bytes 16928 | tf_op jit(solution)/shard_map/ppermute | solution.py:606
  794.8 15.3 %collective-permute-done.102 = bf16[128,1536]{1,0:T(8,128)(2,1)S(1)} collective-permute-done((bf16[128,1536]{1,0:T(8,128)(2,1)S(1)}, bf16[128,1536]{1,0:T(8,128)(2,1)S(1)}, u32[]{:S(2)}, u32[]{:S(2)}) %collective-permute-start.102) | collective-permute-done | bytes 393248 | tf_op jit(solution)/shard_map/ppermute | solution.py:447
  816.0 10.3 %collective-permute-done.94 = bf16[512,640]{1,0:T(8,128)(2,1)S(1)} collective-permute-done((bf16[512,640]{1,0:T(8,128)(2,1)S(1)}, bf16[512,640]{1,0:T(8,128)(2,1)S(1)}, u32[]{:S(2)}, u32[]{:S(2)}) %collective-permute-start.94) | collective-permute-done | bytes 655392 | tf_op jit(solution)/shard_map/ppermute | solution.py:455
  826.4 4.1 collective-permute-start.95
  831.8 11.1 %collective-permute-done.95 = bf16[512,640]{1,0:T(8,128)(2,1)S(1)} collective-permute-done((bf16[512,640]{1,0:T(8,128)(2,1)S(1)}, bf16[512,640]{1,0:T(8,128)(2,1)S(1)}, u32[]{:S(2)}, u32[]{:S(2)}) %collective-permute-start.95) | collective-permute-done | bytes 655392 | tf_op jit(solution)/shard_map/ppermute | solution.py:455
  855.8 5.3 shard_map.248
  (597 shorter events, 289.5 us)
Async XLA Ops:
  0.7 25.3 %collective-permute-start.13 = (s32[1,512]{1,0:T(1,128)}, s32[1,512]{1,0:T(1,128)S(1)}, u32[]{:S(2)}, u32[]{:S(2)}) collective-permute-start(s32[1,512]{1,0:T(1,128)} %param.17), channel_id=1, source_target_pairs={{0,6},{2,4},{4,2},{6,0},{8,14},{10,12},{12,10},{14,8},{16,22},{18,... | collective-permute-start | bytes 6152 | tf_op jit(solution)/shard_map/ppermute | solution.py:447
  71.3 30.2 %collective-permute-start.14 = (bf16[1024,2048]{1,0:T(8,128)(2,1)S(1)}, bf16[1024,2048]{1,0:T(8,128)(2,1)S(1)}, u32[]{:S(2)}, u32[]{:S(2)}) collective-permute-start(bf16[1024,2048]{1,0:T(8,128)(2,1)S(1)} %constant_dynamic-update-slice_fusion.refs_0_), channel_id=1, source_target_pairs={{0,1},{1,0},{2,3},{3,2},{4,5},{5,4},{6,7},{7,6},{8,9},{9,8},{10,11... | collective-permute-start | bytes 12582920 | tf_op jit(solution)/shard_map/ppermute | solution.py:435
  101.6 23.9 %collective-permute-start.22 = (bf16[256,2048]{1,0:T(8,128)(2,1)}, bf16[256,2048]{1,0:T(8,128)(2,1)}, u32[]{:S(2)}, u32[]{:S(2)}) collective-permute-start(bf16[256,2048]{1,0:T(8,128)(2,1)} %fusion.25), channel_id=1, source_target_pairs={{0,2},{2,0},{4,6},{6,4},{8,10},{10,8},{12,14},{14,12},{16,18},{18,... | collective-permute-start | bytes 3145736 | tf_op jit(solution)/shard_map/ppermute | solution.py:447
  102.6 24.3 %collective-permute-start.23 = (bf16[256,2048]{1,0:T(8,128)(2,1)}, bf16[256,2048]{1,0:T(8,128)(2,1)}, u32[]{:S(2)}, u32[]{:S(2)}) collective-permute-start(bf16[256,2048]{1,0:T(8,128)(2,1)} %fusion.25), channel_id=1, source_target_pairs={{0,4},{2,6},{4,0},{6,2},{8,12},{10,14},{12,8},{14,10},{16,20},{18,... | collective-permute-start | bytes 3145736 | tf_op jit(solution)/shard_map/ppermute | solution.py:447
  104.1 55.3 %collective-permute-start.20 = (bf16[512,1536]{1,0:T(8,128)(2,1)S(1)}, bf16[512,1536]{1,0:T(8,128)(2,1)}, u32[]{:S(2)}, u32[]{:S(2)}) collective-permute-start(bf16[512,1536]{1,0:T(8,128)(2,1)S(1)} %pad_maximum_fusion.refs_4_), channel_id=1, source_target_pairs={{0,8},{2,10},{4,12},{6,14},{8,16},{10,18},{12,20},{14,22},{16,24},... | collective-permute-start | bytes 4718600 | tf_op jit(solution)/shard_map/ppermute | solution.py:455
  108.9 50.4 %collective-permute-start.21 = (bf16[512,1536]{1,0:T(8,128)(2,1)S(1)}, bf16[512,1536]{1,0:T(8,128)(2,1)}, u32[]{:S(2)}, u32[]{:S(2)}) collective-permute-start(bf16[512,1536]{1,0:T(8,128)(2,1)S(1)} %pad_maximum_fusion.refs_4_), channel_id=1, source_target_pairs={{8,0},{10,2},{12,4},{14,6},{16,8},{18,10},{20,12},{22,14},{24,16},... | collective-permute-start | bytes 4718600 | tf_op jit(solution)/shard_map/ppermute | solution.py:455
  126.6 32.8 %collective-permute-start.24 = (bf16[128,2048]{1,0:T(8,128)(2,1)S(1)}, bf16[128,2048]{1,0:T(8,128)(2,1)S(1)}, u32[]{:S(2)}, u32[]{:S(2)}) collective-permute-start(bf16[128,2048]{1,0:T(8,128)(2,1)S(1)} %slice.475), channel_id=1, source_target_pairs={{0,4},{2,6},{4,0},{6,2},{8,12},{10,14},{12,8},{14,10},{16,20},{18,... | collective-permute-start | bytes 1572872 | tf_op jit(solution)/shard_map/ppermute | solution.py:447
  128.0 31.4 %collective-permute-start.25 = (bf16[128,2048]{1,0:T(8,128)(2,1)S(1)}, bf16[128,2048]{1,0:T(8,128)(2,1)S(1)}, u32[]{:S(2)}, u32[]{:S(2)}) collective-permute-start(bf16[128,2048]{1,0:T(8,128)(2,1)S(1)} %slice.476), channel_id=1, source_target_pairs={{0,2},{2,0},{4,6},{6,4},{8,10},{10,8},{12,14},{14,12},{16,18},{18,... | collective-permute-start | bytes 1572872 | tf_op jit(solution)/shard_map/ppermute | solution.py:447
  159.4 23.2 %collective-permute-start.26 = (bf16[1024,2048]{1,0:T(8,128)(2,1)}, bf16[1024,2048]{1,0:T(8,128)(2,1)S(1)}, u32[]{:S(2)}, u32[]{:S(2)}) collective-permute-start(bf16[1024,2048]{1,0:T(8,128)(2,1)} %get-tuple-element.244), channel_id=1, source_target_pairs={{0,1},{1,0},{2,3},{3,2},{4,5},{5,4},{6,7},{7,6},{8,9},{9,8},{10,11... | collective-permute-start | bytes 12582920 | tf_op jit(solution)/shard_map/ppermute | solution.py:435
  168.9 66.6 %collective-permute-start.36 = (bf16[1024,2048]{1,0:T(8,128)(2,1)S(1)}, bf16[1024,2048]{1,0:T(8,128)(2,1)}, u32[]{:S(2)}, u32[]{:S(2)}) collective-permute-start(bf16[1024,2048]{1,0:T(8,128)(2,1)S(1)} %constant_dynamic-update-slice_fusion.5.refs_2_), channel_id=1, source_target_pairs={{0,1},{1,0},{2,3},{3,2},{4,5},{5,4},{6,7},{7,6},{8,9},{9,8},{10,11... | collective-permute-start | bytes 12582920 | tf_op jit(solution)/shard_map/ppermute | solution.py:435
  196.8 22.9 %collective-permute-start.33 = (bf16[256,2048]{1,0:T(8,128)(2,1)S(1)}, bf16[256,2048]{1,0:T(8,128)(2,1)S(1)}, u32[]{:S(2)}, u32[]{:S(2)}) collective-permute-start(bf16[256,2048]{1,0:T(8,128)(2,1)S(1)} %pad_maximum_fusion.3), channel_id=1, source_target_pairs={{0,4},{2,6},{4,0},{6,2},{8,12},{10,14},{12,8},{14,10},{16,20},{18,... | collective-permute-start | bytes 3145736 | tf_op jit(solution)/shard_map/ppermute | solution.py:447
  198.3 23.3 %collective-permute-start.34 = (bf16[512,1536]{1,0:T(8,128)(2,1)}, bf16[512,1536]{1,0:T(8,128)(2,1)S(1)}, u32[]{:S(2)}, u32[]{:S(2)}) collective-permute-start(bf16[512,1536]{1,0:T(8,128)(2,1)} %collective-permute-done.20), channel_id=1, source_target_pairs={{8,16},{10,18},{12,20},{14,22},{16,24},{18,26},{20,28},{22,30},{9,... | collective-permute-start | bytes 4718600 | tf_op jit(solution)/shard_map/ppermute | solution.py:455
  199.1 36.4 %collective-permute-start.35 = (bf16[512,1536]{1,0:T(8,128)(2,1)}, bf16[512,1536]{1,0:T(8,128)(2,1)S(1)}, u32[]{:S(2)}, u32[]{:S(2)}) collective-permute-start(bf16[512,1536]{1,0:T(8,128)(2,1)} %collective-permute-done.21), channel_id=1, source_target_pairs={{8,0},{10,2},{12,4},{14,6},{16,8},{18,10},{20,12},{22,14},{9,1},{1... | collective-permute-start | bytes 4718600 | tf_op jit(solution)/shard_map/ppermute | solution.py:455
  238.0 34.1 %collective-permute-start.41 = (bf16[512,1536]{1,0:T(8,128)(2,1)S(1)}, bf16[512,1536]{1,0:T(8,128)(2,1)S(1)}, u32[]{:S(2)}, u32[]{:S(2)}) collective-permute-start(bf16[512,1536]{1,0:T(8,128)(2,1)S(1)} %collective-permute-done.34), channel_id=1, source_target_pairs={{16,24},{18,26},{20,28},{22,30},{17,25},{19,27},{21,29},{23,31}} | collective-permute-start | bytes 4718600 | tf_op jit(solution)/shard_map/ppermute | solution.py:455
  238.7 33.8 %collective-permute-start.42 = (bf16[512,1536]{1,0:T(8,128)(2,1)S(1)}, bf16[512,1536]{1,0:T(8,128)(2,1)S(1)}, u32[]{:S(2)}, u32[]{:S(2)}) collective-permute-start(bf16[512,1536]{1,0:T(8,128)(2,1)S(1)} %collective-permute-done.35), channel_id=1, source_target_pairs={{8,0},{10,2},{12,4},{14,6},{9,1},{11,3},{13,5},{15,7}} | collective-permute-start | bytes 4718600 | tf_op jit(solution)/shard_map/ppermute | solution.py:455
  279.1 34.4 %collective-permute-start.44 = (bf16[512,1536]{1,0:T(8,128)(2,1)}, bf16[512,1536]{1,0:T(8,128)(2,1)S(1)}, u32[]{:S(2)}, u32[]{:S(2)}) collective-permute-start(bf16[512,1536]{1,0:T(8,128)(2,1)} %pad_maximum_fusion.1.refs_4_.refs_8_), channel_id=1, source_target_pairs={{0,8},{2,10},{4,12},{6,14},{8,16},{10,18},{12,20},{14,22},{16,24},... | collective-permute-start | bytes 4718600 | tf_op jit(solution)/shard_map/ppermute | solution.py:455
  280.5 36.8 %collective-permute-start.45 = (bf16[512,1536]{1,0:T(8,128)(2,1)}, bf16[512,1536]{1,0:T(8,128)(2,1)S(1)}, u32[]{:S(2)}, u32[]{:S(2)}) collective-permute-start(bf16[512,1536]{1,0:T(8,128)(2,1)} %pad_maximum_fusion.1.refs_4_.refs_8_), channel_id=1, source_target_pairs={{8,0},{10,2},{12,4},{14,6},{16,8},{18,10},{20,12},{22,14},{24,16},... | collective-permute-start | bytes 4718600 | tf_op jit(solution)/shard_map/ppermute | solution.py:455
  317.4 23.0 %collective-permute-start.46 = (bf16[512,1536]{1,0:T(8,128)(2,1)S(1)}, bf16[512,1536]{1,0:T(8,128)(2,1)S(1)}, u32[]{:S(2)}, u32[]{:S(2)}) collective-permute-start(bf16[512,1536]{1,0:T(8,128)(2,1)S(1)} %collective-permute-done.44), channel_id=1, source_target_pairs={{8,16},{10,18},{12,20},{14,22},{16,24},{18,26},{20,28},{22,30},{9,... | collective-permute-start | bytes 4718600 | tf_op jit(solution)/shard_map/ppermute | solution.py:455
  318.1 35.8 %collective-permute-start.47 = (bf16[512,1536]{1,0:T(8,128)(2,1)S(1)}, bf16[512,1536]{1,0:T(8,128)(2,1)}, u32[]{:S(2)}, u32[]{:S(2)}) collective-permute-start(bf16[512,1536]{1,0:T(8,128)(2,1)S(1)} %collective-permute-done.45), channel_id=1, source_target_pairs={{8,0},{10,2},{12,4},{14,6},{16,8},{18,10},{20,12},{22,14},{9,1},{1... | collective-permute-start | bytes 4718600 | tf_op jit(solution)/shard_map/ppermute | solution.py:455
  354.7 35.0 %collective-permute-start.49 = (bf16[512,1536]{1,0:T(8,128)(2,1)}, bf16[512,1536]{1,0:T(8,128)(2,1)S(1)}, u32[]{:S(2)}, u32[]{:S(2)}) collective-permute-start(bf16[512,1536]{1,0:T(8,128)(2,1)} %collective-permute-done.47), channel_id=1, source_target_pairs={{8,0},{10,2},{12,4},{14,6},{9,1},{11,3},{13,5},{15,7}} | collective-permute-start | bytes 4718600 | tf_op jit(solution)/shard_map/ppermute | solution.py:455
  393.0 47.8 %collective-permute-start.50 = (bf16[512,1536]{1,0:T(8,128)(2,1)S(1)}, bf16[512,1536]{1,0:T(8,128)(2,1)}, u32[]{:S(2)}, u32[]{:S(2)}) collective-permute-start(bf16[512,1536]{1,0:T(8,128)(2,1)S(1)} %copy-done.31), channel_id=1, source_target_pairs={{0,8},{2,10},{4,12},{6,14},{1,9},{3,11},{5,13},{7,15}} | collective-permute-start | bytes 4718600 | tf_op jit(solution)/shard_map/ppermute | solution.py:455
  395.5 45.2 %collective-permute-start.51 = (bf16[512,1536]{1,0:T(8,128)(2,1)S(1)}, bf16[512,1536]{1,0:T(8,128)(2,1)}, u32[]{:S(2)}, u32[]{:S(2)}) collective-permute-start(bf16[512,1536]{1,0:T(8,128)(2,1)S(1)} %copy-done.33), channel_id=1, source_target_pairs={{24,16},{26,18},{28,20},{30,22},{25,17},{27,19},{29,21},{31,23}} | collective-permute-start | bytes 4718600 | tf_op jit(solution)/shard_map/ppermute | solution.py:455
  462.7 35.0 %collective-permute-start.57 = (bf16[512,1536]{1,0:T(8,128)(2,1)}, bf16[512,1536]{1,0:T(8,128)(2,1)}, u32[]{:S(2)}, u32[]{:S(2)}) collective-permute-start(bf16[512,1536]{1,0:T(8,128)(2,1)} %get-tuple-element.433), channel_id=1, source_target_pairs={{0,8},{2,10},{4,12},{6,14},{8,16},{10,18},{12,20},{14,22},{1,9},{3... | collective-permute-start | bytes 4718600 | tf_op jit(solution)/shard_map/ppermute | solution.py:455
  465.2 32.5 %collective-permute-start.58 = (bf16[512,1536]{1,0:T(8,128)(2,1)}, bf16[512,1536]{1,0:T(8,128)(2,1)}, u32[]{:S(2)}, u32[]{:S(2)}) collective-permute-start(bf16[512,1536]{1,0:T(8,128)(2,1)} %get-tuple-element.432), channel_id=1, source_target_pairs={{16,8},{18,10},{20,12},{22,14},{24,16},{26,18},{28,20},{30,22},{17... | collective-permute-start | bytes 4718600 | tf_op jit(solution)/shard_map/ppermute | solution.py:455
  470.9 23.3 %collective-permute-start.56 = (bf16[256,2048]{1,0:T(8,128)(2,1)S(1)}, bf16[256,2048]{1,0:T(8,128)(2,1)S(1)}, u32[]{:S(2)}, u32[]{:S(2)}) collective-permute-start(bf16[256,2048]{1,0:T(8,128)(2,1)S(1)} %pad_maximum_fusion.5), channel_id=1, source_target_pairs={{0,4},{2,6},{4,0},{6,2},{8,12},{10,14},{12,8},{14,10},{16,20},{18,... | collective-permute-start | bytes 3145736 | tf_op jit(solution)/shard_map/ppermute | solution.py:447
  472.0 23.2 %collective-permute-start.55 = (bf16[256,2048]{1,0:T(8,128)(2,1)S(1)}, bf16[256,2048]{1,0:T(8,128)(2,1)S(1)}, u32[]{:S(2)}, u32[]{:S(2)}) collective-permute-start(bf16[256,2048]{1,0:T(8,128)(2,1)S(1)} %pad_maximum_fusion.4), channel_id=1, source_target_pairs={{0,2},{2,0},{4,6},{6,4},{8,10},{10,8},{12,14},{14,12},{16,18},{18,... | collective-permute-start | bytes 3145736 | tf_op jit(solution)/shard_map/ppermute | solution.py:447
  502.2 23.8 %collective-permute-start.59 = (bf16[256,2048]{1,0:T(8,128)(2,1)}, bf16[256,2048]{1,0:T(8,128)(2,1)S(1)}, u32[]{:S(2)}, u32[]{:S(2)}) collective-permute-start(bf16[256,2048]{1,0:T(8,128)(2,1)} %get-tuple-element.389), channel_id=1, source_target_pairs={{0,2},{2,0},{4,6},{6,4},{8,10},{10,8},{12,14},{14,12},{16,18},{18,... | collective-permute-start | bytes 3145736 | tf_op jit(solution)/shard_map/ppermute | solution.py:447
  505.8 34.9 %collective-permute-start.63 = (bf16[512,1536]{1,0:T(8,128)(2,1)S(1)}, bf16[512,1536]{1,0:T(8,128)(2,1)S(1)}, u32[]{:S(2)}, u32[]{:S(2)}) collective-permute-start(bf16[512,1536]{1,0:T(8,128)(2,1)S(1)} %add_convert_fusion.5), channel_id=1, source_target_pairs={{0,8},{2,10},{4,12},{6,14},{8,16},{10,18},{12,20},{14,22},{16,24},... | collective-permute-start | bytes 4718600 | tf_op jit(solution)/shard_map/ppermute | solution.py:455
  511.3 35.1 %collective-permute-start.64 = (bf16[512,1536]{1,0:T(8,128)(2,1)S(1)}, bf16[512,1536]{1,0:T(8,128)(2,1)S(1)}, u32[]{:S(2)}, u32[]{:S(2)}) collective-permute-start(bf16[512,1536]{1,0:T(8,128)(2,1)S(1)} %add_convert_fusion.4), channel_id=1, source_target_pairs={{8,0},{10,2},{12,4},{14,6},{16,8},{18,10},{20,12},{22,14},{24,16},... | collective-permute-start | bytes 4718600 | tf_op jit(solution)/shard_map/ppermute | solution.py:455
  553.9 26.7 %collective-permute-start.65 = (bf16[1024,2048]{1,0:T(8,128)(2,1)}, bf16[1024,2048]{1,0:T(8,128)(2,1)}, u32[]{:S(2)}, u32[]{:S(2)}) collective-permute-start(bf16[1024,2048]{1,0:T(8,128)(2,1)} %constant_dynamic-update-slice_fusion.15.refs_0_.refs_2_), channel_id=1, source_target_pairs={{0,1},{1,0},{2,3},{3,2},{4,5},{5,4},{6,7},{7,6},{8,9},{9,8},{10,11... | collective-permute-start | bytes 12582920 | tf_op jit(solution)/shard_map/ppermute | solution.py:435
  562.7 66.5 %collective-permute-start.74 = (bf16[512,1536]{1,0:T(8,128)(2,1)}, bf16[512,1536]{1,0:T(8,128)(2,1)S(1)}, u32[]{:S(2)}, u32[]{:S(2)}) collective-permute-start(bf16[512,1536]{1,0:T(8,128)(2,1)} %get-tuple-element.351), channel_id=1, source_target_pairs={{0,8},{2,10},{4,12},{6,14},{1,9},{3,11},{5,13},{7,15}} | collective-permute-start | bytes 4718600 | tf_op jit(solution)/shard_map/ppermute | solution.py:455
  564.7 64.4 %collective-permute-start.75 = (bf16[512,1536]{1,0:T(8,128)(2,1)}, bf16[512,1536]{1,0:T(8,128)(2,1)S(1)}, u32[]{:S(2)}, u32[]{:S(2)}) collective-permute-start(bf16[512,1536]{1,0:T(8,128)(2,1)} %get-tuple-element.352), channel_id=1, source_target_pairs={{24,16},{26,18},{28,20},{30,22},{25,17},{27,19},{29,21},{31,23}} | collective-permute-start | bytes 4718600 | tf_op jit(solution)/shard_map/ppermute | solution.py:455
  575.7 48.5 %collective-permute-start.73 = (bf16[256,2048]{1,0:T(8,128)(2,1)S(1)}, bf16[256,2048]{1,0:T(8,128)(2,1)S(1)}, u32[]{:S(2)}, u32[]{:S(2)}) collective-permute-start(bf16[256,2048]{1,0:T(8,128)(2,1)S(1)} %pad_maximum_fusion.7), channel_id=1, source_target_pairs={{0,4},{2,6},{4,0},{6,2},{8,12},{10,14},{12,8},{14,10},{16,20},{18,... | collective-permute-start | bytes 3145736 | tf_op jit(solution)/shard_map/ppermute | solution.py:447
  579.8 44.6 %collective-permute-start.71 = (bf16[256,2048]{1,0:T(8,128)(2,1)S(1)}, bf16[256,2048]{1,0:T(8,128)(2,1)S(1)}, u32[]{:S(2)}, u32[]{:S(2)}) collective-permute-start(bf16[256,2048]{1,0:T(8,128)(2,1)S(1)} %pad_maximum_fusion.6), channel_id=1, source_target_pairs={{0,2},{2,0},{4,6},{6,4},{8,10},{10,8},{12,14},{14,12},{16,18},{18,... | collective-permute-start | bytes 3145736 | tf_op jit(solution)/shard_map/ppermute | solution.py:447
  580.6 48.5 %collective-permute-start.66 = (bf16[128,1536]{1,0:T(8,128)(2,1)S(1)}, bf16[128,1536]{1,0:T(8,128)(2,1)S(1)}, u32[]{:S(2)}, u32[]{:S(2)}) collective-permute-start(bf16[128,1536]{1,0:T(8,128)(2,1)S(1)} %get-tuple-element.430), channel_id=1, source_target_pairs={{0,2},{2,0},{4,6},{6,4},{8,10},{10,8},{12,14},{14,12},{16,18},{18,... | collective-permute-start | bytes 1179656 | tf_op jit(solution)/shard_map/ppermute | solution.py:447
  658.2 56.8 %collective-permute-start.76 = (f32[256,2048]{1,0:T(8,128)S(1)}, f32[256,2048]{1,0:T(8,128)}, u32[]{:S(2)}, u32[]{:S(2)}) collective-permute-start(f32[256,2048]{1,0:T(8,128)S(1)} %add.466.mine), channel_id=1, source_target_pairs={{0,1},{1,0},{2,3},{3,2},{4,5},{5,4},{6,7},{7,6},{8,9},{9,8},{10,11... | collective-permute-start | bytes 6291464 | tf_op jit(solution)/shard_map/ppermute | solution.py:435
  661.4 35.7 %collective-permute-start.80 = (bf16[512,1536]{1,0:T(8,128)(2,1)}, bf16[512,1536]{1,0:T(8,128)(2,1)}, u32[]{:S(2)}, u32[]{:S(2)}) collective-permute-start(bf16[512,1536]{1,0:T(8,128)(2,1)} %get-tuple-element.425), channel_id=1, source_target_pairs={{0,8},{2,10},{4,12},{6,14},{8,16},{10,18},{12,20},{14,22},{1,9},{3... | collective-permute-start | bytes 4718600 | tf_op jit(solution)/shard_map/ppermute | solution.py:455
  664.3 32.8 %collective-permute-start.81 = (bf16[512,1536]{1,0:T(8,128)(2,1)}, bf16[512,1536]{1,0:T(8,128)(2,1)S(1)}, u32[]{:S(2)}, u32[]{:S(2)}) collective-permute-start(bf16[512,1536]{1,0:T(8,128)(2,1)} %get-tuple-element.424), channel_id=1, source_target_pairs={{16,8},{18,10},{20,12},{22,14},{24,16},{26,18},{28,20},{30,22},{17... | collective-permute-start | bytes 4718600 | tf_op jit(solution)/shard_map/ppermute | solution.py:455
  670.2 26.9 %collective-permute-start.78 = (bf16[128,2048]{1,0:T(8,128)(2,1)}, bf16[128,2048]{1,0:T(8,128)(2,1)S(1)}, u32[]{:S(2)}, u32[]{:S(2)}) collective-permute-start(bf16[128,2048]{1,0:T(8,128)(2,1)} %get-tuple-element.461), channel_id=1, source_target_pairs={{0,2},{2,0},{4,6},{6,4},{8,10},{10,8},{12,14},{14,12},{16,18},{18,... | collective-permute-start | bytes 1572872 | tf_op jit(solution)/shard_map/ppermute | solution.py:447
  670.3 26.9 %collective-permute-start.79 = (bf16[128,2048]{1,0:T(8,128)(2,1)}, bf16[128,2048]{1,0:T(8,128)(2,1)S(1)}, u32[]{:S(2)}, u32[]{:S(2)}) collective-permute-start(bf16[128,2048]{1,0:T(8,128)(2,1)} %get-tuple-element.460), channel_id=1, source_target_pairs={{0,4},{2,6},{4,0},{6,2},{8,12},{10,14},{12,8},{14,10},{16,20},{18,... | collective-permute-start | bytes 1572872 | tf_op jit(solution)/shard_map/ppermute | solution.py:447
  699.2 24.0 %collective-permute-start.83 = (bf16[256,2048]{1,0:T(8,128)(2,1)S(1)}, bf16[256,2048]{1,0:T(8,128)(2,1)S(1)}, u32[]{:S(2)}, u32[]{:S(2)}) collective-permute-start(bf16[256,2048]{1,0:T(8,128)(2,1)S(1)} %pad_maximum_fusion.9), channel_id=1, source_target_pairs={{0,4},{2,6},{4,0},{6,2},{8,12},{10,14},{12,8},{14,10},{16,20},{18,... | collective-permute-start | bytes 3145736 | tf_op jit(solution)/shard_map/ppermute | solution.py:447
  700.4 30.5 %collective-permute-start.82 = (bf16[256,2048]{1,0:T(8,128)(2,1)}, bf16[256,2048]{1,0:T(8,128)(2,1)}, u32[]{:S(2)}, u32[]{:S(2)}) collective-permute-start(bf16[256,2048]{1,0:T(8,128)(2,1)} %pad_maximum_fusion.8), channel_id=1, source_target_pairs={{0,2},{2,0},{4,6},{6,4},{8,10},{10,8},{12,14},{14,12},{16,18},{18,... | collective-permute-start | bytes 3145736 | tf_op jit(solution)/shard_map/ppermute | solution.py:447
  703.6 52.3 %collective-permute-start.86 = (bf16[512,1536]{1,0:T(8,128)(2,1)S(1)}, bf16[512,1536]{1,0:T(8,128)(2,1)}, u32[]{:S(2)}, u32[]{:S(2)}) collective-permute-start(bf16[512,1536]{1,0:T(8,128)(2,1)S(1)} %add_convert_fusion.2), channel_id=1, source_target_pairs={{0,8},{2,10},{4,12},{6,14},{8,16},{10,18},{12,20},{14,22},{16,24},... | collective-permute-start | bytes 4718600 | tf_op jit(solution)/shard_map/ppermute | solution.py:455
  711.2 44.8 %collective-permute-start.87 = (bf16[512,1536]{1,0:T(8,128)(2,1)S(1)}, bf16[512,1536]{1,0:T(8,128)(2,1)}, u32[]{:S(2)}, u32[]{:S(2)}) collective-permute-start(bf16[512,1536]{1,0:T(8,128)(2,1)S(1)} %add_convert_fusion.1), channel_id=1, source_target_pairs={{8,0},{10,2},{12,4},{14,6},{16,8},{18,10},{20,12},{22,14},{24,16},... | collective-permute-start | bytes 4718600 | tf_op jit(solution)/shard_map/ppermute | solution.py:455
  715.0 40.9 %collective-permute-start.84 = (bf16[512,640]{1,0:T(8,128)(2,1)S(1)}, bf16[512,640]{1,0:T(8,128)(2,1)S(1)}, u32[]{:S(2)}, u32[]{:S(2)}) collective-permute-start(bf16[512,640]{1,0:T(8,128)(2,1)S(1)} %copy-done.65), channel_id=1, source_target_pairs={{0,8},{2,10},{4,12},{6,14},{1,9},{3,11},{5,13},{7,15}} | collective-permute-start | bytes 1966088 | tf_op jit(solution)/shard_map/ppermute | solution.py:455
  724.2 31.7 %collective-permute-start.85 = (bf16[512,640]{1,0:T(8,128)(2,1)S(1)}, bf16[512,640]{1,0:T(8,128)(2,1)S(1)}, u32[]{:S(2)}, u32[]{:S(2)}) collective-permute-start(bf16[512,640]{1,0:T(8,128)(2,1)S(1)} %copy-done.63), channel_id=1, source_target_pairs={{24,16},{26,18},{28,20},{30,22},{25,17},{27,19},{29,21},{31,23}} | collective-permute-start | bytes 1966088 | tf_op jit(solution)/shard_map/ppermute | solution.py:455
  764.8 89.6 %collective-permute-start.88 = (f32[256,2048]{1,0:T(8,128)S(1)}, f32[256,2048]{1,0:T(8,128)S(1)}, u32[]{:S(2)}, u32[]{:S(2)}) collective-permute-start(f32[256,2048]{1,0:T(8,128)S(1)} %fusion.10.mine), channel_id=1, source_target_pairs={{0,1},{1,0},{2,3},{3,2},{4,5},{5,4},{6,7},{7,6},{8,9},{9,8},{10,11... | collective-permute-start | bytes 6291464 | tf_op jit(solution)/shard_map/ppermute | solution.py:435
  771.3 42.7 %collective-permute-start.96 = (bf16[512,640]{1,0:T(8,128)(2,1)S(1)}, bf16[512,640]{1,0:T(8,128)(2,1)S(1)}, u32[]{:S(2)}, u32[]{:S(2)}) collective-permute-start(bf16[512,640]{1,0:T(8,128)(2,1)S(1)} %get-tuple-element.496), channel_id=1, source_target_pairs={{16,8},{18,10},{20,12},{22,14},{24,16},{26,18},{28,20},{30,22},{17... | collective-permute-start | bytes 1966088 | tf_op jit(solution)/shard_map/ppermute | solution.py:455
  (170 other events, 2354.5 us)

commit v3 on v2

--- a/solution.py
+++ b/solution.py
@@ -56,10 +56,10 @@
     )
 
 
-def exact_dot(left, right):
-    return jnp.dot(
-        left, right, preferred_element_type=jnp.float32, precision=lax.Precision.HIGHEST
-    )
+def pick_dot(left, right):
+    high = left.astype(jnp.bfloat16)
+    low = (left - high.astype(jnp.float32)).astype(jnp.bfloat16)
+    return dot_nn(high, right) + dot_nn(low, right)
 
 
 def kernel_call(body, grid, in_specs, out_specs, out_shape, flops, moved):
@@ -99,20 +99,23 @@
     )
 
 
-def spread(values, offset, columns, head_dim):
-    row, column = index_pair(values.shape[1], columns)
-    return exact_dot(values, (row - offset == column % head_dim).astype(jnp.float32))
+def ones_where(condition):
+    return condition.astype(jnp.float32).astype(jnp.bfloat16)
+
+
+def spread_of(rows, offset, columns, head_dim):
+    row, column = index_pair(rows, columns)
+    return ones_where(row - offset == column % head_dim)
 
 
 def fold(values, head_dim):
     row, column = index_pair(values.shape[1], values.shape[1])
-    return exact_dot(values, (row % head_dim == column % head_dim).astype(jnp.float32))
+    return pick_dot(values, ones_where(row % head_dim == column % head_dim))
 
 
 def head_mean(values, head_dim):
     row, column = index_pair(values.shape[1], values.shape[1])
-    same = (row // head_dim == column // head_dim).astype(jnp.float32)
-    return exact_dot(values, same) * (1.0 / head_dim)
+    return pick_dot(values, ones_where(row // head_dim == column // head_dim)) * (1.0 / head_dim)
 
 
 def prepare_heads(raw, gain, cosine, sine, head_dim):
@@ -131,11 +134,13 @@
 def head_inputs(raw, gains, cosine, sine, head_dim, width):
     query, query_scale = prepare_heads(raw[:, :width], gains[0:1], cosine, sine, head_dim)
     rest = raw[:, width:]
-    key_raw = spread(rest, 0, width, head_dim)
+    key_raw = pick_dot(rest, spread_of(rest.shape[1], 0, width, head_dim))
     key, key_scale = prepare_heads(key_raw, gains[1:2], cosine, sine, head_dim)
-    value = spread(rest, head_dim, width, head_dim).astype(jnp.bfloat16)
+    value = dot_nn(
+        rest.astype(jnp.bfloat16), spread_of(rest.shape[1], head_dim, width, head_dim)
+    ).astype(jnp.bfloat16)
     return (
-        query.astype(jnp.bfloat16),
+        query.astype(jnp.bfloat16) * jnp.bfloat16(0.125),
         query_scale,
         key_raw,
         key.astype(jnp.bfloat16),
@@ -149,11 +154,8 @@
     return jnp.where(lane // head_dim == head, values, jnp.zeros_like(values))
 
 
-def softmax_of(query_h, key, allowed):
-    scores = 0.125 * dot_nt(query_h, key)
-    scores = jnp.where(allowed, scores, -1000000000.0)
-    exps = jnp.exp(scores - jnp.max(scores, axis=-1, keepdims=True))
-    return exps * (1.0 / jnp.sum(exps, axis=-1, keepdims=True))
+def exps_of(scores, allowed):
+    return jnp.exp(jnp.where(allowed, scores, -1000000000.0))
 
 
 def block_product(kept, other, blocks, start, stop):
@@ -168,32 +170,51 @@
     return total
 
 
-def allowed_of(start_ref, index_column, index_row):
-    key_index = index_row[...]
-    return (key_index <= index_column[...]) & (key_index >= start_ref[0])
+def by_halves(swapped, one, two):
+    return jnp.where(swapped, two, one), jnp.where(swapped, one, two)
+
+
+def head_tables(cosine_ref, sine_ref, width):
+    repeat = width // cosine_ref.shape[-1]
+    return (
+        jnp.concatenate([cosine_ref[0]] * repeat, axis=1),
+        jnp.concatenate([sine_ref[0]] * repeat, axis=1),
+    )
 
 
 def attention_forward(count, head_dim, width, *refs):
-    kept, other, cosine_ref, sine_ref, start_ref, index_column, index_row, gains = refs[:8]
-    blocks = refs[8 : 8 + count]
-    raw_ref, heads_ref, part_kept, part_other = refs[8 + count :]
+    kept, other = refs[:2]
+    refs = refs[2:]
+    swap_ref, cosine_ref, sine_ref, start_ref, index_column, index_row, gains = refs[:7]
+    blocks = refs[7 : 7 + count]
+    raw_ref, heads_kept, heads_other, part_kept, part_other = refs[7 + count :]
     half = kept.shape[0]
     attn_width = raw_ref.shape[-1]
     raw = block_product(kept, other, blocks, 0, attn_width)
-    raw_ref[0, 0] = raw[:half]
-    raw_ref[1, 0] = raw[half:]
-    repeat = width // cosine_ref.shape[-1]
-    cosine = jnp.concatenate([cosine_ref[0]] * repeat, axis=1)
-    sine = jnp.concatenate([sine_ref[0]] * repeat, axis=1)
+    swapped = swap_ref[...] == 1
+    raw = jnp.concatenate(by_halves(swapped, raw[:half], raw[half:]), axis=0)
+    raw_ref[0] = raw
+    cosine, sine = head_tables(cosine_ref, sine_ref, width)
     query, _, _, key, _, value = head_inputs(raw, gains[...], cosine, sine, head_dim, width)
-    allowed = allowed_of(start_ref, index_column, index_row)
-    heads = jnp.zeros((2 * half, width), jnp.float32)
+    allowed = (index_row[...] <= index_column[...]) & (index_row[...] >= start_ref[0])
+    one = jnp.zeros((half, width), jnp.float32)
+    two = one
     for head in range(width // head_dim):
-        probs = softmax_of(only_head(query, head, head_dim), key, allowed).astype(jnp.bfloat16)
-        heads = heads + only_head(dot_nn(probs, value), head, head_dim)
-    heads = heads.astype(jnp.bfloat16)
-    heads_ref[0, 0] = heads[:half]
-    heads_ref[1, 0] = heads[half:]
+        query_h = only_head(query, head, head_dim)
+        for first in (True, False):
+            span, keys = (slice(0, half), half) if first else (slice(half, 2 * half), 2 * half)
+            exps = exps_of(dot_nt(query_h[span], key[:keys]), allowed[span, :keys])
+            part = dot_nn(exps.astype(jnp.bfloat16), value[:keys])
+            part = part * (1.0 / jnp.sum(exps, axis=-1, keepdims=True))
+            part = only_head(part, head, head_dim)
+            if first:
+                one = one + part
+            else:
+                two = two + part
+    heads = by_halves(swapped, one.astype(jnp.bfloat16), two.astype(jnp.bfloat16))
+    heads_kept[...] = heads[0]
+    heads_other[...] = heads[1]
+    heads = jnp.concatenate(heads, axis=0)
     rows = blocks[0].shape[0]
     for k, block in enumerate(blocks):
         out = dot_nt(heads, block[:, attn_width : attn_width + width]).astype(jnp.bfloat16)
@@ -202,49 +223,61 @@
 
 
 def attention_backward(count, head_dim, width, *refs):
-    kept, other, raw_ref, cosine_ref, sine_ref, start_ref, index_column, index_row, gains = refs[:9]
-    blocks = refs[9 : 9 + count]
-    grad_ref, gain_ref = refs[9 + count :]
+    kept, other, raw_ref = refs[:3]
+    refs = refs[3:]
+    swap_ref, cosine_ref, sine_ref, start_ref, index_column, index_row, gains = refs[:7]
+    blocks = refs[7 : 7 + count]
+    grad_kept, grad_other, gain_ref = refs[7 + count :]
     half = kept.shape[0]
     attn_width = raw_ref.shape[-1]
-    heads_grad = block_product(kept, other, blocks, attn_width, attn_width + width)
-    heads_grad = heads_grad.astype(jnp.bfloat16)
-    raw = jnp.concatenate([raw_ref[0, 0], raw_ref[1, 0]], axis=0)
-    repeat = width // cosine_ref.shape[-1]
-    cosine = jnp.concatenate([cosine_ref[0]] * repeat, axis=1)
-    sine = jnp.concatenate([sine_ref[0]] * repeat, axis=1)
+    grads = block_product(kept, other, blocks, attn_width, attn_width + width)
+    grads = grads.astype(jnp.bfloat16)
+    swapped = swap_ref[...] == 1
+    grads = jnp.concatenate(by_halves(swapped, grads[:half], grads[half:]), axis=0)
+    raw = raw_ref[0]
+    cosine, sine = head_tables(cosine_ref, sine_ref, width)
     query, query_scale, key_raw, key, key_scale, value = head_inputs(
         raw, gains[...], cosine, sine, head_dim, width
     )
-    allowed = allowed_of(start_ref, index_column, index_row)
-    zero = jnp.zeros((2 * half, width), jnp.float32)
-    query_grad, key_grad, value_grad = zero, zero, zero
+    allowed = (index_column[...] <= index_row[...]) & (index_column[...] >= start_ref[0])
+    zero = jnp.zeros((half, width), jnp.float32)
+    query_grads, key_grads, value_grads = [zero, zero], [zero, zero], [zero, zero]
     for head in range(width // head_dim):
         query_h = only_head(query, head, head_dim)
-        grad_h = only_head(heads_grad, head, head_dim)
-        probs_f = softmax_of(query_h, key, allowed)
-        value_grad = value_grad + dot_tn(probs_f.astype(jnp.bfloat16), grad_h)
-        probs_grad = dot_nt(grad_h, value)
-        inner = jnp.sum(probs_f * probs_grad, axis=-1, keepdims=True)
-        score_grad = (probs_f * (probs_grad - inner)).astype(jnp.bfloat16)
-        query_grad = query_grad + only_head(dot_nn(score_grad, key), head, head_dim)
-        key_grad = key_grad + dot_tn(score_grad, query_h)
+        grad_h = only_head(grads, head, head_dim)
+        for part in range(2):
+            span, keys = slice(part * half, (part + 1) * half), (part + 1) * half
+            exps = exps_of(dot_nt(key[:keys], query_h[span]), allowed[:keys, span])
+            probs_f = exps * (1.0 / jnp.sum(exps, axis=0, keepdims=True))
+            weighted = probs_f * dot_nt(value[:keys], grad_h[span])
+            score_grad = weighted - probs_f * jnp.sum(weighted, axis=0, keepdims=True)
+            score_grad = score_grad.astype(jnp.bfloat16)
+            query_grads[part] += only_head(dot_tn(score_grad, key[:keys]), head, head_dim)
+            value_part = dot_nn(probs_f.astype(jnp.bfloat16), grad_h[span])
+            key_part = dot_nn(score_grad, query_h[span])
+            for block in range(part + 1):
+                rows = slice(block * half, (block + 1) * half)
+                value_grads[block] += value_part[rows]
+                key_grads[block] += key_part[rows]
+    query_grad = 0.125 * jnp.concatenate(query_grads, axis=0)
+    key_grad = fold(jnp.concatenate(key_grads, axis=0), head_dim)
+    value_grad = fold(jnp.concatenate(value_grads, axis=0), head_dim)
     query_grad, query_gain_part = prepare_back(
-        raw[:, :width], query_scale, gains[0:1], cosine, sine, 0.125 * query_grad, head_dim
+        raw[:, :width], query_scale, gains[0:1], cosine, sine, query_grad, head_dim
     )
     key_grad, key_gain_part = prepare_back(
-        key_raw, key_scale, gains[1:2], cosine, sine, 0.125 * fold(key_grad, head_dim), head_dim
-    )
-    value_grad = fold(value_grad, head_dim)
+        key_raw, key_scale, gains[1:2], cosine, sine, key_grad, head_dim
+    )
     rest = attn_width - width
     lane = lax.broadcasted_iota(jnp.int32, (2 * half, rest), 1)
     rest_grad = jnp.where(lane < head_dim, key_grad[:, :rest], value_grad[:, :rest])
     query_grad = query_grad.astype(jnp.bfloat16)
     rest_grad = rest_grad.astype(jnp.bfloat16)
-    for side in range(2):
-        rows = slice(side * half, (side + 1) * half)
-        grad_ref[side, 0, :, :width] = query_grad[rows]
-        grad_ref[side, 0, :, width:] = rest_grad[rows]
+    query_sides = by_halves(swapped, query_grad[:half], query_grad[half:])
+    rest_sides = by_halves(swapped, rest_grad[:half], rest_grad[half:])
+    for side, out in enumerate((grad_kept, grad_other)):
+        out[:, :width] = query_sides[side]
+        out[:, width:] = rest_sides[side]
     parts = jnp.concatenate([query_gain_part, key_gain_part], axis=0)
 
     @pl.when(pl.program_id(0) == 0)
@@ -259,42 +292,41 @@
 def run_attention(forward, pair, blocks, tables, gains, head_dim, width, attn_width, raw=None):
     half = pair[0].shape[0] // group
     model = pair[0].shape[1]
-    cosine, sine, starts, index = tables
-    rows = pl.BlockSpec((half, model), lambda s: (s, 0))
-    halves = lambda n: pl.BlockSpec((2, 1, half, n), lambda s: (0, s, 0, 0))
-    per_sequence = lambda a: pl.BlockSpec((1,) + a.shape[1:], lambda s: (s, 0, 0))
+    swapped, cosine, sine, start_columns, start_rows, index = tables
+    starts = start_columns if forward else start_rows
+    rows = lambda n: pl.BlockSpec((half, n), lambda s: (s, 0))
+    per_sequence = lambda shape: pl.BlockSpec((1,) + shape[1:], lambda s: (s, 0, 0))
     column, row = index[:, None], index[None, :]
-    common = [cosine, sine, starts, column, row, gains]
-    common_specs = [per_sequence(cosine), per_sequence(sine), per_sequence(starts)]
+    common = [swapped, cosine, sine, starts, column, row, gains]
+    common_specs = [whole(swapped)] + [per_sequence(a.shape) for a in (cosine, sine, starts)]
     common_specs += [whole(column), whole(row), whole(gains)]
-    flops = 2 * 2 * group * half * model * attn_width
+    common += blocks
+    common_specs += [whole(b) for b in blocks]
+    raw_shape = (group, 2 * half, attn_width)
+    flops = 2 * 2 * group * half * model * attn_width * 10
+    moved = 16 * group * half * model
+    side = lambda n: shape_of((group * half, n), jnp.bfloat16)
     if forward:
-        return kernel_call(
+        results = kernel_call(
             functools.partial(attention_forward, len(blocks), head_dim, width),
             (group,),
-            [rows, rows] + common_specs + [whole(b) for b in blocks],
-            [halves(attn_width), halves(width), rows, rows],
-            [
-                shape_of((2, group, half, attn_width), jnp.float32),
-                shape_of((2, group, half, width), jnp.bfloat16),
-                shape_of((group * half, model), jnp.bfloat16),
-                shape_of((group * half, model), jnp.bfloat16),
-            ],
+            [rows(model)] * 2 + common_specs,
+            [per_sequence(raw_shape), rows(width), rows(width), rows(model), rows(model)],
+            [shape_of(raw_shape, jnp.float32), side(width), side(width), side(model), side(model)],
             flops,
-            16 * group * half * model,
-        )(*pair, *common, *blocks)
-    return kernel_call(
+            moved,
+        )(*pair, *common)
+        return results[0], tuple(results[1:3]), results[3], results[4]
+    results = kernel_call(
         functools.partial(attention_backward, len(blocks), head_dim, width),
         (group,),
-        [rows, rows, halves(attn_width)] + common_specs + [whole(b) for b in blocks],
-        [halves(attn_width), pl.BlockSpec((2, width), lambda s: (0, 0))],
-        [
-            shape_of((2, group, half, attn_width), jnp.bfloat16),
-            shape_of((2, width), jnp.float32),
-        ],
+        [rows(model)] * 2 + [per_sequence(raw_shape)] + common_specs,
+        [rows(attn_width), rows(attn_width), pl.BlockSpec((2, width), lambda s: (0, 0))],
+        [side(attn_width), side(attn_width), shape_of((2, width), jnp.float32)],
         flops,
-        16 * group * half * model,
-    )(*pair, raw, *common, *blocks)
+        moved,
+    )(*pair, raw, *common)
+    return tuple(results[:2]), results[2]
 
 
 def ffn_units(count, ff_sub, *refs):
@@ -369,24 +401,36 @@
     )(*first, *second, *first_grad, *second_grad)
 
 
-def transposed_product(parts, count, *refs):
+def transposed_product(parts, count, gain, *refs):
     lefts = refs[: 2 * parts]
     blocks = refs[2 * parts : 2 * parts + parts * count]
-    outs = refs[2 * parts + parts * count :]
+    rest = refs[2 * parts + parts * count :]
+    normed, outs = (rest[:2], rest[2:]) if gain else ((), rest)
     tile = lefts[0].shape[0]
     rows = blocks[0].shape[0]
+    if gain:
+
+        @pl.when(pl.program_id(0) == 0)
+        def _():
+            outs[2][...] = jnp.zeros_like(outs[2])
+
     for k in range(count):
         total = None
+        span = slice(k * rows, (k + 1) * rows)
         for p in range(parts):
             left = jnp.concatenate([lefts[2 * p][...], lefts[2 * p + 1][...]], axis=0)
             more = dot_nt(left, blocks[p * count + k][...])
             total = more if total is None else total + more
+        if gain:
+            here = total[:tile] * normed[0][:, span].astype(jnp.float32)
+            here = here + total[tile:] * normed[1][:, span].astype(jnp.float32)
+            outs[2][:, span] += jnp.sum(here, axis=0, keepdims=True)
         total = total.astype(jnp.bfloat16)
-        outs[0][:, k * rows : (k + 1) * rows] = total[:tile]
-        outs[1][:, k * rows : (k + 1) * rows] = total[tile:]
-
-
-def run_transposed_product(pairs, blocks, column, columns):
+        outs[0][:, span] = total[:tile]
+        outs[1][:, span] = total[tile:]
+
+
+def run_transposed_product(pairs, blocks, column, columns, normed=()):
     count = len(blocks[0])
     tokens = pairs[0][0].shape[0]
     model = count * blocks[0][0].shape[0]
@@ -394,16 +438,72 @@
     rows = lambda n: pl.BlockSpec((tile, n), lambda i: (i, 0))
     lefts = [a for pair in pairs for a in pair]
     flat = [b for one in blocks for b in one]
+    gain = len(normed) > 0
     return kernel_call(
-        functools.partial(transposed_product, len(pairs), count),
+        functools.partial(transposed_product, len(pairs), count, gain),
         (tokens // tile,),
         [rows(a.shape[1]) for a in lefts]
-        + [pl.BlockSpec((b.shape[0], columns), lambda i: (0, column)) for b in flat],
-        [rows(model)] * 2,
-        [shape_of((tokens, model), jnp.bfloat16)] * 2,
-        4 * tokens * model * columns * len(pairs),
-        8 * tokens * model,
-    )(*lefts, *flat)
+        + [pl.BlockSpec((b.shape[0], columns), lambda i: (0, column)) for b in flat]
+        + [rows(model) for _ in normed],
+        [rows(model)] * 2 + [pl.BlockSpec((1, model), lambda i: (0, 0))] * gain,
+        [shape_of((tokens, model), jnp.bfloat16)] * 2 + [shape_of((1, model), jnp.float32)] * gain,
+        1 if gain else 4 * tokens * model * columns * len(pairs),
+        1 if gain else 8 * tokens * model,
+    )(*lefts, *flat, *normed)
+
+
+def add_both(*refs):
+    for left, right, out in zip(refs[0:2], refs[2:4], refs[4:6]):
+        out[...] = (left[...].astype(jnp.float32) + right[...].astype(jnp.float32)).astype(
+            jnp.bfloat16
+        )
+
+
+def run_add_both(blocks, got):
+    rows, width = blocks[0].shape
+    tile = min(128, rows)
+    spec = pl.BlockSpec((tile, width), lambda i: (i, 0))
+    return kernel_call(
+        add_both,
+        (rows // tile,),
+        [spec] * 4,
+        [spec] * 2,
+        [shape_of((rows, width), jnp.bfloat16)] * 2,
+        1,
+        12 * rows * width,
+    )(*blocks, *got)
+
+
+def place_columns(subs, place_ref, *refs):
+    ins, outs = refs[: group * subs], refs[group * subs :]
+    place = place_ref[0]
+    rows = ins[0].shape[0]
+    width = ins[0].shape[1] // len(outs)
+    for s in range(subs):
+        for r, ref in enumerate(ins[group * s : group * (s + 1)]):
+            start = ref.shape[0] - rows if r == group - 1 else 0
+            column = pl.multiple_of((s * group + (place ^ r)) * width, width)
+            for m, out in enumerate(outs):
+                piece = ref[start : start + rows, m * width : (m + 1) * width]
+                out[:, pl.ds(column, width)] = piece.astype(jnp.float32)
+
+
+def run_place_columns(place, parts, count):
+    rows, width = parts[0][0].shape
+    flat = [a for part in parts for a in part]
+    full = lambda a: pl.BlockSpec(a.shape, lambda i, place: (0, 0))
+    shape = shape_of((rows, width // count * group * len(parts)), jnp.float32)
+    return pl.pallas_call(
+        functools.partial(place_columns, len(parts)),
+        grid_spec=pltpu.PrefetchScalarGridSpec(
+            num_scalar_prefetch=1,
+            grid=(1,),
+            in_specs=[full(a) for a in flat],
+            out_specs=[full(shape)] * count,
+        ),
+        out_shape=[shape] * count,
+        compiler_params=pltpu.CompilerParams(vmem_limit_bytes=vmem_limit),
+    )(place.reshape(1).astype(jnp.int32), *flat)
 
 
 def place_halves(place, mine, other, out):
@@ -483,6 +583,16 @@
     def flip_pieces(self, pieces):
         return [pieces[0]] + [self.flip(pieces[r], r) for r in range(1, group)]
 
+    def flip_first(self, pieces):
+        return self.flip(jnp.concatenate([pieces[1], pieces[3]]), 1)
+
+    def flip_second(self, pieces, got):
+        return self.flip(jnp.concatenate([pieces[2], got[got.shape[0] // 2 :]]), 2)
+
+    def flipped(self, pieces, first, second):
+        rows = pieces[0].shape[0]
+        return [pieces[0], first[:rows], second[:rows], second[rows:]]
+
     def row_pieces(self, total):
         rows = total.shape[0] // group
         return [
@@ -519,14 +629,23 @@
     def across_terms(self, kept, other):
         return self.scatter_across(self.terms(kept, other, 3).astype(jnp.bfloat16))
 
-    def near_terms(self, kept, other, got):
+    def near_sends(self, kept, other, got):
         one, two = self.terms(kept, other, 1), self.terms(kept, other, 2)
         middle = one.shape[0] // 2
         one = jnp.concatenate([one[:middle], one[middle:] + got[1].astype(jnp.float32)])
         two = jnp.concatenate([two[:middle] + got[0].astype(jnp.float32), two[middle:]])
-        one = self.flip(one.astype(jnp.bfloat16), 1)
-        two = self.flip(two.astype(jnp.bfloat16), 2)
+        return [one.astype(jnp.bfloat16), two.astype(jnp.bfloat16)]
+
+    def near_flips(self, kept, other, got):
+        one, two = self.near_sends(kept, other, got)
+        return [self.flip(one, 1), self.flip(two, 2)]
+
+    def near_sum(self, kept, other, near):
+        one, two = near
         return self.terms(kept, other, 0) + one.astype(jnp.float32) + two.astype(jnp.float32)
+
+    def near_terms(self, kept, other, got):
+        return self.near_sum(kept, other, self.near_flips(kept, other, got))
 
     def scatter_tokens(self, kept, other):
         return self.near_terms(kept, other, self.across_terms(kept, other))
@@ -568,15 +687,20 @@
     def __init__(self, lines, blocks):
         self.lines, self.blocks, self.got = lines, blocks, []
 
-    def hop(self):
+    def ready(self):
+        step = len(self.got) + 1
+        if self.lines.length != 4:
+            return []
+        blocks = [self.blocks[self.lines.length - step], self.blocks[step]]
+        return run_add_both(blocks, self.got[-1]) if self.got else blocks
+
+    def hop(self, ready=None):
         lines, step = self.lines, len(self.got) + 1
         if lines.length != 4:
             turns = range(1, lines.length) if step == 1 else ()
             self.got.append([lines.turn(self.blocks[k], k) for k in turns])
             return
-        up, down = self.blocks[lines.length - step], self.blocks[step]
-        if self.got:
-            up, down = add(up, self.got[-1][0]), add(down, self.got[-1][1])
+        up, down = self.ready() if ready is None else ready
         self.got.append(
             [
                 lines.hop(up, 0, min(step - 1, lines.length - 2), 1),
@@ -592,20 +716,8 @@
         return result.astype(jnp.bfloat16)
 
 
-def add(left, right):
-    return (left.astype(jnp.float32) + right.astype(jnp.float32)).astype(jnp.bfloat16)
-
-
 def tie(*values):
     return lax.optimization_barrier(values)
-
-
-def sum_all(values, dp):
-    bit = 1
-    while bit < dp:
-        values = values + lax.ppermute(values, "dp", [(i, i ^ bit) for i in range(dp)])
-        bit *= 2
-    return values + swap_cores(values)
 
 
 def local(
@@ -643,9 +755,6 @@
     def back_around(values):
         return jnp.roll(values, lines.spot * block_rows, axis=-1)
 
-    def halves(values, axis=0):
-        return jnp.roll(values, -core * half, axis=axis)
-
     attn_gain_r, ffn_gain_r = around(attn_gain), around(ffn_gain)
 
     def columns(weight, start, size):
@@ -667,16 +776,10 @@
     normed_f, scale_first = norm_rows(source, attn_gain_r)
     normed_mine = normed_f.astype(jnp.bfloat16)
 
-    seg_all = jnp.stack([segments[0]] + [lines.flip(segments, r)[0] for r in range(1, group)])
-    positions = halves(jax.vmap(positions_of)(seg_all), axis=1)
-    index = halves(jnp.arange(length, dtype=jnp.int32))
-    cosine, sine = angles(positions, head_dim, 2 * head_dim)
-    tables = (cosine, sine, (index[None] - positions)[..., None], index)
-    gains_two = jnp.stack(
-        [
-            jnp.tile(query_gain, query_width // head_dim),
-            jnp.tile(key_gain, query_width // head_dim),
-        ]
+    seg_near = jnp.concatenate([segments, lines.flip(segments, 1)])
+    seg_second = lines.flip(seg_near, 2)
+    attn_shared, normed_mine, seg_near, seg_second = tie(
+        attn_shared, normed_mine, seg_near, seg_second
     )
 
     def ffn_piece(s):
@@ -690,20 +793,47 @@
             )
         )
 
-    pieces_0, pieces_1 = ffn_piece(0), ffn_piece(1)
-    cot_half = around(lax.dynamic_slice_in_dim(cotangent, core * half, half))
-    out_mine = cot_half.astype(jnp.bfloat16)
-    attn_shared, normed_mine, pieces_0, out_mine = tie(attn_shared, normed_mine, pieces_0, out_mine)
+
+    seg_all = jnp.concatenate([seg_near, seg_second])
+    positions = jax.vmap(positions_of)(seg_all)
+    index = jnp.arange(length, dtype=jnp.int32)
+    cosine, sine = angles(positions, head_dim, 2 * head_dim)
+    swapped = jnp.full((1, 1), core, jnp.int32)
+    starts = index[None] - positions
+    tables = (swapped, cosine, sine, starts[..., None], starts[:, None, :], index)
+    gains_two = jnp.stack(
+        [
+            jnp.tile(query_gain, query_width // head_dim),
+            jnp.tile(key_gain, query_width // head_dim),
+        ]
+    )
 
     attn_line = LineGather(lines, jnp.concatenate(lines.by_place(attn_shared), axis=0))
     attn_line.hop()
     near = lines.gather_near(normed_mine)
-    near, attn_line.got[0], pieces_0 = tie(near, attn_line.got[0], pieces_0)
+    mine_other = swap_cores(normed_mine)
+    near, attn_line.got[0], tables, mine_other, w_gate, w_up, w_down = tie(
+        near, attn_line.got[0], tables, mine_other, w_gate, w_up, w_down
+    )
     attn_line.hop()
     across = lines.gather_across(near)
-    across, attn_line.got[1], pieces_0, tables = tie(across, attn_line.got[1], pieces_0, tables)
+    pieces_0 = ffn_piece(0)
+    near_other = swap_cores(near[0])
+    near_other, near_two = tie(near_other, near[1])
+    near = [near[0], near_two]
+    near_other = [near_other, swap_cores(near_two)]
+    across, attn_line.got[1], pieces_0, near_other, w_gate, w_up, w_down, cotangent = tie(
+        across, attn_line.got[1], pieces_0, near_other, w_gate, w_up, w_down, cotangent
+    )
     attn_line.hop()
-    normed = lines.both_cores(normed_mine, near, across)
+    pieces_1 = ffn_piece(1)
+    cot_half = around(lax.dynamic_slice_in_dim(cotangent, core * half, half))
+    out_mine = cot_half.astype(jnp.bfloat16)
+    across = jnp.concatenate(across)
+    normed = (
+        jnp.concatenate([normed_mine] + near + [across]),
+        jnp.concatenate([mine_other] + near_other + [swap_cores(across)]),
+    )
     shared_0 = lines.flip_pieces(pieces_0)
     normed, attn_line.got[2], shared_0, pieces_1, out_mine = tie(
         normed, attn_line.got[2], shared_0, pieces_1, out_mine
@@ -712,40 +842,52 @@
 
     line_0 = LineGather(lines, jnp.concatenate(lines.by_place(shared_0), axis=0))
     line_0.hop()
-    out_near, out_across = lines.gather_far(out_mine)
+    out_near = lines.gather_near(out_mine)
     qkv_raw, heads_out, attended_kept, attended_other = run_attention(
         True, normed, attn_w, tables, gains_two, head_dim, query_width, attn_width
     )
-    attended_other, line_0.got[0], out_near, out_across, pieces_1 = tie(
-        attended_other, line_0.got[0], out_near, out_across, pieces_1
+    attended_other, line_0.got[0], out_near, pieces_1 = tie(
+        attended_other, line_0.got[0], out_near, pieces_1
     )
 
     line_0.hop()
-    shared_1 = lines.flip_pieces(pieces_1)
     attended_other = swap_cores(attended_other)
-    attended_other, shared_1 = tie(attended_other, shared_1)
-    out_b = lines.both_cores(out_mine, out_near, out_across)
-    attended = lines.scatter_tokens(attended_kept, attended_other)
-    attended, line_0.got[1], out_b, shared_1 = tie(attended, line_0.got[1], out_b, shared_1)
-
+    middle = half // 2
+    out_first = lines.flip(out_near[0][:middle], 2)
+    attended_other, out_first = tie(attended_other, out_first)
+    first_1 = lines.flip_first(pieces_1)
+    got = lines.across_terms(attended_kept, attended_other)
+    got, first_1, line_0.got[1] = tie(got, first_1, line_0.got[1])
     line_0.hop()
-    line_1 = LineGather(lines, jnp.concatenate(lines.by_place(shared_1), axis=0))
+    second_1 = lines.flip_second(pieces_1, first_1)
+    attended = lines.near_terms(attended_kept, attended_other, got)
+    attended, out_near = tie(attended, out_near)
+    out_second = lines.flip(out_near[1][middle:], 1)
+    attended, line_0.got[2], out_first, out_second, second_1 = tie(
+        attended, line_0.got[2], out_first, out_second, second_1
+    )
+    shared_1 = lines.flipped(pieces_1, first_1, second_1)
+    block_1 = jnp.concatenate(lines.by_place(shared_1), axis=0)
+
+    line_1 = LineGather(lines, block_1)
+    out_b = lines.both_cores(out_mine, out_near, [out_first, out_second])
+    line_1.hop()
     state = source + attended
     normed2_f, scale_second = norm_rows(state, ffn_gain_r)
     near, across = lines.gather_far(normed2_f.astype(jnp.bfloat16))
-    near, across, line_0.got[2], line_1.block = tie(near, across, line_0.got[2], line_1.block)
+    ffn_w = [line_0.blocks()]
+    near, across, line_1.got[0], out_b, ffn_w[0] = tie(
+        near, across, line_1.got[0], out_b, ffn_w[0]
+    )
 
     line_1.hop()
     normed2 = lines.both_cores(normed2_f.astype(jnp.bfloat16), near, across)
-    ffn_w = [line_0.blocks()]
     units_0 = run_ffn_units(normed2, out_b, ffn_w[0], ff_sub)
-    units_0, line_1.got[0] = tie(units_0, line_1.got[0])
+    units_0, line_1.got[1] = tie(units_0, line_1.got[1])
     line_1.hop()
     ffn_g = run_weight_gradients(normed2, units_0[2:], out_b, units_0[:2], lines.length)
-    ffn_g, line_1.got[1], units_0 = tie(ffn_g, line_1.got[1], units_0)
-    line_1.hop()
+    ffn_g, line_1.got[2], units_0 = tie(ffn_g, line_1.got[2], units_0)
     sum_0 = LineScatter(lines, ffn_g)
-    line_1.got[2], sum_0.blocks = tie(line_1.got[2], sum_0.blocks)
     ffn_w.append(line_1.blocks())
 
     sum_0.hop()
@@ -756,94 +898,106 @@
     sum_0.hop()
     other = swap_cores(other)
     got = lines.across_terms(kept, other)
-    got, units_1 = tie(got, units_1)
+    branch_kept, branch_other = run_transposed_product(
+        [units_0[:2], units_1[:2]], ffn_w, 2, ff_sub
+    )
+    branch_other = swap_cores(branch_other)
+    got, sum_0.got[1], units_1, branch_kept, branch_other = tie(
+        got, sum_0.got[1], units_1, branch_kept, branch_other
+    )
+    sum_0.hop()
+    near = lines.near_flips(kept, other, got)
     sum_1 = LineScatter(
         lines, run_weight_gradients(normed2, units_1[2:], out_b, units_1[:2], lines.length)
     )
-    normed2_grad = lines.near_terms(kept, other, got)
-    normed2_grad, sum_0.got[1], sum_1.blocks, units_0, units_1 = tie(
-        normed2_grad, sum_0.got[1], sum_1.blocks, units_0, units_1
-    )
-
-    sum_0.hop()
+    near, branch_kept, branch_other = tie(near, branch_kept, branch_other)
+    normed2_grad = lines.near_sum(kept, other, near)
+    branch_got = lines.across_terms(branch_kept, branch_other)
+    normed2_grad, sum_0.got[2], branch_got, sum_1.blocks = tie(
+        normed2_grad, sum_0.got[2], branch_got, sum_1.blocks
+    )
+
+    sum_1.hop()
     ffn_gain_part = jnp.sum(normed2_grad * state * scale_second, axis=0)
     state_grad = cot_half + norm_back(state, scale_second, ffn_gain_r, normed2_grad)
     grad_mine = state_grad.astype(jnp.bfloat16)
-    near = lines.gather_near(grad_mine)
-    branch_kept, branch_other = run_transposed_product(
-        [units_0[:2], units_1[:2]], ffn_w, 2, ff_sub
-    )
-    near, branch_kept, branch_other = tie(near, branch_kept, branch_other)
-    across = lines.gather_across(near)
-    across, sum_0.got[2], branch_kept, branch_other = tie(
-        across, sum_0.got[2], branch_kept, branch_other
+    near, across = lines.gather_far(grad_mine)
+    back_0 = lines.row_pieces(sum_0.total())
+    branch_terms = lines.near_sends(branch_kept, branch_other, branch_got)
+    near, across, sum_1.got[0], back_0, branch_terms = tie(
+        near, across, sum_1.got[0], back_0, branch_terms
     )
 
     sum_1.hop()
     attended_b = lines.both_cores(grad_mine, near, across)
 
-    def owners_rows(total):
-        return lines.flip_pieces(lines.row_pieces(total))
-
-    branch = lines.scatter_tokens(branch_kept, swap_cores(branch_other))
-    ffn_grads = [owners_rows(sum_0.total())]
+    branch = [lines.flip(branch_terms[0], 1), lines.flip(branch_terms[1], 2)]
+    back_0_first = lines.flip_first(back_0)
     qkv_grad, gain_parts = run_attention(
         False, attended_b, attn_w, tables, gains_two, head_dim, query_width, attn_width, qkv_raw
     )
-    qkv_grad, ffn_grads[0], branch, sum_1.got[0] = tie(
-        qkv_grad, ffn_grads[0], branch, sum_1.got[0]
+    kept, other, attn_gain_part = run_transposed_product(
+        [qkv_grad], [attn_w], 0, attn_width, normed
+    )
+    kept, other, qkv_grad, branch, sum_1.got[1], back_0, back_0_first = tie(
+        kept, other, qkv_grad, branch, sum_1.got[1], back_0, back_0_first
     )
 
     sum_1.hop()
-    qkv_grad = tuple(qkv_grad.reshape(2, group * half, attn_width))
-    heads_out = tuple(heads_out.reshape(2, group * half, query_width))
-    kept, other = run_transposed_product([qkv_grad], [attn_w], 0, attn_width)
+    gains = jnp.concatenate(
+        [
+            back_around(attn_gain_part[0] / attn_gain_r),
+            back_around(ffn_gain_part),
+            jnp.sum(gain_parts[0].reshape(-1, head_dim), axis=0),
+            gain_parts[1][:head_dim],
+        ]
+    )
     other = swap_cores(other)
+    back_0_second = lines.flip_second(back_0, back_0_first)
     got = lines.across_terms(kept, other)
     attn_sum = LineScatter(
         lines, run_weight_gradients(normed, qkv_grad, attended_b, heads_out, lines.length)
     )
-    got, sum_1.got[1], attn_sum.blocks = tie(got, sum_1.got[1], attn_sum.blocks)
+    got, sum_1.got[2], attn_sum.blocks, back_0_second, gains = tie(
+        got, sum_1.got[2], attn_sum.blocks, back_0_second, gains
+    )
     attn_sum.hop()
-    sum_1.hop()
-    normed_grad = lines.near_terms(kept, other, got)
-    normed_grad, attn_sum.got[0], sum_1.got[2] = tie(normed_grad, attn_sum.got[0], sum_1.got[2])
+    back_1 = lines.row_pieces(sum_1.total())
+    near = lines.near_flips(kept, other, got)
     attn_sum.hop()
+    near, attn_sum.got[1], back_1 = tie(near, attn_sum.got[1], back_1)
     attn_sum.hop()
-    ffn_grads.append(owners_rows(sum_1.total()))
-    attn_grads = owners_rows(attn_sum.total())
-    mixed = state + branch
-    attn_gain_part = jnp.sum(normed_grad * source * scale_first, axis=0)
+    back_1 = lines.flip_pieces(back_1)
+    attn_sum.got[2], back_1, near, gains = tie(attn_sum.got[2], back_1, near, gains)
+    attn_grads = lines.flip_pieces(lines.row_pieces(attn_sum.total()))
+    normed_grad = lines.near_sum(kept, other, near)
     input_grad = state_grad + norm_back(source, scale_first, attn_gain_r, normed_grad)
-
-    def whole_rows(mine):
-        return run_place_halves(core, lines.spot, lines.length, mine, swap_cores(mine))
-
-    gains = sum_all(
-        jnp.concatenate(
-            [
-                back_around(attn_gain_part),
-                back_around(ffn_gain_part),
-                jnp.sum(gain_parts[0].reshape(-1, head_dim), axis=0),
-                gain_parts[1][:head_dim],
-            ]
-        ),
-        dp,
-    )
+    input_other = swap_cores(input_grad)
+    bit = 1
+    while bit < dp:
+        gains = gains + lines.flip(gains, bit)
+        bit *= 2
+    gains = gains + swap_cores(gains)
+    ffn_grads = run_place_columns(
+        lines.place,
+        [
+            (back_0[0], back_0_first, back_0_second, back_0_second),
+            back_1,
+        ],
+        3,
+    )
+    mixed = state + lines.near_sum(branch_kept, branch_other, branch)
+
+    def whole_rows(mine, other):
+        return run_place_halves(core, lines.spot, lines.length, mine, other)
 
     def columns_of(related, start, stop):
         blocks = lines.by_place([b[:, start:stop] for b in related])
         return jnp.concatenate(blocks, axis=1).astype(jnp.float32)
 
-    def ffn_columns(which):
-        return jnp.concatenate(
-            [columns_of(blocks, which * ff_sub, (which + 1) * ff_sub) for blocks in ffn_grads],
-            axis=1,
-        )
-
     return (
-        whole_rows(mixed),
-        whole_rows(input_grad),
+        whole_rows(mixed, swap_cores(mixed)),
+        whole_rows(input_grad, input_other),
         gains[:width],
         gains[width : 2 * width],
         gains[2 * width : 2 * width + head_dim],
@@ -852,9 +1006,7 @@
         columns_of(attn_grads, query_width, query_width + key_width),
         columns_of(attn_grads, query_width + key_width, attn_width),
         columns_of(attn_grads, attn_width, attn_width + query_width),
-        ffn_columns(0),
-        ffn_columns(1),
-        ffn_columns(2),
+        *ffn_grads,
     )
 
 

time: 873 us -> 778 us (0.89)
  waiting for transfers between devices: 336 us -> 252 us
  other arithmetic: 108 us -> 89.7 us
  Pallas kernels: 221 us -> 230 us
    ppermute x36, waiting for transfers between devices: 146 us -> 111 us  [hop(): return lax.ppermute(values, 'dp', pairs)]
    pallas_call x3 -> x10, Pallas kernels: 45.1 us -> 76.6 us  [the longest x3 47.2 us: run_transposed_product(): kernel_call(functools.partial(transposed_product, len(pairs), count, gain...]
    ppermute x53 -> x54, waiting for transfers between devices: 165 us -> 136 us  [flip(): lax.ppermute(values, 'dp', [(i, i ^ relation) for i in range(self.dp)])]
    pallas_call x1, Pallas kernels: 42.1 us -> 26.3 us  [run_attention(): kernel_call(functools.partial(attention_backward, len(blocks), head_dim,...]
    ppermute x4 -> x0, waiting for transfers between devices: 14.6 us -> none  [sum_all(): lax.ppermute(values, 'dp', [(i, i ^ bit) for i in range(dp)])]
    convert_element_type x9 -> x1, other arithmetic: 13 us -> 0.01 us  [angles(): phases = positions.astype(jnp.float32)[..., None] * frequency]
    ppermute x11 -> x14, starting transfers between devices: 30.7 us -> 36.5 us  [swap_cores(): return lax.ppermute(values, 'tensor', [(0, 1), (1, 0)])]
    unnamed x242 -> x190, local copies, waits for them, and re-layouts: 20.4 us -> 22.7 us
  transfers between devices with their start and end apart: 104 -> 104, of which waited for: 45 -> 42; matrix products, arithmetic and copies ran while one was open for 14% -> 13% of each run, Pallas kernels for 24% -> 29%
where the time goes in v3:
time: 778 us; the launch traced here: 770 us
  waiting for transfers between devices  252 us (32%)
  Pallas kernels  230 us (30%)
  starting transfers between devices  154 us (20%)
  other arithmetic  89.7 us (12%)
  local copies, waits for them, and re-layouts  42.1 us (5%)
    ppermute x54, waiting for transfers between devices, flip(): lax.ppermute(values, 'dp', [(i, i ^ relation) for i in range(self.dp)])  136 us
    ppermute x36, waiting for transfers between devices, hop(): return lax.ppermute(values, 'dp', pairs)  111 us
    ppermute x36, starting transfers between devices, hop(): return lax.ppermute(values, 'dp', pairs)  74.1 us
    pallas_call x3, Pallas kernels, run_weight_gradients(): kernel_call(functools.partial(weight_gradients, count, per), (model // ti...  55.9 us
    pallas_call x3, Pallas kernels, run_transposed_product(): kernel_call(functools.partial(transposed_product, len(pairs), count, gain...  47.2 us
    ppermute x54, starting transfers between devices, flip(): lax.ppermute(values, 'dp', [(i, i ^ relation) for i in range(self.dp)])  43.1 us
    pallas_call x2, Pallas kernels, run_ffn_units(): kernel_call(functools.partial(ffn_units, len(blocks), ff_sub), (tokens //...  39.1 us
    ppermute x14, starting transfers between devices, swap_cores(): return lax.ppermute(values, 'tensor', [(0, 1), (1, 0)])  36.5 us
  transfers between devices with their start and end apart: 104, of which 42 were waited for; matrix products, arithmetic and copies ran while one was open for 13% of the time, Pallas kernels for 29%

profile of v3, /device:TPU:1, one launch (start us, length us, event | category | flops | bytes accessed | tf_op | source)
XLA Modules:
  0.0 769.7 jit_solution(940013413258633443)
XLA Ops:
  31.3 5.5 multiply_sine_fusion
  38.3 7.9 %collective-permute-done.5 = bf16[256,2048]{1,0:T(8,128)(2,1)} collective-permute-done((bf16[256,2048]{1,0:T(8,128)(2,1)S(1)}, bf16[256,2048]{1,0:T(8,128)(2,1)}, u32[]{:S(2)}, u32[]{:S(2)}) %collective-permute-start.5) | collective-permute-done | bytes 1048608 | tf_op jit(solution)/shard_map/ppermute | solution.py:547
  47.1 4.2 collective-permute-start.10
  70.1 8.4 %collective-permute-done.14 = bf16[512,640]{1,0:T(8,128)(2,1)} collective-permute-done((bf16[512,640]{1,0:T(8,128)(2,1)}, bf16[512,640]{1,0:T(8,128)(2,1)}, u32[]{:S(2)}, u32[]{:S(2)}) %collective-permute-start.14) | collective-permute-done | bytes 655392 | tf_op jit(solution)/shard_map/ppermute | solution.py:555
  94.8 8.4 %collective-permute-done.20 = bf16[128,1536]{1,0:T(8,128)(2,1)S(1)} collective-permute-done((bf16[128,1536]{1,0:T(8,128)(2,1)S(1)}, bf16[128,1536]{1,0:T(8,128)(2,1)S(1)}, u32[]{:S(2)}, u32[]{:S(2)}) %collective-permute-start.20) | collective-permute-done | bytes 393248 | tf_op jit(solution)/shard_map/ppermute | solution.py:547
  104.7 4.8 collective-permute-start.22
  115.4 20.8 %shard_map.237 = (f32[4,512,384]{2,1,0:T(8,128)}, bf16[1024,256]{1,0:T(8,128)(2,1)S(1)}, bf16[1024,256]{1,0:T(8,128)(2,1)S(1)}, bf16[1024,2048]{1,0:T(8,128)(2,1)}, bf16[1024,2048]{1,0:T(8,128)(2,1)}) custom-call(bf16[1024,2048]{1,0:T(8,128)(2,1)} %constant_dynamic-update-slice_fusion.refs_0_.refs_6_, bf16[1024,2048]{1,0:T(8,128)(2,1)} %pad_maximum_fusion.refs_1_.refs_7_, ...), custom_call_target="tpu_custom_call" | custom-call | flops 32212254720 | bytes 33554432 | tf_op jit(solution)/shard_map/pallas_call | solution.py:310
  136.2 4.6 collective-permute-done.22
  140.8 5.1 collective-permute-done.23
  152.0 10.0 %collective-permute-done.27 = bf16[128,2048]{1,0:T(8,128)(2,1)S(1)} collective-permute-done((bf16[128,2048]{1,0:T(8,128)(2,1)S(1)}, bf16[128,2048]{1,0:T(8,128)(2,1)S(1)}, u32[]{:S(2)}, u32[]{:S(2)}) %collective-permute-start.27) | collective-permute-done | bytes 524320 | tf_op jit(solution)/shard_map/ppermute | solution.py:547
  168.6 19.6 %collective-permute-done.32 = bf16[512,1536]{1,0:T(8,128)(2,1)S(1)} collective-permute-done((bf16[512,1536]{1,0:T(8,128)(2,1)}, bf16[512,1536]{1,0:T(8,128)(2,1)S(1)}, u32[]{:S(2)}, u32[]{:S(2)}) %collective-permute-start.32) | collective-permute-done | bytes 1572896 | tf_op jit(solution)/shard_map/ppermute | solution.py:555
  193.7 18.0 %collective-permute-done.33 = bf16[256,2048]{1,0:T(8,128)(2,1)S(1)} collective-permute-done((bf16[256,2048]{1,0:T(8,128)(2,1)S(1)}, bf16[256,2048]{1,0:T(8,128)(2,1)S(1)}, u32[]{:S(2)}, u32[]{:S(2)}) %collective-permute-start.33) | collective-permute-done | bytes 1048608 | tf_op jit(solution)/shard_map/ppermute | solution.py:547
  215.5 14.4 %collective-permute-done.38 = bf16[256,1536]{1,0:T(8,128)(2,1)S(1)} collective-permute-done((bf16[256,1536]{1,0:T(8,128)(2,1)S(1)}, bf16[256,1536]{1,0:T(8,128)(2,1)S(1)}, u32[]{:S(2)}, u32[]{:S(2)}) %collective-permute-start.38) | collective-permute-done | bytes 786464 | tf_op jit(solution)/shard_map/ppermute | solution.py:547
  242.0 18.6 %collective-permute-done.39 = bf16[256,2048]{1,0:T(8,128)(2,1)S(1)} collective-permute-done((bf16[256,2048]{1,0:T(8,128)(2,1)S(1)}, bf16[256,2048]{1,0:T(8,128)(2,1)S(1)}, u32[]{:S(2)}, u32[]{:S(2)}) %collective-permute-start.39) | collective-permute-done | bytes 1048608 | tf_op jit(solution)/shard_map/ppermute | solution.py:547
  280.2 4.4 collective-permute-done.46.refs_1_
  284.6 19.5 %shard_map.238 = (bf16[1024,512]{1,0:T(8,128)(2,1)S(1)}, bf16[1024,512]{1,0:T(8,128)(2,1)}, bf16[1024,1024]{1,0:T(8,128)(2,1)}, bf16[1024,1024]{1,0:T(8,128)(2,1)}) custom-call(bf16[1024,2048]{1,0:T(8,128)(2,1)} %copy-done.71, bf16[1024,2048]{1,0:T(8,128)(2,1)} %collective-permute-done.46.refs_1_, bf16[1024,2048]{1,0:T(8,128)(2,1)} %copy-done.72, ...), custom_call_target="tpu_custom_call" | custom-call | flops 12884901888 | bytes 16777216 | tf_op jit(solution)/shard_map/pallas_call | solution.py:356
  304.2 14.0 %collective-permute-done.48 = bf16[512,1536]{1,0:T(8,128)(2,1)S(1)} collective-permute-done((bf16[512,1536]{1,0:T(8,128)(2,1)S(1)}, bf16[512,1536]{1,0:T(8,128)(2,1)S(1)}, u32[]{:S(2)}, u32[]{:S(2)}) %collective-permute-start.48) | collective-permute-done | bytes 1572896 | tf_op jit(solution)/shard_map/ppermute | solution.py:555
  321.5 20.9 %shard_map.239 = (bf16[512,1536]{1,0:T(8,128)(2,1)}, bf16[512,1536]{1,0:T(8,128)(2,1)}, bf16[512,1536]{1,0:T(8,128)(2,1)}, bf16[512,1536]{1,0:T(8,128)(2,1)}) custom-call(bf16[1024,2048]{1,0:T(8,128)(2,1)} %copy-done.71, bf16[1024,2048]{1,0:T(8,128)(2,1)} %collective-permute-done.46.refs_1_, bf16[1024,2048]{1,0:T(8,128)(2,1)} %copy-done.72, ...), custom_call_target="tpu_custom_call" | custom-call | flops 12884901888 | bytes 16777216 | tf_op jit(solution)/shard_map/pallas_call | solution.py:393
  342.5 13.6 %collective-permute-done.50 = bf16[512,1536]{1,0:T(8,128)(2,1)} collective-permute-done((bf16[512,1536]{1,0:T(8,128)(2,1)S(1)}, bf16[512,1536]{1,0:T(8,128)(2,1)}, u32[]{:S(2)}, u32[]{:S(2)}) %collective-permute-start.50) | collective-permute-done | bytes 1572896 | tf_op jit(solution)/shard_map/ppermute | solution.py:555
  363.1 19.6 %shard_map.240 = (bf16[1024,512]{1,0:T(8,128)(2,1)S(1)}, bf16[1024,512]{1,0:T(8,128)(2,1)}, bf16[1024,1024]{1,0:T(8,128)(2,1)}, bf16[1024,1024]{1,0:T(8,128)(2,1)}) custom-call(bf16[1024,2048]{1,0:T(8,128)(2,1)} %copy-done.71, bf16[1024,2048]{1,0:T(8,128)(2,1)} %collective-permute-done.46.refs_1_, bf16[1024,2048]{1,0:T(8,128)(2,1)} %copy-done.72, ...), custom_call_target="tpu_custom_call" | custom-call | flops 12884901888 | bytes 16777216 | tf_op jit(solution)/shard_map/pallas_call | solution.py:356
  382.7 23.6 %shard_map.241 = (bf16[1024,2048]{1,0:T(8,128)(2,1)}, bf16[1024,2048]{1,0:T(8,128)(2,1)}) custom-call(bf16[1024,1024]{1,0:T(8,128)(2,1)} %get-tuple-element.350.refs_4_.refs_0_, bf16[1024,1024]{1,0:T(8,128)(2,1)} %get-tuple-element.351.refs_5_.refs_1_, bf16[1024,1024]{1,0:T(8,128)(2,1)} %get-tuple-element.389.refs_2_.refs_4_, ...), custom_call_target="tpu_custom_call" | custom-call | flops 17179869184 | bytes 16777216 | tf_op jit(solution)/shard_map/pallas_call | solution.py:442
  409.1 13.4 %shard_map.243 = (bf16[1024,2048]{1,0:T(8,128)(2,1)}, bf16[1024,2048]{1,0:T(8,128)(2,1)}) custom-call(bf16[1024,512]{1,0:T(8,128)(2,1)S(1)} %get-tuple-element.373.refs_6_.refs_0_, bf16[1024,512]{1,0:T(8,128)(2,1)} %get-tuple-element.374.refs_7_.refs_1_, bf16[1024,512]{1,0:T(8,128)(2,1)} %copy-done.14, bf16[1024,512]{1,0:T(8,128)(2,1)} %get-tuple-element.392.refs_3_.refs_7_, ...), custom_call_target="tpu_custom_call" | custom-call | flops 8589934592 | bytes 16777216 | tf_op jit(solution)/shard_map/pallas_call | solution.py:442
  422.6 4.9 shard_map.242
  440.3 22.3 %collective-permute-done.56.refs_2_ = bf16[512,1536]{1,0:T(8,128)(2,1)} collective-permute-done((bf16[512,1536]{1,0:T(8,128)(2,1)S(1)}, bf16[512,1536]{1,0:T(8,128)(2,1)}, u32[]{:S(2)}, u32[]{:S(2)}) %collective-permute-start.56) | collective-permute-done | bytes 1572896 | tf_op jit(solution)/shard_map/ppermute | solution.py:555
  465.9 4.5 shard_map.244
  470.4 4.4 collective-permute-start.61
  476.3 21.1 %shard_map.245 = (bf16[512,1536]{1,0:T(8,128)(2,1)}, bf16[512,1536]{1,0:T(8,128)(2,1)}, bf16[512,1536]{1,0:T(8,128)(2,1)}, bf16[512,1536]{1,0:T(8,128)(2,1)}) custom-call(bf16[1024,2048]{1,0:T(8,128)(2,1)} %copy-done.71, bf16[1024,2048]{1,0:T(8,128)(2,1)} %collective-permute-done.46.refs_1_, bf16[1024,2048]{1,0:T(8,128)(2,1)} %copy-done.72, ...), custom_call_target="tpu_custom_call" | custom-call | flops 12884901888 | bytes 16777216 | tf_op jit(solution)/shard_map/pallas_call | solution.py:393
  505.5 6.9 collective-permute-done.63
  526.9 12.0 %collective-permute-done.65 = bf16[256,2048]{1,0:T(8,128)(2,1)S(1)} collective-permute-done((bf16[256,2048]{1,0:T(8,128)(2,1)S(1)}, bf16[256,2048]{1,0:T(8,128)(2,1)S(1)}, u32[]{:S(2)}, u32[]{:S(2)}) %collective-permute-start.65) | collective-permute-done | bytes 1048608 | tf_op jit(solution)/shard_map/ppermute | solution.py:547
  540.9 9.7 %collective-permute-done.67 = bf16[128,2048]{1,0:T(8,128)(2,1)S(1)} collective-permute-done((bf16[128,2048]{1,0:T(8,128)(2,1)S(1)}, bf16[128,2048]{1,0:T(8,128)(2,1)S(1)}, u32[]{:S(2)}, u32[]{:S(2)}) %collective-permute-start.67) | collective-permute-done | bytes 524320 | tf_op jit(solution)/shard_map/ppermute | solution.py:547
  556.7 5.0 collective-permute-start.71
  562.1 4.8 shard_map.248
  566.9 4.2 collective-permute-start.74
  573.6 26.3 %shard_map.246 = (bf16[1024,384]{1,0:T(8,128)(2,1)}, bf16[1024,384]{1,0:T(8,128)(2,1)}, f32[2,256]{1,0:T(2,128)S(1)}) custom-call(bf16[1024,2048]{1,0:T(8,128)(2,1)} %constant_dynamic-update-slice_fusion.15.refs_0_.refs_2_, bf16[1024,2048]{1,0:T(8,128)(2,1)} %collective-permute-done.71.refs_1_.refs_3_, f32[4,512,384]{2,1,0:T(8,128)} %get-tuple-element.409.refs_2_, ...), custom_call_target="tpu_custom_call" | custom-call | flops 32212254720 | bytes 33554432 | tf_op jit(solution)/shard_map/pallas_call | solution.py:320
  599.9 10.1 %shard_map.247 = (bf16[1024,2048]{1,0:T(8,128)(2,1)}, bf16[1024,2048]{1,0:T(8,128)(2,1)}, f32[1,2048]{1,0:T(1,128)S(1)}) custom-call(bf16[1024,384]{1,0:T(8,128)(2,1)} %get-tuple-element.434.refs_0_.refs_4_, bf16[1024,384]{1,0:T(8,128)(2,1)} %get-tuple-element.435.refs_1_.refs_5_, bf16[512,640]{1,0:T(8,128)(2,1)S(1)} %pad_maximum_fusion.16.refs_9_.refs_10_.refs_2_, ...), custom_call_target="tpu_custom_call" | custom-call | flops 1 | bytes 1 | tf_op jit(solution)/shard_map/pallas_call | solution.py:442
  616.0 4.5 shard_map.250
  620.5 4.3 collective-permute-start.81
  630.4 5.3 convert_add_fusion.1
  639.5 13.8 %shard_map.251 = (bf16[512,640]{1,0:T(8,128)(2,1)S(1)}, bf16[512,640]{1,0:T(8,128)(2,1)}, bf16[512,640]{1,0:T(8,128)(2,1)}, bf16[512,640]{1,0:T(8,128)(2,1)}) custom-call(bf16[1024,2048]{1,0:T(8,128)(2,1)} %constant_dynamic-update-slice_fusion.refs_0_.refs_6_, bf16[1024,2048]{1,0:T(8,128)(2,1)} %pad_maximum_fusion.refs_1_.refs_7_, ...), custom_call_target="tpu_custom_call" | custom-call | flops 5368709120 | bytes 16777216 | tf_op jit(solution)/shard_map/pallas_call | solution.py:393
  657.1 5.2 collective-permute-done.82
  673.3 4.8 collective-permute-done.86.refs_2_
  681.3 4.1 collective-permute-start.88
  701.7 7.3 collective-permute-start.90
  713.2 5.5 shard_map.249
  718.8 7.0 collective-permute-done.94.refs_7_
  736.5 7.1 collective-permute-start.95
  751.2 4.7 shard_map.255
  764.1 5.3 shard_map.254
  (534 shorter events, 272.2 us)
Async XLA Ops:
  104.7 36.1 %collective-permute-start.22 = (bf16[512,1536]{1,0:T(8,128)(2,1)S(1)}, bf16[512,1536]{1,0:T(8,128)(2,1)}, u32[]{:S(2)}, u32[]{:S(2)}) collective-permute-start(bf16[512,1536]{1,0:T(8,128)(2,1)S(1)} %pad_maximum_fusion.1.refs_4_), channel_id=1, source_target_pairs={{0,8},{2,10},{4,12},{6,14},{8,16},{10,18},{12,20},{14,22},{16,24},... | collective-permute-start | bytes 4718600 | tf_op jit(solution)/shard_map/ppermute | solution.py:555
  109.5 36.3 %collective-permute-start.23 = (bf16[512,1536]{1,0:T(8,128)(2,1)S(1)}, bf16[512,1536]{1,0:T(8,128)(2,1)}, u32[]{:S(2)}, u32[]{:S(2)}) collective-permute-start(bf16[512,1536]{1,0:T(8,128)(2,1)S(1)} %pad_maximum_fusion.1.refs_4_), channel_id=1, source_target_pairs={{8,0},{10,2},{12,4},{14,6},{16,8},{18,10},{20,12},{22,14},{24,16},... | collective-permute-start | bytes 4718600 | tf_op jit(solution)/shard_map/ppermute | solution.py:555
  111.0 25.2 %collective-permute-start.24 = (bf16[256,2048]{1,0:T(8,128)(2,1)S(1)}, bf16[256,2048]{1,0:T(8,128)(2,1)S(1)}, u32[]{:S(2)}, u32[]{:S(2)}) collective-permute-start(bf16[256,2048]{1,0:T(8,128)(2,1)S(1)} %fusion.17), channel_id=1, source_target_pairs={{0,2},{2,0},{4,6},{6,4},{8,10},{10,8},{12,14},{14,12},{16,18},{18,... | collective-permute-start | bytes 3145736 | tf_op jit(solution)/shard_map/ppermute | solution.py:547
  112.2 24.0 %collective-permute-start.25 = (bf16[256,2048]{1,0:T(8,128)(2,1)S(1)}, bf16[256,2048]{1,0:T(8,128)(2,1)S(1)}, u32[]{:S(2)}, u32[]{:S(2)}) collective-permute-start(bf16[256,2048]{1,0:T(8,128)(2,1)S(1)} %fusion.17), channel_id=1, source_target_pairs={{0,4},{2,6},{4,0},{6,2},{8,12},{10,14},{12,8},{14,10},{16,20},{18,... | collective-permute-start | bytes 3145736 | tf_op jit(solution)/shard_map/ppermute | solution.py:547
  150.7 37.5 %collective-permute-start.32 = (bf16[512,1536]{1,0:T(8,128)(2,1)}, bf16[512,1536]{1,0:T(8,128)(2,1)S(1)}, u32[]{:S(2)}, u32[]{:S(2)}) collective-permute-start(bf16[512,1536]{1,0:T(8,128)(2,1)} %collective-permute-done.23), channel_id=1, source_target_pairs={{8,0},{10,2},{12,4},{14,6},{16,8},{18,10},{20,12},{22,14},{9,1},{1... | collective-permute-start | bytes 4718600 | tf_op jit(solution)/shard_map/ppermute | solution.py:555
  165.2 23.0 %collective-permute-start.28 = (bf16[128,2048]{1,0:T(8,128)(2,1)S(1)}, bf16[128,2048]{1,0:T(8,128)(2,1)S(1)}, u32[]{:S(2)}, u32[]{:S(2)}) collective-permute-start(bf16[128,2048]{1,0:T(8,128)(2,1)S(1)} %get-tuple-element.544), channel_id=1, source_target_pairs={{0,2},{2,0},{4,6},{6,4},{8,10},{10,8},{12,14},{14,12},{16,18},{18,... | collective-permute-start | bytes 1572872 | tf_op jit(solution)/shard_map/ppermute | solution.py:547
  188.4 23.3 %collective-permute-start.33 = (bf16[256,2048]{1,0:T(8,128)(2,1)S(1)}, bf16[256,2048]{1,0:T(8,128)(2,1)S(1)}, u32[]{:S(2)}, u32[]{:S(2)}) collective-permute-start(bf16[256,2048]{1,0:T(8,128)(2,1)S(1)} %pad_maximum_fusion.4), channel_id=1, source_target_pairs={{0,2},{2,0},{4,6},{6,4},{8,10},{10,8},{12,14},{14,12},{16,18},{18,... | collective-permute-start | bytes 3145736 | tf_op jit(solution)/shard_map/ppermute | solution.py:547
  190.0 23.0 %collective-permute-start.34 = (bf16[256,2048]{1,0:T(8,128)(2,1)S(1)}, bf16[256,2048]{1,0:T(8,128)(2,1)S(1)}, u32[]{:S(2)}, u32[]{:S(2)}) collective-permute-start(bf16[256,2048]{1,0:T(8,128)(2,1)S(1)} %pad_maximum_fusion.5), channel_id=1, source_target_pairs={{0,4},{2,6},{4,0},{6,2},{8,12},{10,14},{12,8},{14,10},{16,20},{18,... | collective-permute-start | bytes 3145736 | tf_op jit(solution)/shard_map/ppermute | solution.py:547
  190.4 39.5 %collective-permute-start.35 = (bf16[512,1536]{1,0:T(8,128)(2,1)S(1)}, bf16[512,1536]{1,0:T(8,128)(2,1)S(1)}, u32[]{:S(2)}, u32[]{:S(2)}) collective-permute-start(bf16[512,1536]{1,0:T(8,128)(2,1)S(1)} %collective-permute-done.31), channel_id=1, source_target_pairs={{16,24},{18,26},{20,28},{22,30},{17,25},{19,27},{21,29},{23,31}} | collective-permute-start | bytes 4718600 | tf_op jit(solution)/shard_map/ppermute | solution.py:555
  191.2 38.7 %collective-permute-start.36 = (bf16[512,1536]{1,0:T(8,128)(2,1)S(1)}, bf16[512,1536]{1,0:T(8,128)(2,1)S(1)}, u32[]{:S(2)}, u32[]{:S(2)}) collective-permute-start(bf16[512,1536]{1,0:T(8,128)(2,1)S(1)} %collective-permute-done.32), channel_id=1, source_target_pairs={{8,0},{10,2},{12,4},{14,6},{9,1},{11,3},{13,5},{15,7}} | collective-permute-start | bytes 4718600 | tf_op jit(solution)/shard_map/ppermute | solution.py:555
  192.5 37.3 %collective-permute-start.38 = (bf16[256,1536]{1,0:T(8,128)(2,1)S(1)}, bf16[256,1536]{1,0:T(8,128)(2,1)S(1)}, u32[]{:S(2)}, u32[]{:S(2)}) collective-permute-start(bf16[256,1536]{1,0:T(8,128)(2,1)S(1)} %pad_maximum_fusion.13), channel_id=1, source_target_pairs={{0,4},{2,6},{4,0},{6,2},{8,12},{10,14},{12,8},{14,10},{16,20},{18,... | collective-permute-start | bytes 2359304 | tf_op jit(solution)/shard_map/ppermute | solution.py:547
  230.0 41.6 %collective-permute-start.45 = (bf16[1024,2048]{1,0:T(8,128)(2,1)S(1)}, bf16[1024,2048]{1,0:T(8,128)(2,1)S(1)}, u32[]{:S(2)}, u32[]{:S(2)}) collective-permute-start(bf16[1024,2048]{1,0:T(8,128)(2,1)S(1)} %constant_dynamic-update-slice_fusion.5.refs_2_), channel_id=1, source_target_pairs={{0,1},{1,0},{2,3},{3,2},{4,5},{5,4},{6,7},{7,6},{8,9},{9,8},{10,11... | collective-permute-start | bytes 12582920 | tf_op jit(solution)/shard_map/ppermute | solution.py:535
  233.0 33.8 %collective-permute-start.43 = (bf16[512,1536]{1,0:T(8,128)(2,1)S(1)}, bf16[512,1536]{1,0:T(8,128)(2,1)S(1)}, u32[]{:S(2)}, u32[]{:S(2)}) collective-permute-start(bf16[512,1536]{1,0:T(8,128)(2,1)S(1)} %pad_maximum_fusion.2.refs_4_.refs_8_), channel_id=1, source_target_pairs={{0,8},{2,10},{4,12},{6,14},{8,16},{10,18},{12,20},{14,22},{16,24},... | collective-permute-start | bytes 4718600 | tf_op jit(solution)/shard_map/ppermute | solution.py:555
  234.8 35.9 %collective-permute-start.44 = (bf16[512,1536]{1,0:T(8,128)(2,1)S(1)}, bf16[512,1536]{1,0:T(8,128)(2,1)S(1)}, u32[]{:S(2)}, u32[]{:S(2)}) collective-permute-start(bf16[512,1536]{1,0:T(8,128)(2,1)S(1)} %pad_maximum_fusion.2.refs_4_.refs_8_), channel_id=1, source_target_pairs={{8,0},{10,2},{12,4},{14,6},{16,8},{18,10},{20,12},{22,14},{24,16},... | collective-permute-start | bytes 4718600 | tf_op jit(solution)/shard_map/ppermute | solution.py:555
  237.8 22.8 %collective-permute-start.39 = (bf16[256,2048]{1,0:T(8,128)(2,1)S(1)}, bf16[256,2048]{1,0:T(8,128)(2,1)S(1)}, u32[]{:S(2)}, u32[]{:S(2)}) collective-permute-start(bf16[256,2048]{1,0:T(8,128)(2,1)S(1)} %get-tuple-element.488), channel_id=1, source_target_pairs={{0,2},{2,0},{4,6},{6,4},{8,10},{10,8},{12,14},{14,12},{16,18},{18,... | collective-permute-start | bytes 3145736 | tf_op jit(solution)/shard_map/ppermute | solution.py:547
  238.0 23.0 %collective-permute-start.40 = (bf16[256,2048]{1,0:T(8,128)(2,1)S(1)}, bf16[256,2048]{1,0:T(8,128)(2,1)S(1)}, u32[]{:S(2)}, u32[]{:S(2)}) collective-permute-start(bf16[256,2048]{1,0:T(8,128)(2,1)S(1)} %get-tuple-element.488), channel_id=1, source_target_pairs={{0,4},{2,6},{4,0},{6,2},{8,12},{10,14},{12,8},{14,10},{16,20},{18,... | collective-permute-start | bytes 3145736 | tf_op jit(solution)/shard_map/ppermute | solution.py:547
  277.7 26.5 %collective-permute-start.47 = (bf16[512,1536]{1,0:T(8,128)(2,1)S(1)}, bf16[512,1536]{1,0:T(8,128)(2,1)S(1)}, u32[]{:S(2)}, u32[]{:S(2)}) collective-permute-start(bf16[512,1536]{1,0:T(8,128)(2,1)S(1)} %collective-permute-done.43), channel_id=1, source_target_pairs={{8,16},{10,18},{12,20},{14,22},{16,24},{18,26},{20,28},{22,30},{9,... | collective-permute-start | bytes 4718600 | tf_op jit(solution)/shard_map/ppermute | solution.py:555
  278.5 39.7 %collective-permute-start.48 = (bf16[512,1536]{1,0:T(8,128)(2,1)S(1)}, bf16[512,1536]{1,0:T(8,128)(2,1)S(1)}, u32[]{:S(2)}, u32[]{:S(2)}) collective-permute-start(bf16[512,1536]{1,0:T(8,128)(2,1)S(1)} %collective-permute-done.44), channel_id=1, source_target_pairs={{8,0},{10,2},{12,4},{14,6},{16,8},{18,10},{20,12},{22,14},{9,1},{1... | collective-permute-start | bytes 4718600 | tf_op jit(solution)/shard_map/ppermute | solution.py:555
  318.2 24.3 %collective-permute-start.49 = (bf16[512,1536]{1,0:T(8,128)(2,1)S(1)}, bf16[512,1536]{1,0:T(8,128)(2,1)S(1)}, u32[]{:S(2)}, u32[]{:S(2)}) collective-permute-start(bf16[512,1536]{1,0:T(8,128)(2,1)S(1)} %collective-permute-done.47), channel_id=1, source_target_pairs={{16,24},{18,26},{20,28},{22,30},{17,25},{19,27},{21,29},{23,31}} | collective-permute-start | bytes 4718600 | tf_op jit(solution)/shard_map/ppermute | solution.py:555
  318.9 37.1 %collective-permute-start.50 = (bf16[512,1536]{1,0:T(8,128)(2,1)S(1)}, bf16[512,1536]{1,0:T(8,128)(2,1)}, u32[]{:S(2)}, u32[]{:S(2)}) collective-permute-start(bf16[512,1536]{1,0:T(8,128)(2,1)S(1)} %collective-permute-done.48), channel_id=1, source_target_pairs={{8,0},{10,2},{12,4},{14,6},{9,1},{11,3},{13,5},{15,7}} | collective-permute-start | bytes 4718600 | tf_op jit(solution)/shard_map/ppermute | solution.py:555
  360.8 45.5 %collective-permute-start.51 = (bf16[512,1536]{1,0:T(8,128)(2,1)S(1)}, bf16[512,1536]{1,0:T(8,128)(2,1)S(1)}, u32[]{:S(2)}, u32[]{:S(2)}) collective-permute-start(bf16[512,1536]{1,0:T(8,128)(2,1)S(1)} %copy-done.46), channel_id=1, source_target_pairs={{0,8},{2,10},{4,12},{6,14},{1,9},{3,11},{5,13},{7,15}} | collective-permute-start | bytes 4718600 | tf_op jit(solution)/shard_map/ppermute | solution.py:555
  362.3 44.0 %collective-permute-start.52 = (bf16[512,1536]{1,0:T(8,128)(2,1)S(1)}, bf16[512,1536]{1,0:T(8,128)(2,1)S(1)}, u32[]{:S(2)}, u32[]{:S(2)}) collective-permute-start(bf16[512,1536]{1,0:T(8,128)(2,1)S(1)} %copy-done.45), channel_id=1, source_target_pairs={{24,16},{26,18},{28,20},{30,22},{25,17},{27,19},{29,21},{31,23}} | collective-permute-start | bytes 4718600 | tf_op jit(solution)/shard_map/ppermute | solution.py:555
  407.5 24.3 %collective-permute-start.53 = (bf16[1024,2048]{1,0:T(8,128)(2,1)}, bf16[1024,2048]{1,0:T(8,128)(2,1)S(1)}, u32[]{:S(2)}, u32[]{:S(2)}) collective-permute-start(bf16[1024,2048]{1,0:T(8,128)(2,1)} %get-tuple-element.363), channel_id=1, source_target_pairs={{0,1},{1,0},{2,3},{3,2},{4,5},{5,4},{6,7},{7,6},{8,9},{9,8},{10,11... | collective-permute-start | bytes 12582920 | tf_op jit(solution)/shard_map/ppermute | solution.py:535
  422.5 40.1 %collective-permute-start.58 = (bf16[1024,2048]{1,0:T(8,128)(2,1)}, bf16[1024,2048]{1,0:T(8,128)(2,1)}, u32[]{:S(2)}, u32[]{:S(2)}) collective-permute-start(bf16[1024,2048]{1,0:T(8,128)(2,1)} %get-tuple-element.376), channel_id=1, source_target_pairs={{0,1},{1,0},{2,3},{3,2},{4,5},{5,4},{6,7},{7,6},{8,9},{9,8},{10,11... | collective-permute-start | bytes 12582920 | tf_op jit(solution)/shard_map/ppermute | solution.py:535
  427.6 35.0 %collective-permute-start.56 = (bf16[512,1536]{1,0:T(8,128)(2,1)S(1)}, bf16[512,1536]{1,0:T(8,128)(2,1)}, u32[]{:S(2)}, u32[]{:S(2)}) collective-permute-start(bf16[512,1536]{1,0:T(8,128)(2,1)S(1)} %get-tuple-element.367), channel_id=1, source_target_pairs={{0,8},{2,10},{4,12},{6,14},{8,16},{10,18},{12,20},{14,22},{1,9},{3... | collective-permute-start | bytes 4718600 | tf_op jit(solution)/shard_map/ppermute | solution.py:555
  430.0 32.6 %collective-permute-start.57 = (bf16[512,1536]{1,0:T(8,128)(2,1)}, bf16[512,1536]{1,0:T(8,128)(2,1)}, u32[]{:S(2)}, u32[]{:S(2)}) collective-permute-start(bf16[512,1536]{1,0:T(8,128)(2,1)} %get-tuple-element.368), channel_id=1, source_target_pairs={{16,8},{18,10},{20,12},{22,14},{24,16},{26,18},{28,20},{30,22},{17... | collective-permute-start | bytes 4718600 | tf_op jit(solution)/shard_map/ppermute | solution.py:555
  436.2 26.4 %collective-permute-start.54 = (bf16[128,2048]{1,0:T(8,128)(2,1)}, bf16[128,2048]{1,0:T(8,128)(2,1)}, u32[]{:S(2)}, u32[]{:S(2)}) collective-permute-start(bf16[128,2048]{1,0:T(8,128)(2,1)} %get-tuple-element.542), channel_id=1, source_target_pairs={{0,2},{2,0},{4,6},{6,4},{8,10},{10,8},{12,14},{14,12},{16,18},{18,... | collective-permute-start | bytes 1572872 | tf_op jit(solution)/shard_map/ppermute | solution.py:547
  437.3 25.3 %collective-permute-start.55 = (bf16[128,2048]{1,0:T(8,128)(2,1)}, bf16[128,2048]{1,0:T(8,128)(2,1)S(1)}, u32[]{:S(2)}, u32[]{:S(2)}) collective-permute-start(bf16[128,2048]{1,0:T(8,128)(2,1)} %get-tuple-element.541), channel_id=1, source_target_pairs={{0,4},{2,6},{4,0},{6,2},{8,12},{10,14},{12,8},{14,10},{16,20},{18,... | collective-permute-start | bytes 1572872 | tf_op jit(solution)/shard_map/ppermute | solution.py:547
  464.1 33.3 %collective-permute-start.60 = (bf16[256,2048]{1,0:T(8,128)(2,1)S(1)}, bf16[256,2048]{1,0:T(8,128)(2,1)}, u32[]{:S(2)}, u32[]{:S(2)}) collective-permute-start(bf16[256,2048]{1,0:T(8,128)(2,1)S(1)} %pad_maximum_fusion.7), channel_id=1, source_target_pairs={{0,4},{2,6},{4,0},{6,2},{8,12},{10,14},{12,8},{14,10},{16,20},{18,... | collective-permute-start | bytes 3145736 | tf_op jit(solution)/shard_map/ppermute | solution.py:547
  465.6 31.9 %collective-permute-start.59 = (bf16[256,2048]{1,0:T(8,128)(2,1)S(1)}, bf16[256,2048]{1,0:T(8,128)(2,1)}, u32[]{:S(2)}, u32[]{:S(2)}) collective-permute-start(bf16[256,2048]{1,0:T(8,128)(2,1)S(1)} %pad_maximum_fusion.6), channel_id=1, source_target_pairs={{0,2},{2,0},{4,6},{6,4},{8,10},{10,8},{12,14},{14,12},{16,18},{18,... | collective-permute-start | bytes 3145736 | tf_op jit(solution)/shard_map/ppermute | solution.py:547
  470.4 42.9 %collective-permute-start.61 = (bf16[512,1536]{1,0:T(8,128)(2,1)S(1)}, bf16[512,1536]{1,0:T(8,128)(2,1)S(1)}, u32[]{:S(2)}, u32[]{:S(2)}) collective-permute-start(bf16[512,1536]{1,0:T(8,128)(2,1)S(1)} %get-tuple-element.387), channel_id=1, source_target_pairs={{0,8},{2,10},{4,12},{6,14},{8,16},{10,18},{12,20},{14,22},{16,24},... | collective-permute-start | bytes 4718600 | tf_op jit(solution)/shard_map/ppermute | solution.py:555
  474.8 38.5 %collective-permute-start.62 = (bf16[512,1536]{1,0:T(8,128)(2,1)}, bf16[512,1536]{1,0:T(8,128)(2,1)}, u32[]{:S(2)}, u32[]{:S(2)}) collective-permute-start(bf16[512,1536]{1,0:T(8,128)(2,1)} %get-tuple-element.388), channel_id=1, source_target_pairs={{8,0},{10,2},{12,4},{14,6},{16,8},{18,10},{20,12},{22,14},{24,16},... | collective-permute-start | bytes 4718600 | tf_op jit(solution)/shard_map/ppermute | solution.py:555
  519.1 33.4 %collective-permute-start.69 = (bf16[512,1536]{1,0:T(8,128)(2,1)S(1)}, bf16[512,1536]{1,0:T(8,128)(2,1)S(1)}, u32[]{:S(2)}, u32[]{:S(2)}) collective-permute-start(bf16[512,1536]{1,0:T(8,128)(2,1)S(1)} %copy-done.44), channel_id=1, source_target_pairs={{0,8},{2,10},{4,12},{6,14},{1,9},{3,11},{5,13},{7,15}} | collective-permute-start | bytes 4718600 | tf_op jit(solution)/shard_map/ppermute | solution.py:555
  522.9 29.5 %collective-permute-start.70 = (bf16[512,1536]{1,0:T(8,128)(2,1)S(1)}, bf16[512,1536]{1,0:T(8,128)(2,1)S(1)}, u32[]{:S(2)}, u32[]{:S(2)}) collective-permute-start(bf16[512,1536]{1,0:T(8,128)(2,1)S(1)} %copy-done.43), channel_id=1, source_target_pairs={{24,16},{26,18},{28,20},{30,22},{25,17},{27,19},{29,21},{31,23}} | collective-permute-start | bytes 4718600 | tf_op jit(solution)/shard_map/ppermute | solution.py:555
  561.7 48.4 %collective-permute-start.76 = (bf16[256,1536]{1,0:T(8,128)(2,1)S(1)}, bf16[256,1536]{1,0:T(8,128)(2,1)S(1)}, u32[]{:S(2)}, u32[]{:S(2)}) collective-permute-start(bf16[256,1536]{1,0:T(8,128)(2,1)S(1)} %pad_maximum_fusion.14), channel_id=1, source_target_pairs={{0,2},{2,0},{4,6},{6,4},{8,10},{10,8},{12,14},{14,12},{16,18},{18,... | collective-permute-start | bytes 2359304 | tf_op jit(solution)/shard_map/ppermute | solution.py:547
  566.9 43.3 %collective-permute-start.74 = (bf16[512,1536]{1,0:T(8,128)(2,1)S(1)}, bf16[512,1536]{1,0:T(8,128)(2,1)S(1)}, u32[]{:S(2)}, u32[]{:S(2)}) collective-permute-start(bf16[512,1536]{1,0:T(8,128)(2,1)S(1)} %get-tuple-element.420), channel_id=1, source_target_pairs={{0,8},{2,10},{4,12},{6,14},{8,16},{10,18},{12,20},{14,22},{1,9},{3... | collective-permute-start | bytes 4718600 | tf_op jit(solution)/shard_map/ppermute | solution.py:555
  571.1 40.3 %collective-permute-start.75 = (bf16[512,1536]{1,0:T(8,128)(2,1)}, bf16[512,1536]{1,0:T(8,128)(2,1)S(1)}, u32[]{:S(2)}, u32[]{:S(2)}) collective-permute-start(bf16[512,1536]{1,0:T(8,128)(2,1)} %get-tuple-element.421), channel_id=1, source_target_pairs={{16,8},{18,10},{20,12},{22,14},{24,16},{26,18},{28,20},{30,22},{17... | collective-permute-start | bytes 4718600 | tf_op jit(solution)/shard_map/ppermute | solution.py:555
  572.1 38.1 %collective-permute-start.72 = (bf16[256,2048]{1,0:T(8,128)(2,1)S(1)}, bf16[256,2048]{1,0:T(8,128)(2,1)S(1)}, u32[]{:S(2)}, u32[]{:S(2)}) collective-permute-start(bf16[256,2048]{1,0:T(8,128)(2,1)S(1)} %pad_maximum_fusion.8), channel_id=1, source_target_pairs={{0,2},{2,0},{4,6},{6,4},{8,10},{10,8},{12,14},{14,12},{16,18},{18,... | collective-permute-start | bytes 3145736 | tf_op jit(solution)/shard_map/ppermute | solution.py:547
  573.3 36.8 %collective-permute-start.73 = (bf16[256,2048]{1,0:T(8,128)(2,1)}, bf16[256,2048]{1,0:T(8,128)(2,1)}, u32[]{:S(2)}, u32[]{:S(2)}) collective-permute-start(bf16[256,2048]{1,0:T(8,128)(2,1)} %pad_maximum_fusion.9), channel_id=1, source_target_pairs={{0,4},{2,6},{4,0},{6,2},{8,12},{10,14},{12,8},{14,10},{16,20},{18,... | collective-permute-start | bytes 3145736 | tf_op jit(solution)/shard_map/ppermute | solution.py:547
  614.7 38.8 %collective-permute-start.83 = (bf16[256,1536]{1,0:T(8,128)(2,1)}, bf16[256,1536]{1,0:T(8,128)(2,1)}, u32[]{:S(2)}, u32[]{:S(2)}) collective-permute-start(bf16[256,1536]{1,0:T(8,128)(2,1)} %pad_maximum_fusion.15), channel_id=1, source_target_pairs={{0,4},{2,6},{4,0},{6,2},{8,12},{10,14},{12,8},{14,10},{16,20},{18,... | collective-permute-start | bytes 2359304 | tf_op jit(solution)/shard_map/ppermute | solution.py:547
  620.5 36.6 %collective-permute-start.81 = (bf16[512,1536]{1,0:T(8,128)(2,1)S(1)}, bf16[512,1536]{1,0:T(8,128)(2,1)}, u32[]{:S(2)}, u32[]{:S(2)}) collective-permute-start(bf16[512,1536]{1,0:T(8,128)(2,1)S(1)} %get-tuple-element.432), channel_id=1, source_target_pairs={{0,8},{2,10},{4,12},{6,14},{8,16},{10,18},{12,20},{14,22},{16,24},... | collective-permute-start | bytes 4718600 | tf_op jit(solution)/shard_map/ppermute | solution.py:555
  624.8 37.6 %collective-permute-start.82 = (bf16[512,1536]{1,0:T(8,128)(2,1)}, bf16[512,1536]{1,0:T(8,128)(2,1)}, u32[]{:S(2)}, u32[]{:S(2)}) collective-permute-start(bf16[512,1536]{1,0:T(8,128)(2,1)} %get-tuple-element.433), channel_id=1, source_target_pairs={{8,0},{10,2},{12,4},{14,6},{16,8},{18,10},{20,12},{22,14},{24,16},... | collective-permute-start | bytes 4718600 | tf_op jit(solution)/shard_map/ppermute | solution.py:555
  636.8 25.6 %collective-permute-start.79 = (bf16[128,2048]{1,0:T(8,128)(2,1)}, bf16[128,2048]{1,0:T(8,128)(2,1)}, u32[]{:S(2)}, u32[]{:S(2)}) collective-permute-start(bf16[128,2048]{1,0:T(8,128)(2,1)} %get-tuple-element.538), channel_id=1, source_target_pairs={{0,2},{2,0},{4,6},{6,4},{8,10},{10,8},{12,14},{14,12},{16,18},{18,... | collective-permute-start | bytes 1572872 | tf_op jit(solution)/shard_map/ppermute | solution.py:547
  637.3 25.1 %collective-permute-start.80 = (bf16[128,2048]{1,0:T(8,128)(2,1)}, bf16[128,2048]{1,0:T(8,128)(2,1)}, u32[]{:S(2)}, u32[]{:S(2)}) collective-permute-start(bf16[128,2048]{1,0:T(8,128)(2,1)} %get-tuple-element.537), channel_id=1, source_target_pairs={{0,4},{2,6},{4,0},{6,2},{8,12},{10,14},{12,8},{14,10},{16,20},{18,... | collective-permute-start | bytes 1572872 | tf_op jit(solution)/shard_map/ppermute | solution.py:547
  653.6 58.3 %collective-permute-start.77 = (f32[256,2048]{1,0:T(8,128)S(1)}, f32[256,2048]{1,0:T(8,128)}, u32[]{:S(2)}, u32[]{:S(2)}) collective-permute-start(f32[256,2048]{1,0:T(8,128)S(1)} %copy-done.24), channel_id=1, source_target_pairs={{0,1},{1,0},{2,3},{3,2},{4,5},{5,4},{6,7},{7,6},{8,9},{9,8},{10,11... | collective-permute-start | bytes 6291464 | tf_op jit(solution)/shard_map/ppermute | solution.py:535
  669.6 23.2 %collective-permute-start.85 = (bf16[256,2048]{1,0:T(8,128)(2,1)}, bf16[256,2048]{1,0:T(8,128)(2,1)S(1)}, u32[]{:S(2)}, u32[]{:S(2)}) collective-permute-start(bf16[256,2048]{1,0:T(8,128)(2,1)} %pad_maximum_fusion.11), channel_id=1, source_target_pairs={{0,4},{2,6},{4,0},{6,2},{8,12},{10,14},{12,8},{14,10},{16,20},{18,... | collective-permute-start | bytes 3145736 | tf_op jit(solution)/shard_map/ppermute | solution.py:547
  701.7 24.0 %collective-permute-start.90 = (bf16[512,640]{1,0:T(8,128)(2,1)}, bf16[512,640]{1,0:T(8,128)(2,1)}, u32[]{:S(2)}, u32[]{:S(2)}) collective-permute-start(bf16[512,640]{1,0:T(8,128)(2,1)} %get-tuple-element.458), channel_id=1, source_target_pairs={{0,8},{2,10},{4,12},{6,14},{8,16},{10,18},{12,20},{14,22},{16,24},... | collective-permute-start | bytes 1966088 | tf_op jit(solution)/shard_map/ppermute | solution.py:555
  736.5 26.2 %collective-permute-start.95 = (f32[256,2048]{1,0:T(8,128)S(1)}, f32[256,2048]{1,0:T(8,128)S(1)}, u32[]{:S(2)}, u32[]{:S(2)}) collective-permute-start(f32[256,2048]{1,0:T(8,128)S(1)} %fusion.5.mine), channel_id=1, source_target_pairs={{0,1},{1,0},{2,3},{3,2},{4,5},{5,4},{6,7},{7,6},{8,9},{9,8},{10,11... | collective-permute-start | bytes 6291464 | tf_op jit(solution)/shard_map/ppermute | solution.py:535
  (144 other events, 1895.3 us)

commit v4 on v3

--- a/solution.py
+++ b/solution.py
@@ -223,11 +223,11 @@
 
 
 def attention_backward(count, head_dim, width, *refs):
-    kept, other, raw_ref = refs[:3]
-    refs = refs[3:]
+    kept, other, raw_ref, normed_kept, normed_other = refs[:5]
+    refs = refs[5:]
     swap_ref, cosine_ref, sine_ref, start_ref, index_column, index_row, gains = refs[:7]
     blocks = refs[7 : 7 + count]
-    grad_kept, grad_other, gain_ref = refs[7 + count :]
+    grad_kept, grad_other, gain_ref, part_kept, part_other, scaled_ref = refs[7 + count :]
     half = kept.shape[0]
     attn_width = raw_ref.shape[-1]
     grads = block_product(kept, other, blocks, attn_width, attn_width + width)
@@ -275,10 +275,28 @@
     rest_grad = rest_grad.astype(jnp.bfloat16)
     query_sides = by_halves(swapped, query_grad[:half], query_grad[half:])
     rest_sides = by_halves(swapped, rest_grad[:half], rest_grad[half:])
+    all_sides = []
     for side, out in enumerate((grad_kept, grad_other)):
-        out[:, :width] = query_sides[side]
-        out[:, width:] = rest_sides[side]
+        both = jnp.concatenate([query_sides[side], rest_sides[side]], axis=1)
+        out[...] = both
+        all_sides.append(both)
+    all_sides = jnp.concatenate(all_sides, axis=0)
     parts = jnp.concatenate([query_gain_part, key_gain_part], axis=0)
+
+    @pl.when(pl.program_id(0) == 0)
+    def _():
+        scaled_ref[...] = jnp.zeros_like(scaled_ref)
+
+    rows = blocks[0].shape[0]
+    for k, block in enumerate(blocks):
+        span = slice(k * rows, (k + 1) * rows)
+        out = dot_nt(all_sides, block[:, :attn_width])
+        scaled = out[:half] * normed_kept[:, span].astype(jnp.float32)
+        scaled = scaled + out[half:] * normed_other[:, span].astype(jnp.float32)
+        scaled_ref[:, span] += jnp.sum(scaled, axis=0, keepdims=True)
+        out = out.astype(jnp.bfloat16)
+        part_kept[:, span] = out[:half]
+        part_other[:, span] = out[half:]
 
     @pl.when(pl.program_id(0) == 0)
     def _():
@@ -289,7 +307,7 @@
         gain_ref[...] = gain_ref[...] + parts
 
 
-def run_attention(forward, pair, blocks, tables, gains, head_dim, width, attn_width, raw=None):
+def run_attention(forward, pair, blocks, tables, gains, head_dim, width, attn_width, raw=None, normed=None):
     half = pair[0].shape[0] // group
     model = pair[0].shape[1]
     swapped, cosine, sine, start_columns, start_rows, index = tables
@@ -320,19 +338,25 @@
     results = kernel_call(
         functools.partial(attention_backward, len(blocks), head_dim, width),
         (group,),
-        [rows(model)] * 2 + [per_sequence(raw_shape)] + common_specs,
-        [rows(attn_width), rows(attn_width), pl.BlockSpec((2, width), lambda s: (0, 0))],
-        [side(attn_width), side(attn_width), shape_of((2, width), jnp.float32)],
+        [rows(model)] * 2 + [per_sequence(raw_shape)] + [rows(model)] * 2 + common_specs,
+        [rows(attn_width), rows(attn_width), pl.BlockSpec((2, width), lambda s: (0, 0))]
+        + [rows(model)] * 2
+        + [pl.BlockSpec((1, model), lambda s: (0, 0))],
+        [side(attn_width), side(attn_width), shape_of((2, width), jnp.float32)]
+        + [side(model)] * 2
+        + [shape_of((1, model), jnp.float32)],
         flops,
         moved,
-    )(*pair, raw, *common)
-    return tuple(results[:2]), results[2]
-
-
-def ffn_units(count, ff_sub, *refs):
+    )(*pair, raw, *normed, *common)
+    return tuple(results[:2]), *results[2:]
+
+
+def ffn_units(count, ff_sub, earlier, *refs):
     normed, out = refs[0:2], refs[2:4]
-    blocks = refs[4 : 4 + count]
-    inner_refs, grad_refs = refs[4 + count : 6 + count], refs[6 + count :]
+    blocks, refs = refs[4 : 4 + count], refs[4 + count :]
+    if earlier:
+        before, before_blocks, refs = refs[0:2], refs[2 : 2 + count], refs[2 + count :]
+    inner_refs, grad_refs, terms = refs[0:2], refs[2:4], refs[4:6]
     tile = normed[0].shape[0]
     gate_up = block_product(normed[0], normed[1], blocks, 0, 2 * ff_sub)
     inner_grad = block_product(out[0], out[1], blocks, 2 * ff_sub, 3 * ff_sub)
@@ -347,22 +371,37 @@
         inner_refs[side][...] = inner[rows]
         grad_refs[side][:, :ff_sub] = gate_grad[rows]
         grad_refs[side][:, ff_sub:] = up_grad[rows]
-
-
-def run_ffn_units(normed, out, blocks, ff_sub):
+    if not earlier:
+        return
+    here = jnp.concatenate([gate_grad, up_grad], axis=1)
+    there = jnp.concatenate([before[0][...], before[1][...]], axis=0)
+    rows = blocks[0].shape[0]
+    for k in range(count):
+        span = slice(k * rows, (k + 1) * rows)
+        total = dot_nt(here, blocks[k][:, : 2 * ff_sub]) + dot_nt(there, before_blocks[k][...])
+        total = total.astype(jnp.bfloat16)
+        terms[0][:, span] = total[:tile]
+        terms[1][:, span] = total[tile:]
+
+
+def run_ffn_units(normed, out, blocks, ff_sub, before=None, before_blocks=()):
     tokens, model = normed[0].shape
     tile = min(256, tokens)
     rows = lambda n: pl.BlockSpec((tile, n), lambda i: (i, 0))
+    earlier = before is not None
+    shapes = [ff_sub] * 2 + [2 * ff_sub] * 2 + [model] * 2 * earlier
     return kernel_call(
-        functools.partial(ffn_units, len(blocks), ff_sub),
+        functools.partial(ffn_units, len(blocks), ff_sub, earlier),
         (tokens // tile,),
-        [rows(model)] * 4 + [whole(b) for b in blocks],
-        [rows(ff_sub)] * 2 + [rows(2 * ff_sub)] * 2,
-        [shape_of((tokens, ff_sub), jnp.bfloat16)] * 2
-        + [shape_of((tokens, 2 * ff_sub), jnp.bfloat16)] * 2,
+        [rows(model)] * 4
+        + [whole(b) for b in blocks]
+        + [rows(2 * ff_sub)] * 2 * earlier
+        + [pl.BlockSpec((b.shape[0], 2 * ff_sub), lambda i: (0, 0)) for b in before_blocks],
+        [rows(n) for n in shapes],
+        [shape_of((tokens, n), jnp.bfloat16) for n in shapes],
         12 * tokens * model * ff_sub,
         8 * tokens * model,
-    )(*normed, *out, *blocks)
+    )(*normed, *out, *blocks, *(before if earlier else ()), *before_blocks)
 
 
 def weight_gradients(count, per, *refs):
@@ -396,24 +435,54 @@
         [columns] * 4 + [whole(a) for a in (*first_grad, *second_grad)],
         [out_spec(k) for k in range(count)],
         [shape_of((block_rows, width), jnp.bfloat16)] * count,
-        4 * tokens * model * width,
-        8 * tokens * model,
+        2 * tokens * model * 256,
+        tokens * model,
     )(*first, *second, *first_grad, *second_grad)
 
 
-def transposed_product(parts, count, gain, *refs):
+def partial_gradients(count, per, *refs):
+    left, right, outs = refs[0:2], refs[2:4], refs[-count:]
+    product = dot_tn(left[0][...], right[0][...]) + dot_tn(left[1][...], right[1][...])
+    product = product.astype(jnp.bfloat16)
+    for k in range(count):
+
+        @pl.when(pl.program_id(0) // per == k)
+        def _(k=k):
+            outs[k][...] = product
+
+
+def run_partial_gradients(left, right, count, width, column, into=()):
+    tokens, model = left[0].shape
+    block_rows = model // count
+    tile = min(256, block_rows)
+    per = block_rows // tile
+    columns = pl.BlockSpec((tokens, tile), lambda i: (0, i))
+    part = right[0].shape[1]
+    out_spec = lambda k: pl.BlockSpec(
+        (tile, part), lambda i: (jnp.clip(i - per * k, 0, per - 1), column)
+    )
+    return pl.pallas_call(
+        functools.partial(partial_gradients, count, per),
+        grid=(model // tile,),
+        in_specs=[columns] * 2
+        + [whole(a) for a in right]
+        + [pl.BlockSpec(memory_space=pl.ANY)] * len(into),
+        out_specs=[out_spec(k) for k in range(count)],
+        out_shape=[shape_of((block_rows, width), jnp.bfloat16)] * count,
+        input_output_aliases={4 + k: k for k in range(len(into))},
+        compiler_params=pltpu.CompilerParams(vmem_limit_bytes=vmem_limit),
+        cost_estimate=pl.CostEstimate(
+            flops=2 * tokens * model * 128, bytes_accessed=tokens * model // 2, transcendentals=0
+        ),
+    )(*left, *right, *into)
+
+
+def transposed_product(parts, count, *refs):
     lefts = refs[: 2 * parts]
     blocks = refs[2 * parts : 2 * parts + parts * count]
-    rest = refs[2 * parts + parts * count :]
-    normed, outs = (rest[:2], rest[2:]) if gain else ((), rest)
+    outs = refs[2 * parts + parts * count :]
     tile = lefts[0].shape[0]
     rows = blocks[0].shape[0]
-    if gain:
-
-        @pl.when(pl.program_id(0) == 0)
-        def _():
-            outs[2][...] = jnp.zeros_like(outs[2])
-
     for k in range(count):
         total = None
         span = slice(k * rows, (k + 1) * rows)
@@ -421,16 +490,12 @@
             left = jnp.concatenate([lefts[2 * p][...], lefts[2 * p + 1][...]], axis=0)
             more = dot_nt(left, blocks[p * count + k][...])
             total = more if total is None else total + more
-        if gain:
-            here = total[:tile] * normed[0][:, span].astype(jnp.float32)
-            here = here + total[tile:] * normed[1][:, span].astype(jnp.float32)
-            outs[2][:, span] += jnp.sum(here, axis=0, keepdims=True)
         total = total.astype(jnp.bfloat16)
         outs[0][:, span] = total[:tile]
         outs[1][:, span] = total[tile:]
 
 
-def run_transposed_product(pairs, blocks, column, columns, normed=()):
+def run_transposed_product(pairs, blocks, column, columns):
     count = len(blocks[0])
     tokens = pairs[0][0].shape[0]
     model = count * blocks[0][0].shape[0]
@@ -438,18 +503,16 @@
     rows = lambda n: pl.BlockSpec((tile, n), lambda i: (i, 0))
     lefts = [a for pair in pairs for a in pair]
     flat = [b for one in blocks for b in one]
-    gain = len(normed) > 0
     return kernel_call(
-        functools.partial(transposed_product, len(pairs), count, gain),
+        functools.partial(transposed_product, len(pairs), count),
         (tokens // tile,),
         [rows(a.shape[1]) for a in lefts]
-        + [pl.BlockSpec((b.shape[0], columns), lambda i: (0, column)) for b in flat]
-        + [rows(model) for _ in normed],
-        [rows(model)] * 2 + [pl.BlockSpec((1, model), lambda i: (0, 0))] * gain,
-        [shape_of((tokens, model), jnp.bfloat16)] * 2 + [shape_of((1, model), jnp.float32)] * gain,
-        1 if gain else 4 * tokens * model * columns * len(pairs),
-        1 if gain else 8 * tokens * model,
-    )(*lefts, *flat, *normed)
+        + [pl.BlockSpec((b.shape[0], columns), lambda i: (0, column)) for b in flat],
+        [rows(model)] * 2,
+        [shape_of((tokens, model), jnp.bfloat16)] * 2,
+        2 * tokens * model * 256,
+        tokens * model,
+    )(*lefts, *flat)
 
 
 def add_both(*refs):
@@ -461,7 +524,7 @@
 
 def run_add_both(blocks, got):
     rows, width = blocks[0].shape
-    tile = min(128, rows)
+    tile = min(256, rows)
     spec = pl.BlockSpec((tile, width), lambda i: (i, 0))
     return kernel_call(
         add_both,
@@ -891,31 +954,31 @@
     ffn_w.append(line_1.blocks())
 
     sum_0.hop()
-    units_1 = run_ffn_units(normed2, out_b, ffn_w[1], ff_sub)
-    kept, other = run_transposed_product([units_0[2:], units_1[2:]], ffn_w, 0, 2 * ff_sub)
+    units_1 = run_ffn_units(normed2, out_b, ffn_w[1], ff_sub, units_0[2:], ffn_w[0])
+    kept, other = units_1[4:]
     kept, other, sum_0.got[0], units_1 = tie(kept, other, sum_0.got[0], units_1)
 
     sum_0.hop()
     other = swap_cores(other)
-    got = lines.across_terms(kept, other)
+    send = lines.terms(kept, other, 3).astype(jnp.bfloat16)
+    send, units_1 = tie(send, units_1)
+    got = lines.scatter_across(send)
     branch_kept, branch_other = run_transposed_product(
         [units_0[:2], units_1[:2]], ffn_w, 2, ff_sub
     )
+    ffn_g = run_partial_gradients(normed2, units_1[2:4], lines.length, 3 * ff_sub, 0)
+    got, sum_0.got[1], ffn_g, branch_kept, branch_other, units_1 = tie(
+        got, sum_0.got[1], ffn_g, branch_kept, branch_other, units_1
+    )
+    sum_0.hop()
     branch_other = swap_cores(branch_other)
-    got, sum_0.got[1], units_1, branch_kept, branch_other = tie(
-        got, sum_0.got[1], units_1, branch_kept, branch_other
-    )
-    sum_0.hop()
     near = lines.near_flips(kept, other, got)
-    sum_1 = LineScatter(
-        lines, run_weight_gradients(normed2, units_1[2:], out_b, units_1[:2], lines.length)
-    )
-    near, branch_kept, branch_other = tie(near, branch_kept, branch_other)
+    ffn_g = run_partial_gradients(out_b, units_1[:2], lines.length, 3 * ff_sub, 2, ffn_g)
+    near, branch_kept, branch_other, ffn_g = tie(near, branch_kept, branch_other, ffn_g)
+    sum_1 = LineScatter(lines, ffn_g)
     normed2_grad = lines.near_sum(kept, other, near)
     branch_got = lines.across_terms(branch_kept, branch_other)
-    normed2_grad, sum_0.got[2], branch_got, sum_1.blocks = tie(
-        normed2_grad, sum_0.got[2], branch_got, sum_1.blocks
-    )
+    normed2_grad, sum_0.got[2], branch_got = tie(normed2_grad, sum_0.got[2], branch_got)
 
     sum_1.hop()
     ffn_gain_part = jnp.sum(normed2_grad * state * scale_second, axis=0)
@@ -924,20 +987,25 @@
     near, across = lines.gather_far(grad_mine)
     back_0 = lines.row_pieces(sum_0.total())
     branch_terms = lines.near_sends(branch_kept, branch_other, branch_got)
-    near, across, sum_1.got[0], back_0, branch_terms = tie(
-        near, across, sum_1.got[0], back_0, branch_terms
-    )
-
-    sum_1.hop()
+    ready = sum_1.ready()
+    near, across, ready, back_0, branch_terms = tie(near, across, ready, back_0, branch_terms)
+
+    sum_1.hop(ready)
     attended_b = lines.both_cores(grad_mine, near, across)
 
     branch = [lines.flip(branch_terms[0], 1), lines.flip(branch_terms[1], 2)]
     back_0_first = lines.flip_first(back_0)
-    qkv_grad, gain_parts = run_attention(
-        False, attended_b, attn_w, tables, gains_two, head_dim, query_width, attn_width, qkv_raw
-    )
-    kept, other, attn_gain_part = run_transposed_product(
-        [qkv_grad], [attn_w], 0, attn_width, normed
+    qkv_grad, gain_parts, kept, other, attn_gain_part = run_attention(
+        False,
+        attended_b,
+        attn_w,
+        tables,
+        gains_two,
+        head_dim,
+        query_width,
+        attn_width,
+        qkv_raw,
+        normed,
     )
     kept, other, qkv_grad, branch, sum_1.got[1], back_0, back_0_first = tie(
         kept, other, qkv_grad, branch, sum_1.got[1], back_0, back_0_first
@@ -965,18 +1033,31 @@
     back_1 = lines.row_pieces(sum_1.total())
     near = lines.near_flips(kept, other, got)
     attn_sum.hop()
-    near, attn_sum.got[1], back_1 = tie(near, attn_sum.got[1], back_1)
+    gains_got = lines.flip(gains, 1)
+    mixed = state + lines.near_sum(branch_kept, branch_other, branch)
+    mixed_other = swap_cores(mixed)
+    near, attn_sum.got[1], back_1, mixed, mixed_other, gains_got = tie(
+        near, attn_sum.got[1], back_1, mixed, mixed_other, gains_got
+    )
     attn_sum.hop()
     back_1 = lines.flip_pieces(back_1)
-    attn_sum.got[2], back_1, near, gains = tie(attn_sum.got[2], back_1, near, gains)
+    gains = gains + gains_got
+    gains_got = lines.flip(gains, 2)
+    mixed = run_place_halves(core, lines.spot, lines.length, mixed, mixed_other)
+    attn_sum.got[2], back_1, near, gains, gains_got, mixed = tie(
+        attn_sum.got[2], back_1, near, gains, gains_got, mixed
+    )
+    gains = gains + gains_got
     attn_grads = lines.flip_pieces(lines.row_pieces(attn_sum.total()))
     normed_grad = lines.near_sum(kept, other, near)
     input_grad = state_grad + norm_back(source, scale_first, attn_gain_r, normed_grad)
     input_other = swap_cores(input_grad)
-    bit = 1
+    bit = group
     while bit < dp:
         gains = gains + lines.flip(gains, bit)
         bit *= 2
+        if bit == 2 * group:
+            gains, attn_grads = tie(gains, attn_grads)
     gains = gains + swap_cores(gains)
     ffn_grads = run_place_columns(
         lines.place,
@@ -986,18 +1067,14 @@
         ],
         3,
     )
-    mixed = state + lines.near_sum(branch_kept, branch_other, branch)
-
-    def whole_rows(mine, other):
-        return run_place_halves(core, lines.spot, lines.length, mine, other)
 
     def columns_of(related, start, stop):
         blocks = lines.by_place([b[:, start:stop] for b in related])
         return jnp.concatenate(blocks, axis=1).astype(jnp.float32)
 
     return (
-        whole_rows(mixed, swap_cores(mixed)),
-        whole_rows(input_grad, input_other),
+        mixed,
+        run_place_halves(core, lines.spot, lines.length, input_grad, input_other),
         gains[:width],
         gains[width : 2 * width],
         gains[2 * width : 2 * width + head_dim],

time: 778 us -> 739 us (0.950)
  waiting for transfers between devices: 252 us -> 220 us
    ppermute x54, waiting for transfers between devices: 136 us -> 111 us  [flip(): lax.ppermute(values, 'dp', [(i, i ^ relation) for i in range(self.dp)])]
    pallas_call x3 -> x2, Pallas kernels: 55.9 us -> 34.7 us  [run_weight_gradients(): kernel_call(functools.partial(weight_gradients, count, per), (model // ti...]
    pallas_call x5, Pallas kernels: 86.3 us -> 98.9 us  [the longest x2 59.7 us: run_ffn_units(): kernel_call(functools.partial(ffn_units, len(blocks), ff_sub, earlier), (...]
    pallas_call x1, Pallas kernels: 26.3 us -> 34.3 us  [run_attention(): kernel_call(functools.partial(attention_backward, len(blocks), head_dim,...]
    unnamed x190 -> x182, local copies, waits for them, and re-layouts: 22.7 us -> 23.6 us
  transfers between devices with their start and end apart: 104 -> 104, of which waited for: 42 -> 40; matrix products, arithmetic and copies ran while one was open for 13% -> 14% of each run, Pallas kernels for 29% -> 30%
where the time goes in v4:
time: 739 us; the launch traced here: 730 us
  Pallas kernels  225 us (30%)
  waiting for transfers between devices  220 us (30%)
  starting transfers between devices  151 us (20%)
  other arithmetic  88.6 us (12%)
  local copies, waits for them, and re-layouts  42.1 us (6%)
    ppermute x54, waiting for transfers between devices, flip(): lax.ppermute(values, 'dp', [(i, i ^ relation) for i in range(self.dp)])  111 us
    ppermute x36, waiting for transfers between devices, hop(): return lax.ppermute(values, 'dp', pairs)  104 us
    ppermute x36, starting transfers between devices, hop(): return lax.ppermute(values, 'dp', pairs)  66.7 us
    pallas_call x2, Pallas kernels, run_ffn_units(): kernel_call(functools.partial(ffn_units, len(blocks), ff_sub, earlier), (...  59.7 us
    ppermute x54, starting transfers between devices, flip(): lax.ppermute(values, 'dp', [(i, i ^ relation) for i in range(self.dp)])  48.2 us
    ppermute x14, starting transfers between devices, swap_cores(): return lax.ppermute(values, 'tensor', [(0, 1), (1, 0)])  36.6 us
    pallas_call x2, Pallas kernels, run_weight_gradients(): kernel_call(functools.partial(weight_gradients, count, per), (model // ti...  34.7 us
    pallas_call x1, Pallas kernels, run_attention(): kernel_call(functools.partial(attention_backward, len(blocks), head_dim,...  34.3 us
  transfers between devices with their start and end apart: 104, of which 40 were waited for; matrix products, arithmetic and copies ran while one was open for 14% of the time, Pallas kernels for 30%

profile of v4, /device:TPU:1, one launch (start us, length us, event | category | flops | bytes accessed | tf_op | source)
XLA Modules:
  0.0 730.1 jit_solution(9007019144485683812)
XLA Ops:
  19.7 4.1 collective-permute-start.7
  25.1 3.5 collective-permute-start.9
  30.6 5.6 multiply_sine_fusion
  62.9 8.9 %collective-permute-done.13 = bf16[512,640]{1,0:T(8,128)(2,1)} collective-permute-done((bf16[512,640]{1,0:T(8,128)(2,1)}, bf16[512,640]{1,0:T(8,128)(2,1)}, u32[]{:S(2)}, u32[]{:S(2)}) %collective-permute-start.13) | collective-permute-done | bytes 655392 | tf_op jit(solution)/shard_map/ppermute | solution.py:618
  85.3 3.6 pad_maximum_fusion.refs_1_.refs_4_
  88.9 8.0 %collective-permute-done.20 = bf16[128,1536]{1,0:T(8,128)(2,1)S(1)} collective-permute-done((bf16[128,1536]{1,0:T(8,128)(2,1)}, bf16[128,1536]{1,0:T(8,128)(2,1)S(1)}, u32[]{:S(2)}, u32[]{:S(2)}) %collective-permute-start.20) | collective-permute-done | bytes 393248 | tf_op jit(solution)/shard_map/ppermute | solution.py:610
  107.1 20.8 %shard_map.237 = (f32[4,512,384]{2,1,0:T(8,128)}, bf16[1024,256]{1,0:T(8,128)(2,1)S(1)}, bf16[1024,256]{1,0:T(8,128)(2,1)S(1)}, bf16[1024,2048]{1,0:T(8,128)(2,1)}, bf16[1024,2048]{1,0:T(8,128)(2,1)}) custom-call(bf16[1024,2048]{1,0:T(8,128)(2,1)} %constant_dynamic-update-slice_fusion.refs_0_.refs_3_, bf16[1024,2048]{1,0:T(8,128)(2,1)} %pad_maximum_fusion.refs_1_.refs_4_, ...), custom_call_target="tpu_custom_call" | custom-call | flops 32212254720 | bytes 33554432 | tf_op jit(solution)/shard_map/pallas_call | solution.py:328
  127.9 4.4 collective-permute-done.22
  132.3 3.9 collective-permute-done.23
  143.6 9.4 %collective-permute-done.27 = bf16[128,2048]{1,0:T(8,128)(2,1)S(1)} collective-permute-done((bf16[128,2048]{1,0:T(8,128)(2,1)S(1)}, bf16[128,2048]{1,0:T(8,128)(2,1)S(1)}, u32[]{:S(2)}, u32[]{:S(2)}) %collective-permute-start.27) | collective-permute-done | bytes 524320 | tf_op jit(solution)/shard_map/ppermute | solution.py:610
  159.6 19.9 %collective-permute-done.32 = bf16[512,1536]{1,0:T(8,128)(2,1)S(1)} collective-permute-done((bf16[512,1536]{1,0:T(8,128)(2,1)S(1)}, bf16[512,1536]{1,0:T(8,128)(2,1)S(1)}, u32[]{:S(2)}, u32[]{:S(2)}) %collective-permute-start.32) | collective-permute-done | bytes 1572896 | tf_op jit(solution)/shard_map/ppermute | solution.py:618
  184.6 18.5 %collective-permute-done.34 = bf16[256,2048]{1,0:T(8,128)(2,1)S(1)} collective-permute-done((bf16[256,2048]{1,0:T(8,128)(2,1)S(1)}, bf16[256,2048]{1,0:T(8,128)(2,1)S(1)}, u32[]{:S(2)}, u32[]{:S(2)}) %collective-permute-start.34) | collective-permute-done | bytes 1048608 | tf_op jit(solution)/shard_map/ppermute | solution.py:610
  206.3 13.6 %collective-permute-done.38 = bf16[256,1536]{1,0:T(8,128)(2,1)S(1)} collective-permute-done((bf16[256,1536]{1,0:T(8,128)(2,1)S(1)}, bf16[256,1536]{1,0:T(8,128)(2,1)S(1)}, u32[]{:S(2)}, u32[]{:S(2)}) %collective-permute-start.38) | collective-permute-done | bytes 786464 | tf_op jit(solution)/shard_map/ppermute | solution.py:610
  225.5 3.7 collective-permute-start.43
  233.1 14.4 %collective-permute-done.39 = bf16[256,2048]{1,0:T(8,128)(2,1)S(1)} collective-permute-done((bf16[256,2048]{1,0:T(8,128)(2,1)S(1)}, bf16[256,2048]{1,0:T(8,128)(2,1)S(1)}, u32[]{:S(2)}, u32[]{:S(2)}) %collective-permute-start.39) | collective-permute-done | bytes 1048608 | tf_op jit(solution)/shard_map/ppermute | solution.py:610
  250.2 8.6 %collective-permute-done.41 = bf16[128,2048]{1,0:T(8,128)(2,1)S(1)} collective-permute-done((bf16[128,2048]{1,0:T(8,128)(2,1)S(1)}, bf16[128,2048]{1,0:T(8,128)(2,1)S(1)}, u32[]{:S(2)}, u32[]{:S(2)}) %collective-permute-start.41) | collective-permute-done | bytes 524320 | tf_op jit(solution)/shard_map/ppermute | solution.py:610
  259.7 5.1 collective-permute-done.44
  272.6 4.5 collective-permute-done.46.refs_1_
  277.0 19.6 %shard_map.238 = (bf16[1024,512]{1,0:T(8,128)(2,1)S(1)}, bf16[1024,512]{1,0:T(8,128)(2,1)}, bf16[1024,1024]{1,0:T(8,128)(2,1)}, bf16[1024,1024]{1,0:T(8,128)(2,1)}) custom-call(bf16[1024,2048]{1,0:T(8,128)(2,1)} %copy-done.14, bf16[1024,2048]{1,0:T(8,128)(2,1)} %collective-permute-done.46.refs_1_, bf16[1024,2048]{1,0:T(8,128)(2,1)} %copy-done.15, ...), custom_call_target="tpu_custom_call" | custom-call | flops 12884901888 | bytes 16777216 | tf_op jit(solution)/shard_map/pallas_call | solution.py:393
  296.6 12.4 %collective-permute-done.48 = bf16[512,1536]{1,0:T(8,128)(2,1)S(1)} collective-permute-done((bf16[512,1536]{1,0:T(8,128)(2,1)}, bf16[512,1536]{1,0:T(8,128)(2,1)S(1)}, u32[]{:S(2)}, u32[]{:S(2)}) %collective-permute-start.48) | collective-permute-done | bytes 1572896 | tf_op jit(solution)/shard_map/ppermute | solution.py:618
  311.0 21.0 %shard_map.239 = (bf16[512,1536]{1,0:T(8,128)(2,1)}, bf16[512,1536]{1,0:T(8,128)(2,1)}, bf16[512,1536]{1,0:T(8,128)(2,1)}, bf16[512,1536]{1,0:T(8,128)(2,1)}) custom-call(bf16[1024,2048]{1,0:T(8,128)(2,1)} %copy-done.14, bf16[1024,2048]{1,0:T(8,128)(2,1)} %collective-permute-done.46.refs_1_, bf16[1024,2048]{1,0:T(8,128)(2,1)} %copy-done.15, ...), custom_call_target="tpu_custom_call" | custom-call | flops 1073741824 | bytes 2097152 | tf_op jit(solution)/shard_map/pallas_call | solution.py:432
  333.4 13.3 %collective-permute-done.50 = bf16[512,1536]{1,0:T(8,128)(2,1)S(1)} collective-permute-done((bf16[512,1536]{1,0:T(8,128)(2,1)S(1)}, bf16[512,1536]{1,0:T(8,128)(2,1)S(1)}, u32[]{:S(2)}, u32[]{:S(2)}) %collective-permute-start.50) | collective-permute-done | bytes 1572896 | tf_op jit(solution)/shard_map/ppermute | solution.py:618
  353.2 40.1 %shard_map.240 = (bf16[1024,512]{1,0:T(8,128)(2,1)S(1)}, bf16[1024,512]{1,0:T(8,128)(2,1)}, bf16[1024,1024]{1,0:T(8,128)(2,1)}, bf16[1024,1024]{1,0:T(8,128)(2,1...) custom-call(bf16[1024,2048]{1,0:T(8,128)(2,1)} %copy-done.14, ...), custom_call_target="tpu_custom_call" | custom-call | flops 12884901888 | bytes 16777216 | tf_op jit(solution)/shard_map/pallas_call | solution.py:393
  396.2 4.1 shard_map.241
  405.8 4.2 convert_add_fusion.6
  413.0 15.0 %shard_map.242 = (bf16[512,1536]{1,0:T(8,128)(2,1)S(1)}, bf16[512,1536]{1,0:T(8,128)(2,1)}, bf16[512,1536]{1,0:T(8,128)(2,1)}, bf16[512,1536]{1,0:T(8,128)(2,1)}) custom-call(bf16[1024,2048]{1,0:T(8,128)(2,1)} %copy-done.14, bf16[1024,2048]{1,0:T(8,128)(2,1)} %collective-permute-done.46.refs_1_, bf16[1024,1024]{1,0:T(8,128)(2,1)} %get-tuple-element.395.refs_2_, ...), custom_call_target="tpu_custom_call" | custom-call | flops 536870912 | bytes 1048576 | tf_op jit(solution)/shard_map/pallas_call | solution.py:464
  429.2 13.4 %shard_map.243 = (bf16[1024,2048]{1,0:T(8,128)(2,1)}, bf16[1024,2048]{1,0:T(8,128)(2,1)}) custom-call(bf16[1024,512]{1,0:T(8,128)(2,1)S(1)} %get-tuple-element.401.refs_6_.refs_0_, bf16[1024,512]{1,0:T(8,128)(2,1)} %get-tuple-element.402.refs_7_.refs_1_, bf16[1024,512]{1,0:T(8,128)(2,1)} %copy-done.4, bf16[1024,512]{1,0:T(8,128)(2,1)} %get-tuple-element.412.refs_3_, ...), custom_call_target="tpu_custom_call" | custom-call | flops 1073741824 | bytes 2097152 | tf_op jit(solution)/shard_map/pallas_call | solution.py:506
  449.8 4.1 shard_map.245
  457.6 10.8 %shard_map.244 = (bf16[512,1536]{1,0:T(8,128)(2,1)}, bf16[512,1536]{1,0:T(8,128)(2,1)}, bf16[512,1536]{1,0:T(8,128)(2,1)}, bf16[512,1536]{1,0:T(8,128)(2,1)}) custom-call(bf16[1024,2048]{1,0:T(8,128)(2,1)} %copy-done.15, bf16[1024,2048]{1,0:T(8,128)(2,1)} %copy-done.18, ...), custom_call_target="tpu_custom_call", output_to_operand_aliasing={{0}: (4, {}), {1}: (5, {}), {2}: (6, {}), {3}: (7, {})} | custom-call | flops 536870912 | bytes 1048576 | tf_op jit(solution)/shard_map/pallas_call | solution.py:464
  468.4 3.6 collective-permute-done.58
  482.8 5.2 collective-permute-done.61
  502.8 16.2 %collective-permute-done.65 = bf16[256,2048]{1,0:T(8,128)(2,1)S(1)} collective-permute-done((bf16[256,2048]{1,0:T(8,128)(2,1)S(1)}, bf16[256,2048]{1,0:T(8,128)(2,1)S(1)}, u32[]{:S(2)}, u32[]{:S(2)}) %collective-permute-start.65) | collective-permute-done | bytes 1048608 | tf_op jit(solution)/shard_map/ppermute | solution.py:610
  526.0 4.7 shard_map.246
  534.8 4.3 collective-permute-start.71
  548.0 34.3 %shard_map.247 = (bf16[1024,384]{1,0:T(8,128)(2,1)}, bf16[1024,384]{1,0:T(8,128)(2,1)}, f32[2,256]{1,0:T(2,128)S(1)}, bf16[1024,2048]{1,0:T(8,128)(2,1)}, bf16[1...) custom-call(bf16[1024,2048]{1,0:T(8,128)(2,1)} %copy-done.23, bf16[1024,2048]{1,0:T(8,128)(2,1)} %copy-done.30, ...), custom_call_target="tpu_custom_call" | custom-call | flops 32212254720 | bytes 33554432 | tf_op jit(solution)/shard_map/pallas_call | solution.py:338
  584.8 4.3 shard_map.248
  596.1 13.7 %shard_map.249 = (bf16[512,640]{1,0:T(8,128)(2,1)S(1)}, bf16[512,640]{1,0:T(8,128)(2,1)}, bf16[512,640]{1,0:T(8,128)(2,1)}, bf16[512,640]{1,0:T(8,128)(2,1)}) custom-call(bf16[1024,2048]{1,0:T(8,128)(2,1)} %constant_dynamic-update-slice_fusion.refs_0_.refs_3_, bf16[1024,2048]{1,0:T(8,128)(2,1)} %pad_maximum_fusion.refs_1_.refs_4_, ...), custom_call_target="tpu_custom_call" | custom-call | flops 1073741824 | bytes 2097152 | tf_op jit(solution)/shard_map/pallas_call | solution.py:432
  618.8 6.0 collective-permute-done.80
  624.9 4.9 collective-permute-done.81
  638.4 8.6 %collective-permute-done.85.refs_2_ = bf16[512,640]{1,0:T(8,128)(2,1)S(1)} collective-permute-done((bf16[512,640]{1,0:T(8,128)(2,1)S(1)}, bf16[512,640]{1,0:T(8,128)(2,1)S(1)}, u32[]{:S(2)}, u32[]{:S(2)}) %collective-permute-start.85) | collective-permute-done | bytes 655392 | tf_op jit(solution)/shard_map/ppermute | solution.py:618
  649.3 4.1 collective-permute-start.87
  660.4 4.8 collective-permute-done.87.refs_2_
  667.9 6.0 collective-permute-start.91
  680.0 5.5 shard_map.252
  687.1 4.7 collective-permute-done.95.refs_7_
  697.3 6.3 collective-permute-start.97
  709.7 4.8 shard_map.254
  724.4 5.3 shard_map.253
  (526 shorter events, 261.2 us)
Async XLA Ops:
  97.3 35.0 %collective-permute-start.22 = (bf16[512,1536]{1,0:T(8,128)(2,1)S(1)}, bf16[512,1536]{1,0:T(8,128)(2,1)S(1)}, u32[]{:S(2)}, u32[]{:S(2)}) collective-permute-start(bf16[512,1536]{1,0:T(8,128)(2,1)S(1)} %pad_maximum_fusion.1.refs_4_.refs_10_), channel_id=1, source_target_pairs={{0,8},{2,10},{4,12},{6,14},{8,16},{10,18},{12,20},{14,22},{16,24},... | collective-permute-start | bytes 4718600 | tf_op jit(solution)/shard_map/ppermute | solution.py:618
  100.6 35.6 %collective-permute-start.23 = (bf16[512,1536]{1,0:T(8,128)(2,1)S(1)}, bf16[512,1536]{1,0:T(8,128)(2,1)S(1)}, u32[]{:S(2)}, u32[]{:S(2)}) collective-permute-start(bf16[512,1536]{1,0:T(8,128)(2,1)S(1)} %pad_maximum_fusion.1.refs_4_.refs_10_), channel_id=1, source_target_pairs={{8,0},{10,2},{12,4},{14,6},{16,8},{18,10},{20,12},{22,14},{24,16},... | collective-permute-start | bytes 4718600 | tf_op jit(solution)/shard_map/ppermute | solution.py:618
  102.1 25.8 %collective-permute-start.24 = (bf16[256,2048]{1,0:T(8,128)(2,1)S(1)}, bf16[256,2048]{1,0:T(8,128)(2,1)S(1)}, u32[]{:S(2)}, u32[]{:S(2)}) collective-permute-start(bf16[256,2048]{1,0:T(8,128)(2,1)S(1)} %fusion.17), channel_id=1, source_target_pairs={{0,2},{2,0},{4,6},{6,4},{8,10},{10,8},{12,14},{14,12},{16,18},{18,... | collective-permute-start | bytes 3145736 | tf_op jit(solution)/shard_map/ppermute | solution.py:610
  103.0 24.9 %collective-permute-start.25 = (bf16[256,2048]{1,0:T(8,128)(2,1)S(1)}, bf16[256,2048]{1,0:T(8,128)(2,1)S(1)}, u32[]{:S(2)}, u32[]{:S(2)}) collective-permute-start(bf16[256,2048]{1,0:T(8,128)(2,1)S(1)} %fusion.17), channel_id=1, source_target_pairs={{0,4},{2,6},{4,0},{6,2},{8,12},{10,14},{12,8},{14,10},{16,20},{18,... | collective-permute-start | bytes 3145736 | tf_op jit(solution)/shard_map/ppermute | solution.py:610
  142.3 37.3 %collective-permute-start.32 = (bf16[512,1536]{1,0:T(8,128)(2,1)S(1)}, bf16[512,1536]{1,0:T(8,128)(2,1)S(1)}, u32[]{:S(2)}, u32[]{:S(2)}) collective-permute-start(bf16[512,1536]{1,0:T(8,128)(2,1)S(1)} %collective-permute-done.23), channel_id=1, source_target_pairs={{8,0},{10,2},{12,4},{14,6},{16,8},{18,10},{20,12},{22,14},{9,1},{1... | collective-permute-start | bytes 4718600 | tf_op jit(solution)/shard_map/ppermute | solution.py:618
  156.2 23.4 %collective-permute-start.28 = (bf16[128,2048]{1,0:T(8,128)(2,1)S(1)}, bf16[128,2048]{1,0:T(8,128)(2,1)S(1)}, u32[]{:S(2)}, u32[]{:S(2)}) collective-permute-start(bf16[128,2048]{1,0:T(8,128)(2,1)S(1)} %get-tuple-element.570), channel_id=1, source_target_pairs={{0,2},{2,0},{4,6},{6,4},{8,10},{10,8},{12,14},{14,12},{16,18},{18,... | collective-permute-start | bytes 1572872 | tf_op jit(solution)/shard_map/ppermute | solution.py:610
  179.8 23.3 %collective-permute-start.34 = (bf16[256,2048]{1,0:T(8,128)(2,1)S(1)}, bf16[256,2048]{1,0:T(8,128)(2,1)S(1)}, u32[]{:S(2)}, u32[]{:S(2)}) collective-permute-start(bf16[256,2048]{1,0:T(8,128)(2,1)S(1)} %pad_maximum_fusion.5), channel_id=1, source_target_pairs={{0,4},{2,6},{4,0},{6,2},{8,12},{10,14},{12,8},{14,10},{16,20},{18,... | collective-permute-start | bytes 3145736 | tf_op jit(solution)/shard_map/ppermute | solution.py:610
  180.4 23.0 %collective-permute-start.33 = (bf16[256,2048]{1,0:T(8,128)(2,1)S(1)}, bf16[256,2048]{1,0:T(8,128)(2,1)S(1)}, u32[]{:S(2)}, u32[]{:S(2)}) collective-permute-start(bf16[256,2048]{1,0:T(8,128)(2,1)S(1)} %pad_maximum_fusion.4), channel_id=1, source_target_pairs={{0,2},{2,0},{4,6},{6,4},{8,10},{10,8},{12,14},{14,12},{16,18},{18,... | collective-permute-start | bytes 3145736 | tf_op jit(solution)/shard_map/ppermute | solution.py:610
  181.1 38.8 %collective-permute-start.35 = (bf16[512,1536]{1,0:T(8,128)(2,1)S(1)}, bf16[512,1536]{1,0:T(8,128)(2,1)S(1)}, u32[]{:S(2)}, u32[]{:S(2)}) collective-permute-start(bf16[512,1536]{1,0:T(8,128)(2,1)S(1)} %collective-permute-done.31), channel_id=1, source_target_pairs={{16,24},{18,26},{20,28},{22,30},{17,25},{19,27},{21,29},{23,31}} | collective-permute-start | bytes 4718600 | tf_op jit(solution)/shard_map/ppermute | solution.py:618
  181.9 38.1 %collective-permute-start.36 = (bf16[512,1536]{1,0:T(8,128)(2,1)S(1)}, bf16[512,1536]{1,0:T(8,128)(2,1)S(1)}, u32[]{:S(2)}, u32[]{:S(2)}) collective-permute-start(bf16[512,1536]{1,0:T(8,128)(2,1)S(1)} %collective-permute-done.32), channel_id=1, source_target_pairs={{8,0},{10,2},{12,4},{14,6},{9,1},{11,3},{13,5},{15,7}} | collective-permute-start | bytes 4718600 | tf_op jit(solution)/shard_map/ppermute | solution.py:618
  183.3 36.6 %collective-permute-start.38 = (bf16[256,1536]{1,0:T(8,128)(2,1)S(1)}, bf16[256,1536]{1,0:T(8,128)(2,1)S(1)}, u32[]{:S(2)}, u32[]{:S(2)}) collective-permute-start(bf16[256,1536]{1,0:T(8,128)(2,1)S(1)} %pad_maximum_fusion.13), channel_id=1, source_target_pairs={{0,4},{2,6},{4,0},{6,2},{8,12},{10,14},{12,8},{14,10},{16,20},{18,... | collective-permute-start | bytes 2359304 | tf_op jit(solution)/shard_map/ppermute | solution.py:610
  220.0 44.7 %collective-permute-start.45 = (bf16[1024,2048]{1,0:T(8,128)(2,1)S(1)}, bf16[1024,2048]{1,0:T(8,128)(2,1)S(1)}, u32[]{:S(2)}, u32[]{:S(2)}) collective-permute-start(bf16[1024,2048]{1,0:T(8,128)(2,1)S(1)} %constant_dynamic-update-slice_fusion.5.refs_2_.refs_0_), channel_id=1, source_target_pairs={{0,1},{1,0},{2,3},{3,2},{4,5},{5,4},{6,7},{7,6},{8,9},{9,8},{10,11... | collective-permute-start | bytes 12582920 | tf_op jit(solution)/shard_map/ppermute | solution.py:598
  224.3 23.3 %collective-permute-start.39 = (bf16[256,2048]{1,0:T(8,128)(2,1)S(1)}, bf16[256,2048]{1,0:T(8,128)(2,1)S(1)}, u32[]{:S(2)}, u32[]{:S(2)}) collective-permute-start(bf16[256,2048]{1,0:T(8,128)(2,1)S(1)} %get-tuple-element.530), channel_id=1, source_target_pairs={{0,2},{2,0},{4,6},{6,4},{8,10},{10,8},{12,14},{14,12},{16,18},{18,... | collective-permute-start | bytes 3145736 | tf_op jit(solution)/shard_map/ppermute | solution.py:610
  225.0 23.0 %collective-permute-start.40 = (bf16[256,2048]{1,0:T(8,128)(2,1)S(1)}, bf16[256,2048]{1,0:T(8,128)(2,1)S(1)}, u32[]{:S(2)}, u32[]{:S(2)}) collective-permute-start(bf16[256,2048]{1,0:T(8,128)(2,1)S(1)} %get-tuple-element.530), channel_id=1, source_target_pairs={{0,4},{2,6},{4,0},{6,2},{8,12},{10,14},{12,8},{14,10},{16,20},{18,... | collective-permute-start | bytes 3145736 | tf_op jit(solution)/shard_map/ppermute | solution.py:610
  225.5 34.2 %collective-permute-start.43 = (bf16[512,1536]{1,0:T(8,128)(2,1)S(1)}, bf16[512,1536]{1,0:T(8,128)(2,1)}, u32[]{:S(2)}, u32[]{:S(2)}) collective-permute-start(bf16[512,1536]{1,0:T(8,128)(2,1)S(1)} %pad_maximum_fusion.2.refs_4_.refs_8_), channel_id=1, source_target_pairs={{0,8},{2,10},{4,12},{6,14},{8,16},{10,18},{12,20},{14,22},{16,24},... | collective-permute-start | bytes 4718600 | tf_op jit(solution)/shard_map/ppermute | solution.py:618
  229.2 35.6 %collective-permute-start.44 = (bf16[512,1536]{1,0:T(8,128)(2,1)S(1)}, bf16[512,1536]{1,0:T(8,128)(2,1)}, u32[]{:S(2)}, u32[]{:S(2)}) collective-permute-start(bf16[512,1536]{1,0:T(8,128)(2,1)S(1)} %pad_maximum_fusion.2.refs_4_.refs_8_), channel_id=1, source_target_pairs={{8,0},{10,2},{12,4},{14,6},{16,8},{18,10},{20,12},{22,14},{24,16},... | collective-permute-start | bytes 4718600 | tf_op jit(solution)/shard_map/ppermute | solution.py:618
  270.1 26.5 %collective-permute-start.47 = (bf16[512,1536]{1,0:T(8,128)(2,1)}, bf16[512,1536]{1,0:T(8,128)(2,1)S(1)}, u32[]{:S(2)}, u32[]{:S(2)}) collective-permute-start(bf16[512,1536]{1,0:T(8,128)(2,1)} %collective-permute-done.43), channel_id=1, source_target_pairs={{8,16},{10,18},{12,20},{14,22},{16,24},{18,26},{20,28},{22,30},{9,... | collective-permute-start | bytes 4718600 | tf_op jit(solution)/shard_map/ppermute | solution.py:618
  270.9 38.1 %collective-permute-start.48 = (bf16[512,1536]{1,0:T(8,128)(2,1)}, bf16[512,1536]{1,0:T(8,128)(2,1)S(1)}, u32[]{:S(2)}, u32[]{:S(2)}) collective-permute-start(bf16[512,1536]{1,0:T(8,128)(2,1)} %collective-permute-done.44), channel_id=1, source_target_pairs={{8,0},{10,2},{12,4},{14,6},{16,8},{18,10},{20,12},{22,14},{9,1},{1... | collective-permute-start | bytes 4718600 | tf_op jit(solution)/shard_map/ppermute | solution.py:618
  309.0 24.4 %collective-permute-start.49 = (bf16[512,1536]{1,0:T(8,128)(2,1)S(1)}, bf16[512,1536]{1,0:T(8,128)(2,1)S(1)}, u32[]{:S(2)}, u32[]{:S(2)}) collective-permute-start(bf16[512,1536]{1,0:T(8,128)(2,1)S(1)} %collective-permute-done.47), channel_id=1, source_target_pairs={{16,24},{18,26},{20,28},{22,30},{17,25},{19,27},{21,29},{23,31}} | collective-permute-start | bytes 4718600 | tf_op jit(solution)/shard_map/ppermute | solution.py:618
  309.7 37.0 %collective-permute-start.50 = (bf16[512,1536]{1,0:T(8,128)(2,1)S(1)}, bf16[512,1536]{1,0:T(8,128)(2,1)S(1)}, u32[]{:S(2)}, u32[]{:S(2)}) collective-permute-start(bf16[512,1536]{1,0:T(8,128)(2,1)S(1)} %collective-permute-done.48), channel_id=1, source_target_pairs={{8,0},{10,2},{12,4},{14,6},{9,1},{11,3},{13,5},{15,7}} | collective-permute-start | bytes 4718600 | tf_op jit(solution)/shard_map/ppermute | solution.py:618
  349.7 44.6 %collective-permute-start.51 = (bf16[512,1536]{1,0:T(8,128)(2,1)S(1)}, bf16[512,1536]{1,0:T(8,128)(2,1)S(1)}, u32[]{:S(2)}, u32[]{:S(2)}) collective-permute-start(bf16[512,1536]{1,0:T(8,128)(2,1)S(1)} %copy-done.44), channel_id=1, source_target_pairs={{0,8},{2,10},{4,12},{6,14},{1,9},{3,11},{5,13},{7,15}} | collective-permute-start | bytes 4718600 | tf_op jit(solution)/shard_map/ppermute | solution.py:618
  351.1 43.2 %collective-permute-start.52 = (bf16[512,1536]{1,0:T(8,128)(2,1)S(1)}, bf16[512,1536]{1,0:T(8,128)(2,1)S(1)}, u32[]{:S(2)}, u32[]{:S(2)}) collective-permute-start(bf16[512,1536]{1,0:T(8,128)(2,1)S(1)} %copy-done.43), channel_id=1, source_target_pairs={{24,16},{26,18},{28,20},{30,22},{25,17},{27,19},{29,21},{31,23}} | collective-permute-start | bytes 4718600 | tf_op jit(solution)/shard_map/ppermute | solution.py:618
  400.3 42.2 %collective-permute-start.56 = (bf16[512,1536]{1,0:T(8,128)(2,1)S(1)}, bf16[512,1536]{1,0:T(8,128)(2,1)}, u32[]{:S(2)}, u32[]{:S(2)}) collective-permute-start(bf16[512,1536]{1,0:T(8,128)(2,1)S(1)} %get-tuple-element.393), channel_id=1, source_target_pairs={{0,8},{2,10},{4,12},{6,14},{8,16},{10,18},{12,20},{14,22},{1,9},{3... | collective-permute-start | bytes 4718600 | tf_op jit(solution)/shard_map/ppermute | solution.py:618
  403.8 38.8 %collective-permute-start.57 = (bf16[512,1536]{1,0:T(8,128)(2,1)}, bf16[512,1536]{1,0:T(8,128)(2,1)}, u32[]{:S(2)}, u32[]{:S(2)}) collective-permute-start(bf16[512,1536]{1,0:T(8,128)(2,1)} %get-tuple-element.394), channel_id=1, source_target_pairs={{16,8},{18,10},{20,12},{22,14},{24,16},{26,18},{28,20},{30,22},{17... | collective-permute-start | bytes 4718600 | tf_op jit(solution)/shard_map/ppermute | solution.py:618
  411.0 31.5 %collective-permute-start.54 = (bf16[128,2048]{1,0:T(8,128)(2,1)}, bf16[128,2048]{1,0:T(8,128)(2,1)S(1)}, u32[]{:S(2)}, u32[]{:S(2)}) collective-permute-start(bf16[128,2048]{1,0:T(8,128)(2,1)} %get-tuple-element.568), channel_id=1, source_target_pairs={{0,2},{2,0},{4,6},{6,4},{8,10},{10,8},{12,14},{14,12},{16,18},{18,... | collective-permute-start | bytes 1572872 | tf_op jit(solution)/shard_map/ppermute | solution.py:610
  411.8 30.7 %collective-permute-start.55 = (bf16[128,2048]{1,0:T(8,128)(2,1)}, bf16[128,2048]{1,0:T(8,128)(2,1)}, u32[]{:S(2)}, u32[]{:S(2)}) collective-permute-start(bf16[128,2048]{1,0:T(8,128)(2,1)} %get-tuple-element.567), channel_id=1, source_target_pairs={{0,4},{2,6},{4,0},{6,2},{8,12},{10,14},{12,8},{14,10},{16,20},{18,... | collective-permute-start | bytes 1572872 | tf_op jit(solution)/shard_map/ppermute | solution.py:610
  442.6 31.0 %collective-permute-start.60 = (bf16[1024,2048]{1,0:T(8,128)(2,1)}, bf16[1024,2048]{1,0:T(8,128)(2,1)}, u32[]{:S(2)}, u32[]{:S(2)}) collective-permute-start(bf16[1024,2048]{1,0:T(8,128)(2,1)} %get-tuple-element.410), channel_id=1, source_target_pairs={{0,1},{1,0},{2,3},{3,2},{4,5},{5,4},{6,7},{7,6},{8,9},{9,8},{10,11... | collective-permute-start | bytes 12582920 | tf_op jit(solution)/shard_map/ppermute | solution.py:598
  447.6 24.4 %collective-permute-start.58 = (bf16[256,2048]{1,0:T(8,128)(2,1)}, bf16[256,2048]{1,0:T(8,128)(2,1)}, u32[]{:S(2)}, u32[]{:S(2)}) collective-permute-start(bf16[256,2048]{1,0:T(8,128)(2,1)} %pad_maximum_fusion.6), channel_id=1, source_target_pairs={{0,2},{2,0},{4,6},{6,4},{8,10},{10,8},{12,14},{14,12},{16,18},{18,... | collective-permute-start | bytes 3145736 | tf_op jit(solution)/shard_map/ppermute | solution.py:610
  449.5 24.1 %collective-permute-start.59 = (bf16[256,2048]{1,0:T(8,128)(2,1)}, bf16[256,2048]{1,0:T(8,128)(2,1)}, u32[]{:S(2)}, u32[]{:S(2)}) collective-permute-start(bf16[256,2048]{1,0:T(8,128)(2,1)} %pad_maximum_fusion.7), channel_id=1, source_target_pairs={{0,4},{2,6},{4,0},{6,2},{8,12},{10,14},{12,8},{14,10},{16,20},{18,... | collective-permute-start | bytes 3145736 | tf_op jit(solution)/shard_map/ppermute | solution.py:610
  453.9 34.1 %collective-permute-start.61 = (bf16[512,1536]{1,0:T(8,128)(2,1)S(1)}, bf16[512,1536]{1,0:T(8,128)(2,1)}, u32[]{:S(2)}, u32[]{:S(2)}) collective-permute-start(bf16[512,1536]{1,0:T(8,128)(2,1)S(1)} %get-tuple-element.425), channel_id=1, source_target_pairs={{0,8},{2,10},{4,12},{6,14},{8,16},{10,18},{12,20},{14,22},{16,24},... | collective-permute-start | bytes 4718600 | tf_op jit(solution)/shard_map/ppermute | solution.py:618
  456.3 36.9 %collective-permute-start.62 = (bf16[512,1536]{1,0:T(8,128)(2,1)}, bf16[512,1536]{1,0:T(8,128)(2,1)}, u32[]{:S(2)}, u32[]{:S(2)}) collective-permute-start(bf16[512,1536]{1,0:T(8,128)(2,1)} %get-tuple-element.426), channel_id=1, source_target_pairs={{8,0},{10,2},{12,4},{14,6},{16,8},{18,10},{20,12},{22,14},{24,16},... | collective-permute-start | bytes 4718600 | tf_op jit(solution)/shard_map/ppermute | solution.py:618
  478.2 46.6 %collective-permute-start.69 = (bf16[512,1536]{1,0:T(8,128)(2,1)S(1)}, bf16[512,1536]{1,0:T(8,128)(2,1)S(1)}, u32[]{:S(2)}, u32[]{:S(2)}) collective-permute-start(bf16[512,1536]{1,0:T(8,128)(2,1)S(1)} %copy-done.29), channel_id=1, source_target_pairs={{0,8},{2,10},{4,12},{6,14},{1,9},{3,11},{5,13},{7,15}} | collective-permute-start | bytes 4718600 | tf_op jit(solution)/shard_map/ppermute | solution.py:618
  488.0 38.0 %collective-permute-start.70 = (bf16[512,1536]{1,0:T(8,128)(2,1)S(1)}, bf16[512,1536]{1,0:T(8,128)(2,1)}, u32[]{:S(2)}, u32[]{:S(2)}) collective-permute-start(bf16[512,1536]{1,0:T(8,128)(2,1)S(1)} %copy-done.28), channel_id=1, source_target_pairs={{24,16},{26,18},{28,20},{30,22},{25,17},{27,19},{29,21},{31,23}} | collective-permute-start | bytes 4718600 | tf_op jit(solution)/shard_map/ppermute | solution.py:618
  497.3 23.8 %collective-permute-start.66 = (bf16[256,2048]{1,0:T(8,128)(2,1)S(1)}, bf16[256,2048]{1,0:T(8,128)(2,1)S(1)}, u32[]{:S(2)}, u32[]{:S(2)}) collective-permute-start(bf16[256,2048]{1,0:T(8,128)(2,1)S(1)} %get-tuple-element.527), channel_id=1, source_target_pairs={{0,4},{2,6},{4,0},{6,2},{8,12},{10,14},{12,8},{14,10},{16,20},{18,... | collective-permute-start | bytes 3145736 | tf_op jit(solution)/shard_map/ppermute | solution.py:610
  539.1 43.2 %collective-permute-start.72 = (bf16[256,2048]{1,0:T(8,128)(2,1)}, bf16[256,2048]{1,0:T(8,128)(2,1)}, u32[]{:S(2)}, u32[]{:S(2)}) collective-permute-start(bf16[256,2048]{1,0:T(8,128)(2,1)} %pad_maximum_fusion.8), channel_id=1, source_target_pairs={{0,2},{2,0},{4,6},{6,4},{8,10},{10,8},{12,14},{14,12},{16,18},{18,... | collective-permute-start | bytes 3145736 | tf_op jit(solution)/shard_map/ppermute | solution.py:610
  539.9 42.4 %collective-permute-start.73 = (bf16[256,2048]{1,0:T(8,128)(2,1)}, bf16[256,2048]{1,0:T(8,128)(2,1)}, u32[]{:S(2)}, u32[]{:S(2)}) collective-permute-start(bf16[256,2048]{1,0:T(8,128)(2,1)} %pad_maximum_fusion.9), channel_id=1, source_target_pairs={{0,4},{2,6},{4,0},{6,2},{8,12},{10,14},{12,8},{14,10},{16,20},{18,... | collective-permute-start | bytes 3145736 | tf_op jit(solution)/shard_map/ppermute | solution.py:610
  540.2 42.1 %collective-permute-start.74 = (bf16[512,1536]{1,0:T(8,128)(2,1)S(1)}, bf16[512,1536]{1,0:T(8,128)(2,1)S(1)}, u32[]{:S(2)}, u32[]{:S(2)}) collective-permute-start(bf16[512,1536]{1,0:T(8,128)(2,1)S(1)} %get-tuple-element.452), channel_id=1, source_target_pairs={{0,8},{2,10},{4,12},{6,14},{8,16},{10,18},{12,20},{14,22},{1,9},{3... | collective-permute-start | bytes 4718600 | tf_op jit(solution)/shard_map/ppermute | solution.py:618
  541.6 41.6 %collective-permute-start.75 = (bf16[512,1536]{1,0:T(8,128)(2,1)}, bf16[512,1536]{1,0:T(8,128)(2,1)}, u32[]{:S(2)}, u32[]{:S(2)}) collective-permute-start(bf16[512,1536]{1,0:T(8,128)(2,1)} %get-tuple-element.453), channel_id=1, source_target_pairs={{16,8},{18,10},{20,12},{22,14},{24,16},{26,18},{28,20},{30,22},{17... | collective-permute-start | bytes 4718600 | tf_op jit(solution)/shard_map/ppermute | solution.py:618
  545.9 36.4 %collective-permute-start.76 = (bf16[256,1536]{1,0:T(8,128)(2,1)}, bf16[256,1536]{1,0:T(8,128)(2,1)S(1)}, u32[]{:S(2)}, u32[]{:S(2)}) collective-permute-start(bf16[256,1536]{1,0:T(8,128)(2,1)} %pad_maximum_fusion.14), channel_id=1, source_target_pairs={{0,2},{2,0},{4,6},{6,4},{8,10},{10,8},{12,14},{14,12},{16,18},{18,... | collective-permute-start | bytes 2359304 | tf_op jit(solution)/shard_map/ppermute | solution.py:610
  584.4 25.4 %collective-permute-start.77 = (bf16[1024,2048]{1,0:T(8,128)(2,1)}, bf16[1024,2048]{1,0:T(8,128)(2,1)}, u32[]{:S(2)}, u32[]{:S(2)}) collective-permute-start(bf16[1024,2048]{1,0:T(8,128)(2,1)} %get-tuple-element.459), channel_id=1, source_target_pairs={{0,1},{1,0},{2,3},{3,2},{4,5},{5,4},{6,7},{7,6},{8,9},{9,8},{10,11... | collective-permute-start | bytes 12582920 | tf_op jit(solution)/shard_map/ppermute | solution.py:598
  589.2 35.7 %collective-permute-start.80 = (bf16[512,1536]{1,0:T(8,128)(2,1)}, bf16[512,1536]{1,0:T(8,128)(2,1)}, u32[]{:S(2)}, u32[]{:S(2)}) collective-permute-start(bf16[512,1536]{1,0:T(8,128)(2,1)} %get-tuple-element.462), channel_id=1, source_target_pairs={{0,8},{2,10},{4,12},{6,14},{8,16},{10,18},{12,20},{14,22},{16,24},... | collective-permute-start | bytes 4718600 | tf_op jit(solution)/shard_map/ppermute | solution.py:618
  591.8 38.0 %collective-permute-start.81 = (bf16[512,1536]{1,0:T(8,128)(2,1)}, bf16[512,1536]{1,0:T(8,128)(2,1)}, u32[]{:S(2)}, u32[]{:S(2)}) collective-permute-start(bf16[512,1536]{1,0:T(8,128)(2,1)} %get-tuple-element.463), channel_id=1, source_target_pairs={{8,0},{10,2},{12,4},{14,6},{16,8},{18,10},{20,12},{22,14},{24,16},... | collective-permute-start | bytes 4718600 | tf_op jit(solution)/shard_map/ppermute | solution.py:618
  594.3 23.5 %collective-permute-start.82 = (bf16[256,1536]{1,0:T(8,128)(2,1)}, bf16[256,1536]{1,0:T(8,128)(2,1)}, u32[]{:S(2)}, u32[]{:S(2)}) collective-permute-start(bf16[256,1536]{1,0:T(8,128)(2,1)} %pad_maximum_fusion.15), channel_id=1, source_target_pairs={{0,4},{2,6},{4,0},{6,2},{8,12},{10,14},{12,8},{14,10},{16,20},{18,... | collective-permute-start | bytes 2359304 | tf_op jit(solution)/shard_map/ppermute | solution.py:610
  617.8 38.9 %collective-permute-start.89 = (f32[256,2048]{1,0:T(8,128)S(1)}, f32[256,2048]{1,0:T(8,128)}, u32[]{:S(2)}, u32[]{:S(2)}) collective-permute-start(f32[256,2048]{1,0:T(8,128)S(1)} %add_add_fusion.mine), channel_id=1, source_target_pairs={{0,1},{1,0},{2,3},{3,2},{4,5},{5,4},{6,7},{7,6},{8,9},{9,8},{10,11... | collective-permute-start | bytes 6291464 | tf_op jit(solution)/shard_map/ppermute | solution.py:598
  631.0 28.9 %collective-permute-start.83 = (bf16[256,2048]{1,0:T(8,128)(2,1)}, bf16[256,2048]{1,0:T(8,128)(2,1)S(1)}, u32[]{:S(2)}, u32[]{:S(2)}) collective-permute-start(bf16[256,2048]{1,0:T(8,128)(2,1)} %pad_maximum_fusion.10), channel_id=1, source_target_pairs={{0,2},{2,0},{4,6},{6,4},{8,10},{10,8},{12,14},{14,12},{16,18},{18,... | collective-permute-start | bytes 3145736 | tf_op jit(solution)/shard_map/ppermute | solution.py:610
  637.2 23.2 %collective-permute-start.84 = (bf16[256,2048]{1,0:T(8,128)(2,1)}, bf16[256,2048]{1,0:T(8,128)(2,1)S(1)}, u32[]{:S(2)}, u32[]{:S(2)}) collective-permute-start(bf16[256,2048]{1,0:T(8,128)(2,1)} %pad_maximum_fusion.11), channel_id=1, source_target_pairs={{0,4},{2,6},{4,0},{6,2},{8,12},{10,14},{12,8},{14,10},{16,20},{18,... | collective-permute-start | bytes 3145736 | tf_op jit(solution)/shard_map/ppermute | solution.py:610
  667.9 24.0 %collective-permute-start.91 = (bf16[512,640]{1,0:T(8,128)(2,1)S(1)}, bf16[512,640]{1,0:T(8,128)(2,1)S(1)}, u32[]{:S(2)}, u32[]{:S(2)}) collective-permute-start(bf16[512,640]{1,0:T(8,128)(2,1)S(1)} %get-tuple-element.491), channel_id=1, source_target_pairs={{0,8},{2,10},{4,12},{6,14},{8,16},{10,18},{12,20},{14,22},{16,24},... | collective-permute-start | bytes 1966088 | tf_op jit(solution)/shard_map/ppermute | solution.py:618
  697.3 25.8 %collective-permute-start.97 = (f32[256,2048]{1,0:T(8,128)S(1)}, f32[256,2048]{1,0:T(8,128)S(1)}, u32[]{:S(2)}, u32[]{:S(2)}) collective-permute-start(f32[256,2048]{1,0:T(8,128)S(1)} %fusion.5.mine), channel_id=1, source_target_pairs={{0,1},{1,0},{2,3},{3,2},{4,5},{5,4},{6,7},{7,6},{8,9},{9,8},{10,11... | collective-permute-start | bytes 6291464 | tf_op jit(solution)/shard_map/ppermute | solution.py:598
  (141 other events, 1448.1 us)

commit v5 on v4

--- a/solution.py
+++ b/solution.py
@@ -355,7 +355,7 @@
     normed, out = refs[0:2], refs[2:4]
     blocks, refs = refs[4 : 4 + count], refs[4 + count :]
     if earlier:
-        before, before_blocks, refs = refs[0:2], refs[2 : 2 + count], refs[2 + count :]
+        before, refs = refs[0:2], refs[2:]
     inner_refs, grad_refs, terms = refs[0:2], refs[2:4], refs[4:6]
     tile = normed[0].shape[0]
     gate_up = block_product(normed[0], normed[1], blocks, 0, 2 * ff_sub)
@@ -374,17 +374,17 @@
     if not earlier:
         return
     here = jnp.concatenate([gate_grad, up_grad], axis=1)
-    there = jnp.concatenate([before[0][...], before[1][...]], axis=0)
     rows = blocks[0].shape[0]
     for k in range(count):
         span = slice(k * rows, (k + 1) * rows)
-        total = dot_nt(here, blocks[k][:, : 2 * ff_sub]) + dot_nt(there, before_blocks[k][...])
-        total = total.astype(jnp.bfloat16)
-        terms[0][:, span] = total[:tile]
-        terms[1][:, span] = total[tile:]
-
-
-def run_ffn_units(normed, out, blocks, ff_sub, before=None, before_blocks=()):
+        total = dot_nt(here, blocks[k][:, : 2 * ff_sub])
+        for side in range(2):
+            part = total[side * tile : (side + 1) * tile]
+            part = part + before[side][:, span].astype(jnp.float32)
+            terms[side][:, span] = part.astype(jnp.bfloat16)
+
+
+def run_ffn_units(normed, out, blocks, ff_sub, before=None):
     tokens, model = normed[0].shape
     tile = min(256, tokens)
     rows = lambda n: pl.BlockSpec((tile, n), lambda i: (i, 0))
@@ -395,13 +395,12 @@
         (tokens // tile,),
         [rows(model)] * 4
         + [whole(b) for b in blocks]
-        + [rows(2 * ff_sub)] * 2 * earlier
-        + [pl.BlockSpec((b.shape[0], 2 * ff_sub), lambda i: (0, 0)) for b in before_blocks],
+        + [rows(model)] * 2 * earlier,
         [rows(n) for n in shapes],
         [shape_of((tokens, n), jnp.bfloat16) for n in shapes],
         12 * tokens * model * ff_sub,
         8 * tokens * model,
-    )(*normed, *out, *blocks, *(before if earlier else ()), *before_blocks)
+    )(*normed, *out, *blocks, *(before if earlier else ()))
 
 
 def weight_gradients(count, per, *refs):
@@ -515,26 +514,32 @@
     )(*lefts, *flat)
 
 
-def add_both(*refs):
-    for left, right, out in zip(refs[0:2], refs[2:4], refs[4:6]):
-        out[...] = (left[...].astype(jnp.float32) + right[...].astype(jnp.float32)).astype(
-            jnp.bfloat16
-        )
-
-
-def run_add_both(blocks, got):
-    rows, width = blocks[0].shape
+def add_three(first, second, third, out):
+    total = first[...].astype(jnp.float32) + second[...].astype(jnp.float32)
+    out[...] = (total + third[...].astype(jnp.float32)).astype(jnp.bfloat16)
+
+
+def add_swapped(odd_ref, one, two, first, second, out_first, out_second):
+    odd = odd_ref[...] == 1
+    for left, right, got, out in ((one, two, first, out_first), (two, one, second, out_second)):
+        here = jnp.where(odd, right[...].astype(jnp.float32), left[...].astype(jnp.float32))
+        out[...] = (here + got[...].astype(jnp.float32)).astype(jnp.bfloat16)
+
+
+def run_add(body, arrays, outs, flag=None):
+    rows, width = arrays[0].shape
     tile = min(256, rows)
     spec = pl.BlockSpec((tile, width), lambda i: (i, 0))
+    flags = [] if flag is None else [flag]
     return kernel_call(
-        add_both,
+        body,
         (rows // tile,),
-        [spec] * 4,
-        [spec] * 2,
-        [shape_of((rows, width), jnp.bfloat16)] * 2,
+        [whole(f) for f in flags] + [spec] * len(arrays),
+        [spec] * outs,
+        [shape_of((rows, width), jnp.bfloat16)] * outs,
         1,
         12 * rows * width,
-    )(*blocks, *got)
+    )(*flags, *arrays)
 
 
 def place_columns(subs, place_ref, *refs):
@@ -598,6 +603,12 @@
     return lax.ppermute(values, "tensor", [(0, 1), (1, 0)])
 
 
+sides = ((0, 1), (1, 0), (2, 3), (3, 2))
+middle = ((1, 2), (2, 1))
+outward = ((2, 3), (1, 0))
+inward = ((0, 1), (3, 2))
+
+
 class Lines:
     def __init__(self, dp):
         self.dp = dp
@@ -609,10 +620,10 @@
     def flip(self, values, relation):
         return lax.ppermute(values, "dp", [(i, i ^ relation) for i in range(self.dp)])
 
-    def hop(self, values, first, last, step):
+    def ends(self, values, moves):
         pairs = [
-            (spot * group + place, (spot + step) * group + place)
-            for spot in range(first, last + 1)
+            (one * group + place, two * group + place)
+            for one, two in moves
             for place in range(group)
         ]
         return lax.ppermute(values, "dp", pairs)
@@ -723,26 +734,25 @@
         if lines.length != 4:
             turns = range(1, lines.length) if step == 1 else ()
             self.got.append([lines.turn(self.block, -k) for k in turns])
-            return
-        up, down = self.got[-1] if self.got else (self.block, self.block)
-        self.got.append(
-            [
-                lines.hop(up, step - 1, lines.length - 2, 1),
-                lines.hop(down, 1, lines.length - step, -1),
-            ]
-        )
+        elif step == 1:
+            self.got.append([lines.ends(self.block, sides), lines.ends(self.block, middle)])
+        elif step == 2:
+            outer, inner = self.got[0]
+            self.got.append([lines.ends(outer, middle), lines.ends(inner, outward)])
+        else:
+            self.got.append([lines.ends(self.got[1][0], outward)])
 
     def blocks(self):
         lines = self.lines
         if lines.length != 4:
             return [self.block] + self.got[0]
-        return [self.block] + [
-            jnp.where(
-                lines.spot + k < lines.length,
-                self.got[k - 1][1],
-                self.got[lines.length - k - 1][0],
-            )
-            for k in range(1, lines.length)
+        (outer, inner), (inner_two, outer_two), (outer_three,) = self.got
+        spot = lines.spot
+        return [
+            self.block,
+            jnp.where(spot == 3, outer_three, jnp.where(spot == 1, inner, outer)),
+            jnp.where((spot == 1) | (spot == 2), inner_two, outer_two),
+            jnp.where(spot == 0, outer_three, jnp.where(spot == 2, inner, outer)),
         ]
 
 
@@ -754,8 +764,12 @@
         step = len(self.got) + 1
         if self.lines.length != 4:
             return []
-        blocks = [self.blocks[self.lines.length - step], self.blocks[step]]
-        return run_add_both(blocks, self.got[-1]) if self.got else blocks
+        if step == 1:
+            return [self.blocks[3], self.blocks[1]]
+        if step == 2:
+            return run_add(add_three, [self.blocks[2], *self.got[0]], 1)
+        odd = (self.lines.spot % 2).astype(jnp.int32).reshape(1, 1)
+        return run_add(add_swapped, [self.blocks[1], self.blocks[3], *self.got[1]], 2, odd)
 
     def hop(self, ready=None):
         lines, step = self.lines, len(self.got) + 1
@@ -763,13 +777,13 @@
             turns = range(1, lines.length) if step == 1 else ()
             self.got.append([lines.turn(self.blocks[k], k) for k in turns])
             return
-        up, down = self.ready() if ready is None else ready
-        self.got.append(
-            [
-                lines.hop(up, 0, min(step - 1, lines.length - 2), 1),
-                lines.hop(down, max(lines.length - step, 1), lines.length - 1, -1),
-            ]
-        )
+        ready = self.ready() if ready is None else ready
+        if step == 1:
+            self.got.append([lines.ends(ready[0], ((0, 1),)), lines.ends(ready[1], ((3, 2),))])
+        elif step == 2:
+            self.got.append([lines.ends(ready[0], middle), lines.ends(ready[0], inward)])
+        else:
+            self.got.append([lines.ends(ready[0], sides), lines.ends(ready[1], middle)])
 
     def total(self):
         last = self.got[-1] if self.lines.length == 4 else self.got[0]
@@ -949,12 +963,13 @@
     units_0, line_1.got[1] = tie(units_0, line_1.got[1])
     line_1.hop()
     ffn_g = run_weight_gradients(normed2, units_0[2:], out_b, units_0[:2], lines.length)
-    ffn_g, line_1.got[2], units_0 = tie(ffn_g, line_1.got[2], units_0)
+    terms_0 = run_transposed_product([units_0[2:]], [ffn_w[0]], 0, 2 * ff_sub)
+    ffn_g, line_1.got[2], units_0, terms_0 = tie(ffn_g, line_1.got[2], units_0, terms_0)
     sum_0 = LineScatter(lines, ffn_g)
     ffn_w.append(line_1.blocks())
 
     sum_0.hop()
-    units_1 = run_ffn_units(normed2, out_b, ffn_w[1], ff_sub, units_0[2:], ffn_w[0])
+    units_1 = run_ffn_units(normed2, out_b, ffn_w[1], ff_sub, terms_0)
     kept, other = units_1[4:]
     kept, other, sum_0.got[0], units_1 = tie(kept, other, sum_0.got[0], units_1)
 
@@ -1022,43 +1037,38 @@
     )
     other = swap_cores(other)
     back_0_second = lines.flip_second(back_0, back_0_first)
-    got = lines.across_terms(kept, other)
     attn_sum = LineScatter(
         lines, run_weight_gradients(normed, qkv_grad, attended_b, heads_out, lines.length)
     )
-    got, sum_1.got[2], attn_sum.blocks, back_0_second, gains = tie(
-        got, sum_1.got[2], attn_sum.blocks, back_0_second, gains
-    )
+    other, attn_sum.blocks = tie(other, attn_sum.blocks)
+    got = lines.across_terms(kept, other)
+    got, sum_1.got[2], back_0_second, branch = tie(got, sum_1.got[2], back_0_second, branch)
     attn_sum.hop()
+    mixed = state + lines.near_sum(branch_kept, branch_other, branch)
+    mixed_other = swap_cores(mixed)
     back_1 = lines.row_pieces(sum_1.total())
     near = lines.near_flips(kept, other, got)
     attn_sum.hop()
-    gains_got = lines.flip(gains, 1)
-    mixed = state + lines.near_sum(branch_kept, branch_other, branch)
-    mixed_other = swap_cores(mixed)
-    near, attn_sum.got[1], back_1, mixed, mixed_other, gains_got = tie(
-        near, attn_sum.got[1], back_1, mixed, mixed_other, gains_got
-    )
-    attn_sum.hop()
+    near, attn_sum.got[1], back_1, mixed, mixed_other = tie(
+        near, attn_sum.got[1], back_1, mixed, mixed_other
+    )
+    ready = attn_sum.ready()
+    near, ready = tie(near, ready)
+    attn_sum.hop(ready)
     back_1 = lines.flip_pieces(back_1)
-    gains = gains + gains_got
-    gains_got = lines.flip(gains, 2)
-    mixed = run_place_halves(core, lines.spot, lines.length, mixed, mixed_other)
-    attn_sum.got[2], back_1, near, gains, gains_got, mixed = tie(
-        attn_sum.got[2], back_1, near, gains, gains_got, mixed
-    )
-    gains = gains + gains_got
-    attn_grads = lines.flip_pieces(lines.row_pieces(attn_sum.total()))
     normed_grad = lines.near_sum(kept, other, near)
     input_grad = state_grad + norm_back(source, scale_first, attn_gain_r, normed_grad)
+    mixed = run_place_halves(core, lines.spot, lines.length, mixed, mixed_other)
+    attn_sum.got[2], back_1, input_grad, gains, mixed = tie(
+        attn_sum.got[2], back_1, input_grad, gains, mixed
+    )
+    gains_got = [lines.flip(gains, r) for r in range(1, group)]
+    attn_send = lines.row_pieces(attn_sum.total())
+    attn_grads = lines.flip_pieces(attn_send)
     input_other = swap_cores(input_grad)
-    bit = group
-    while bit < dp:
-        gains = gains + lines.flip(gains, bit)
-        bit *= 2
-        if bit == 2 * group:
-            gains, attn_grads = tie(gains, attn_grads)
-    gains = gains + swap_cores(gains)
+    gains_got, input_other = tie(gains_got, input_other)
+    gains = gains + gains_got[0] + gains_got[1] + gains_got[2]
+    gains_got = [lines.turn(gains, k) for k in range(1, lines.length)]
     ffn_grads = run_place_columns(
         lines.place,
         [
@@ -1067,6 +1077,11 @@
         ],
         3,
     )
+    input_grad = run_place_halves(core, lines.spot, lines.length, input_grad, input_other)
+    gains_got, attn_grads, input_grad = tie(gains_got, attn_grads, input_grad)
+    for one in gains_got:
+        gains = gains + one
+    gains = gains + swap_cores(gains)
 
     def columns_of(related, start, stop):
         blocks = lines.by_place([b[:, start:stop] for b in related])
@@ -1074,7 +1089,7 @@
 
     return (
         mixed,
-        run_place_halves(core, lines.spot, lines.length, input_grad, input_other),
+        input_grad,
         gains[:width],
         gains[width : 2 * width],
         gains[2 * width : 2 * width + head_dim],

time: 739 us -> 710 us (0.961)
  waiting for transfers between devices: 220 us -> 194 us
    ppermute x36, waiting for transfers between devices: 104 us -> 70.4 us  [the longest x33 70.4 us: ends(): return lax.ppermute(values, 'dp', pairs)]
    pallas_call x1 -> x2, Pallas kernels: 13.4 us -> 26.4 us  [run_transposed_product(): kernel_call(functools.partial(transposed_product, len(pairs), count), (to...]
    pallas_call x2, Pallas kernels: 59.7 us -> 49.7 us  [run_ffn_units(): kernel_call(functools.partial(ffn_units, len(blocks), ff_sub, earlier), (...]
    ppermute x54 -> x53, waiting for transfers between devices: 111 us -> 120 us  [flip(): lax.ppermute(values, 'dp', [(i, i ^ relation) for i in range(self.dp)])]
    unnamed x182 -> x168, local copies, waits for them, and re-layouts: 23.6 us -> 18.5 us
    select_n x9 -> x6, other arithmetic: 14.9 us -> 16.3 us  [the longest x3 10.1 us: blocks(): jnp.where(spot == 0, outer_three, jnp.where(spot == 2, inner, outer))]
    ppermute x54 -> x53, starting transfers between devices: 48.2 us -> 47.5 us  [flip(): lax.ppermute(values, 'dp', [(i, i ^ relation) for i in range(self.dp)])]
  transfers between devices with their start and end apart: 104 -> 103, of which waited for: 40 -> 34; matrix products, arithmetic and copies ran while one was open for 14% -> 15% of each run, Pallas kernels for 30% -> 32%
where the time goes in v5:
time: 710 us; the launch traced here: 703 us
  Pallas kernels  226 us (32%)
  waiting for transfers between devices  194 us (27%)
  starting transfers between devices  151 us (21%)
  other arithmetic  90.5 us (13%)
  local copies, waits for them, and re-layouts  37.8 us (5%)
    ppermute x53, waiting for transfers between devices, flip(): lax.ppermute(values, 'dp', [(i, i ^ relation) for i in range(self.dp)])  120 us
    ppermute x33, waiting for transfers between devices, ends(): return lax.ppermute(values, 'dp', pairs)  70.4 us
    ppermute x33, starting transfers between devices, ends(): return lax.ppermute(values, 'dp', pairs)  64.4 us
    pallas_call x2, Pallas kernels, run_ffn_units(): kernel_call(functools.partial(ffn_units, len(blocks), ff_sub, earlier), (...  49.7 us
    ppermute x53, starting transfers between devices, flip(): lax.ppermute(values, 'dp', [(i, i ^ relation) for i in range(self.dp)])  47.5 us
    ppermute x14, starting transfers between devices, swap_cores(): return lax.ppermute(values, 'tensor', [(0, 1), (1, 0)])  35.2 us
    pallas_call x2, Pallas kernels, run_weight_gradients(): kernel_call(functools.partial(weight_gradients, count, per), (model // ti...  34.7 us
    pallas_call x1, Pallas kernels, run_attention(): kernel_call(functools.partial(attention_backward, len(blocks), head_dim,...  34.2 us
  transfers between devices with their start and end apart: 103, of which 34 were waited for; matrix products, arithmetic and copies ran while one was open for 15% of the time, Pallas kernels for 32%

profile of v5, /device:TPU:1, one launch (start us, length us, event | category | flops | bytes accessed | tf_op | source)
XLA Modules:
  0.0 702.6 jit_solution(1945721591604498790)
XLA Ops:
  20.8 3.6 collective-permute-start.9
  26.3 5.6 multiply_sine_fusion
  31.9 5.6 collective-permute-done.5
  38.3 3.8 collective-permute-start.14
  60.9 7.3 %collective-permute-done.13 = bf16[512,640]{1,0:T(8,128)(2,1)} collective-permute-done((bf16[512,640]{1,0:T(8,128)(2,1)}, bf16[512,640]{1,0:T(8,128)(2,1)}, u32[]{:S(2)}, u32[]{:S(2)}) %collective-permute-start.13) | collective-permute-done | bytes 655392 | tf_op jit(solution)/shard_map/ppermute | solution.py:629
  79.3 3.6 pad_maximum_fusion.refs_1_.refs_4_
  84.6 7.0 %collective-permute-done.20 = bf16[128,1536]{1,0:T(8,128)(2,1)S(1)} collective-permute-done((bf16[128,1536]{1,0:T(8,128)(2,1)S(1)}, bf16[128,1536]{1,0:T(8,128)(2,1)S(1)}, u32[]{:S(2)}, u32[]{:S(2)}) %collective-permute-start.20) | collective-permute-done | bytes 393248 | tf_op jit(solution)/shard_map/ppermute | solution.py:621
  100.6 20.9 %shard_map.237 = (f32[4,512,384]{2,1,0:T(8,128)}, bf16[1024,256]{1,0:T(8,128)(2,1)S(1)}, bf16[1024,256]{1,0:T(8,128)(2,1)S(1)}, bf16[1024,2048]{1,0:T(8,128)(2,1)}, bf16[1024,2048]{1,0:T(8,128)(2,1)}) custom-call(bf16[1024,2048]{1,0:T(8,128)(2,1)} %constant_dynamic-update-slice_fusion.refs_0_.refs_3_, bf16[1024,2048]{1,0:T(8,128)(2,1)} %pad_maximum_fusion.refs_1_.refs_4_, ...), custom_call_target="tpu_custom_call" | custom-call | flops 32212254720 | bytes 33554432 | tf_op jit(solution)/shard_map/pallas_call | solution.py:328
  121.5 4.6 collective-permute-done.21
  133.7 9.2 %collective-permute-done.26 = bf16[128,2048]{1,0:T(8,128)(2,1)S(1)} collective-permute-done((bf16[128,2048]{1,0:T(8,128)(2,1)S(1)}, bf16[128,2048]{1,0:T(8,128)(2,1)S(1)}, u32[]{:S(2)}, u32[]{:S(2)}) %collective-permute-start.26) | collective-permute-done | bytes 524320 | tf_op jit(solution)/shard_map/ppermute | solution.py:621
  149.5 24.3 %collective-permute-done.31 = bf16[512,1536]{1,0:T(8,128)(2,1)S(1)} collective-permute-done((bf16[512,1536]{1,0:T(8,128)(2,1)}, bf16[512,1536]{1,0:T(8,128)(2,1)S(1)}, u32[]{:S(2)}, u32[]{:S(2)}) %collective-permute-start.31) | collective-permute-done | bytes 1572896 | tf_op jit(solution)/shard_map/ppermute | solution.py:629
  177.8 19.5 %collective-permute-done.33 = bf16[256,2048]{1,0:T(8,128)(2,1)S(1)} collective-permute-done((bf16[256,2048]{1,0:T(8,128)(2,1)S(1)}, bf16[256,2048]{1,0:T(8,128)(2,1)S(1)}, u32[]{:S(2)}, u32[]{:S(2)}) %collective-permute-start.33) | collective-permute-done | bytes 1048608 | tf_op jit(solution)/shard_map/ppermute | solution.py:621
  200.4 13.8 %collective-permute-done.36 = bf16[256,1536]{1,0:T(8,128)(2,1)S(1)} collective-permute-done((bf16[256,1536]{1,0:T(8,128)(2,1)S(1)}, bf16[256,1536]{1,0:T(8,128)(2,1)S(1)}, u32[]{:S(2)}, u32[]{:S(2)}) %collective-permute-start.36) | collective-permute-done | bytes 786464 | tf_op jit(solution)/shard_map/ppermute | solution.py:621
  222.8 19.0 %collective-permute-done.37 = bf16[256,2048]{1,0:T(8,128)(2,1)S(1)} collective-permute-done((bf16[256,2048]{1,0:T(8,128)(2,1)S(1)}, bf16[256,2048]{1,0:T(8,128)(2,1)S(1)}, u32[]{:S(2)}, u32[]{:S(2)}) %collective-permute-start.37) | collective-permute-done | bytes 1048608 | tf_op jit(solution)/shard_map/ppermute | solution.py:621
  243.0 3.8 select_select_fusion.2
  246.8 6.2 collective-permute-done.39
  261.3 4.4 collective-permute-done.44.refs_1_
  265.7 19.5 %shard_map.238 = (bf16[1024,512]{1,0:T(8,128)(2,1)S(1)}, bf16[1024,512]{1,0:T(8,128)(2,1)}, bf16[1024,1024]{1,0:T(8,128)(2,1)}, bf16[1024,1024]{1,0:T(8,128)(2,1)}) custom-call(bf16[1024,2048]{1,0:T(8,128)(2,1)} %copy-done.20, bf16[1024,2048]{1,0:T(8,128)(2,1)} %collective-permute-done.44.refs_1_, bf16[1024,2048]{1,0:T(8,128)(2,1)} %copy-done.21, ...), custom_call_target="tpu_custom_call" | custom-call | flops 12884901888 | bytes 16777216 | tf_op jit(solution)/shard_map/pallas_call | solution.py:393
  285.2 14.5 %collective-permute-done.46 = bf16[512,1536]{1,0:T(8,128)(2,1)} collective-permute-done((bf16[512,1536]{1,0:T(8,128)(2,1)}, bf16[512,1536]{1,0:T(8,128)(2,1)}, u32[]{:S(2)}, u32[]{:S(2)}) %collective-permute-start.46) | collective-permute-done | bytes 1572896 | tf_op jit(solution)/shard_map/ppermute | solution.py:629
  301.0 13.0 %shard_map.240 = (bf16[1024,2048]{1,0:T(8,128)(2,1)}, bf16[1024,2048]{1,0:T(8,128)(2,1)}) custom-call(bf16[1024,1024]{1,0:T(8,128)(2,1)} %get-tuple-element.361.refs_4_.refs_0_, bf16[1024,1024]{1,0:T(8,128)(2,1)} %get-tuple-element.362.refs_5_.refs_1_, bf16[512,1536]{1,0:T(8,128)(2,1)S(1)} %copy-done.3, ...), custom_call_target="tpu_custom_call" | custom-call | flops 1073741824 | bytes 2097152 | tf_op jit(solution)/shard_map/pallas_call | solution.py:505
  314.0 21.0 %shard_map.239 = (bf16[512,1536]{1,0:T(8,128)(2,1)}, bf16[512,1536]{1,0:T(8,128)(2,1)}, bf16[512,1536]{1,0:T(8,128)(2,1)}, bf16[512,1536]{1,0:T(8,128)(2,1)}) custom-call(bf16[1024,2048]{1,0:T(8,128)(2,1)} %copy-done.20, bf16[1024,2048]{1,0:T(8,128)(2,1)} %collective-permute-done.44.refs_1_, bf16[1024,2048]{1,0:T(8,128)(2,1)} %copy-done.21, ...), custom_call_target="tpu_custom_call" | custom-call | flops 1073741824 | bytes 2097152 | tf_op jit(solution)/shard_map/pallas_call | solution.py:431
  338.0 3.2 collective-permute-start.48
  343.0 3.7 select_select_fusion
  346.8 30.1 %shard_map.241 = (bf16[1024,512]{1,0:T(8,128)(2,1)S(1)}, bf16[1024,512]{1,0:T(8,128)(2,1)}, bf16[1024,1024]{1,0:T(8,128)(2,1)}, bf16[1024,1024]{1,0:T(8,128)(2,1...) custom-call(bf16[1024,2048]{1,0:T(8,128)(2,1)} %copy-done.20, ...), custom_call_target="tpu_custom_call" | custom-call | flops 12884901888 | bytes 16777216 | tf_op jit(solution)/shard_map/pallas_call | solution.py:393
  384.1 3.9 collective-permute-start.54
  388.0 4.1 convert_add_fusion.6
  395.2 15.1 %shard_map.243 = (bf16[512,1536]{1,0:T(8,128)(2,1)S(1)}, bf16[512,1536]{1,0:T(8,128)(2,1)}, bf16[512,1536]{1,0:T(8,128)(2,1)}, bf16[512,1536]{1,0:T(8,128)(2,1)}) custom-call(bf16[1024,2048]{1,0:T(8,128)(2,1)} %copy-done.20, bf16[1024,2048]{1,0:T(8,128)(2,1)} %collective-permute-done.44.refs_1_, bf16[1024,1024]{1,0:T(8,128)(2,1)} %get-tuple-element.394.refs_2_, ...), custom_call_target="tpu_custom_call" | custom-call | flops 536870912 | bytes 1048576 | tf_op jit(solution)/shard_map/pallas_call | solution.py:463
  411.5 13.3 %shard_map.244 = (bf16[1024,2048]{1,0:T(8,128)(2,1)}, bf16[1024,2048]{1,0:T(8,128)(2,1)}) custom-call(bf16[1024,512]{1,0:T(8,128)(2,1)S(1)} %get-tuple-element.400.refs_6_.refs_0_, bf16[1024,512]{1,0:T(8,128)(2,1)} %get-tuple-element.401.refs_7_.refs_1_, bf16[1024,512]{1,0:T(8,128)(2,1)} %copy-done.6, bf16[1024,512]{1,0:T(8,128)(2,1)} %get-tuple-element.411.refs_3_, ...), custom_call_target="tpu_custom_call" | custom-call | flops 1073741824 | bytes 2097152 | tf_op jit(solution)/shard_map/pallas_call | solution.py:505
  430.3 4.9 shard_map.246
  437.0 10.9 %shard_map.245 = (bf16[512,1536]{1,0:T(8,128)(2,1)}, bf16[512,1536]{1,0:T(8,128)(2,1)}, bf16[512,1536]{1,0:T(8,128)(2,1)}, bf16[512,1536]{1,0:T(8,128)(2,1)}) custom-call(bf16[1024,2048]{1,0:T(8,128)(2,1)} %copy-done.21, bf16[1024,2048]{1,0:T(8,128)(2,1)} %copy-done.24, ...), custom_call_target="tpu_custom_call", output_to_operand_aliasing={{0}: (4, {}), {1}: (5, {}), {2}: (6, {}), {3}: (7, {})} | custom-call | flops 536870912 | bytes 1048576 | tf_op jit(solution)/shard_map/pallas_call | solution.py:463
  447.9 4.7 collective-permute-done.55
  463.1 6.7 collective-permute-done.58
  481.6 15.8 %collective-permute-done.62 = bf16[256,2048]{1,0:T(8,128)(2,1)S(1)} collective-permute-done((bf16[256,2048]{1,0:T(8,128)(2,1)S(1)}, bf16[256,2048]{1,0:T(8,128)(2,1)S(1)}, u32[]{:S(2)}, u32[]{:S(2)}) %collective-permute-start.62) | collective-permute-done | bytes 1048608 | tf_op jit(solution)/shard_map/ppermute | solution.py:621
  504.4 3.3 shard_map.247
  512.6 4.4 collective-permute-start.68
  517.8 6.6 collective-permute-start.72
  528.8 34.2 %shard_map.248 = (bf16[1024,384]{1,0:T(8,128)(2,1)}, bf16[1024,384]{1,0:T(8,128)(2,1)}, f32[2,256]{1,0:T(2,128)S(1)}, bf16[1024,2048]{1,0:T(8,128)(2,1)}, bf16[1...) custom-call(bf16[1024,2048]{1,0:T(8,128)(2,1)} %copy-done.28, bf16[1024,2048]{1,0:T(8,128)(2,1)} %copy-done.35, ...), custom_call_target="tpu_custom_call" | custom-call | flops 32212254720 | bytes 33554432 | tf_op jit(solution)/shard_map/pallas_call | solution.py:338
  568.7 4.9 shard_map.250
  576.8 13.7 %shard_map.249 = (bf16[512,640]{1,0:T(8,128)(2,1)S(1)}, bf16[512,640]{1,0:T(8,128)(2,1)}, bf16[512,640]{1,0:T(8,128)(2,1)}, bf16[512,640]{1,0:T(8,128)(2,1)}) custom-call(bf16[1024,2048]{1,0:T(8,128)(2,1)} %constant_dynamic-update-slice_fusion.refs_0_.refs_3_, bf16[1024,2048]{1,0:T(8,128)(2,1)} %pad_maximum_fusion.refs_1_.refs_4_, ...), custom_call_target="tpu_custom_call" | custom-call | flops 1073741824 | bytes 2097152 | tf_op jit(solution)/shard_map/pallas_call | solution.py:431
  590.5 5.2 convert_add_fusion.1
  602.0 4.7 collective-permute-start.82
  611.5 4.2 add_add_fusion.mine
  625.2 8.3 %collective-permute-start.85 = (bf16[512,640]{1,0:T(8,128)(2,1)S(1)}, bf16[512,640]{1,0:T(8,128)(2,1)S(1)}, u32[]{:S(2)}, u32[]{:S(2)}) collective-permute-start(bf16[512,640]{1,0:T(8,128)(2,1)S(1)} %shard_map.251), channel_id=1, source_target_pairs={{0,8},{2,10},{4,12},{6,14},{24,16},{26,18},{28,20},{30,22},{1,9},{... | collective-permute-start | bytes 1966088 | tf_op jit(solution)/shard_map/ppermute | solution.py:629
  636.2 9.6 %collective-permute-done.85.second = bf16[512,640]{1,0:T(8,128)(2,1)S(1)} collective-permute-done((bf16[512,640]{1,0:T(8,128)(2,1)S(1)}, bf16[512,640]{1,0:T(8,128)(2,1)S(1)}, u32[]{:S(2)}, u32[]{:S(2)}) %collective-permute-start.85) | collective-permute-done | bytes 655392 | tf_op jit(solution)/shard_map/ppermute | solution.py:629
  658.5 5.3 shard_map.253
  669.3 4.4 collective-permute-start.95
  684.7 4.7 shard_map.255
  689.4 5.3 shard_map.254
  (506 shorter events, 233.9 us)
Async XLA Ops:
  15.2 22.3 %collective-permute-start.5 = (bf16[256,2048]{1,0:T(8,128)(2,1)S(1)}, bf16[256,2048]{1,0:T(8,128)(2,1)}, u32[]{:S(2)}, u32[]{:S(2)}) collective-permute-start(bf16[256,2048]{1,0:T(8,128)(2,1)S(1)} %fusion.2), channel_id=1, source_target_pairs={{0,2},{2,0},{4,6},{6,4},{8,10},{10,8},{12,14},{14,12},{16,18},{18,... | collective-permute-start | bytes 3145736 | tf_op jit(solution)/shard_map/ppermute | solution.py:621
  16.5 21.8 %collective-permute-start.6 = (bf16[256,2048]{1,0:T(8,128)(2,1)S(1)}, bf16[256,2048]{1,0:T(8,128)(2,1)S(1)}, u32[]{:S(2)}, u32[]{:S(2)}) collective-permute-start(bf16[256,2048]{1,0:T(8,128)(2,1)S(1)} %fusion.2), channel_id=1, source_target_pairs={{0,4},{2,6},{4,0},{6,2},{8,12},{10,14},{12,8},{14,10},{16,20},{18,... | collective-permute-start | bytes 3145736 | tf_op jit(solution)/shard_map/ppermute | solution.py:621
  91.9 34.3 %collective-permute-start.21 = (bf16[512,1536]{1,0:T(8,128)(2,1)S(1)}, bf16[512,1536]{1,0:T(8,128)(2,1)}, u32[]{:S(2)}, u32[]{:S(2)}) collective-permute-start(bf16[512,1536]{1,0:T(8,128)(2,1)S(1)} %pad_maximum_fusion.1.refs_4_.refs_2_), channel_id=1, source_target_pairs={{0,8},{2,10},{4,12},{6,14},{8,0},{10,2},{12,4},{14,6},{16,24},{18,... | collective-permute-start | bytes 4718600 | tf_op jit(solution)/shard_map/ppermute | solution.py:629
  93.8 32.4 %collective-permute-start.22 = (bf16[512,1536]{1,0:T(8,128)(2,1)S(1)}, bf16[512,1536]{1,0:T(8,128)(2,1)}, u32[]{:S(2)}, u32[]{:S(2)}) collective-permute-start(bf16[512,1536]{1,0:T(8,128)(2,1)S(1)} %pad_maximum_fusion.1.refs_4_.refs_2_), channel_id=1, source_target_pairs={{8,16},{10,18},{12,20},{14,22},{16,8},{18,10},{20,12},{22,14},{9,1... | collective-permute-start | bytes 4718600 | tf_op jit(solution)/shard_map/ppermute | solution.py:629
  95.8 25.7 %collective-permute-start.23 = (bf16[256,2048]{1,0:T(8,128)(2,1)S(1)}, bf16[256,2048]{1,0:T(8,128)(2,1)S(1)}, u32[]{:S(2)}, u32[]{:S(2)}) collective-permute-start(bf16[256,2048]{1,0:T(8,128)(2,1)S(1)} %fusion.17), channel_id=1, source_target_pairs={{0,2},{2,0},{4,6},{6,4},{8,10},{10,8},{12,14},{14,12},{16,18},{18,... | collective-permute-start | bytes 3145736 | tf_op jit(solution)/shard_map/ppermute | solution.py:621
  96.9 24.6 %collective-permute-start.24 = (bf16[256,2048]{1,0:T(8,128)(2,1)S(1)}, bf16[256,2048]{1,0:T(8,128)(2,1)S(1)}, u32[]{:S(2)}, u32[]{:S(2)}) collective-permute-start(bf16[256,2048]{1,0:T(8,128)(2,1)S(1)} %fusion.17), channel_id=1, source_target_pairs={{0,4},{2,6},{4,0},{6,2},{8,12},{10,14},{12,8},{14,10},{16,20},{18,... | collective-permute-start | bytes 3145736 | tf_op jit(solution)/shard_map/ppermute | solution.py:621
  132.4 41.4 %collective-permute-start.31 = (bf16[512,1536]{1,0:T(8,128)(2,1)}, bf16[512,1536]{1,0:T(8,128)(2,1)S(1)}, u32[]{:S(2)}, u32[]{:S(2)}) collective-permute-start(bf16[512,1536]{1,0:T(8,128)(2,1)} %collective-permute-done.22), channel_id=1, source_target_pairs={{16,24},{18,26},{20,28},{22,30},{8,0},{10,2},{12,4},{14,6},{17,25}... | collective-permute-start | bytes 4718600 | tf_op jit(solution)/shard_map/ppermute | solution.py:629
  146.1 27.7 %collective-permute-start.27 = (bf16[128,2048]{1,0:T(8,128)(2,1)S(1)}, bf16[128,2048]{1,0:T(8,128)(2,1)S(1)}, u32[]{:S(2)}, u32[]{:S(2)}) collective-permute-start(bf16[128,2048]{1,0:T(8,128)(2,1)S(1)} %get-tuple-element.580), channel_id=1, source_target_pairs={{0,2},{2,0},{4,6},{6,4},{8,10},{10,8},{12,14},{14,12},{16,18},{18,... | collective-permute-start | bytes 1572872 | tf_op jit(solution)/shard_map/ppermute | solution.py:621
  147.2 26.6 %collective-permute-start.28 = (bf16[128,2048]{1,0:T(8,128)(2,1)S(1)}, bf16[128,2048]{1,0:T(8,128)(2,1)S(1)}, u32[]{:S(2)}, u32[]{:S(2)}) collective-permute-start(bf16[128,2048]{1,0:T(8,128)(2,1)S(1)} %get-tuple-element.579), channel_id=1, source_target_pairs={{0,4},{2,6},{4,0},{6,2},{8,12},{10,14},{12,8},{14,10},{16,20},{18,... | collective-permute-start | bytes 1572872 | tf_op jit(solution)/shard_map/ppermute | solution.py:621
  174.1 23.3 %collective-permute-start.33 = (bf16[256,2048]{1,0:T(8,128)(2,1)S(1)}, bf16[256,2048]{1,0:T(8,128)(2,1)S(1)}, u32[]{:S(2)}, u32[]{:S(2)}) collective-permute-start(bf16[256,2048]{1,0:T(8,128)(2,1)S(1)} %pad_maximum_fusion.5), channel_id=1, source_target_pairs={{0,4},{2,6},{4,0},{6,2},{8,12},{10,14},{12,8},{14,10},{16,20},{18,... | collective-permute-start | bytes 3145736 | tf_op jit(solution)/shard_map/ppermute | solution.py:621
  174.7 23.0 %collective-permute-start.32 = (bf16[256,2048]{1,0:T(8,128)(2,1)S(1)}, bf16[256,2048]{1,0:T(8,128)(2,1)S(1)}, u32[]{:S(2)}, u32[]{:S(2)}) collective-permute-start(bf16[256,2048]{1,0:T(8,128)(2,1)S(1)} %pad_maximum_fusion.4), channel_id=1, source_target_pairs={{0,2},{2,0},{4,6},{6,4},{8,10},{10,8},{12,14},{14,12},{16,18},{18,... | collective-permute-start | bytes 3145736 | tf_op jit(solution)/shard_map/ppermute | solution.py:621
  175.2 39.0 %collective-permute-start.34 = (bf16[512,1536]{1,0:T(8,128)(2,1)S(1)}, bf16[512,1536]{1,0:T(8,128)(2,1)S(1)}, u32[]{:S(2)}, u32[]{:S(2)}) collective-permute-start(bf16[512,1536]{1,0:T(8,128)(2,1)S(1)} %collective-permute-done.30), channel_id=1, source_target_pairs={{16,24},{18,26},{20,28},{22,30},{8,0},{10,2},{12,4},{14,6},{17,25}... | collective-permute-start | bytes 4718600 | tf_op jit(solution)/shard_map/ppermute | solution.py:629
  176.6 37.6 %collective-permute-start.36 = (bf16[256,1536]{1,0:T(8,128)(2,1)S(1)}, bf16[256,1536]{1,0:T(8,128)(2,1)S(1)}, u32[]{:S(2)}, u32[]{:S(2)}) collective-permute-start(bf16[256,1536]{1,0:T(8,128)(2,1)S(1)} %pad_maximum_fusion.13), channel_id=1, source_target_pairs={{0,4},{2,6},{4,0},{6,2},{8,12},{10,14},{12,8},{14,10},{16,20},{18,... | collective-permute-start | bytes 2359304 | tf_op jit(solution)/shard_map/ppermute | solution.py:621
  214.3 39.2 %collective-permute-start.43 = (bf16[1024,2048]{1,0:T(8,128)(2,1)S(1)}, bf16[1024,2048]{1,0:T(8,128)(2,1)S(1)}, u32[]{:S(2)}, u32[]{:S(2)}) collective-permute-start(bf16[1024,2048]{1,0:T(8,128)(2,1)S(1)} %constant_dynamic-update-slice_fusion.5.refs_2_.refs_0_), channel_id=1, source_target_pairs={{0,1},{1,0},{2,3},{3,2},{4,5},{5,4},{6,7},{7,6},{8,9},{9,8},{10,11... | collective-permute-start | bytes 12582920 | tf_op jit(solution)/shard_map/ppermute | solution.py:603
  218.5 23.3 %collective-permute-start.37 = (bf16[256,2048]{1,0:T(8,128)(2,1)S(1)}, bf16[256,2048]{1,0:T(8,128)(2,1)S(1)}, u32[]{:S(2)}, u32[]{:S(2)}) collective-permute-start(bf16[256,2048]{1,0:T(8,128)(2,1)S(1)} %get-tuple-element.534), channel_id=1, source_target_pairs={{0,2},{2,0},{4,6},{6,4},{8,10},{10,8},{12,14},{14,12},{16,18},{18,... | collective-permute-start | bytes 3145736 | tf_op jit(solution)/shard_map/ppermute | solution.py:621
  219.0 23.2 %collective-permute-start.38 = (bf16[256,2048]{1,0:T(8,128)(2,1)S(1)}, bf16[256,2048]{1,0:T(8,128)(2,1)S(1)}, u32[]{:S(2)}, u32[]{:S(2)}) collective-permute-start(bf16[256,2048]{1,0:T(8,128)(2,1)S(1)} %get-tuple-element.534), channel_id=1, source_target_pairs={{0,4},{2,6},{4,0},{6,2},{8,12},{10,14},{12,8},{14,10},{16,20},{18,... | collective-permute-start | bytes 3145736 | tf_op jit(solution)/shard_map/ppermute | solution.py:621
  219.5 34.0 %collective-permute-start.41 = (bf16[512,1536]{1,0:T(8,128)(2,1)S(1)}, bf16[512,1536]{1,0:T(8,128)(2,1)}, u32[]{:S(2)}, u32[]{:S(2)}) collective-permute-start(bf16[512,1536]{1,0:T(8,128)(2,1)S(1)} %pad_maximum_fusion.2.refs_4_.refs_8_), channel_id=1, source_target_pairs={{0,8},{2,10},{4,12},{6,14},{8,0},{10,2},{12,4},{14,6},{16,24},{18,... | collective-permute-start | bytes 4718600 | tf_op jit(solution)/shard_map/ppermute | solution.py:629
  219.6 33.9 %collective-permute-start.42 = (bf16[512,1536]{1,0:T(8,128)(2,1)S(1)}, bf16[512,1536]{1,0:T(8,128)(2,1)}, u32[]{:S(2)}, u32[]{:S(2)}) collective-permute-start(bf16[512,1536]{1,0:T(8,128)(2,1)S(1)} %pad_maximum_fusion.2.refs_4_.refs_8_), channel_id=1, source_target_pairs={{8,16},{10,18},{12,20},{14,22},{16,8},{18,10},{20,12},{22,14},{9,1... | collective-permute-start | bytes 4718600 | tf_op jit(solution)/shard_map/ppermute | solution.py:629
  258.8 26.5 %collective-permute-start.45 = (bf16[512,1536]{1,0:T(8,128)(2,1)}, bf16[512,1536]{1,0:T(8,128)(2,1)S(1)}, u32[]{:S(2)}, u32[]{:S(2)}) collective-permute-start(bf16[512,1536]{1,0:T(8,128)(2,1)} %collective-permute-done.41), channel_id=1, source_target_pairs={{8,16},{10,18},{12,20},{14,22},{16,8},{18,10},{20,12},{22,14},{9,1... | collective-permute-start | bytes 4718600 | tf_op jit(solution)/shard_map/ppermute | solution.py:629
  259.5 40.2 %collective-permute-start.46 = (bf16[512,1536]{1,0:T(8,128)(2,1)}, bf16[512,1536]{1,0:T(8,128)(2,1)}, u32[]{:S(2)}, u32[]{:S(2)}) collective-permute-start(bf16[512,1536]{1,0:T(8,128)(2,1)} %collective-permute-done.42), channel_id=1, source_target_pairs={{16,24},{18,26},{20,28},{22,30},{8,0},{10,2},{12,4},{14,6},{17,25}... | collective-permute-start | bytes 4718600 | tf_op jit(solution)/shard_map/ppermute | solution.py:629
  299.7 38.2 %collective-permute-start.47 = (bf16[512,1536]{1,0:T(8,128)(2,1)S(1)}, bf16[512,1536]{1,0:T(8,128)(2,1)S(1)}, u32[]{:S(2)}, u32[]{:S(2)}) collective-permute-start(bf16[512,1536]{1,0:T(8,128)(2,1)S(1)} %collective-permute-done.45), channel_id=1, source_target_pairs={{16,24},{18,26},{20,28},{22,30},{8,0},{10,2},{12,4},{14,6},{17,25}... | collective-permute-start | bytes 4718600 | tf_op jit(solution)/shard_map/ppermute | solution.py:629
  338.0 39.9 %collective-permute-start.48 = (bf16[512,1536]{1,0:T(8,128)(2,1)S(1)}, bf16[512,1536]{1,0:T(8,128)(2,1)S(1)}, u32[]{:S(2)}, u32[]{:S(2)}) collective-permute-start(bf16[512,1536]{1,0:T(8,128)(2,1)S(1)} %copy-done.43), channel_id=1, source_target_pairs={{0,8},{2,10},{4,12},{6,14},{1,9},{3,11},{5,13},{7,15}} | collective-permute-start | bytes 4718600 | tf_op jit(solution)/shard_map/ppermute | solution.py:629
  341.2 36.7 %collective-permute-start.49 = (bf16[512,1536]{1,0:T(8,128)(2,1)S(1)}, bf16[512,1536]{1,0:T(8,128)(2,1)}, u32[]{:S(2)}, u32[]{:S(2)}) collective-permute-start(bf16[512,1536]{1,0:T(8,128)(2,1)S(1)} %copy-done.42), channel_id=1, source_target_pairs={{24,16},{26,18},{28,20},{30,22},{25,17},{27,19},{29,21},{31,23}} | collective-permute-start | bytes 4718600 | tf_op jit(solution)/shard_map/ppermute | solution.py:629
  382.3 42.6 %collective-permute-start.53 = (bf16[512,1536]{1,0:T(8,128)(2,1)S(1)}, bf16[512,1536]{1,0:T(8,128)(2,1)}, u32[]{:S(2)}, u32[]{:S(2)}) collective-permute-start(bf16[512,1536]{1,0:T(8,128)(2,1)S(1)} %shard_map.242), channel_id=1, source_target_pairs={{8,16},{10,18},{12,20},{14,22},{16,8},{18,10},{20,12},{22,14},{9,1... | collective-permute-start | bytes 4718600 | tf_op jit(solution)/shard_map/ppermute | solution.py:629
  384.1 40.7 %collective-permute-start.54 = (bf16[512,1536]{1,0:T(8,128)(2,1)S(1)}, bf16[512,1536]{1,0:T(8,128)(2,1)}, u32[]{:S(2)}, u32[]{:S(2)}) collective-permute-start(bf16[512,1536]{1,0:T(8,128)(2,1)S(1)} %shard_map.242), channel_id=1, source_target_pairs={{0,8},{2,10},{4,12},{6,14},{24,16},{26,18},{28,20},{30,22},{1,9},{... | collective-permute-start | bytes 4718600 | tf_op jit(solution)/shard_map/ppermute | solution.py:629
  393.0 31.9 %collective-permute-start.51 = (bf16[128,2048]{1,0:T(8,128)(2,1)}, bf16[128,2048]{1,0:T(8,128)(2,1)S(1)}, u32[]{:S(2)}, u32[]{:S(2)}) collective-permute-start(bf16[128,2048]{1,0:T(8,128)(2,1)} %get-tuple-element.578), channel_id=1, source_target_pairs={{0,2},{2,0},{4,6},{6,4},{8,10},{10,8},{12,14},{14,12},{16,18},{18,... | collective-permute-start | bytes 1572872 | tf_op jit(solution)/shard_map/ppermute | solution.py:621
  394.0 30.9 %collective-permute-start.52 = (bf16[128,2048]{1,0:T(8,128)(2,1)S(1)}, bf16[128,2048]{1,0:T(8,128)(2,1)S(1)}, u32[]{:S(2)}, u32[]{:S(2)}) collective-permute-start(bf16[128,2048]{1,0:T(8,128)(2,1)S(1)} %get-tuple-element.577), channel_id=1, source_target_pairs={{0,4},{2,6},{4,0},{6,2},{8,12},{10,14},{12,8},{14,10},{16,20},{18,... | collective-permute-start | bytes 1572872 | tf_op jit(solution)/shard_map/ppermute | solution.py:621
  424.9 29.1 %collective-permute-start.57 = (bf16[1024,2048]{1,0:T(8,128)(2,1)}, bf16[1024,2048]{1,0:T(8,128)(2,1)}, u32[]{:S(2)}, u32[]{:S(2)}) collective-permute-start(bf16[1024,2048]{1,0:T(8,128)(2,1)} %get-tuple-element.409), channel_id=1, source_target_pairs={{0,1},{1,0},{2,3},{3,2},{4,5},{5,4},{6,7},{7,6},{8,9},{9,8},{10,11... | collective-permute-start | bytes 12582920 | tf_op jit(solution)/shard_map/ppermute | solution.py:603
  428.4 24.2 %collective-permute-start.55 = (bf16[256,2048]{1,0:T(8,128)(2,1)}, bf16[256,2048]{1,0:T(8,128)(2,1)}, u32[]{:S(2)}, u32[]{:S(2)}) collective-permute-start(bf16[256,2048]{1,0:T(8,128)(2,1)} %pad_maximum_fusion.6), channel_id=1, source_target_pairs={{0,2},{2,0},{4,6},{6,4},{8,10},{10,8},{12,14},{14,12},{16,18},{18,... | collective-permute-start | bytes 3145736 | tf_op jit(solution)/shard_map/ppermute | solution.py:621
  430.1 23.9 %collective-permute-start.56 = (bf16[256,2048]{1,0:T(8,128)(2,1)}, bf16[256,2048]{1,0:T(8,128)(2,1)}, u32[]{:S(2)}, u32[]{:S(2)}) collective-permute-start(bf16[256,2048]{1,0:T(8,128)(2,1)} %pad_maximum_fusion.7), channel_id=1, source_target_pairs={{0,4},{2,6},{4,0},{6,2},{8,12},{10,14},{12,8},{14,10},{16,20},{18,... | collective-permute-start | bytes 3145736 | tf_op jit(solution)/shard_map/ppermute | solution.py:621
  435.2 34.7 %collective-permute-start.58 = (bf16[512,1536]{1,0:T(8,128)(2,1)S(1)}, bf16[512,1536]{1,0:T(8,128)(2,1)}, u32[]{:S(2)}, u32[]{:S(2)}) collective-permute-start(bf16[512,1536]{1,0:T(8,128)(2,1)S(1)} %get-tuple-element.424), channel_id=1, source_target_pairs={{0,8},{2,10},{4,12},{6,14},{8,0},{10,2},{12,4},{14,6},{16,24},{18,... | collective-permute-start | bytes 4718600 | tf_op jit(solution)/shard_map/ppermute | solution.py:629
  435.2 36.5 %collective-permute-start.59 = (bf16[512,1536]{1,0:T(8,128)(2,1)}, bf16[512,1536]{1,0:T(8,128)(2,1)}, u32[]{:S(2)}, u32[]{:S(2)}) collective-permute-start(bf16[512,1536]{1,0:T(8,128)(2,1)} %get-tuple-element.425), channel_id=1, source_target_pairs={{8,16},{10,18},{12,20},{14,22},{16,8},{18,10},{20,12},{22,14},{9,1... | collective-permute-start | bytes 4718600 | tf_op jit(solution)/shard_map/ppermute | solution.py:629
  458.6 44.7 %collective-permute-start.66 = (bf16[512,1536]{1,0:T(8,128)(2,1)S(1)}, bf16[512,1536]{1,0:T(8,128)(2,1)S(1)}, u32[]{:S(2)}, u32[]{:S(2)}) collective-permute-start(bf16[512,1536]{1,0:T(8,128)(2,1)S(1)} %copy-done.34), channel_id=1, source_target_pairs={{0,8},{2,10},{4,12},{6,14},{1,9},{3,11},{5,13},{7,15}} | collective-permute-start | bytes 4718600 | tf_op jit(solution)/shard_map/ppermute | solution.py:629
  469.9 34.5 %collective-permute-start.67 = (bf16[512,1536]{1,0:T(8,128)(2,1)S(1)}, bf16[512,1536]{1,0:T(8,128)(2,1)}, u32[]{:S(2)}, u32[]{:S(2)}) collective-permute-start(bf16[512,1536]{1,0:T(8,128)(2,1)S(1)} %copy-done.33), channel_id=1, source_target_pairs={{24,16},{26,18},{28,20},{30,22},{25,17},{27,19},{29,21},{31,23}} | collective-permute-start | bytes 4718600 | tf_op jit(solution)/shard_map/ppermute | solution.py:629
  475.0 22.4 %collective-permute-start.62 = (bf16[256,2048]{1,0:T(8,128)(2,1)S(1)}, bf16[256,2048]{1,0:T(8,128)(2,1)S(1)}, u32[]{:S(2)}, u32[]{:S(2)}) collective-permute-start(bf16[256,2048]{1,0:T(8,128)(2,1)S(1)} %get-tuple-element.531), channel_id=1, source_target_pairs={{0,2},{2,0},{4,6},{6,4},{8,10},{10,8},{12,14},{14,12},{16,18},{18,... | collective-permute-start | bytes 3145736 | tf_op jit(solution)/shard_map/ppermute | solution.py:621
  476.0 23.4 %collective-permute-start.63 = (bf16[256,2048]{1,0:T(8,128)(2,1)S(1)}, bf16[256,2048]{1,0:T(8,128)(2,1)S(1)}, u32[]{:S(2)}, u32[]{:S(2)}) collective-permute-start(bf16[256,2048]{1,0:T(8,128)(2,1)S(1)} %get-tuple-element.531), channel_id=1, source_target_pairs={{0,4},{2,6},{4,0},{6,2},{8,12},{10,14},{12,8},{14,10},{16,20},{18,... | collective-permute-start | bytes 3145736 | tf_op jit(solution)/shard_map/ppermute | solution.py:621
  517.0 48.7 %collective-permute-start.71 = (bf16[512,1536]{1,0:T(8,128)(2,1)S(1)}, bf16[512,1536]{1,0:T(8,128)(2,1)S(1)}, u32[]{:S(2)}, u32[]{:S(2)}) collective-permute-start(bf16[512,1536]{1,0:T(8,128)(2,1)S(1)} %shard_map.247), channel_id=1, source_target_pairs={{8,16},{10,18},{12,20},{14,22},{16,8},{18,10},{20,12},{22,14},{9,1... | collective-permute-start | bytes 4718600 | tf_op jit(solution)/shard_map/ppermute | solution.py:629
  517.8 47.9 %collective-permute-start.72 = (bf16[512,1536]{1,0:T(8,128)(2,1)S(1)}, bf16[512,1536]{1,0:T(8,128)(2,1)}, u32[]{:S(2)}, u32[]{:S(2)}) collective-permute-start(bf16[512,1536]{1,0:T(8,128)(2,1)S(1)} %shard_map.247), channel_id=1, source_target_pairs={{0,8},{2,10},{4,12},{6,14},{24,16},{26,18},{28,20},{30,22},{1,9},{... | collective-permute-start | bytes 4718600 | tf_op jit(solution)/shard_map/ppermute | solution.py:629
  524.5 41.3 %collective-permute-start.69 = (bf16[256,2048]{1,0:T(8,128)(2,1)}, bf16[256,2048]{1,0:T(8,128)(2,1)}, u32[]{:S(2)}, u32[]{:S(2)}) collective-permute-start(bf16[256,2048]{1,0:T(8,128)(2,1)} %pad_maximum_fusion.8), channel_id=1, source_target_pairs={{0,2},{2,0},{4,6},{6,4},{8,10},{10,8},{12,14},{14,12},{16,18},{18,... | collective-permute-start | bytes 3145736 | tf_op jit(solution)/shard_map/ppermute | solution.py:621
  525.5 40.2 %collective-permute-start.70 = (bf16[256,2048]{1,0:T(8,128)(2,1)}, bf16[256,2048]{1,0:T(8,128)(2,1)}, u32[]{:S(2)}, u32[]{:S(2)}) collective-permute-start(bf16[256,2048]{1,0:T(8,128)(2,1)} %pad_maximum_fusion.9), channel_id=1, source_target_pairs={{0,4},{2,6},{4,0},{6,2},{8,12},{10,14},{12,8},{14,10},{16,20},{18,... | collective-permute-start | bytes 3145736 | tf_op jit(solution)/shard_map/ppermute | solution.py:621
  526.7 39.0 %collective-permute-start.73 = (bf16[256,1536]{1,0:T(8,128)(2,1)}, bf16[256,1536]{1,0:T(8,128)(2,1)S(1)}, u32[]{:S(2)}, u32[]{:S(2)}) collective-permute-start(bf16[256,1536]{1,0:T(8,128)(2,1)} %pad_maximum_fusion.14), channel_id=1, source_target_pairs={{0,2},{2,0},{4,6},{6,4},{8,10},{10,8},{12,14},{14,12},{16,18},{18,... | collective-permute-start | bytes 2359304 | tf_op jit(solution)/shard_map/ppermute | solution.py:621
  567.1 23.4 %collective-permute-start.74 = (bf16[1024,2048]{1,0:T(8,128)(2,1)}, bf16[1024,2048]{1,0:T(8,128)(2,1)}, u32[]{:S(2)}, u32[]{:S(2)}) collective-permute-start(bf16[1024,2048]{1,0:T(8,128)(2,1)} %get-tuple-element.455), channel_id=1, source_target_pairs={{0,1},{1,0},{2,3},{3,2},{4,5},{5,4},{6,7},{7,6},{8,9},{9,8},{10,11... | collective-permute-start | bytes 12582920 | tf_op jit(solution)/shard_map/ppermute | solution.py:603
  573.6 36.1 %collective-permute-start.77 = (bf16[512,1536]{1,0:T(8,128)(2,1)S(1)}, bf16[512,1536]{1,0:T(8,128)(2,1)}, u32[]{:S(2)}, u32[]{:S(2)}) collective-permute-start(bf16[512,1536]{1,0:T(8,128)(2,1)S(1)} %get-tuple-element.467), channel_id=1, source_target_pairs={{0,8},{2,10},{4,12},{6,14},{8,0},{10,2},{12,4},{14,6},{16,24},{18,... | collective-permute-start | bytes 4718600 | tf_op jit(solution)/shard_map/ppermute | solution.py:629
  573.6 37.9 %collective-permute-start.78 = (bf16[512,1536]{1,0:T(8,128)(2,1)}, bf16[512,1536]{1,0:T(8,128)(2,1)}, u32[]{:S(2)}, u32[]{:S(2)}) collective-permute-start(bf16[512,1536]{1,0:T(8,128)(2,1)} %get-tuple-element.468), channel_id=1, source_target_pairs={{8,16},{10,18},{12,20},{14,22},{16,8},{18,10},{20,12},{22,14},{9,1... | collective-permute-start | bytes 4718600 | tf_op jit(solution)/shard_map/ppermute | solution.py:629
  576.5 25.5 %collective-permute-start.79 = (bf16[256,1536]{1,0:T(8,128)(2,1)}, bf16[256,1536]{1,0:T(8,128)(2,1)}, u32[]{:S(2)}, u32[]{:S(2)}) collective-permute-start(bf16[256,1536]{1,0:T(8,128)(2,1)} %pad_maximum_fusion.15), channel_id=1, source_target_pairs={{0,4},{2,6},{4,0},{6,2},{8,12},{10,14},{12,8},{14,10},{16,20},{18,... | collective-permute-start | bytes 2359304 | tf_op jit(solution)/shard_map/ppermute | solution.py:621
  615.8 30.8 %collective-permute-start.86 = (f32[256,2048]{1,0:T(8,128)}, f32[256,2048]{1,0:T(8,128)}, u32[]{:S(2)}, u32[]{:S(2)}) collective-permute-start(f32[256,2048]{1,0:T(8,128)} %add_add_fusion.mine), channel_id=1, source_target_pairs={{0,1},{1,0},{2,3},{3,2},{4,5},{5,4},{6,7},{7,6},{8,9},{9,8},{10,11... | collective-permute-start | bytes 6291464 | tf_op jit(solution)/shard_map/ppermute | solution.py:603
  619.0 26.8 %collective-permute-start.80 = (bf16[256,2048]{1,0:T(8,128)(2,1)}, bf16[256,2048]{1,0:T(8,128)(2,1)}, u32[]{:S(2)}, u32[]{:S(2)}) collective-permute-start(bf16[256,2048]{1,0:T(8,128)(2,1)} %pad_maximum_fusion.10), channel_id=1, source_target_pairs={{0,2},{2,0},{4,6},{6,4},{8,10},{10,8},{12,14},{14,12},{16,18},{18,... | collective-permute-start | bytes 3145736 | tf_op jit(solution)/shard_map/ppermute | solution.py:621
  622.0 24.6 %collective-permute-start.81 = (bf16[256,2048]{1,0:T(8,128)(2,1)}, bf16[256,2048]{1,0:T(8,128)(2,1)}, u32[]{:S(2)}, u32[]{:S(2)}) collective-permute-start(bf16[256,2048]{1,0:T(8,128)(2,1)} %pad_maximum_fusion.11), channel_id=1, source_target_pairs={{0,4},{2,6},{4,0},{6,2},{8,12},{10,14},{12,8},{14,10},{16,20},{18,... | collective-permute-start | bytes 3145736 | tf_op jit(solution)/shard_map/ppermute | solution.py:621
  (133 other events, 1445.3 us)

commit v6 on v5

--- a/solution.py
+++ b/solution.py
@@ -11,7 +11,8 @@
 rope_base = 1000000.0
 group = 4
 sub_count = 2
-vmem_limit = 52 * 1024 * 1024
+mebibyte = 1024 * 1024
+vmem_limit = 52 * mebibyte
 
 
 def norm_rows(values, gain):
@@ -62,14 +63,14 @@
     return dot_nn(high, right) + dot_nn(low, right)
 
 
-def kernel_call(body, grid, in_specs, out_specs, out_shape, flops, moved):
+def kernel_call(body, grid, in_specs, out_specs, out_shape, flops, moved, room=vmem_limit):
     return pl.pallas_call(
         body,
         grid=grid,
         in_specs=in_specs,
         out_specs=out_specs,
         out_shape=out_shape,
-        compiler_params=pltpu.CompilerParams(vmem_limit_bytes=vmem_limit),
+        compiler_params=pltpu.CompilerParams(vmem_limit_bytes=room),
         cost_estimate=pl.CostEstimate(flops=flops, bytes_accessed=moved, transcendentals=0),
     )
 
@@ -436,6 +437,7 @@
         [shape_of((block_rows, width), jnp.bfloat16)] * count,
         2 * tokens * model * 256,
         tokens * model,
+        vmem_limit,
     )(*first, *second, *first_grad, *second_grad)
 
 
@@ -511,6 +513,7 @@
         [shape_of((tokens, model), jnp.bfloat16)] * 2,
         2 * tokens * model * 256,
         tokens * model,
+        vmem_limit,
     )(*lefts, *flat)
 
 
@@ -539,6 +542,7 @@
         [shape_of((rows, width), jnp.bfloat16)] * outs,
         1,
         12 * rows * width,
+        16 * mebibyte if rows * width > mebibyte // 2 else vmem_limit,
     )(*flags, *arrays)
 
 
@@ -570,7 +574,7 @@
             out_specs=[full(shape)] * count,
         ),
         out_shape=[shape] * count,
-        compiler_params=pltpu.CompilerParams(vmem_limit_bytes=vmem_limit),
+        compiler_params=pltpu.CompilerParams(vmem_limit_bytes=32 * mebibyte),
     )(place.reshape(1).astype(jnp.int32), *flat)
 
 
@@ -594,7 +598,7 @@
             out_specs=pl.BlockSpec((2 * half, block), lambda k, place: (0, (k + place[1]) % count)),
         ),
         out_shape=shape_of((2 * half, model), jnp.float32),
-        compiler_params=pltpu.CompilerParams(vmem_limit_bytes=vmem_limit),
+        compiler_params=pltpu.CompilerParams(vmem_limit_bytes=12 * mebibyte),
         cost_estimate=pl.CostEstimate(flops=1, bytes_accessed=16 * half * model, transcendentals=0),
     )(jnp.stack([core, spot]).astype(jnp.int32), mine, other)
 
@@ -1044,30 +1048,31 @@
     got = lines.across_terms(kept, other)
     got, sum_1.got[2], back_0_second, branch = tie(got, sum_1.got[2], back_0_second, branch)
     attn_sum.hop()
-    mixed = state + lines.near_sum(branch_kept, branch_other, branch)
-    mixed_other = swap_cores(mixed)
     back_1 = lines.row_pieces(sum_1.total())
     near = lines.near_flips(kept, other, got)
+    back_got = [lines.flip(back_1[1], 1)]
     attn_sum.hop()
-    near, attn_sum.got[1], back_1, mixed, mixed_other = tie(
-        near, attn_sum.got[1], back_1, mixed, mixed_other
+    mixed = state + lines.near_sum(branch_kept, branch_other, branch)
+    near, attn_sum.got[1], back_1, back_got, mixed = tie(
+        near, attn_sum.got[1], back_1, back_got, mixed
     )
     ready = attn_sum.ready()
     near, ready = tie(near, ready)
     attn_sum.hop(ready)
-    back_1 = lines.flip_pieces(back_1)
+    mixed_other = swap_cores(mixed)
+    back_got = back_got + [lines.flip(back_1[r], r) for r in (2, 3)]
+    gains, mixed_other = tie(gains, mixed_other)
+    gains = gains + lines.flip(gains, 1)
+    gains = gains + lines.flip(gains, 2)
     normed_grad = lines.near_sum(kept, other, near)
     input_grad = state_grad + norm_back(source, scale_first, attn_gain_r, normed_grad)
     mixed = run_place_halves(core, lines.spot, lines.length, mixed, mixed_other)
-    attn_sum.got[2], back_1, input_grad, gains, mixed = tie(
-        attn_sum.got[2], back_1, input_grad, gains, mixed
-    )
-    gains_got = [lines.flip(gains, r) for r in range(1, group)]
-    attn_send = lines.row_pieces(attn_sum.total())
-    attn_grads = lines.flip_pieces(attn_send)
+    attn_sum.got[2], back_got, input_grad, gains, mixed = tie(
+        attn_sum.got[2], back_got, input_grad, gains, mixed
+    )
+    back_1 = [back_1[0]] + back_got
+    attn_grads = lines.flip_pieces(lines.row_pieces(attn_sum.total()))
     input_other = swap_cores(input_grad)
-    gains_got, input_other = tie(gains_got, input_other)
-    gains = gains + gains_got[0] + gains_got[1] + gains_got[2]
     gains_got = [lines.turn(gains, k) for k in range(1, lines.length)]
     ffn_grads = run_place_columns(
         lines.place,

time: 710 us -> 704 us (level)
  waiting for transfers between devices: 194 us -> 215 us
  Pallas kernels: 226 us -> 212 us
  starting transfers between devices: 151 us -> 143 us
  other arithmetic: 90.5 us -> 83.3 us
    ppermute x53 -> x52, waiting for transfers between devices: 120 us -> 131 us  [flip(): lax.ppermute(values, 'dp', [(i, i ^ relation) for i in range(self.dp)])]
    pallas_call x6, Pallas kernels: 19.3 us -> 9.37 us  [run_add(): kernel_call(body, (rows // tile,), [whole(f) for f in flags] + [spec] * l...]
    ppermute x53 -> x52, starting transfers between devices: 47.5 us -> 43.1 us  [flip(): lax.ppermute(values, 'dp', [(i, i ^ relation) for i in range(self.dp)])]
    unnamed x168 -> x206, local copies, waits for them, and re-layouts: 18.5 us -> 21.9 us
  transfers between devices with their start and end apart: 103 -> 102, of which waited for: 34 -> 35; matrix products, arithmetic and copies ran while one was open for 15% -> 15% of each run, Pallas kernels for 32% -> 30%
where the time goes in v6:
time: 704 us; the launch traced here: 696 us
  waiting for transfers between devices  215 us (31%)
  Pallas kernels  212 us (30%)
  starting transfers between devices  143 us (20%)
  other arithmetic  83.3 us (12%)
  local copies, waits for them, and re-layouts  40.1 us (6%)
    ppermute x52, waiting for transfers between devices, flip(): lax.ppermute(values, 'dp', [(i, i ^ relation) for i in range(self.dp)])  131 us
    ppermute x33, waiting for transfers between devices, ends(): return lax.ppermute(values, 'dp', pairs)  76.4 us
    ppermute x33, starting transfers between devices, ends(): return lax.ppermute(values, 'dp', pairs)  62.6 us
    pallas_call x2, Pallas kernels, run_ffn_units(): kernel_call(functools.partial(ffn_units, len(blocks), ff_sub, earlier), (...  49.8 us
    ppermute x52, starting transfers between devices, flip(): lax.ppermute(values, 'dp', [(i, i ^ relation) for i in range(self.dp)])  43.1 us
    pallas_call x2, Pallas kernels, run_weight_gradients(): kernel_call(functools.partial(weight_gradients, count, per), (model // ti...  34.6 us
    pallas_call x1, Pallas kernels, run_attention(): kernel_call(functools.partial(attention_backward, len(blocks), head_dim,...  34.2 us
    ppermute x14, starting transfers between devices, swap_cores(): return lax.ppermute(values, 'tensor', [(0, 1), (1, 0)])  33.7 us
  transfers between devices with their start and end apart: 102, of which 35 were waited for; matrix products, arithmetic and copies ran while one was open for 15% of the time, Pallas kernels for 30%

profile of v6, /device:TPU:1, one launch (start us, length us, event | category | flops | bytes accessed | tf_op | source)
XLA Modules:
  0.0 696.2 jit_solution(12326931718291931130)
XLA Ops:
  21.2 3.8 collective-permute-start.9
  27.0 5.6 multiply_sine_fusion
  32.5 5.7 collective-permute-done.5
  39.3 3.7 collective-permute-start.14
  62.8 7.3 %collective-permute-done.13 = bf16[512,640]{1,0:T(8,128)(2,1)} collective-permute-done((bf16[512,640]{1,0:T(8,128)(2,1)}, bf16[512,640]{1,0:T(8,128)(2,1)}, u32[]{:S(2)}, u32[]{:S(2)}) %collective-permute-start.13) | collective-permute-done | bytes 655392 | tf_op jit(solution)/shard_map/ppermute | solution.py:633
  81.4 3.6 pad_maximum_fusion.refs_1_.refs_4_
  85.7 7.9 %collective-permute-done.20 = bf16[128,1536]{1,0:T(8,128)(2,1)S(1)} collective-permute-done((bf16[128,1536]{1,0:T(8,128)(2,1)S(1)}, bf16[128,1536]{1,0:T(8,128)(2,1)S(1)}, u32[]{:S(2)}, u32[]{:S(2)}) %collective-permute-start.20) | collective-permute-done | bytes 393248 | tf_op jit(solution)/shard_map/ppermute | solution.py:625
  102.1 20.8 %shard_map.237 = (f32[4,512,384]{2,1,0:T(8,128)}, bf16[1024,256]{1,0:T(8,128)(2,1)S(1)}, bf16[1024,256]{1,0:T(8,128)(2,1)S(1)}, bf16[1024,2048]{1,0:T(8,128)(2,1)}, bf16[1024,2048]{1,0:T(8,128)(2,1)}) custom-call(bf16[1024,2048]{1,0:T(8,128)(2,1)} %constant_dynamic-update-slice_fusion.refs_0_.refs_3_, bf16[1024,2048]{1,0:T(8,128)(2,1)} %pad_maximum_fusion.refs_1_.refs_4_, ...), custom_call_target="tpu_custom_call" | custom-call | flops 32212254720 | bytes 33554432 | tf_op jit(solution)/shard_map/pallas_call | solution.py:329
  123.0 5.6 collective-permute-done.21
  135.2 9.6 %collective-permute-done.26 = bf16[128,2048]{1,0:T(8,128)(2,1)S(1)} collective-permute-done((bf16[128,2048]{1,0:T(8,128)(2,1)S(1)}, bf16[128,2048]{1,0:T(8,128)(2,1)S(1)}, u32[]{:S(2)}, u32[]{:S(2)}) %collective-permute-start.26) | collective-permute-done | bytes 524320 | tf_op jit(solution)/shard_map/ppermute | solution.py:625
  144.9 3.1 convert_add_fusion.10
  151.5 23.9 %collective-permute-done.31 = bf16[512,1536]{1,0:T(8,128)(2,1)S(1)} collective-permute-done((bf16[512,1536]{1,0:T(8,128)(2,1)}, bf16[512,1536]{1,0:T(8,128)(2,1)S(1)}, u32[]{:S(2)}, u32[]{:S(2)}) %collective-permute-start.31) | collective-permute-done | bytes 1572896 | tf_op jit(solution)/shard_map/ppermute | solution.py:633
  179.9 19.1 %collective-permute-done.33 = bf16[256,2048]{1,0:T(8,128)(2,1)S(1)} collective-permute-done((bf16[256,2048]{1,0:T(8,128)(2,1)S(1)}, bf16[256,2048]{1,0:T(8,128)(2,1)S(1)}, u32[]{:S(2)}, u32[]{:S(2)}) %collective-permute-start.33) | collective-permute-done | bytes 1048608 | tf_op jit(solution)/shard_map/ppermute | solution.py:625
  202.4 13.4 %collective-permute-done.36 = bf16[256,1536]{1,0:T(8,128)(2,1)S(1)} collective-permute-done((bf16[256,1536]{1,0:T(8,128)(2,1)S(1)}, bf16[256,1536]{1,0:T(8,128)(2,1)S(1)}, u32[]{:S(2)}, u32[]{:S(2)}) %collective-permute-start.36) | collective-permute-done | bytes 786464 | tf_op jit(solution)/shard_map/ppermute | solution.py:625
  224.8 18.6 %collective-permute-done.37 = bf16[256,2048]{1,0:T(8,128)(2,1)S(1)} collective-permute-done((bf16[256,2048]{1,0:T(8,128)(2,1)S(1)}, bf16[256,2048]{1,0:T(8,128)(2,1)S(1)}, u32[]{:S(2)}, u32[]{:S(2)}) %collective-permute-start.37) | collective-permute-done | bytes 1048608 | tf_op jit(solution)/shard_map/ppermute | solution.py:625
  244.8 3.8 select_select_fusion.2
  248.6 6.1 collective-permute-done.39
  263.2 4.4 collective-permute-done.44.refs_1_
  267.6 19.5 %shard_map.238 = (bf16[1024,512]{1,0:T(8,128)(2,1)S(1)}, bf16[1024,512]{1,0:T(8,128)(2,1)}, bf16[1024,1024]{1,0:T(8,128)(2,1)}, bf16[1024,1024]{1,0:T(8,128)(2,1)}) custom-call(bf16[1024,2048]{1,0:T(8,128)(2,1)} %copy-done.44, bf16[1024,2048]{1,0:T(8,128)(2,1)} %collective-permute-done.44.refs_1_, bf16[1024,2048]{1,0:T(8,128)(2,1)} %copy-done.45, ...), custom_call_target="tpu_custom_call" | custom-call | flops 12884901888 | bytes 16777216 | tf_op jit(solution)/shard_map/pallas_call | solution.py:394
  287.1 14.5 %collective-permute-done.46 = bf16[512,1536]{1,0:T(8,128)(2,1)S(1)} collective-permute-done((bf16[512,1536]{1,0:T(8,128)(2,1)}, bf16[512,1536]{1,0:T(8,128)(2,1)S(1)}, u32[]{:S(2)}, u32[]{:S(2)}) %collective-permute-start.46) | collective-permute-done | bytes 1572896 | tf_op jit(solution)/shard_map/ppermute | solution.py:633
  302.9 13.0 %shard_map.240 = (bf16[1024,2048]{1,0:T(8,128)(2,1)}, bf16[1024,2048]{1,0:T(8,128)(2,1)}) custom-call(bf16[1024,1024]{1,0:T(8,128)(2,1)} %get-tuple-element.357.refs_4_.refs_0_, bf16[1024,1024]{1,0:T(8,128)(2,1)} %get-tuple-element.358.refs_5_.refs_1_, bf16[512,1536]{1,0:T(8,128)(2,1)S(1)} %copy-done.3, ...), custom_call_target="tpu_custom_call" | custom-call | flops 1073741824 | bytes 2097152 | tf_op jit(solution)/shard_map/pallas_call | solution.py:507
  316.0 21.1 %shard_map.239 = (bf16[512,1536]{1,0:T(8,128)(2,1)}, bf16[512,1536]{1,0:T(8,128)(2,1)}, bf16[512,1536]{1,0:T(8,128)(2,1)}, bf16[512,1536]{1,0:T(8,128)(2,1)}) custom-call(bf16[1024,2048]{1,0:T(8,128)(2,1)} %copy-done.44, bf16[1024,2048]{1,0:T(8,128)(2,1)} %collective-permute-done.44.refs_1_, bf16[1024,2048]{1,0:T(8,128)(2,1)} %copy-done.45, ...), custom_call_target="tpu_custom_call" | custom-call | flops 1073741824 | bytes 2097152 | tf_op jit(solution)/shard_map/pallas_call | solution.py:432
  339.9 3.3 collective-permute-start.48
  344.0 3.8 select_select_fusion
  347.7 30.2 %shard_map.241 = (bf16[1024,512]{1,0:T(8,128)(2,1)S(1)}, bf16[1024,512]{1,0:T(8,128)(2,1)}, bf16[1024,1024]{1,0:T(8,128)(2,1)}, bf16[1024,1024]{1,0:T(8,128)(2,1...) custom-call(bf16[1024,2048]{1,0:T(8,128)(2,1)} %copy-done.44, ...), custom_call_target="tpu_custom_call" | custom-call | flops 12884901888 | bytes 16777216 | tf_op jit(solution)/shard_map/pallas_call | solution.py:394
  381.1 5.7 collective-permute-start.54
  386.9 3.3 convert_add_fusion.6
  393.0 15.1 %shard_map.243 = (bf16[512,1536]{1,0:T(8,128)(2,1)S(1)}, bf16[512,1536]{1,0:T(8,128)(2,1)}, bf16[512,1536]{1,0:T(8,128)(2,1)}, bf16[512,1536]{1,0:T(8,128)(2,1)}) custom-call(bf16[1024,2048]{1,0:T(8,128)(2,1)} %copy-done.44, bf16[1024,2048]{1,0:T(8,128)(2,1)} %collective-permute-done.44.refs_1_, bf16[1024,1024]{1,0:T(8,128)(2,1)} %get-tuple-element.390.refs_2_, ...), custom_call_target="tpu_custom_call" | custom-call | flops 536870912 | bytes 1048576 | tf_op jit(solution)/shard_map/pallas_call | solution.py:465
  409.3 13.4 %shard_map.244 = (bf16[1024,2048]{1,0:T(8,128)(2,1)}, bf16[1024,2048]{1,0:T(8,128)(2,1)}) custom-call(bf16[1024,512]{1,0:T(8,128)(2,1)S(1)} %get-tuple-element.396.refs_6_.refs_0_, bf16[1024,512]{1,0:T(8,128)(2,1)} %get-tuple-element.397.refs_7_.refs_1_, bf16[1024,512]{1,0:T(8,128)(2,1)} %copy-done.9, bf16[1024,512]{1,0:T(8,128)(2,1)} %get-tuple-element.407.refs_3_, ...), custom_call_target="tpu_custom_call" | custom-call | flops 1073741824 | bytes 2097152 | tf_op jit(solution)/shard_map/pallas_call | solution.py:507
  438.9 10.8 %shard_map.245 = (bf16[512,1536]{1,0:T(8,128)(2,1)}, bf16[512,1536]{1,0:T(8,128)(2,1)}, bf16[512,1536]{1,0:T(8,128)(2,1)}, bf16[512,1536]{1,0:T(8,128)(2,1)}) custom-call(bf16[1024,2048]{1,0:T(8,128)(2,1)} %copy-done.45, bf16[1024,2048]{1,0:T(8,128)(2,1)} %copy-done.48, ...), custom_call_target="tpu_custom_call", output_to_operand_aliasing={{0}: (4, {}), {1}: (5, {}), {2}: (6, {}), {3}: (7, {})} | custom-call | flops 536870912 | bytes 1048576 | tf_op jit(solution)/shard_map/pallas_call | solution.py:465
  449.7 4.0 collective-permute-done.55
  455.6 3.2 convert_add_fusion.3
  465.8 5.8 collective-permute-done.58
  481.6 16.6 %collective-permute-done.62 = bf16[256,2048]{1,0:T(8,128)(2,1)S(1)} collective-permute-done((bf16[256,2048]{1,0:T(8,128)(2,1)S(1)}, bf16[256,2048]{1,0:T(8,128)(2,1)S(1)}, u32[]{:S(2)}, u32[]{:S(2)}) %collective-permute-start.62) | collective-permute-done | bytes 1048608 | tf_op jit(solution)/shard_map/ppermute | solution.py:625
  503.7 5.9 collective-permute-done.64
  509.9 4.4 collective-permute-start.68
  515.1 7.4 %collective-permute-start.72 = (bf16[512,1536]{1,0:T(8,128)(2,1)S(1)}, bf16[512,1536]{1,0:T(8,128)(2,1)S(1)}, u32[]{:S(2)}, u32[]{:S(2)}) collective-permute-start(bf16[512,1536]{1,0:T(8,128)(2,1)S(1)} %shard_map.247), channel_id=1, source_target_pairs={{0,8},{2,10},{4,12},{6,14},{24,16},{26,18},{28,20},{30,22},{1,9},{... | collective-permute-start | bytes 4718600 | tf_op jit(solution)/shard_map/ppermute | solution.py:633
  526.9 34.2 %shard_map.248 = (bf16[1024,384]{1,0:T(8,128)(2,1)}, bf16[1024,384]{1,0:T(8,128)(2,1)}, f32[2,256]{1,0:T(2,128)S(1)}, bf16[1024,2048]{1,0:T(8,128)(2,1)}, bf16[1...) custom-call(bf16[1024,2048]{1,0:T(8,128)(2,1)} %copy-done.50, bf16[1024,2048]{1,0:T(8,128)(2,1)} %copy-done.54, ...), custom_call_target="tpu_custom_call" | custom-call | flops 32212254720 | bytes 33554432 | tf_op jit(solution)/shard_map/pallas_call | solution.py:339
  570.2 13.6 %shard_map.249 = (bf16[512,640]{1,0:T(8,128)(2,1)S(1)}, bf16[512,640]{1,0:T(8,128)(2,1)}, bf16[512,640]{1,0:T(8,128)(2,1)}, bf16[512,640]{1,0:T(8,128)(2,1)}) custom-call(bf16[1024,2048]{1,0:T(8,128)(2,1)} %constant_dynamic-update-slice_fusion.refs_0_.refs_3_, bf16[1024,2048]{1,0:T(8,128)(2,1)} %pad_maximum_fusion.refs_1_.refs_4_, ...), custom_call_target="tpu_custom_call" | custom-call | flops 1073741824 | bytes 2097152 | tf_op jit(solution)/shard_map/pallas_call | solution.py:432
  583.8 4.4 convert_add_fusion.1
  590.1 3.4 collective-permute-start.82
  593.5 10.4 %collective-permute-done.77 = bf16[512,1536]{1,0:T(8,128)(2,1)} collective-permute-done((bf16[512,1536]{1,0:T(8,128)(2,1)}, bf16[512,1536]{1,0:T(8,128)(2,1)}, u32[]{:S(2)}, u32[]{:S(2)}) %collective-permute-start.77) | collective-permute-done | bytes 1572896 | tf_op jit(solution)/shard_map/ppermute | solution.py:633
  611.2 4.7 collective-permute-done.82.second
  618.9 9.0 %collective-permute-start.85 = (bf16[512,640]{1,0:T(8,128)(2,1)S(1)}, bf16[512,640]{1,0:T(8,128)(2,1)S(1)}, u32[]{:S(2)}, u32[]{:S(2)}) collective-permute-start(bf16[512,640]{1,0:T(8,128)(2,1)S(1)} %shard_map.251), channel_id=1, source_target_pairs={{0,8},{2,10},{4,12},{6,14},{24,16},{26,18},{28,20},{30,22},{1,9},{... | collective-permute-start | bytes 1966088 | tf_op jit(solution)/shard_map/ppermute | solution.py:633
  630.8 6.7 collective-permute-done.86.refs_5_
  656.8 6.3 collective-permute-done.92
  666.2 4.8 shard_map.253
  685.4 3.2 shard_map.254
  (542 shorter events, 225.5 us)
Async XLA Ops:
  16.3 22.0 %collective-permute-start.5 = (bf16[256,2048]{1,0:T(8,128)(2,1)S(1)}, bf16[256,2048]{1,0:T(8,128)(2,1)}, u32[]{:S(2)}, u32[]{:S(2)}) collective-permute-start(bf16[256,2048]{1,0:T(8,128)(2,1)S(1)} %fusion.2), channel_id=1, source_target_pairs={{0,2},{2,0},{4,6},{6,4},{8,10},{10,8},{12,14},{14,12},{16,18},{18,... | collective-permute-start | bytes 3145736 | tf_op jit(solution)/shard_map/ppermute | solution.py:625
  17.3 22.0 %collective-permute-start.6 = (bf16[256,2048]{1,0:T(8,128)(2,1)S(1)}, bf16[256,2048]{1,0:T(8,128)(2,1)}, u32[]{:S(2)}, u32[]{:S(2)}) collective-permute-start(bf16[256,2048]{1,0:T(8,128)(2,1)S(1)} %fusion.2), channel_id=1, source_target_pairs={{0,4},{2,6},{4,0},{6,2},{8,12},{10,14},{12,8},{14,10},{16,20},{18,... | collective-permute-start | bytes 3145736 | tf_op jit(solution)/shard_map/ppermute | solution.py:625
  93.9 34.7 %collective-permute-start.21 = (bf16[512,1536]{1,0:T(8,128)(2,1)S(1)}, bf16[512,1536]{1,0:T(8,128)(2,1)}, u32[]{:S(2)}, u32[]{:S(2)}) collective-permute-start(bf16[512,1536]{1,0:T(8,128)(2,1)S(1)} %pad_maximum_fusion.1.refs_4_.refs_2_), channel_id=1, source_target_pairs={{0,8},{2,10},{4,12},{6,14},{8,0},{10,2},{12,4},{14,6},{16,24},{18,... | collective-permute-start | bytes 4718600 | tf_op jit(solution)/shard_map/ppermute | solution.py:633
  95.8 32.8 %collective-permute-start.22 = (bf16[512,1536]{1,0:T(8,128)(2,1)S(1)}, bf16[512,1536]{1,0:T(8,128)(2,1)}, u32[]{:S(2)}, u32[]{:S(2)}) collective-permute-start(bf16[512,1536]{1,0:T(8,128)(2,1)S(1)} %pad_maximum_fusion.1.refs_4_.refs_2_), channel_id=1, source_target_pairs={{8,16},{10,18},{12,20},{14,22},{16,8},{18,10},{20,12},{22,14},{9,1... | collective-permute-start | bytes 4718600 | tf_op jit(solution)/shard_map/ppermute | solution.py:633
  97.8 25.2 %collective-permute-start.23 = (bf16[256,2048]{1,0:T(8,128)(2,1)S(1)}, bf16[256,2048]{1,0:T(8,128)(2,1)S(1)}, u32[]{:S(2)}, u32[]{:S(2)}) collective-permute-start(bf16[256,2048]{1,0:T(8,128)(2,1)S(1)} %fusion.17), channel_id=1, source_target_pairs={{0,2},{2,0},{4,6},{6,4},{8,10},{10,8},{12,14},{14,12},{16,18},{18,... | collective-permute-start | bytes 3145736 | tf_op jit(solution)/shard_map/ppermute | solution.py:625
  98.4 24.6 %collective-permute-start.24 = (bf16[256,2048]{1,0:T(8,128)(2,1)S(1)}, bf16[256,2048]{1,0:T(8,128)(2,1)S(1)}, u32[]{:S(2)}, u32[]{:S(2)}) collective-permute-start(bf16[256,2048]{1,0:T(8,128)(2,1)S(1)} %fusion.17), channel_id=1, source_target_pairs={{0,4},{2,6},{4,0},{6,2},{8,12},{10,14},{12,8},{14,10},{16,20},{18,... | collective-permute-start | bytes 3145736 | tf_op jit(solution)/shard_map/ppermute | solution.py:625
  133.9 41.4 %collective-permute-start.31 = (bf16[512,1536]{1,0:T(8,128)(2,1)}, bf16[512,1536]{1,0:T(8,128)(2,1)S(1)}, u32[]{:S(2)}, u32[]{:S(2)}) collective-permute-start(bf16[512,1536]{1,0:T(8,128)(2,1)} %collective-permute-done.22), channel_id=1, source_target_pairs={{16,24},{18,26},{20,28},{22,30},{8,0},{10,2},{12,4},{14,6},{17,25}... | collective-permute-start | bytes 4718600 | tf_op jit(solution)/shard_map/ppermute | solution.py:633
  148.1 27.2 %collective-permute-start.27 = (bf16[128,2048]{1,0:T(8,128)(2,1)S(1)}, bf16[128,2048]{1,0:T(8,128)(2,1)S(1)}, u32[]{:S(2)}, u32[]{:S(2)}) collective-permute-start(bf16[128,2048]{1,0:T(8,128)(2,1)S(1)} %get-tuple-element.572), channel_id=1, source_target_pairs={{0,2},{2,0},{4,6},{6,4},{8,10},{10,8},{12,14},{14,12},{16,18},{18,... | collective-permute-start | bytes 1572872 | tf_op jit(solution)/shard_map/ppermute | solution.py:625
  148.7 26.6 %collective-permute-start.28 = (bf16[128,2048]{1,0:T(8,128)(2,1)S(1)}, bf16[128,2048]{1,0:T(8,128)(2,1)S(1)}, u32[]{:S(2)}, u32[]{:S(2)}) collective-permute-start(bf16[128,2048]{1,0:T(8,128)(2,1)S(1)} %get-tuple-element.571), channel_id=1, source_target_pairs={{0,4},{2,6},{4,0},{6,2},{8,12},{10,14},{12,8},{14,10},{16,20},{18,... | collective-permute-start | bytes 1572872 | tf_op jit(solution)/shard_map/ppermute | solution.py:625
  175.6 23.3 %collective-permute-start.33 = (bf16[256,2048]{1,0:T(8,128)(2,1)S(1)}, bf16[256,2048]{1,0:T(8,128)(2,1)S(1)}, u32[]{:S(2)}, u32[]{:S(2)}) collective-permute-start(bf16[256,2048]{1,0:T(8,128)(2,1)S(1)} %pad_maximum_fusion.5), channel_id=1, source_target_pairs={{0,4},{2,6},{4,0},{6,2},{8,12},{10,14},{12,8},{14,10},{16,20},{18,... | collective-permute-start | bytes 3145736 | tf_op jit(solution)/shard_map/ppermute | solution.py:625
  176.2 23.0 %collective-permute-start.32 = (bf16[256,2048]{1,0:T(8,128)(2,1)S(1)}, bf16[256,2048]{1,0:T(8,128)(2,1)S(1)}, u32[]{:S(2)}, u32[]{:S(2)}) collective-permute-start(bf16[256,2048]{1,0:T(8,128)(2,1)S(1)} %pad_maximum_fusion.4), channel_id=1, source_target_pairs={{0,2},{2,0},{4,6},{6,4},{8,10},{10,8},{12,14},{14,12},{16,18},{18,... | collective-permute-start | bytes 3145736 | tf_op jit(solution)/shard_map/ppermute | solution.py:625
  177.2 38.6 %collective-permute-start.34 = (bf16[512,1536]{1,0:T(8,128)(2,1)S(1)}, bf16[512,1536]{1,0:T(8,128)(2,1)S(1)}, u32[]{:S(2)}, u32[]{:S(2)}) collective-permute-start(bf16[512,1536]{1,0:T(8,128)(2,1)S(1)} %collective-permute-done.30), channel_id=1, source_target_pairs={{16,24},{18,26},{20,28},{22,30},{8,0},{10,2},{12,4},{14,6},{17,25}... | collective-permute-start | bytes 4718600 | tf_op jit(solution)/shard_map/ppermute | solution.py:633
  178.6 37.2 %collective-permute-start.36 = (bf16[256,1536]{1,0:T(8,128)(2,1)S(1)}, bf16[256,1536]{1,0:T(8,128)(2,1)S(1)}, u32[]{:S(2)}, u32[]{:S(2)}) collective-permute-start(bf16[256,1536]{1,0:T(8,128)(2,1)S(1)} %pad_maximum_fusion.13), channel_id=1, source_target_pairs={{0,4},{2,6},{4,0},{6,2},{8,12},{10,14},{12,8},{14,10},{16,20},{18,... | collective-permute-start | bytes 2359304 | tf_op jit(solution)/shard_map/ppermute | solution.py:625
  215.9 39.7 %collective-permute-start.43 = (bf16[1024,2048]{1,0:T(8,128)(2,1)S(1)}, bf16[1024,2048]{1,0:T(8,128)(2,1)S(1)}, u32[]{:S(2)}, u32[]{:S(2)}) collective-permute-start(bf16[1024,2048]{1,0:T(8,128)(2,1)S(1)} %constant_dynamic-update-slice_fusion.5.refs_2_.refs_0_), channel_id=1, source_target_pairs={{0,1},{1,0},{2,3},{3,2},{4,5},{5,4},{6,7},{7,6},{8,9},{9,8},{10,11... | collective-permute-start | bytes 12582920 | tf_op jit(solution)/shard_map/ppermute | solution.py:607
  220.1 23.3 %collective-permute-start.37 = (bf16[256,2048]{1,0:T(8,128)(2,1)S(1)}, bf16[256,2048]{1,0:T(8,128)(2,1)S(1)}, u32[]{:S(2)}, u32[]{:S(2)}) collective-permute-start(bf16[256,2048]{1,0:T(8,128)(2,1)S(1)} %get-tuple-element.526), channel_id=1, source_target_pairs={{0,2},{2,0},{4,6},{6,4},{8,10},{10,8},{12,14},{14,12},{16,18},{18,... | collective-permute-start | bytes 3145736 | tf_op jit(solution)/shard_map/ppermute | solution.py:625
  221.0 23.0 %collective-permute-start.38 = (bf16[256,2048]{1,0:T(8,128)(2,1)S(1)}, bf16[256,2048]{1,0:T(8,128)(2,1)S(1)}, u32[]{:S(2)}, u32[]{:S(2)}) collective-permute-start(bf16[256,2048]{1,0:T(8,128)(2,1)S(1)} %get-tuple-element.526), channel_id=1, source_target_pairs={{0,4},{2,6},{4,0},{6,2},{8,12},{10,14},{12,8},{14,10},{16,20},{18,... | collective-permute-start | bytes 3145736 | tf_op jit(solution)/shard_map/ppermute | solution.py:625
  221.5 34.0 %collective-permute-start.41 = (bf16[512,1536]{1,0:T(8,128)(2,1)S(1)}, bf16[512,1536]{1,0:T(8,128)(2,1)}, u32[]{:S(2)}, u32[]{:S(2)}) collective-permute-start(bf16[512,1536]{1,0:T(8,128)(2,1)S(1)} %pad_maximum_fusion.2.refs_4_.refs_8_), channel_id=1, source_target_pairs={{0,8},{2,10},{4,12},{6,14},{8,0},{10,2},{12,4},{14,6},{16,24},{18,... | collective-permute-start | bytes 4718600 | tf_op jit(solution)/shard_map/ppermute | solution.py:633
  221.6 34.0 %collective-permute-start.42 = (bf16[512,1536]{1,0:T(8,128)(2,1)S(1)}, bf16[512,1536]{1,0:T(8,128)(2,1)}, u32[]{:S(2)}, u32[]{:S(2)}) collective-permute-start(bf16[512,1536]{1,0:T(8,128)(2,1)S(1)} %pad_maximum_fusion.2.refs_4_.refs_8_), channel_id=1, source_target_pairs={{8,16},{10,18},{12,20},{14,22},{16,8},{18,10},{20,12},{22,14},{9,1... | collective-permute-start | bytes 4718600 | tf_op jit(solution)/shard_map/ppermute | solution.py:633
  260.6 26.5 %collective-permute-start.45 = (bf16[512,1536]{1,0:T(8,128)(2,1)}, bf16[512,1536]{1,0:T(8,128)(2,1)S(1)}, u32[]{:S(2)}, u32[]{:S(2)}) collective-permute-start(bf16[512,1536]{1,0:T(8,128)(2,1)} %collective-permute-done.41), channel_id=1, source_target_pairs={{8,16},{10,18},{12,20},{14,22},{16,8},{18,10},{20,12},{22,14},{9,1... | collective-permute-start | bytes 4718600 | tf_op jit(solution)/shard_map/ppermute | solution.py:633
  261.4 40.2 %collective-permute-start.46 = (bf16[512,1536]{1,0:T(8,128)(2,1)}, bf16[512,1536]{1,0:T(8,128)(2,1)S(1)}, u32[]{:S(2)}, u32[]{:S(2)}) collective-permute-start(bf16[512,1536]{1,0:T(8,128)(2,1)} %collective-permute-done.42), channel_id=1, source_target_pairs={{16,24},{18,26},{20,28},{22,30},{8,0},{10,2},{12,4},{14,6},{17,25}... | collective-permute-start | bytes 4718600 | tf_op jit(solution)/shard_map/ppermute | solution.py:633
  301.6 38.3 %collective-permute-start.47 = (bf16[512,1536]{1,0:T(8,128)(2,1)S(1)}, bf16[512,1536]{1,0:T(8,128)(2,1)S(1)}, u32[]{:S(2)}, u32[]{:S(2)}) collective-permute-start(bf16[512,1536]{1,0:T(8,128)(2,1)S(1)} %collective-permute-done.45), channel_id=1, source_target_pairs={{16,24},{18,26},{20,28},{22,30},{8,0},{10,2},{12,4},{14,6},{17,25}... | collective-permute-start | bytes 4718600 | tf_op jit(solution)/shard_map/ppermute | solution.py:633
  339.9 38.1 %collective-permute-start.48 = (bf16[512,1536]{1,0:T(8,128)(2,1)S(1)}, bf16[512,1536]{1,0:T(8,128)(2,1)S(1)}, u32[]{:S(2)}, u32[]{:S(2)}) collective-permute-start(bf16[512,1536]{1,0:T(8,128)(2,1)S(1)} %copy-done.14), channel_id=1, source_target_pairs={{0,8},{2,10},{4,12},{6,14},{1,9},{3,11},{5,13},{7,15}} | collective-permute-start | bytes 4718600 | tf_op jit(solution)/shard_map/ppermute | solution.py:633
  343.2 34.8 %collective-permute-start.49 = (bf16[512,1536]{1,0:T(8,128)(2,1)S(1)}, bf16[512,1536]{1,0:T(8,128)(2,1)S(1)}, u32[]{:S(2)}, u32[]{:S(2)}) collective-permute-start(bf16[512,1536]{1,0:T(8,128)(2,1)S(1)} %copy-done.13), channel_id=1, source_target_pairs={{24,16},{26,18},{28,20},{30,22},{25,17},{27,19},{29,21},{31,23}} | collective-permute-start | bytes 4718600 | tf_op jit(solution)/shard_map/ppermute | solution.py:633
  380.4 42.3 %collective-permute-start.53 = (bf16[512,1536]{1,0:T(8,128)(2,1)S(1)}, bf16[512,1536]{1,0:T(8,128)(2,1)S(1)}, u32[]{:S(2)}, u32[]{:S(2)}) collective-permute-start(bf16[512,1536]{1,0:T(8,128)(2,1)S(1)} %shard_map.242), channel_id=1, source_target_pairs={{8,16},{10,18},{12,20},{14,22},{16,8},{18,10},{20,12},{22,14},{9,1... | collective-permute-start | bytes 4718600 | tf_op jit(solution)/shard_map/ppermute | solution.py:633
  381.1 41.5 %collective-permute-start.54 = (bf16[512,1536]{1,0:T(8,128)(2,1)S(1)}, bf16[512,1536]{1,0:T(8,128)(2,1)S(1)}, u32[]{:S(2)}, u32[]{:S(2)}) collective-permute-start(bf16[512,1536]{1,0:T(8,128)(2,1)S(1)} %shard_map.242), channel_id=1, source_target_pairs={{0,8},{2,10},{4,12},{6,14},{24,16},{26,18},{28,20},{30,22},{1,9},{... | collective-permute-start | bytes 4718600 | tf_op jit(solution)/shard_map/ppermute | solution.py:633
  391.3 31.4 %collective-permute-start.51 = (bf16[128,2048]{1,0:T(8,128)(2,1)}, bf16[128,2048]{1,0:T(8,128)(2,1)S(1)}, u32[]{:S(2)}, u32[]{:S(2)}) collective-permute-start(bf16[128,2048]{1,0:T(8,128)(2,1)} %get-tuple-element.570), channel_id=1, source_target_pairs={{0,2},{2,0},{4,6},{6,4},{8,10},{10,8},{12,14},{14,12},{16,18},{18,... | collective-permute-start | bytes 1572872 | tf_op jit(solution)/shard_map/ppermute | solution.py:625
  391.8 30.9 %collective-permute-start.52 = (bf16[128,2048]{1,0:T(8,128)(2,1)}, bf16[128,2048]{1,0:T(8,128)(2,1)S(1)}, u32[]{:S(2)}, u32[]{:S(2)}) collective-permute-start(bf16[128,2048]{1,0:T(8,128)(2,1)} %get-tuple-element.569), channel_id=1, source_target_pairs={{0,4},{2,6},{4,0},{6,2},{8,12},{10,14},{12,8},{14,10},{16,20},{18,... | collective-permute-start | bytes 1572872 | tf_op jit(solution)/shard_map/ppermute | solution.py:625
  422.7 32.9 %collective-permute-start.57 = (bf16[1024,2048]{1,0:T(8,128)(2,1)}, bf16[1024,2048]{1,0:T(8,128)(2,1)}, u32[]{:S(2)}, u32[]{:S(2)}) collective-permute-start(bf16[1024,2048]{1,0:T(8,128)(2,1)} %get-tuple-element.405), channel_id=1, source_target_pairs={{0,1},{1,0},{2,3},{3,2},{4,5},{5,4},{6,7},{7,6},{8,9},{9,8},{10,11... | collective-permute-start | bytes 12582920 | tf_op jit(solution)/shard_map/ppermute | solution.py:607
  429.6 24.1 %collective-permute-start.55 = (bf16[256,2048]{1,0:T(8,128)(2,1)}, bf16[256,2048]{1,0:T(8,128)(2,1)}, u32[]{:S(2)}, u32[]{:S(2)}) collective-permute-start(bf16[256,2048]{1,0:T(8,128)(2,1)} %pad_maximum_fusion.6), channel_id=1, source_target_pairs={{0,2},{2,0},{4,6},{6,4},{8,10},{10,8},{12,14},{14,12},{16,18},{18,... | collective-permute-start | bytes 3145736 | tf_op jit(solution)/shard_map/ppermute | solution.py:625
  431.8 23.8 %collective-permute-start.56 = (bf16[256,2048]{1,0:T(8,128)(2,1)}, bf16[256,2048]{1,0:T(8,128)(2,1)}, u32[]{:S(2)}, u32[]{:S(2)}) collective-permute-start(bf16[256,2048]{1,0:T(8,128)(2,1)} %pad_maximum_fusion.7), channel_id=1, source_target_pairs={{0,4},{2,6},{4,0},{6,2},{8,12},{10,14},{12,8},{14,10},{16,20},{18,... | collective-permute-start | bytes 3145736 | tf_op jit(solution)/shard_map/ppermute | solution.py:625
  437.0 34.6 %collective-permute-start.58 = (bf16[512,1536]{1,0:T(8,128)(2,1)S(1)}, bf16[512,1536]{1,0:T(8,128)(2,1)}, u32[]{:S(2)}, u32[]{:S(2)}) collective-permute-start(bf16[512,1536]{1,0:T(8,128)(2,1)S(1)} %get-tuple-element.420), channel_id=1, source_target_pairs={{0,8},{2,10},{4,12},{6,14},{8,0},{10,2},{12,4},{14,6},{16,24},{18,... | collective-permute-start | bytes 4718600 | tf_op jit(solution)/shard_map/ppermute | solution.py:633
  437.1 35.3 %collective-permute-start.59 = (bf16[512,1536]{1,0:T(8,128)(2,1)S(1)}, bf16[512,1536]{1,0:T(8,128)(2,1)}, u32[]{:S(2)}, u32[]{:S(2)}) collective-permute-start(bf16[512,1536]{1,0:T(8,128)(2,1)S(1)} %get-tuple-element.421), channel_id=1, source_target_pairs={{8,16},{10,18},{12,20},{14,22},{16,8},{18,10},{20,12},{22,14},{9,1... | collective-permute-start | bytes 4718600 | tf_op jit(solution)/shard_map/ppermute | solution.py:633
  460.2 42.9 %collective-permute-start.66 = (bf16[512,1536]{1,0:T(8,128)(2,1)S(1)}, bf16[512,1536]{1,0:T(8,128)(2,1)S(1)}, u32[]{:S(2)}, u32[]{:S(2)}) collective-permute-start(bf16[512,1536]{1,0:T(8,128)(2,1)S(1)} %copy-done.8), channel_id=1, source_target_pairs={{0,8},{2,10},{4,12},{6,14},{1,9},{3,11},{5,13},{7,15}} | collective-permute-start | bytes 4718600 | tf_op jit(solution)/shard_map/ppermute | solution.py:633
  471.6 31.4 %collective-permute-start.67 = (bf16[512,1536]{1,0:T(8,128)(2,1)S(1)}, bf16[512,1536]{1,0:T(8,128)(2,1)S(1)}, u32[]{:S(2)}, u32[]{:S(2)}) collective-permute-start(bf16[512,1536]{1,0:T(8,128)(2,1)S(1)} %copy-done.6), channel_id=1, source_target_pairs={{24,16},{26,18},{28,20},{30,22},{25,17},{27,19},{29,21},{31,23}} | collective-permute-start | bytes 4718600 | tf_op jit(solution)/shard_map/ppermute | solution.py:633
  475.9 22.3 %collective-permute-start.62 = (bf16[256,2048]{1,0:T(8,128)(2,1)S(1)}, bf16[256,2048]{1,0:T(8,128)(2,1)S(1)}, u32[]{:S(2)}, u32[]{:S(2)}) collective-permute-start(bf16[256,2048]{1,0:T(8,128)(2,1)S(1)} %get-tuple-element.523), channel_id=1, source_target_pairs={{0,2},{2,0},{4,6},{6,4},{8,10},{10,8},{12,14},{14,12},{16,18},{18,... | collective-permute-start | bytes 3145736 | tf_op jit(solution)/shard_map/ppermute | solution.py:625
  476.4 23.1 %collective-permute-start.63 = (bf16[256,2048]{1,0:T(8,128)(2,1)S(1)}, bf16[256,2048]{1,0:T(8,128)(2,1)S(1)}, u32[]{:S(2)}, u32[]{:S(2)}) collective-permute-start(bf16[256,2048]{1,0:T(8,128)(2,1)S(1)} %get-tuple-element.523), channel_id=1, source_target_pairs={{0,4},{2,6},{4,0},{6,2},{8,12},{10,14},{12,8},{14,10},{16,20},{18,... | collective-permute-start | bytes 3145736 | tf_op jit(solution)/shard_map/ppermute | solution.py:625
  514.4 48.9 %collective-permute-start.71 = (bf16[512,1536]{1,0:T(8,128)(2,1)S(1)}, bf16[512,1536]{1,0:T(8,128)(2,1)S(1)}, u32[]{:S(2)}, u32[]{:S(2)}) collective-permute-start(bf16[512,1536]{1,0:T(8,128)(2,1)S(1)} %shard_map.247), channel_id=1, source_target_pairs={{8,16},{10,18},{12,20},{14,22},{16,8},{18,10},{20,12},{22,14},{9,1... | collective-permute-start | bytes 4718600 | tf_op jit(solution)/shard_map/ppermute | solution.py:633
  515.1 48.2 %collective-permute-start.72 = (bf16[512,1536]{1,0:T(8,128)(2,1)S(1)}, bf16[512,1536]{1,0:T(8,128)(2,1)S(1)}, u32[]{:S(2)}, u32[]{:S(2)}) collective-permute-start(bf16[512,1536]{1,0:T(8,128)(2,1)S(1)} %shard_map.247), channel_id=1, source_target_pairs={{0,8},{2,10},{4,12},{6,14},{24,16},{26,18},{28,20},{30,22},{1,9},{... | collective-permute-start | bytes 4718600 | tf_op jit(solution)/shard_map/ppermute | solution.py:633
  522.5 40.8 %collective-permute-start.69 = (bf16[256,2048]{1,0:T(8,128)(2,1)S(1)}, bf16[256,2048]{1,0:T(8,128)(2,1)}, u32[]{:S(2)}, u32[]{:S(2)}) collective-permute-start(bf16[256,2048]{1,0:T(8,128)(2,1)S(1)} %pad_maximum_fusion.8), channel_id=1, source_target_pairs={{0,2},{2,0},{4,6},{6,4},{8,10},{10,8},{12,14},{14,12},{16,18},{18,... | collective-permute-start | bytes 3145736 | tf_op jit(solution)/shard_map/ppermute | solution.py:625
  523.1 40.1 %collective-permute-start.70 = (bf16[256,2048]{1,0:T(8,128)(2,1)}, bf16[256,2048]{1,0:T(8,128)(2,1)}, u32[]{:S(2)}, u32[]{:S(2)}) collective-permute-start(bf16[256,2048]{1,0:T(8,128)(2,1)} %pad_maximum_fusion.9), channel_id=1, source_target_pairs={{0,4},{2,6},{4,0},{6,2},{8,12},{10,14},{12,8},{14,10},{16,20},{18,... | collective-permute-start | bytes 3145736 | tf_op jit(solution)/shard_map/ppermute | solution.py:625
  524.9 38.4 %collective-permute-start.73 = (bf16[256,1536]{1,0:T(8,128)(2,1)}, bf16[256,1536]{1,0:T(8,128)(2,1)S(1)}, u32[]{:S(2)}, u32[]{:S(2)}) collective-permute-start(bf16[256,1536]{1,0:T(8,128)(2,1)} %pad_maximum_fusion.14), channel_id=1, source_target_pairs={{0,2},{2,0},{4,6},{6,4},{8,10},{10,8},{12,14},{14,12},{16,18},{18,... | collective-permute-start | bytes 2359304 | tf_op jit(solution)/shard_map/ppermute | solution.py:625
  567.6 36.3 %collective-permute-start.77 = (bf16[512,1536]{1,0:T(8,128)(2,1)}, bf16[512,1536]{1,0:T(8,128)(2,1)}, u32[]{:S(2)}, u32[]{:S(2)}) collective-permute-start(bf16[512,1536]{1,0:T(8,128)(2,1)} %get-tuple-element.463), channel_id=1, source_target_pairs={{0,8},{2,10},{4,12},{6,14},{8,0},{10,2},{12,4},{14,6},{16,24},{18,... | collective-permute-start | bytes 4718600 | tf_op jit(solution)/shard_map/ppermute | solution.py:633
  567.6 37.2 %collective-permute-start.78 = (bf16[512,1536]{1,0:T(8,128)(2,1)S(1)}, bf16[512,1536]{1,0:T(8,128)(2,1)}, u32[]{:S(2)}, u32[]{:S(2)}) collective-permute-start(bf16[512,1536]{1,0:T(8,128)(2,1)S(1)} %get-tuple-element.464), channel_id=1, source_target_pairs={{8,16},{10,18},{12,20},{14,22},{16,8},{18,10},{20,12},{22,14},{9,1... | collective-permute-start | bytes 4718600 | tf_op jit(solution)/shard_map/ppermute | solution.py:633
  590.1 25.8 %collective-permute-start.82 = (bf16[512,640]{1,0:T(8,128)(2,1)S(1)}, bf16[512,640]{1,0:T(8,128)(2,1)S(1)}, u32[]{:S(2)}, u32[]{:S(2)}) collective-permute-start(bf16[512,640]{1,0:T(8,128)(2,1)S(1)} %copy-done.74), channel_id=1, source_target_pairs={{0,8},{2,10},{4,12},{6,14},{1,9},{3,11},{5,13},{7,15}} | collective-permute-start | bytes 1966088 | tf_op jit(solution)/shard_map/ppermute | solution.py:633
  605.1 34.9 %collective-permute-start.80 = (bf16[256,2048]{1,0:T(8,128)(2,1)S(1)}, bf16[256,2048]{1,0:T(8,128)(2,1)S(1)}, u32[]{:S(2)}, u32[]{:S(2)}) collective-permute-start(bf16[256,2048]{1,0:T(8,128)(2,1)S(1)} %pad_maximum_fusion.10), channel_id=1, source_target_pairs={{0,2},{2,0},{4,6},{6,4},{8,10},{10,8},{12,14},{14,12},{16,18},{18,... | collective-permute-start | bytes 3145736 | tf_op jit(solution)/shard_map/ppermute | solution.py:625
  606.0 34.0 %collective-permute-start.81 = (bf16[256,2048]{1,0:T(8,128)(2,1)S(1)}, bf16[256,2048]{1,0:T(8,128)(2,1)S(1)}, u32[]{:S(2)}, u32[]{:S(2)}) collective-permute-start(bf16[256,2048]{1,0:T(8,128)(2,1)S(1)} %pad_maximum_fusion.11), channel_id=1, source_target_pairs={{0,4},{2,6},{4,0},{6,2},{8,12},{10,14},{12,8},{14,10},{16,20},{18,... | collective-permute-start | bytes 3145736 | tf_op jit(solution)/shard_map/ppermute | solution.py:625
  610.6 26.9 %collective-permute-start.86 = (bf16[128,1536]{1,0:T(8,128)(2,1)}, bf16[128,1536]{1,0:T(8,128)(2,1)S(1)}, u32[]{:S(2)}, u32[]{:S(2)}) collective-permute-start(bf16[128,1536]{1,0:T(8,128)(2,1)} %get-tuple-element.555), channel_id=1, source_target_pairs={{0,2},{2,0},{4,6},{6,4},{8,10},{10,8},{12,14},{14,12},{16,18},{18,... | collective-permute-start | bytes 1179656 | tf_op jit(solution)/shard_map/ppermute | solution.py:625
  648.2 22.8 %collective-permute-start.87 = (bf16[512,640]{1,0:T(8,128)(2,1)S(1)}, bf16[512,640]{1,0:T(8,128)(2,1)S(1)}, u32[]{:S(2)}, u32[]{:S(2)}) collective-permute-start(bf16[512,640]{1,0:T(8,128)(2,1)S(1)} %get-tuple-element.485), channel_id=1, source_target_pairs={{0,8},{2,10},{4,12},{6,14},{8,0},{10,2},{12,4},{14,6},{16,24},{18,... | collective-permute-start | bytes 1966088 | tf_op jit(solution)/shard_map/ppermute | solution.py:633
  (150 other events, 1918.6 us)

commit v7 on v6

--- a/solution.py
+++ b/solution.py
@@ -1073,7 +1073,6 @@
     back_1 = [back_1[0]] + back_got
     attn_grads = lines.flip_pieces(lines.row_pieces(attn_sum.total()))
     input_other = swap_cores(input_grad)
-    gains_got = [lines.turn(gains, k) for k in range(1, lines.length)]
     ffn_grads = run_place_columns(
         lines.place,
         [
@@ -1083,9 +1082,11 @@
         3,
     )
     input_grad = run_place_halves(core, lines.spot, lines.length, input_grad, input_other)
-    gains_got, attn_grads, input_grad = tie(gains_got, attn_grads, input_grad)
-    for one in gains_got:
-        gains = gains + one
+    bit = group
+    while bit < dp:
+        gains = gains + lines.flip(gains, bit)
+        bit *= 2
+    gains, attn_grads, ffn_grads = tie(gains, attn_grads, ffn_grads)
     gains = gains + swap_cores(gains)
 
     def columns_of(related, start, stop):

time: 704 us -> 702 us (level)
    ppermute x52 -> x54, starting transfers between devices: 43.1 us -> 47.2 us  [flip(): lax.ppermute(values, 'dp', [(i, i ^ relation) for i in range(self.dp)])]
    ppermute x52 -> x54, waiting for transfers between devices: 131 us -> 132 us  [flip(): lax.ppermute(values, 'dp', [(i, i ^ relation) for i in range(self.dp)])]
  transfers between devices with their start and end apart: 102 -> 101, of which waited for: 35 -> 35; matrix products, arithmetic and copies ran while one was open for 15% -> 15% of each run, Pallas kernels for 30% -> 30%
where the time goes in v7:
time: 702 us; the launch traced here: 695 us
  waiting for transfers between devices  213 us (30%)
  Pallas kernels  212 us (30%)
  starting transfers between devices  143 us (20%)
  other arithmetic  83.4 us (12%)
  local copies, waits for them, and re-layouts  40.1 us (6%)
    ppermute x54, waiting for transfers between devices, flip(): lax.ppermute(values, 'dp', [(i, i ^ relation) for i in range(self.dp)])  132 us
    ppermute x33, waiting for transfers between devices, ends(): return lax.ppermute(values, 'dp', pairs)  76.4 us
    ppermute x33, starting transfers between devices, ends(): return lax.ppermute(values, 'dp', pairs)  62.6 us
    pallas_call x2, Pallas kernels, run_ffn_units(): kernel_call(functools.partial(ffn_units, len(blocks), ff_sub, earlier), (...  49.8 us
    ppermute x54, starting transfers between devices, flip(): lax.ppermute(values, 'dp', [(i, i ^ relation) for i in range(self.dp)])  47.2 us
    pallas_call x2, Pallas kernels, run_weight_gradients(): kernel_call(functools.partial(weight_gradients, count, per), (model // ti...  34.6 us
    pallas_call x1, Pallas kernels, run_attention(): kernel_call(functools.partial(attention_backward, len(blocks), head_dim,...  34.2 us
    ppermute x14, starting transfers between devices, swap_cores(): return lax.ppermute(values, 'tensor', [(0, 1), (1, 0)])  33.4 us
  transfers between devices with their start and end apart: 101, of which 35 were waited for; matrix products, arithmetic and copies ran while one was open for 15% of the time, Pallas kernels for 30%

profile of v7, /device:TPU:1, one launch (start us, length us, event | category | flops | bytes accessed | tf_op | source)
XLA Modules:
  0.0 695.0 jit_solution(17322517072133622031)
XLA Ops:
  21.2 3.8 collective-permute-start.9
  27.0 5.6 multiply_sine_fusion
  32.6 5.7 collective-permute-done.5
  39.3 3.7 collective-permute-start.14
  62.8 7.3 %collective-permute-done.13 = bf16[512,640]{1,0:T(8,128)(2,1)} collective-permute-done((bf16[512,640]{1,0:T(8,128)(2,1)}, bf16[512,640]{1,0:T(8,128)(2,1)}, u32[]{:S(2)}, u32[]{:S(2)}) %collective-permute-start.13) | collective-permute-done | bytes 655392 | tf_op jit(solution)/shard_map/ppermute | solution.py:633
  81.4 3.6 pad_maximum_fusion.refs_1_.refs_4_
  85.7 7.9 %collective-permute-done.20 = bf16[128,1536]{1,0:T(8,128)(2,1)S(1)} collective-permute-done((bf16[128,1536]{1,0:T(8,128)(2,1)S(1)}, bf16[128,1536]{1,0:T(8,128)(2,1)S(1)}, u32[]{:S(2)}, u32[]{:S(2)}) %collective-permute-start.20) | collective-permute-done | bytes 393248 | tf_op jit(solution)/shard_map/ppermute | solution.py:625
  102.1 20.8 %shard_map.237 = (f32[4,512,384]{2,1,0:T(8,128)}, bf16[1024,256]{1,0:T(8,128)(2,1)S(1)}, bf16[1024,256]{1,0:T(8,128)(2,1)S(1)}, bf16[1024,2048]{1,0:T(8,128)(2,1)}, bf16[1024,2048]{1,0:T(8,128)(2,1)}) custom-call(bf16[1024,2048]{1,0:T(8,128)(2,1)} %constant_dynamic-update-slice_fusion.refs_0_.refs_3_, bf16[1024,2048]{1,0:T(8,128)(2,1)} %pad_maximum_fusion.refs_1_.refs_4_, ...), custom_call_target="tpu_custom_call" | custom-call | flops 32212254720 | bytes 33554432 | tf_op jit(solution)/shard_map/pallas_call | solution.py:329
  123.0 5.7 collective-permute-done.21
  135.2 9.6 %collective-permute-done.26 = bf16[128,2048]{1,0:T(8,128)(2,1)S(1)} collective-permute-done((bf16[128,2048]{1,0:T(8,128)(2,1)S(1)}, bf16[128,2048]{1,0:T(8,128)(2,1)S(1)}, u32[]{:S(2)}, u32[]{:S(2)}) %collective-permute-start.26) | collective-permute-done | bytes 524320 | tf_op jit(solution)/shard_map/ppermute | solution.py:625
  144.9 3.1 convert_add_fusion.10
  151.5 23.9 %collective-permute-done.31 = bf16[512,1536]{1,0:T(8,128)(2,1)S(1)} collective-permute-done((bf16[512,1536]{1,0:T(8,128)(2,1)}, bf16[512,1536]{1,0:T(8,128)(2,1)S(1)}, u32[]{:S(2)}, u32[]{:S(2)}) %collective-permute-start.31) | collective-permute-done | bytes 1572896 | tf_op jit(solution)/shard_map/ppermute | solution.py:633
  179.9 19.1 %collective-permute-done.33 = bf16[256,2048]{1,0:T(8,128)(2,1)S(1)} collective-permute-done((bf16[256,2048]{1,0:T(8,128)(2,1)S(1)}, bf16[256,2048]{1,0:T(8,128)(2,1)S(1)}, u32[]{:S(2)}, u32[]{:S(2)}) %collective-permute-start.33) | collective-permute-done | bytes 1048608 | tf_op jit(solution)/shard_map/ppermute | solution.py:625
  202.4 13.4 %collective-permute-done.36 = bf16[256,1536]{1,0:T(8,128)(2,1)S(1)} collective-permute-done((bf16[256,1536]{1,0:T(8,128)(2,1)S(1)}, bf16[256,1536]{1,0:T(8,128)(2,1)S(1)}, u32[]{:S(2)}, u32[]{:S(2)}) %collective-permute-start.36) | collective-permute-done | bytes 786464 | tf_op jit(solution)/shard_map/ppermute | solution.py:625
  224.8 18.6 %collective-permute-done.37 = bf16[256,2048]{1,0:T(8,128)(2,1)S(1)} collective-permute-done((bf16[256,2048]{1,0:T(8,128)(2,1)S(1)}, bf16[256,2048]{1,0:T(8,128)(2,1)S(1)}, u32[]{:S(2)}, u32[]{:S(2)}) %collective-permute-start.37) | collective-permute-done | bytes 1048608 | tf_op jit(solution)/shard_map/ppermute | solution.py:625
  244.8 3.8 select_select_fusion.2
  248.6 6.1 collective-permute-done.39
  263.2 4.4 collective-permute-done.44.refs_1_
  267.6 19.5 %shard_map.238 = (bf16[1024,512]{1,0:T(8,128)(2,1)S(1)}, bf16[1024,512]{1,0:T(8,128)(2,1)}, bf16[1024,1024]{1,0:T(8,128)(2,1)}, bf16[1024,1024]{1,0:T(8,128)(2,1)}) custom-call(bf16[1024,2048]{1,0:T(8,128)(2,1)} %copy-done.44, bf16[1024,2048]{1,0:T(8,128)(2,1)} %collective-permute-done.44.refs_1_, bf16[1024,2048]{1,0:T(8,128)(2,1)} %copy-done.45, ...), custom_call_target="tpu_custom_call" | custom-call | flops 12884901888 | bytes 16777216 | tf_op jit(solution)/shard_map/pallas_call | solution.py:394
  287.1 14.5 %collective-permute-done.46 = bf16[512,1536]{1,0:T(8,128)(2,1)S(1)} collective-permute-done((bf16[512,1536]{1,0:T(8,128)(2,1)}, bf16[512,1536]{1,0:T(8,128)(2,1)S(1)}, u32[]{:S(2)}, u32[]{:S(2)}) %collective-permute-start.46) | collective-permute-done | bytes 1572896 | tf_op jit(solution)/shard_map/ppermute | solution.py:633
  302.9 13.0 %shard_map.240 = (bf16[1024,2048]{1,0:T(8,128)(2,1)}, bf16[1024,2048]{1,0:T(8,128)(2,1)}) custom-call(bf16[1024,1024]{1,0:T(8,128)(2,1)} %get-tuple-element.357.refs_4_.refs_0_, bf16[1024,1024]{1,0:T(8,128)(2,1)} %get-tuple-element.358.refs_5_.refs_1_, bf16[512,1536]{1,0:T(8,128)(2,1)S(1)} %copy-done.3, ...), custom_call_target="tpu_custom_call" | custom-call | flops 1073741824 | bytes 2097152 | tf_op jit(solution)/shard_map/pallas_call | solution.py:507
  316.0 21.0 %shard_map.239 = (bf16[512,1536]{1,0:T(8,128)(2,1)}, bf16[512,1536]{1,0:T(8,128)(2,1)}, bf16[512,1536]{1,0:T(8,128)(2,1)}, bf16[512,1536]{1,0:T(8,128)(2,1)}) custom-call(bf16[1024,2048]{1,0:T(8,128)(2,1)} %copy-done.44, bf16[1024,2048]{1,0:T(8,128)(2,1)} %collective-permute-done.44.refs_1_, bf16[1024,2048]{1,0:T(8,128)(2,1)} %copy-done.45, ...), custom_call_target="tpu_custom_call" | custom-call | flops 1073741824 | bytes 2097152 | tf_op jit(solution)/shard_map/pallas_call | solution.py:432
  339.9 3.2 collective-permute-start.48
  344.0 3.8 select_select_fusion
  347.7 30.2 %shard_map.241 = (bf16[1024,512]{1,0:T(8,128)(2,1)S(1)}, bf16[1024,512]{1,0:T(8,128)(2,1)}, bf16[1024,1024]{1,0:T(8,128)(2,1)}, bf16[1024,1024]{1,0:T(8,128)(2,1...) custom-call(bf16[1024,2048]{1,0:T(8,128)(2,1)} %copy-done.44, ...), custom_call_target="tpu_custom_call" | custom-call | flops 12884901888 | bytes 16777216 | tf_op jit(solution)/shard_map/pallas_call | solution.py:394
  381.1 5.7 collective-permute-start.54
  386.9 3.3 convert_add_fusion.6
  393.0 15.1 %shard_map.243 = (bf16[512,1536]{1,0:T(8,128)(2,1)S(1)}, bf16[512,1536]{1,0:T(8,128)(2,1)}, bf16[512,1536]{1,0:T(8,128)(2,1)}, bf16[512,1536]{1,0:T(8,128)(2,1)}) custom-call(bf16[1024,2048]{1,0:T(8,128)(2,1)} %copy-done.44, bf16[1024,2048]{1,0:T(8,128)(2,1)} %collective-permute-done.44.refs_1_, bf16[1024,1024]{1,0:T(8,128)(2,1)} %get-tuple-element.390.refs_2_, ...), custom_call_target="tpu_custom_call" | custom-call | flops 536870912 | bytes 1048576 | tf_op jit(solution)/shard_map/pallas_call | solution.py:465
  409.3 13.4 %shard_map.244 = (bf16[1024,2048]{1,0:T(8,128)(2,1)}, bf16[1024,2048]{1,0:T(8,128)(2,1)}) custom-call(bf16[1024,512]{1,0:T(8,128)(2,1)S(1)} %get-tuple-element.396.refs_6_.refs_0_, bf16[1024,512]{1,0:T(8,128)(2,1)} %get-tuple-element.397.refs_7_.refs_1_, bf16[1024,512]{1,0:T(8,128)(2,1)} %copy-done.9, bf16[1024,512]{1,0:T(8,128)(2,1)} %get-tuple-element.407.refs_3_, ...), custom_call_target="tpu_custom_call" | custom-call | flops 1073741824 | bytes 2097152 | tf_op jit(solution)/shard_map/pallas_call | solution.py:507
  438.9 10.8 %shard_map.245 = (bf16[512,1536]{1,0:T(8,128)(2,1)}, bf16[512,1536]{1,0:T(8,128)(2,1)}, bf16[512,1536]{1,0:T(8,128)(2,1)}, bf16[512,1536]{1,0:T(8,128)(2,1)}) custom-call(bf16[1024,2048]{1,0:T(8,128)(2,1)} %copy-done.45, bf16[1024,2048]{1,0:T(8,128)(2,1)} %copy-done.48, ...), custom_call_target="tpu_custom_call", output_to_operand_aliasing={{0}: (4, {}), {1}: (5, {}), {2}: (6, {}), {3}: (7, {})} | custom-call | flops 536870912 | bytes 1048576 | tf_op jit(solution)/shard_map/pallas_call | solution.py:465
  449.6 4.0 collective-permute-done.55
  455.6 3.2 convert_add_fusion.3
  465.8 5.8 collective-permute-done.58
  481.6 16.5 %collective-permute-done.62 = bf16[256,2048]{1,0:T(8,128)(2,1)S(1)} collective-permute-done((bf16[256,2048]{1,0:T(8,128)(2,1)S(1)}, bf16[256,2048]{1,0:T(8,128)(2,1)S(1)}, u32[]{:S(2)}, u32[]{:S(2)}) %collective-permute-start.62) | collective-permute-done | bytes 1048608 | tf_op jit(solution)/shard_map/ppermute | solution.py:625
  503.7 5.9 collective-permute-done.64
  510.0 4.4 collective-permute-start.68
  515.1 7.4 %collective-permute-start.72 = (bf16[512,1536]{1,0:T(8,128)(2,1)S(1)}, bf16[512,1536]{1,0:T(8,128)(2,1)S(1)}, u32[]{:S(2)}, u32[]{:S(2)}) collective-permute-start(bf16[512,1536]{1,0:T(8,128)(2,1)S(1)} %shard_map.247), channel_id=1, source_target_pairs={{0,8},{2,10},{4,12},{6,14},{24,16},{26,18},{28,20},{30,22},{1,9},{... | collective-permute-start | bytes 4718600 | tf_op jit(solution)/shard_map/ppermute | solution.py:633
  526.9 34.2 %shard_map.248 = (bf16[1024,384]{1,0:T(8,128)(2,1)}, bf16[1024,384]{1,0:T(8,128)(2,1)}, f32[2,256]{1,0:T(2,128)S(1)}, bf16[1024,2048]{1,0:T(8,128)(2,1)}, bf16[1...) custom-call(bf16[1024,2048]{1,0:T(8,128)(2,1)} %copy-done.50, bf16[1024,2048]{1,0:T(8,128)(2,1)} %copy-done.54, ...), custom_call_target="tpu_custom_call" | custom-call | flops 32212254720 | bytes 33554432 | tf_op jit(solution)/shard_map/pallas_call | solution.py:339
  570.2 13.6 %shard_map.249 = (bf16[512,640]{1,0:T(8,128)(2,1)S(1)}, bf16[512,640]{1,0:T(8,128)(2,1)}, bf16[512,640]{1,0:T(8,128)(2,1)}, bf16[512,640]{1,0:T(8,128)(2,1)}) custom-call(bf16[1024,2048]{1,0:T(8,128)(2,1)} %constant_dynamic-update-slice_fusion.refs_0_.refs_3_, bf16[1024,2048]{1,0:T(8,128)(2,1)} %pad_maximum_fusion.refs_1_.refs_4_, ...), custom_call_target="tpu_custom_call" | custom-call | flops 1073741824 | bytes 2097152 | tf_op jit(solution)/shard_map/pallas_call | solution.py:432
  583.8 4.4 convert_add_fusion.1
  590.1 3.4 collective-permute-start.82
  593.5 10.4 %collective-permute-done.77 = bf16[512,1536]{1,0:T(8,128)(2,1)} collective-permute-done((bf16[512,1536]{1,0:T(8,128)(2,1)}, bf16[512,1536]{1,0:T(8,128)(2,1)}, u32[]{:S(2)}, u32[]{:S(2)}) %collective-permute-start.77) | collective-permute-done | bytes 1572896 | tf_op jit(solution)/shard_map/ppermute | solution.py:633
  611.1 4.8 collective-permute-done.82.second
  618.9 9.0 %collective-permute-start.85 = (bf16[512,640]{1,0:T(8,128)(2,1)S(1)}, bf16[512,640]{1,0:T(8,128)(2,1)S(1)}, u32[]{:S(2)}, u32[]{:S(2)}) collective-permute-start(bf16[512,640]{1,0:T(8,128)(2,1)S(1)} %shard_map.251), channel_id=1, source_target_pairs={{0,8},{2,10},{4,12},{6,14},{24,16},{26,18},{28,20},{30,22},{1,9},{... | collective-permute-start | bytes 1966088 | tf_op jit(solution)/shard_map/ppermute | solution.py:633
  630.8 6.7 collective-permute-done.86.refs_5_
  656.8 6.3 collective-permute-done.92
  666.1 4.8 shard_map.253
  691.3 3.2 shard_map.254
  (541 shorter events, 224.2 us)
Async XLA Ops:
  16.3 22.0 %collective-permute-start.5 = (bf16[256,2048]{1,0:T(8,128)(2,1)S(1)}, bf16[256,2048]{1,0:T(8,128)(2,1)}, u32[]{:S(2)}, u32[]{:S(2)}) collective-permute-start(bf16[256,2048]{1,0:T(8,128)(2,1)S(1)} %fusion.2), channel_id=1, source_target_pairs={{0,2},{2,0},{4,6},{6,4},{8,10},{10,8},{12,14},{14,12},{16,18},{18,... | collective-permute-start | bytes 3145736 | tf_op jit(solution)/shard_map/ppermute | solution.py:625
  17.3 22.0 %collective-permute-start.6 = (bf16[256,2048]{1,0:T(8,128)(2,1)S(1)}, bf16[256,2048]{1,0:T(8,128)(2,1)}, u32[]{:S(2)}, u32[]{:S(2)}) collective-permute-start(bf16[256,2048]{1,0:T(8,128)(2,1)S(1)} %fusion.2), channel_id=1, source_target_pairs={{0,4},{2,6},{4,0},{6,2},{8,12},{10,14},{12,8},{14,10},{16,20},{18,... | collective-permute-start | bytes 3145736 | tf_op jit(solution)/shard_map/ppermute | solution.py:625
  93.9 34.7 %collective-permute-start.21 = (bf16[512,1536]{1,0:T(8,128)(2,1)S(1)}, bf16[512,1536]{1,0:T(8,128)(2,1)}, u32[]{:S(2)}, u32[]{:S(2)}) collective-permute-start(bf16[512,1536]{1,0:T(8,128)(2,1)S(1)} %pad_maximum_fusion.1.refs_4_.refs_2_), channel_id=1, source_target_pairs={{0,8},{2,10},{4,12},{6,14},{8,0},{10,2},{12,4},{14,6},{16,24},{18,... | collective-permute-start | bytes 4718600 | tf_op jit(solution)/shard_map/ppermute | solution.py:633
  95.8 32.8 %collective-permute-start.22 = (bf16[512,1536]{1,0:T(8,128)(2,1)S(1)}, bf16[512,1536]{1,0:T(8,128)(2,1)}, u32[]{:S(2)}, u32[]{:S(2)}) collective-permute-start(bf16[512,1536]{1,0:T(8,128)(2,1)S(1)} %pad_maximum_fusion.1.refs_4_.refs_2_), channel_id=1, source_target_pairs={{8,16},{10,18},{12,20},{14,22},{16,8},{18,10},{20,12},{22,14},{9,1... | collective-permute-start | bytes 4718600 | tf_op jit(solution)/shard_map/ppermute | solution.py:633
  97.8 25.2 %collective-permute-start.23 = (bf16[256,2048]{1,0:T(8,128)(2,1)S(1)}, bf16[256,2048]{1,0:T(8,128)(2,1)S(1)}, u32[]{:S(2)}, u32[]{:S(2)}) collective-permute-start(bf16[256,2048]{1,0:T(8,128)(2,1)S(1)} %fusion.17), channel_id=1, source_target_pairs={{0,2},{2,0},{4,6},{6,4},{8,10},{10,8},{12,14},{14,12},{16,18},{18,... | collective-permute-start | bytes 3145736 | tf_op jit(solution)/shard_map/ppermute | solution.py:625
  98.4 24.6 %collective-permute-start.24 = (bf16[256,2048]{1,0:T(8,128)(2,1)S(1)}, bf16[256,2048]{1,0:T(8,128)(2,1)S(1)}, u32[]{:S(2)}, u32[]{:S(2)}) collective-permute-start(bf16[256,2048]{1,0:T(8,128)(2,1)S(1)} %fusion.17), channel_id=1, source_target_pairs={{0,4},{2,6},{4,0},{6,2},{8,12},{10,14},{12,8},{14,10},{16,20},{18,... | collective-permute-start | bytes 3145736 | tf_op jit(solution)/shard_map/ppermute | solution.py:625
  133.9 41.4 %collective-permute-start.31 = (bf16[512,1536]{1,0:T(8,128)(2,1)}, bf16[512,1536]{1,0:T(8,128)(2,1)S(1)}, u32[]{:S(2)}, u32[]{:S(2)}) collective-permute-start(bf16[512,1536]{1,0:T(8,128)(2,1)} %collective-permute-done.22), channel_id=1, source_target_pairs={{16,24},{18,26},{20,28},{22,30},{8,0},{10,2},{12,4},{14,6},{17,25}... | collective-permute-start | bytes 4718600 | tf_op jit(solution)/shard_map/ppermute | solution.py:633
  148.1 27.2 %collective-permute-start.27 = (bf16[128,2048]{1,0:T(8,128)(2,1)S(1)}, bf16[128,2048]{1,0:T(8,128)(2,1)S(1)}, u32[]{:S(2)}, u32[]{:S(2)}) collective-permute-start(bf16[128,2048]{1,0:T(8,128)(2,1)S(1)} %get-tuple-element.572), channel_id=1, source_target_pairs={{0,2},{2,0},{4,6},{6,4},{8,10},{10,8},{12,14},{14,12},{16,18},{18,... | collective-permute-start | bytes 1572872 | tf_op jit(solution)/shard_map/ppermute | solution.py:625
  148.7 26.6 %collective-permute-start.28 = (bf16[128,2048]{1,0:T(8,128)(2,1)S(1)}, bf16[128,2048]{1,0:T(8,128)(2,1)S(1)}, u32[]{:S(2)}, u32[]{:S(2)}) collective-permute-start(bf16[128,2048]{1,0:T(8,128)(2,1)S(1)} %get-tuple-element.571), channel_id=1, source_target_pairs={{0,4},{2,6},{4,0},{6,2},{8,12},{10,14},{12,8},{14,10},{16,20},{18,... | collective-permute-start | bytes 1572872 | tf_op jit(solution)/shard_map/ppermute | solution.py:625
  175.6 23.3 %collective-permute-start.33 = (bf16[256,2048]{1,0:T(8,128)(2,1)S(1)}, bf16[256,2048]{1,0:T(8,128)(2,1)S(1)}, u32[]{:S(2)}, u32[]{:S(2)}) collective-permute-start(bf16[256,2048]{1,0:T(8,128)(2,1)S(1)} %pad_maximum_fusion.5), channel_id=1, source_target_pairs={{0,4},{2,6},{4,0},{6,2},{8,12},{10,14},{12,8},{14,10},{16,20},{18,... | collective-permute-start | bytes 3145736 | tf_op jit(solution)/shard_map/ppermute | solution.py:625
  176.2 23.0 %collective-permute-start.32 = (bf16[256,2048]{1,0:T(8,128)(2,1)S(1)}, bf16[256,2048]{1,0:T(8,128)(2,1)S(1)}, u32[]{:S(2)}, u32[]{:S(2)}) collective-permute-start(bf16[256,2048]{1,0:T(8,128)(2,1)S(1)} %pad_maximum_fusion.4), channel_id=1, source_target_pairs={{0,2},{2,0},{4,6},{6,4},{8,10},{10,8},{12,14},{14,12},{16,18},{18,... | collective-permute-start | bytes 3145736 | tf_op jit(solution)/shard_map/ppermute | solution.py:625
  177.2 38.6 %collective-permute-start.34 = (bf16[512,1536]{1,0:T(8,128)(2,1)S(1)}, bf16[512,1536]{1,0:T(8,128)(2,1)S(1)}, u32[]{:S(2)}, u32[]{:S(2)}) collective-permute-start(bf16[512,1536]{1,0:T(8,128)(2,1)S(1)} %collective-permute-done.30), channel_id=1, source_target_pairs={{16,24},{18,26},{20,28},{22,30},{8,0},{10,2},{12,4},{14,6},{17,25}... | collective-permute-start | bytes 4718600 | tf_op jit(solution)/shard_map/ppermute | solution.py:633
  178.6 37.2 %collective-permute-start.36 = (bf16[256,1536]{1,0:T(8,128)(2,1)S(1)}, bf16[256,1536]{1,0:T(8,128)(2,1)S(1)}, u32[]{:S(2)}, u32[]{:S(2)}) collective-permute-start(bf16[256,1536]{1,0:T(8,128)(2,1)S(1)} %pad_maximum_fusion.13), channel_id=1, source_target_pairs={{0,4},{2,6},{4,0},{6,2},{8,12},{10,14},{12,8},{14,10},{16,20},{18,... | collective-permute-start | bytes 2359304 | tf_op jit(solution)/shard_map/ppermute | solution.py:625
  215.9 39.7 %collective-permute-start.43 = (bf16[1024,2048]{1,0:T(8,128)(2,1)S(1)}, bf16[1024,2048]{1,0:T(8,128)(2,1)S(1)}, u32[]{:S(2)}, u32[]{:S(2)}) collective-permute-start(bf16[1024,2048]{1,0:T(8,128)(2,1)S(1)} %constant_dynamic-update-slice_fusion.5.refs_2_.refs_0_), channel_id=1, source_target_pairs={{0,1},{1,0},{2,3},{3,2},{4,5},{5,4},{6,7},{7,6},{8,9},{9,8},{10,11... | collective-permute-start | bytes 12582920 | tf_op jit(solution)/shard_map/ppermute | solution.py:607
  220.1 23.3 %collective-permute-start.37 = (bf16[256,2048]{1,0:T(8,128)(2,1)S(1)}, bf16[256,2048]{1,0:T(8,128)(2,1)S(1)}, u32[]{:S(2)}, u32[]{:S(2)}) collective-permute-start(bf16[256,2048]{1,0:T(8,128)(2,1)S(1)} %get-tuple-element.526), channel_id=1, source_target_pairs={{0,2},{2,0},{4,6},{6,4},{8,10},{10,8},{12,14},{14,12},{16,18},{18,... | collective-permute-start | bytes 3145736 | tf_op jit(solution)/shard_map/ppermute | solution.py:625
  221.0 23.0 %collective-permute-start.38 = (bf16[256,2048]{1,0:T(8,128)(2,1)S(1)}, bf16[256,2048]{1,0:T(8,128)(2,1)S(1)}, u32[]{:S(2)}, u32[]{:S(2)}) collective-permute-start(bf16[256,2048]{1,0:T(8,128)(2,1)S(1)} %get-tuple-element.526), channel_id=1, source_target_pairs={{0,4},{2,6},{4,0},{6,2},{8,12},{10,14},{12,8},{14,10},{16,20},{18,... | collective-permute-start | bytes 3145736 | tf_op jit(solution)/shard_map/ppermute | solution.py:625
  221.5 34.0 %collective-permute-start.41 = (bf16[512,1536]{1,0:T(8,128)(2,1)S(1)}, bf16[512,1536]{1,0:T(8,128)(2,1)}, u32[]{:S(2)}, u32[]{:S(2)}) collective-permute-start(bf16[512,1536]{1,0:T(8,128)(2,1)S(1)} %pad_maximum_fusion.2.refs_4_.refs_8_), channel_id=1, source_target_pairs={{0,8},{2,10},{4,12},{6,14},{8,0},{10,2},{12,4},{14,6},{16,24},{18,... | collective-permute-start | bytes 4718600 | tf_op jit(solution)/shard_map/ppermute | solution.py:633
  221.6 34.0 %collective-permute-start.42 = (bf16[512,1536]{1,0:T(8,128)(2,1)S(1)}, bf16[512,1536]{1,0:T(8,128)(2,1)}, u32[]{:S(2)}, u32[]{:S(2)}) collective-permute-start(bf16[512,1536]{1,0:T(8,128)(2,1)S(1)} %pad_maximum_fusion.2.refs_4_.refs_8_), channel_id=1, source_target_pairs={{8,16},{10,18},{12,20},{14,22},{16,8},{18,10},{20,12},{22,14},{9,1... | collective-permute-start | bytes 4718600 | tf_op jit(solution)/shard_map/ppermute | solution.py:633
  260.6 26.5 %collective-permute-start.45 = (bf16[512,1536]{1,0:T(8,128)(2,1)}, bf16[512,1536]{1,0:T(8,128)(2,1)S(1)}, u32[]{:S(2)}, u32[]{:S(2)}) collective-permute-start(bf16[512,1536]{1,0:T(8,128)(2,1)} %collective-permute-done.41), channel_id=1, source_target_pairs={{8,16},{10,18},{12,20},{14,22},{16,8},{18,10},{20,12},{22,14},{9,1... | collective-permute-start | bytes 4718600 | tf_op jit(solution)/shard_map/ppermute | solution.py:633
  261.4 40.2 %collective-permute-start.46 = (bf16[512,1536]{1,0:T(8,128)(2,1)}, bf16[512,1536]{1,0:T(8,128)(2,1)S(1)}, u32[]{:S(2)}, u32[]{:S(2)}) collective-permute-start(bf16[512,1536]{1,0:T(8,128)(2,1)} %collective-permute-done.42), channel_id=1, source_target_pairs={{16,24},{18,26},{20,28},{22,30},{8,0},{10,2},{12,4},{14,6},{17,25}... | collective-permute-start | bytes 4718600 | tf_op jit(solution)/shard_map/ppermute | solution.py:633
  301.6 38.3 %collective-permute-start.47 = (bf16[512,1536]{1,0:T(8,128)(2,1)S(1)}, bf16[512,1536]{1,0:T(8,128)(2,1)S(1)}, u32[]{:S(2)}, u32[]{:S(2)}) collective-permute-start(bf16[512,1536]{1,0:T(8,128)(2,1)S(1)} %collective-permute-done.45), channel_id=1, source_target_pairs={{16,24},{18,26},{20,28},{22,30},{8,0},{10,2},{12,4},{14,6},{17,25}... | collective-permute-start | bytes 4718600 | tf_op jit(solution)/shard_map/ppermute | solution.py:633
  339.9 38.1 %collective-permute-start.48 = (bf16[512,1536]{1,0:T(8,128)(2,1)S(1)}, bf16[512,1536]{1,0:T(8,128)(2,1)S(1)}, u32[]{:S(2)}, u32[]{:S(2)}) collective-permute-start(bf16[512,1536]{1,0:T(8,128)(2,1)S(1)} %copy-done.14), channel_id=1, source_target_pairs={{0,8},{2,10},{4,12},{6,14},{1,9},{3,11},{5,13},{7,15}} | collective-permute-start | bytes 4718600 | tf_op jit(solution)/shard_map/ppermute | solution.py:633
  343.2 34.8 %collective-permute-start.49 = (bf16[512,1536]{1,0:T(8,128)(2,1)S(1)}, bf16[512,1536]{1,0:T(8,128)(2,1)S(1)}, u32[]{:S(2)}, u32[]{:S(2)}) collective-permute-start(bf16[512,1536]{1,0:T(8,128)(2,1)S(1)} %copy-done.13), channel_id=1, source_target_pairs={{24,16},{26,18},{28,20},{30,22},{25,17},{27,19},{29,21},{31,23}} | collective-permute-start | bytes 4718600 | tf_op jit(solution)/shard_map/ppermute | solution.py:633
  380.3 42.3 %collective-permute-start.53 = (bf16[512,1536]{1,0:T(8,128)(2,1)S(1)}, bf16[512,1536]{1,0:T(8,128)(2,1)S(1)}, u32[]{:S(2)}, u32[]{:S(2)}) collective-permute-start(bf16[512,1536]{1,0:T(8,128)(2,1)S(1)} %shard_map.242), channel_id=1, source_target_pairs={{8,16},{10,18},{12,20},{14,22},{16,8},{18,10},{20,12},{22,14},{9,1... | collective-permute-start | bytes 4718600 | tf_op jit(solution)/shard_map/ppermute | solution.py:633
  381.1 41.6 %collective-permute-start.54 = (bf16[512,1536]{1,0:T(8,128)(2,1)S(1)}, bf16[512,1536]{1,0:T(8,128)(2,1)S(1)}, u32[]{:S(2)}, u32[]{:S(2)}) collective-permute-start(bf16[512,1536]{1,0:T(8,128)(2,1)S(1)} %shard_map.242), channel_id=1, source_target_pairs={{0,8},{2,10},{4,12},{6,14},{24,16},{26,18},{28,20},{30,22},{1,9},{... | collective-permute-start | bytes 4718600 | tf_op jit(solution)/shard_map/ppermute | solution.py:633
  391.3 31.4 %collective-permute-start.51 = (bf16[128,2048]{1,0:T(8,128)(2,1)}, bf16[128,2048]{1,0:T(8,128)(2,1)S(1)}, u32[]{:S(2)}, u32[]{:S(2)}) collective-permute-start(bf16[128,2048]{1,0:T(8,128)(2,1)} %get-tuple-element.570), channel_id=1, source_target_pairs={{0,2},{2,0},{4,6},{6,4},{8,10},{10,8},{12,14},{14,12},{16,18},{18,... | collective-permute-start | bytes 1572872 | tf_op jit(solution)/shard_map/ppermute | solution.py:625
  391.8 30.9 %collective-permute-start.52 = (bf16[128,2048]{1,0:T(8,128)(2,1)}, bf16[128,2048]{1,0:T(8,128)(2,1)S(1)}, u32[]{:S(2)}, u32[]{:S(2)}) collective-permute-start(bf16[128,2048]{1,0:T(8,128)(2,1)} %get-tuple-element.569), channel_id=1, source_target_pairs={{0,4},{2,6},{4,0},{6,2},{8,12},{10,14},{12,8},{14,10},{16,20},{18,... | collective-permute-start | bytes 1572872 | tf_op jit(solution)/shard_map/ppermute | solution.py:625
  422.7 32.8 %collective-permute-start.57 = (bf16[1024,2048]{1,0:T(8,128)(2,1)}, bf16[1024,2048]{1,0:T(8,128)(2,1)}, u32[]{:S(2)}, u32[]{:S(2)}) collective-permute-start(bf16[1024,2048]{1,0:T(8,128)(2,1)} %get-tuple-element.405), channel_id=1, source_target_pairs={{0,1},{1,0},{2,3},{3,2},{4,5},{5,4},{6,7},{7,6},{8,9},{9,8},{10,11... | collective-permute-start | bytes 12582920 | tf_op jit(solution)/shard_map/ppermute | solution.py:607
  429.6 24.1 %collective-permute-start.55 = (bf16[256,2048]{1,0:T(8,128)(2,1)}, bf16[256,2048]{1,0:T(8,128)(2,1)}, u32[]{:S(2)}, u32[]{:S(2)}) collective-permute-start(bf16[256,2048]{1,0:T(8,128)(2,1)} %pad_maximum_fusion.6), channel_id=1, source_target_pairs={{0,2},{2,0},{4,6},{6,4},{8,10},{10,8},{12,14},{14,12},{16,18},{18,... | collective-permute-start | bytes 3145736 | tf_op jit(solution)/shard_map/ppermute | solution.py:625
  431.8 23.8 %collective-permute-start.56 = (bf16[256,2048]{1,0:T(8,128)(2,1)}, bf16[256,2048]{1,0:T(8,128)(2,1)}, u32[]{:S(2)}, u32[]{:S(2)}) collective-permute-start(bf16[256,2048]{1,0:T(8,128)(2,1)} %pad_maximum_fusion.7), channel_id=1, source_target_pairs={{0,4},{2,6},{4,0},{6,2},{8,12},{10,14},{12,8},{14,10},{16,20},{18,... | collective-permute-start | bytes 3145736 | tf_op jit(solution)/shard_map/ppermute | solution.py:625
  437.0 34.6 %collective-permute-start.58 = (bf16[512,1536]{1,0:T(8,128)(2,1)S(1)}, bf16[512,1536]{1,0:T(8,128)(2,1)}, u32[]{:S(2)}, u32[]{:S(2)}) collective-permute-start(bf16[512,1536]{1,0:T(8,128)(2,1)S(1)} %get-tuple-element.420), channel_id=1, source_target_pairs={{0,8},{2,10},{4,12},{6,14},{8,0},{10,2},{12,4},{14,6},{16,24},{18,... | collective-permute-start | bytes 4718600 | tf_op jit(solution)/shard_map/ppermute | solution.py:633
  437.1 35.3 %collective-permute-start.59 = (bf16[512,1536]{1,0:T(8,128)(2,1)S(1)}, bf16[512,1536]{1,0:T(8,128)(2,1)}, u32[]{:S(2)}, u32[]{:S(2)}) collective-permute-start(bf16[512,1536]{1,0:T(8,128)(2,1)S(1)} %get-tuple-element.421), channel_id=1, source_target_pairs={{8,16},{10,18},{12,20},{14,22},{16,8},{18,10},{20,12},{22,14},{9,1... | collective-permute-start | bytes 4718600 | tf_op jit(solution)/shard_map/ppermute | solution.py:633
  460.2 42.9 %collective-permute-start.66 = (bf16[512,1536]{1,0:T(8,128)(2,1)S(1)}, bf16[512,1536]{1,0:T(8,128)(2,1)S(1)}, u32[]{:S(2)}, u32[]{:S(2)}) collective-permute-start(bf16[512,1536]{1,0:T(8,128)(2,1)S(1)} %copy-done.8), channel_id=1, source_target_pairs={{0,8},{2,10},{4,12},{6,14},{1,9},{3,11},{5,13},{7,15}} | collective-permute-start | bytes 4718600 | tf_op jit(solution)/shard_map/ppermute | solution.py:633
  471.6 31.4 %collective-permute-start.67 = (bf16[512,1536]{1,0:T(8,128)(2,1)S(1)}, bf16[512,1536]{1,0:T(8,128)(2,1)S(1)}, u32[]{:S(2)}, u32[]{:S(2)}) collective-permute-start(bf16[512,1536]{1,0:T(8,128)(2,1)S(1)} %copy-done.6), channel_id=1, source_target_pairs={{24,16},{26,18},{28,20},{30,22},{25,17},{27,19},{29,21},{31,23}} | collective-permute-start | bytes 4718600 | tf_op jit(solution)/shard_map/ppermute | solution.py:633
  475.9 22.3 %collective-permute-start.62 = (bf16[256,2048]{1,0:T(8,128)(2,1)S(1)}, bf16[256,2048]{1,0:T(8,128)(2,1)S(1)}, u32[]{:S(2)}, u32[]{:S(2)}) collective-permute-start(bf16[256,2048]{1,0:T(8,128)(2,1)S(1)} %get-tuple-element.523), channel_id=1, source_target_pairs={{0,2},{2,0},{4,6},{6,4},{8,10},{10,8},{12,14},{14,12},{16,18},{18,... | collective-permute-start | bytes 3145736 | tf_op jit(solution)/shard_map/ppermute | solution.py:625
  476.4 23.1 %collective-permute-start.63 = (bf16[256,2048]{1,0:T(8,128)(2,1)S(1)}, bf16[256,2048]{1,0:T(8,128)(2,1)S(1)}, u32[]{:S(2)}, u32[]{:S(2)}) collective-permute-start(bf16[256,2048]{1,0:T(8,128)(2,1)S(1)} %get-tuple-element.523), channel_id=1, source_target_pairs={{0,4},{2,6},{4,0},{6,2},{8,12},{10,14},{12,8},{14,10},{16,20},{18,... | collective-permute-start | bytes 3145736 | tf_op jit(solution)/shard_map/ppermute | solution.py:625
  514.3 48.9 %collective-permute-start.71 = (bf16[512,1536]{1,0:T(8,128)(2,1)S(1)}, bf16[512,1536]{1,0:T(8,128)(2,1)S(1)}, u32[]{:S(2)}, u32[]{:S(2)}) collective-permute-start(bf16[512,1536]{1,0:T(8,128)(2,1)S(1)} %shard_map.247), channel_id=1, source_target_pairs={{8,16},{10,18},{12,20},{14,22},{16,8},{18,10},{20,12},{22,14},{9,1... | collective-permute-start | bytes 4718600 | tf_op jit(solution)/shard_map/ppermute | solution.py:633
  515.1 48.2 %collective-permute-start.72 = (bf16[512,1536]{1,0:T(8,128)(2,1)S(1)}, bf16[512,1536]{1,0:T(8,128)(2,1)S(1)}, u32[]{:S(2)}, u32[]{:S(2)}) collective-permute-start(bf16[512,1536]{1,0:T(8,128)(2,1)S(1)} %shard_map.247), channel_id=1, source_target_pairs={{0,8},{2,10},{4,12},{6,14},{24,16},{26,18},{28,20},{30,22},{1,9},{... | collective-permute-start | bytes 4718600 | tf_op jit(solution)/shard_map/ppermute | solution.py:633
  522.5 40.8 %collective-permute-start.69 = (bf16[256,2048]{1,0:T(8,128)(2,1)S(1)}, bf16[256,2048]{1,0:T(8,128)(2,1)}, u32[]{:S(2)}, u32[]{:S(2)}) collective-permute-start(bf16[256,2048]{1,0:T(8,128)(2,1)S(1)} %pad_maximum_fusion.8), channel_id=1, source_target_pairs={{0,2},{2,0},{4,6},{6,4},{8,10},{10,8},{12,14},{14,12},{16,18},{18,... | collective-permute-start | bytes 3145736 | tf_op jit(solution)/shard_map/ppermute | solution.py:625
  523.1 40.2 %collective-permute-start.70 = (bf16[256,2048]{1,0:T(8,128)(2,1)}, bf16[256,2048]{1,0:T(8,128)(2,1)}, u32[]{:S(2)}, u32[]{:S(2)}) collective-permute-start(bf16[256,2048]{1,0:T(8,128)(2,1)} %pad_maximum_fusion.9), channel_id=1, source_target_pairs={{0,4},{2,6},{4,0},{6,2},{8,12},{10,14},{12,8},{14,10},{16,20},{18,... | collective-permute-start | bytes 3145736 | tf_op jit(solution)/shard_map/ppermute | solution.py:625
  524.9 38.4 %collective-permute-start.73 = (bf16[256,1536]{1,0:T(8,128)(2,1)}, bf16[256,1536]{1,0:T(8,128)(2,1)S(1)}, u32[]{:S(2)}, u32[]{:S(2)}) collective-permute-start(bf16[256,1536]{1,0:T(8,128)(2,1)} %pad_maximum_fusion.14), channel_id=1, source_target_pairs={{0,2},{2,0},{4,6},{6,4},{8,10},{10,8},{12,14},{14,12},{16,18},{18,... | collective-permute-start | bytes 2359304 | tf_op jit(solution)/shard_map/ppermute | solution.py:625
  567.6 36.3 %collective-permute-start.77 = (bf16[512,1536]{1,0:T(8,128)(2,1)}, bf16[512,1536]{1,0:T(8,128)(2,1)}, u32[]{:S(2)}, u32[]{:S(2)}) collective-permute-start(bf16[512,1536]{1,0:T(8,128)(2,1)} %get-tuple-element.463), channel_id=1, source_target_pairs={{0,8},{2,10},{4,12},{6,14},{8,0},{10,2},{12,4},{14,6},{16,24},{18,... | collective-permute-start | bytes 4718600 | tf_op jit(solution)/shard_map/ppermute | solution.py:633
  567.6 37.2 %collective-permute-start.78 = (bf16[512,1536]{1,0:T(8,128)(2,1)S(1)}, bf16[512,1536]{1,0:T(8,128)(2,1)}, u32[]{:S(2)}, u32[]{:S(2)}) collective-permute-start(bf16[512,1536]{1,0:T(8,128)(2,1)S(1)} %get-tuple-element.464), channel_id=1, source_target_pairs={{8,16},{10,18},{12,20},{14,22},{16,8},{18,10},{20,12},{22,14},{9,1... | collective-permute-start | bytes 4718600 | tf_op jit(solution)/shard_map/ppermute | solution.py:633
  590.1 25.8 %collective-permute-start.82 = (bf16[512,640]{1,0:T(8,128)(2,1)S(1)}, bf16[512,640]{1,0:T(8,128)(2,1)S(1)}, u32[]{:S(2)}, u32[]{:S(2)}) collective-permute-start(bf16[512,640]{1,0:T(8,128)(2,1)S(1)} %copy-done.74), channel_id=1, source_target_pairs={{0,8},{2,10},{4,12},{6,14},{1,9},{3,11},{5,13},{7,15}} | collective-permute-start | bytes 1966088 | tf_op jit(solution)/shard_map/ppermute | solution.py:633
  605.1 34.9 %collective-permute-start.80 = (bf16[256,2048]{1,0:T(8,128)(2,1)S(1)}, bf16[256,2048]{1,0:T(8,128)(2,1)S(1)}, u32[]{:S(2)}, u32[]{:S(2)}) collective-permute-start(bf16[256,2048]{1,0:T(8,128)(2,1)S(1)} %pad_maximum_fusion.10), channel_id=1, source_target_pairs={{0,2},{2,0},{4,6},{6,4},{8,10},{10,8},{12,14},{14,12},{16,18},{18,... | collective-permute-start | bytes 3145736 | tf_op jit(solution)/shard_map/ppermute | solution.py:625
  606.0 34.0 %collective-permute-start.81 = (bf16[256,2048]{1,0:T(8,128)(2,1)S(1)}, bf16[256,2048]{1,0:T(8,128)(2,1)S(1)}, u32[]{:S(2)}, u32[]{:S(2)}) collective-permute-start(bf16[256,2048]{1,0:T(8,128)(2,1)S(1)} %pad_maximum_fusion.11), channel_id=1, source_target_pairs={{0,4},{2,6},{4,0},{6,2},{8,12},{10,14},{12,8},{14,10},{16,20},{18,... | collective-permute-start | bytes 3145736 | tf_op jit(solution)/shard_map/ppermute | solution.py:625
  610.6 26.9 %collective-permute-start.86 = (bf16[128,1536]{1,0:T(8,128)(2,1)}, bf16[128,1536]{1,0:T(8,128)(2,1)S(1)}, u32[]{:S(2)}, u32[]{:S(2)}) collective-permute-start(bf16[128,1536]{1,0:T(8,128)(2,1)} %get-tuple-element.555), channel_id=1, source_target_pairs={{0,2},{2,0},{4,6},{6,4},{8,10},{10,8},{12,14},{14,12},{16,18},{18,... | collective-permute-start | bytes 1179656 | tf_op jit(solution)/shard_map/ppermute | solution.py:625
  648.2 22.8 %collective-permute-start.87 = (bf16[512,640]{1,0:T(8,128)(2,1)S(1)}, bf16[512,640]{1,0:T(8,128)(2,1)S(1)}, u32[]{:S(2)}, u32[]{:S(2)}) collective-permute-start(bf16[512,640]{1,0:T(8,128)(2,1)S(1)} %get-tuple-element.485), channel_id=1, source_target_pairs={{0,8},{2,10},{4,12},{6,14},{8,0},{10,2},{12,4},{14,6},{16,24},{18,... | collective-permute-start | bytes 1966088 | tf_op jit(solution)/shard_map/ppermute | solution.py:633
  (149 other events, 1897.7 us)

commit v8 on v7

--- a/solution.py
+++ b/solution.py
@@ -513,7 +513,7 @@
         [shape_of((tokens, model), jnp.bfloat16)] * 2,
         2 * tokens * model * 256,
         tokens * model,
-        vmem_limit,
+        28 * mebibyte,
     )(*lefts, *flat)
 
 

time: 702 us -> 718 us (1.023)
  local copies, waits for them, and re-layouts: 40.1 us -> 49 us
    unnamed x206 -> x232, local copies, waits for them, and re-layouts: 21.9 us -> 33.8 us
  transfers between devices with their start and end apart: 101 -> 101, of which waited for: 35 -> 36; matrix products, arithmetic and copies ran while one was open for 15% -> 15% of each run, Pallas kernels for 30% -> 30%
where the time goes in v8:
time: 718 us; the launch traced here: 710 us
  Pallas kernels  213 us (30%)
  waiting for transfers between devices  208 us (29%)
  starting transfers between devices  148 us (21%)
  other arithmetic  89 us (12%)
  local copies, waits for them, and re-layouts  49 us (7%)
    ppermute x54, waiting for transfers between devices, flip(): lax.ppermute(values, 'dp', [(i, i ^ relation) for i in range(self.dp)])  131 us
    ppermute x33, waiting for transfers between devices, ends(): return lax.ppermute(values, 'dp', pairs)  73.7 us
    ppermute x33, starting transfers between devices, ends(): return lax.ppermute(values, 'dp', pairs)  67.7 us
    pallas_call x2, Pallas kernels, run_ffn_units(): kernel_call(functools.partial(ffn_units, len(blocks), ff_sub, earlier), (...  49.8 us
    ppermute x54, starting transfers between devices, flip(): lax.ppermute(values, 'dp', [(i, i ^ relation) for i in range(self.dp)])  47.1 us
    pallas_call x2, Pallas kernels, run_weight_gradients(): kernel_call(functools.partial(weight_gradients, count, per), (model // ti...  34.7 us
    pallas_call x1, Pallas kernels, run_attention(): kernel_call(functools.partial(attention_backward, len(blocks), head_dim,...  34.1 us
    unnamed x232, local copies, waits for them, and re-layouts  33.8 us
  transfers between devices with their start and end apart: 101, of which 36 were waited for; matrix products, arithmetic and copies ran while one was open for 15% of the time, Pallas kernels for 30%

profile of v8, /device:TPU:1, one launch (start us, length us, event | category | flops | bytes accessed | tf_op | source)
XLA Modules:
  0.0 710.1 jit_solution(10359333496231934545)
XLA Ops:
  21.2 3.8 collective-permute-start.9
  27.0 5.6 multiply_sine_fusion
  32.6 5.6 collective-permute-done.5
  39.3 3.7 collective-permute-start.14
  62.9 7.3 %collective-permute-done.13 = bf16[512,640]{1,0:T(8,128)(2,1)} collective-permute-done((bf16[512,640]{1,0:T(8,128)(2,1)}, bf16[512,640]{1,0:T(8,128)(2,1)}, u32[]{:S(2)}, u32[]{:S(2)}) %collective-permute-start.13) | collective-permute-done | bytes 655392 | tf_op jit(solution)/shard_map/ppermute | solution.py:633
  81.3 3.6 pad_maximum_fusion.refs_1_.refs_4_
  85.7 7.9 %collective-permute-done.20 = bf16[128,1536]{1,0:T(8,128)(2,1)S(1)} collective-permute-done((bf16[128,1536]{1,0:T(8,128)(2,1)S(1)}, bf16[128,1536]{1,0:T(8,128)(2,1)S(1)}, u32[]{:S(2)}, u32[]{:S(2)}) %collective-permute-start.20) | collective-permute-done | bytes 393248 | tf_op jit(solution)/shard_map/ppermute | solution.py:625
  102.3 20.9 %shard_map.237 = (f32[4,512,384]{2,1,0:T(8,128)}, bf16[1024,256]{1,0:T(8,128)(2,1)S(1)}, bf16[1024,256]{1,0:T(8,128)(2,1)S(1)}, bf16[1024,2048]{1,0:T(8,128)(2,1)}, bf16[1024,2048]{1,0:T(8,128)(2,1)}) custom-call(bf16[1024,2048]{1,0:T(8,128)(2,1)} %constant_dynamic-update-slice_fusion.refs_0_.refs_3_, bf16[1024,2048]{1,0:T(8,128)(2,1)} %pad_maximum_fusion.refs_1_.refs_4_, ...), custom_call_target="tpu_custom_call" | custom-call | flops 32212254720 | bytes 33554432 | tf_op jit(solution)/shard_map/pallas_call | solution.py:329
  123.3 5.4 collective-permute-done.21
  135.3 9.6 %collective-permute-done.26 = bf16[128,2048]{1,0:T(8,128)(2,1)S(1)} collective-permute-done((bf16[128,2048]{1,0:T(8,128)(2,1)S(1)}, bf16[128,2048]{1,0:T(8,128)(2,1)S(1)}, u32[]{:S(2)}, u32[]{:S(2)}) %collective-permute-start.26) | collective-permute-done | bytes 524320 | tf_op jit(solution)/shard_map/ppermute | solution.py:625
  144.9 3.1 convert_add_fusion.10
  151.6 23.9 %collective-permute-done.31 = bf16[512,1536]{1,0:T(8,128)(2,1)S(1)} collective-permute-done((bf16[512,1536]{1,0:T(8,128)(2,1)}, bf16[512,1536]{1,0:T(8,128)(2,1)S(1)}, u32[]{:S(2)}, u32[]{:S(2)}) %collective-permute-start.31) | collective-permute-done | bytes 1572896 | tf_op jit(solution)/shard_map/ppermute | solution.py:633
  179.8 19.1 %collective-permute-done.33 = bf16[256,2048]{1,0:T(8,128)(2,1)S(1)} collective-permute-done((bf16[256,2048]{1,0:T(8,128)(2,1)S(1)}, bf16[256,2048]{1,0:T(8,128)(2,1)S(1)}, u32[]{:S(2)}, u32[]{:S(2)}) %collective-permute-start.33) | collective-permute-done | bytes 1048608 | tf_op jit(solution)/shard_map/ppermute | solution.py:625
  202.4 13.4 %collective-permute-done.36 = bf16[256,1536]{1,0:T(8,128)(2,1)S(1)} collective-permute-done((bf16[256,1536]{1,0:T(8,128)(2,1)S(1)}, bf16[256,1536]{1,0:T(8,128)(2,1)S(1)}, u32[]{:S(2)}, u32[]{:S(2)}) %collective-permute-start.36) | collective-permute-done | bytes 786464 | tf_op jit(solution)/shard_map/ppermute | solution.py:625
  224.8 18.5 %collective-permute-done.37 = bf16[256,2048]{1,0:T(8,128)(2,1)S(1)} collective-permute-done((bf16[256,2048]{1,0:T(8,128)(2,1)S(1)}, bf16[256,2048]{1,0:T(8,128)(2,1)S(1)}, u32[]{:S(2)}, u32[]{:S(2)}) %collective-permute-start.37) | collective-permute-done | bytes 1048608 | tf_op jit(solution)/shard_map/ppermute | solution.py:625
  244.8 4.0 select_select_fusion.2
  248.9 5.9 collective-permute-done.39
  269.6 19.5 %shard_map.238 = (bf16[1024,512]{1,0:T(8,128)(2,1)S(1)}, bf16[1024,512]{1,0:T(8,128)(2,1)}, bf16[1024,1024]{1,0:T(8,128)(2,1)}, bf16[1024,1024]{1,0:T(8,128)(2,1)}) custom-call(bf16[1024,2048]{1,0:T(8,128)(2,1)} %copy-done.58, bf16[1024,2048]{1,0:T(8,128)(2,1)} %copy-done.62, bf16[1024,2048]{1,0:T(8,128)(2,1)} %copy-done.59, bf16[1024,2048]{1,0:T(8,128)(2,1)} %copy-done.63, ...), custom_call_target="tpu_custom_call" | custom-call | flops 12884901888 | bytes 16777216 | tf_op jit(solution)/shard_map/pallas_call | solution.py:394
  289.2 12.7 %collective-permute-done.46 = bf16[512,1536]{1,0:T(8,128)(2,1)} collective-permute-done((bf16[512,1536]{1,0:T(8,128)(2,1)}, bf16[512,1536]{1,0:T(8,128)(2,1)}, u32[]{:S(2)}, u32[]{:S(2)}) %collective-permute-start.46) | collective-permute-done | bytes 1572896 | tf_op jit(solution)/shard_map/ppermute | solution.py:633
  306.4 9.8 %shard_map.240 = (bf16[1024,2048]{1,0:T(8,128)(2,1)S(1)}, bf16[1024,2048]{1,0:T(8,128)(2,1)S(1)}) custom-call(bf16[1024,1024]{1,0:T(8,128)(2,1)S(1)} %copy-done.7, bf16[1024,1024]{1,0:T(8,128)(2,1)S(1)} %copy-done.8, bf16[512,1536]{1,0:T(8,128)(2,1)S(1)} %copy-done.4, bf16[512,1536]{1,0:T(8,128)(2,1)S(1)} %copy-done.6, bf16[512,1536]{1,0:T(8,128)(2,1)S(1)} %copy-done.2, ...), custom_call_target="tpu_custom_call" | custom-call | flops 1073741824 | bytes 2097152 | tf_op jit(solution)/shard_map/pallas_call | solution.py:507
  320.2 21.0 %shard_map.239 = (bf16[512,1536]{1,0:T(8,128)(2,1)}, bf16[512,1536]{1,0:T(8,128)(2,1)}, bf16[512,1536]{1,0:T(8,128)(2,1)}, bf16[512,1536]{1,0:T(8,128)(2,1)}) custom-call(bf16[1024,2048]{1,0:T(8,128)(2,1)} %copy-done.58, bf16[1024,2048]{1,0:T(8,128)(2,1)} %copy-done.62, bf16[1024,2048]{1,0:T(8,128)(2,1)} %copy-done.59, bf16[1024,2048]{1,0:T(8,128)(2,1)} %copy-done.63, ...), custom_call_target="tpu_custom_call" | custom-call | flops 1073741824 | bytes 2097152 | tf_op jit(solution)/shard_map/pallas_call | solution.py:432
  344.1 6.3 collective-permute-start.48
  352.2 4.3 select_select_fusion
  356.5 30.2 %shard_map.241 = (bf16[1024,512]{1,0:T(8,128)(2,1)S(1)}, bf16[1024,512]{1,0:T(8,128)(2,1)}, bf16[1024,1024]{1,0:T(8,128)(2,1)}, bf16[1024,1024]{1,0:T(8,128)(2,1...) custom-call(bf16[1024,2048]{1,0:T(8,128)(2,1)} %copy-done.58, bf16[1024,2048]{1,0:T(8,128)(2,1)} %copy-done.62, ...), custom_call_target="tpu_custom_call" | custom-call | flops 12884901888 | bytes 16777216 | tf_op jit(solution)/shard_map/pallas_call | solution.py:394
  393.5 4.2 collective-permute-start.54
  397.8 3.3 convert_add_fusion.6
  403.9 15.1 %shard_map.243 = (bf16[512,1536]{1,0:T(8,128)(2,1)S(1)}, bf16[512,1536]{1,0:T(8,128)(2,1)}, bf16[512,1536]{1,0:T(8,128)(2,1)}, bf16[512,1536]{1,0:T(8,128)(2,1)}) custom-call(bf16[1024,2048]{1,0:T(8,128)(2,1)} %copy-done.58, bf16[1024,2048]{1,0:T(8,128)(2,1)} %copy-done.62, bf16[1024,1024]{1,0:T(8,128)(2,1)} %get-tuple-element.390.refs_2_, ...), custom_call_target="tpu_custom_call" | custom-call | flops 536870912 | bytes 1048576 | tf_op jit(solution)/shard_map/pallas_call | solution.py:465
  425.5 10.9 %shard_map.244 = (bf16[1024,2048]{1,0:T(8,128)(2,1)S(1)}, bf16[1024,2048]{1,0:T(8,128)(2,1)}) custom-call(bf16[1024,512]{1,0:T(8,128)(2,1)S(1)} %copy-done.21, bf16[1024,512]{1,0:T(8,128)(2,1)S(1)} %copy-done.22, bf16[1024,512]{1,0:T(8,128)(2,1)S(1)} %get-tuple-element.406.refs_2_, bf16[1024,512]{1,0:T(8,128)(2,1)S(1)} %copy-done.19, ...), custom_call_target="tpu_custom_call" | custom-call | flops 1073741824 | bytes 2097152 | tf_op jit(solution)/shard_map/pallas_call | solution.py:507
  445.3 4.1 shard_map.246
  451.2 10.7 %shard_map.245 = (bf16[512,1536]{1,0:T(8,128)(2,1)}, bf16[512,1536]{1,0:T(8,128)(2,1)}, bf16[512,1536]{1,0:T(8,128)(2,1)}, bf16[512,1536]{1,0:T(8,128)(2,1)}) custom-call(bf16[1024,2048]{1,0:T(8,128)(2,1)} %copy-done.59, bf16[1024,2048]{1,0:T(8,128)(2,1)} %copy-done.63, ...), custom_call_target="tpu_custom_call", output_to_operand_aliasing={{0}: (4, {}), {1}: (5, {}), {2}: (6, {}), {3}: (7, {})} | custom-call | flops 536870912 | bytes 1048576 | tf_op jit(solution)/shard_map/pallas_call | solution.py:465
  467.5 3.2 convert_add_fusion.3
  476.7 7.7 %collective-permute-done.58 = bf16[512,1536]{1,0:T(8,128)(2,1)} collective-permute-done((bf16[512,1536]{1,0:T(8,128)(2,1)}, bf16[512,1536]{1,0:T(8,128)(2,1)}, u32[]{:S(2)}, u32[]{:S(2)}) %collective-permute-start.58) | collective-permute-done | bytes 1572896 | tf_op jit(solution)/shard_map/ppermute | solution.py:633
  495.7 15.7 %collective-permute-done.62 = bf16[256,2048]{1,0:T(8,128)(2,1)S(1)} collective-permute-done((bf16[256,2048]{1,0:T(8,128)(2,1)S(1)}, bf16[256,2048]{1,0:T(8,128)(2,1)S(1)}, u32[]{:S(2)}, u32[]{:S(2)}) %collective-permute-start.62) | collective-permute-done | bytes 1048608 | tf_op jit(solution)/shard_map/ppermute | solution.py:625
  516.8 5.8 collective-permute-done.64
  523.0 4.3 collective-permute-start.68
  529.1 5.7 collective-permute-start.72
  539.0 34.1 %shard_map.248 = (bf16[1024,384]{1,0:T(8,128)(2,1)}, bf16[1024,384]{1,0:T(8,128)(2,1)}, f32[2,256]{1,0:T(2,128)S(1)}, bf16[1024,2048]{1,0:T(8,128)(2,1)}, bf16[1...) custom-call(bf16[1024,2048]{1,0:T(8,128)(2,1)} %copy-done.65, bf16[1024,2048]{1,0:T(8,128)(2,1)} %copy-done.69, ...), custom_call_target="tpu_custom_call" | custom-call | flops 32212254720 | bytes 33554432 | tf_op jit(solution)/shard_map/pallas_call | solution.py:339
  577.6 4.3 shard_map.250
  585.5 13.7 %shard_map.249 = (bf16[512,640]{1,0:T(8,128)(2,1)S(1)}, bf16[512,640]{1,0:T(8,128)(2,1)}, bf16[512,640]{1,0:T(8,128)(2,1)}, bf16[512,640]{1,0:T(8,128)(2,1)}) custom-call(bf16[1024,2048]{1,0:T(8,128)(2,1)} %constant_dynamic-update-slice_fusion.refs_0_.refs_3_, bf16[1024,2048]{1,0:T(8,128)(2,1)} %pad_maximum_fusion.refs_1_.refs_4_, ...), custom_call_target="tpu_custom_call" | custom-call | flops 1073741824 | bytes 2097152 | tf_op jit(solution)/shard_map/pallas_call | solution.py:432
  599.2 3.4 convert_add_fusion.1
  604.4 4.3 collective-permute-start.82
  608.7 9.5 %collective-permute-done.77 = bf16[512,1536]{1,0:T(8,128)(2,1)} collective-permute-done((bf16[512,1536]{1,0:T(8,128)(2,1)}, bf16[512,1536]{1,0:T(8,128)(2,1)}, u32[]{:S(2)}, u32[]{:S(2)}) %collective-permute-start.77) | collective-permute-done | bytes 1572896 | tf_op jit(solution)/shard_map/ppermute | solution.py:633
  633.2 9.9 %collective-permute-start.85 = (bf16[512,640]{1,0:T(8,128)(2,1)S(1)}, bf16[512,640]{1,0:T(8,128)(2,1)S(1)}, u32[]{:S(2)}, u32[]{:S(2)}) collective-permute-start(bf16[512,640]{1,0:T(8,128)(2,1)S(1)} %shard_map.251), channel_id=1, source_target_pairs={{0,8},{2,10},{4,12},{6,14},{24,16},{26,18},{28,20},{30,22},{1,9},{... | collective-permute-start | bytes 1966088 | tf_op jit(solution)/shard_map/ppermute | solution.py:633
  645.7 6.9 collective-permute-done.86.refs_5_
  671.6 6.0 collective-permute-done.92
  678.1 3.2 fusion.5.mine
  681.4 4.8 shard_map.253
  706.4 3.2 shard_map.254
  (567 shorter events, 247.5 us)
Async XLA Ops:
  94.0 34.7 %collective-permute-start.21 = (bf16[512,1536]{1,0:T(8,128)(2,1)S(1)}, bf16[512,1536]{1,0:T(8,128)(2,1)}, u32[]{:S(2)}, u32[]{:S(2)}) collective-permute-start(bf16[512,1536]{1,0:T(8,128)(2,1)S(1)} %pad_maximum_fusion.1.refs_4_.refs_2_), channel_id=1, source_target_pairs={{0,8},{2,10},{4,12},{6,14},{8,0},{10,2},{12,4},{14,6},{16,24},{18,... | collective-permute-start | bytes 4718600 | tf_op jit(solution)/shard_map/ppermute | solution.py:633
  95.8 32.9 %collective-permute-start.22 = (bf16[512,1536]{1,0:T(8,128)(2,1)S(1)}, bf16[512,1536]{1,0:T(8,128)(2,1)}, u32[]{:S(2)}, u32[]{:S(2)}) collective-permute-start(bf16[512,1536]{1,0:T(8,128)(2,1)S(1)} %pad_maximum_fusion.1.refs_4_.refs_2_), channel_id=1, source_target_pairs={{8,16},{10,18},{12,20},{14,22},{16,8},{18,10},{20,12},{22,14},{9,1... | collective-permute-start | bytes 4718600 | tf_op jit(solution)/shard_map/ppermute | solution.py:633
  97.9 25.3 %collective-permute-start.23 = (bf16[256,2048]{1,0:T(8,128)(2,1)S(1)}, bf16[256,2048]{1,0:T(8,128)(2,1)S(1)}, u32[]{:S(2)}, u32[]{:S(2)}) collective-permute-start(bf16[256,2048]{1,0:T(8,128)(2,1)S(1)} %fusion.17), channel_id=1, source_target_pairs={{0,2},{2,0},{4,6},{6,4},{8,10},{10,8},{12,14},{14,12},{16,18},{18,... | collective-permute-start | bytes 3145736 | tf_op jit(solution)/shard_map/ppermute | solution.py:625
  98.5 24.7 %collective-permute-start.24 = (bf16[256,2048]{1,0:T(8,128)(2,1)S(1)}, bf16[256,2048]{1,0:T(8,128)(2,1)S(1)}, u32[]{:S(2)}, u32[]{:S(2)}) collective-permute-start(bf16[256,2048]{1,0:T(8,128)(2,1)S(1)} %fusion.17), channel_id=1, source_target_pairs={{0,4},{2,6},{4,0},{6,2},{8,12},{10,14},{12,8},{14,10},{16,20},{18,... | collective-permute-start | bytes 3145736 | tf_op jit(solution)/shard_map/ppermute | solution.py:625
  134.0 41.5 %collective-permute-start.31 = (bf16[512,1536]{1,0:T(8,128)(2,1)}, bf16[512,1536]{1,0:T(8,128)(2,1)S(1)}, u32[]{:S(2)}, u32[]{:S(2)}) collective-permute-start(bf16[512,1536]{1,0:T(8,128)(2,1)} %collective-permute-done.22), channel_id=1, source_target_pairs={{16,24},{18,26},{20,28},{22,30},{8,0},{10,2},{12,4},{14,6},{17,25}... | collective-permute-start | bytes 4718600 | tf_op jit(solution)/shard_map/ppermute | solution.py:633
  148.2 27.3 %collective-permute-start.27 = (bf16[128,2048]{1,0:T(8,128)(2,1)S(1)}, bf16[128,2048]{1,0:T(8,128)(2,1)S(1)}, u32[]{:S(2)}, u32[]{:S(2)}) collective-permute-start(bf16[128,2048]{1,0:T(8,128)(2,1)S(1)} %get-tuple-element.572), channel_id=1, source_target_pairs={{0,2},{2,0},{4,6},{6,4},{8,10},{10,8},{12,14},{14,12},{16,18},{18,... | collective-permute-start | bytes 1572872 | tf_op jit(solution)/shard_map/ppermute | solution.py:625
  148.8 26.7 %collective-permute-start.28 = (bf16[128,2048]{1,0:T(8,128)(2,1)S(1)}, bf16[128,2048]{1,0:T(8,128)(2,1)S(1)}, u32[]{:S(2)}, u32[]{:S(2)}) collective-permute-start(bf16[128,2048]{1,0:T(8,128)(2,1)S(1)} %get-tuple-element.571), channel_id=1, source_target_pairs={{0,4},{2,6},{4,0},{6,2},{8,12},{10,14},{12,8},{14,10},{16,20},{18,... | collective-permute-start | bytes 1572872 | tf_op jit(solution)/shard_map/ppermute | solution.py:625
  175.6 23.3 %collective-permute-start.33 = (bf16[256,2048]{1,0:T(8,128)(2,1)S(1)}, bf16[256,2048]{1,0:T(8,128)(2,1)S(1)}, u32[]{:S(2)}, u32[]{:S(2)}) collective-permute-start(bf16[256,2048]{1,0:T(8,128)(2,1)S(1)} %pad_maximum_fusion.5), channel_id=1, source_target_pairs={{0,4},{2,6},{4,0},{6,2},{8,12},{10,14},{12,8},{14,10},{16,20},{18,... | collective-permute-start | bytes 3145736 | tf_op jit(solution)/shard_map/ppermute | solution.py:625
  176.2 23.0 %collective-permute-start.32 = (bf16[256,2048]{1,0:T(8,128)(2,1)S(1)}, bf16[256,2048]{1,0:T(8,128)(2,1)S(1)}, u32[]{:S(2)}, u32[]{:S(2)}) collective-permute-start(bf16[256,2048]{1,0:T(8,128)(2,1)S(1)} %pad_maximum_fusion.4), channel_id=1, source_target_pairs={{0,2},{2,0},{4,6},{6,4},{8,10},{10,8},{12,14},{14,12},{16,18},{18,... | collective-permute-start | bytes 3145736 | tf_op jit(solution)/shard_map/ppermute | solution.py:625
  177.2 38.6 %collective-permute-start.34 = (bf16[512,1536]{1,0:T(8,128)(2,1)S(1)}, bf16[512,1536]{1,0:T(8,128)(2,1)S(1)}, u32[]{:S(2)}, u32[]{:S(2)}) collective-permute-start(bf16[512,1536]{1,0:T(8,128)(2,1)S(1)} %collective-permute-done.30), channel_id=1, source_target_pairs={{16,24},{18,26},{20,28},{22,30},{8,0},{10,2},{12,4},{14,6},{17,25}... | collective-permute-start | bytes 4718600 | tf_op jit(solution)/shard_map/ppermute | solution.py:633
  178.6 37.2 %collective-permute-start.36 = (bf16[256,1536]{1,0:T(8,128)(2,1)S(1)}, bf16[256,1536]{1,0:T(8,128)(2,1)S(1)}, u32[]{:S(2)}, u32[]{:S(2)}) collective-permute-start(bf16[256,1536]{1,0:T(8,128)(2,1)S(1)} %pad_maximum_fusion.13), channel_id=1, source_target_pairs={{0,4},{2,6},{4,0},{6,2},{8,12},{10,14},{12,8},{14,10},{16,20},{18,... | collective-permute-start | bytes 2359304 | tf_op jit(solution)/shard_map/ppermute | solution.py:625
  215.9 39.7 %collective-permute-start.43 = (bf16[1024,2048]{1,0:T(8,128)(2,1)S(1)}, bf16[1024,2048]{1,0:T(8,128)(2,1)S(1)}, u32[]{:S(2)}, u32[]{:S(2)}) collective-permute-start(bf16[1024,2048]{1,0:T(8,128)(2,1)S(1)} %constant_dynamic-update-slice_fusion.5.refs_2_.refs_0_), channel_id=1, source_target_pairs={{0,1},{1,0},{2,3},{3,2},{4,5},{5,4},{6,7},{7,6},{8,9},{9,8},{10,11... | collective-permute-start | bytes 12582920 | tf_op jit(solution)/shard_map/ppermute | solution.py:607
  220.1 23.3 %collective-permute-start.37 = (bf16[256,2048]{1,0:T(8,128)(2,1)S(1)}, bf16[256,2048]{1,0:T(8,128)(2,1)S(1)}, u32[]{:S(2)}, u32[]{:S(2)}) collective-permute-start(bf16[256,2048]{1,0:T(8,128)(2,1)S(1)} %get-tuple-element.526), channel_id=1, source_target_pairs={{0,2},{2,0},{4,6},{6,4},{8,10},{10,8},{12,14},{14,12},{16,18},{18,... | collective-permute-start | bytes 3145736 | tf_op jit(solution)/shard_map/ppermute | solution.py:625
  221.0 23.0 %collective-permute-start.38 = (bf16[256,2048]{1,0:T(8,128)(2,1)S(1)}, bf16[256,2048]{1,0:T(8,128)(2,1)S(1)}, u32[]{:S(2)}, u32[]{:S(2)}) collective-permute-start(bf16[256,2048]{1,0:T(8,128)(2,1)S(1)} %get-tuple-element.526), channel_id=1, source_target_pairs={{0,4},{2,6},{4,0},{6,2},{8,12},{10,14},{12,8},{14,10},{16,20},{18,... | collective-permute-start | bytes 3145736 | tf_op jit(solution)/shard_map/ppermute | solution.py:625
  221.5 34.0 %collective-permute-start.41 = (bf16[512,1536]{1,0:T(8,128)(2,1)S(1)}, bf16[512,1536]{1,0:T(8,128)(2,1)}, u32[]{:S(2)}, u32[]{:S(2)}) collective-permute-start(bf16[512,1536]{1,0:T(8,128)(2,1)S(1)} %pad_maximum_fusion.2.refs_4_.refs_8_), channel_id=1, source_target_pairs={{0,8},{2,10},{4,12},{6,14},{8,0},{10,2},{12,4},{14,6},{16,24},{18,... | collective-permute-start | bytes 4718600 | tf_op jit(solution)/shard_map/ppermute | solution.py:633
  221.6 34.0 %collective-permute-start.42 = (bf16[512,1536]{1,0:T(8,128)(2,1)S(1)}, bf16[512,1536]{1,0:T(8,128)(2,1)}, u32[]{:S(2)}, u32[]{:S(2)}) collective-permute-start(bf16[512,1536]{1,0:T(8,128)(2,1)S(1)} %pad_maximum_fusion.2.refs_4_.refs_8_), channel_id=1, source_target_pairs={{8,16},{10,18},{12,20},{14,22},{16,8},{18,10},{20,12},{22,14},{9,1... | collective-permute-start | bytes 4718600 | tf_op jit(solution)/shard_map/ppermute | solution.py:633
  260.8 28.3 %collective-permute-start.45 = (bf16[512,1536]{1,0:T(8,128)(2,1)}, bf16[512,1536]{1,0:T(8,128)(2,1)}, u32[]{:S(2)}, u32[]{:S(2)}) collective-permute-start(bf16[512,1536]{1,0:T(8,128)(2,1)} %collective-permute-done.41), channel_id=1, source_target_pairs={{8,16},{10,18},{12,20},{14,22},{16,8},{18,10},{20,12},{22,14},{9,1... | collective-permute-start | bytes 4718600 | tf_op jit(solution)/shard_map/ppermute | solution.py:633
  262.8 39.1 %collective-permute-start.46 = (bf16[512,1536]{1,0:T(8,128)(2,1)}, bf16[512,1536]{1,0:T(8,128)(2,1)}, u32[]{:S(2)}, u32[]{:S(2)}) collective-permute-start(bf16[512,1536]{1,0:T(8,128)(2,1)} %collective-permute-done.42), channel_id=1, source_target_pairs={{16,24},{18,26},{20,28},{22,30},{8,0},{10,2},{12,4},{14,6},{17,25}... | collective-permute-start | bytes 4718600 | tf_op jit(solution)/shard_map/ppermute | solution.py:633
  301.9 42.2 %collective-permute-start.47 = (bf16[512,1536]{1,0:T(8,128)(2,1)}, bf16[512,1536]{1,0:T(8,128)(2,1)}, u32[]{:S(2)}, u32[]{:S(2)}) collective-permute-start(bf16[512,1536]{1,0:T(8,128)(2,1)} %collective-permute-done.45), channel_id=1, source_target_pairs={{16,24},{18,26},{20,28},{22,30},{8,0},{10,2},{12,4},{14,6},{17,25}... | collective-permute-start | bytes 4718600 | tf_op jit(solution)/shard_map/ppermute | solution.py:633
  344.1 42.6 %collective-permute-start.48 = (bf16[512,1536]{1,0:T(8,128)(2,1)S(1)}, bf16[512,1536]{1,0:T(8,128)(2,1)}, u32[]{:S(2)}, u32[]{:S(2)}) collective-permute-start(bf16[512,1536]{1,0:T(8,128)(2,1)S(1)} %copy-done.29), channel_id=1, source_target_pairs={{0,8},{2,10},{4,12},{6,14},{1,9},{3,11},{5,13},{7,15}} | collective-permute-start | bytes 4718600 | tf_op jit(solution)/shard_map/ppermute | solution.py:633
  350.4 36.3 %collective-permute-start.49 = (bf16[512,1536]{1,0:T(8,128)(2,1)S(1)}, bf16[512,1536]{1,0:T(8,128)(2,1)}, u32[]{:S(2)}, u32[]{:S(2)}) collective-permute-start(bf16[512,1536]{1,0:T(8,128)(2,1)S(1)} %copy-done.27), channel_id=1, source_target_pairs={{24,16},{26,18},{28,20},{30,22},{25,17},{27,19},{29,21},{31,23}} | collective-permute-start | bytes 4718600 | tf_op jit(solution)/shard_map/ppermute | solution.py:633
  391.6 44.8 %collective-permute-start.53 = (bf16[512,1536]{1,0:T(8,128)(2,1)}, bf16[512,1536]{1,0:T(8,128)(2,1)}, u32[]{:S(2)}, u32[]{:S(2)}) collective-permute-start(bf16[512,1536]{1,0:T(8,128)(2,1)} %shard_map.242), channel_id=1, source_target_pairs={{8,16},{10,18},{12,20},{14,22},{16,8},{18,10},{20,12},{22,14},{9,1... | collective-permute-start | bytes 4718600 | tf_op jit(solution)/shard_map/ppermute | solution.py:633
  393.5 42.9 %collective-permute-start.54 = (bf16[512,1536]{1,0:T(8,128)(2,1)}, bf16[512,1536]{1,0:T(8,128)(2,1)}, u32[]{:S(2)}, u32[]{:S(2)}) collective-permute-start(bf16[512,1536]{1,0:T(8,128)(2,1)} %shard_map.242), channel_id=1, source_target_pairs={{0,8},{2,10},{4,12},{6,14},{24,16},{26,18},{28,20},{30,22},{1,9},{... | collective-permute-start | bytes 4718600 | tf_op jit(solution)/shard_map/ppermute | solution.py:633
  402.2 34.3 %collective-permute-start.51 = (bf16[128,2048]{1,0:T(8,128)(2,1)}, bf16[128,2048]{1,0:T(8,128)(2,1)}, u32[]{:S(2)}, u32[]{:S(2)}) collective-permute-start(bf16[128,2048]{1,0:T(8,128)(2,1)} %get-tuple-element.570), channel_id=1, source_target_pairs={{0,2},{2,0},{4,6},{6,4},{8,10},{10,8},{12,14},{14,12},{16,18},{18,... | collective-permute-start | bytes 1572872 | tf_op jit(solution)/shard_map/ppermute | solution.py:625
  402.7 33.7 %collective-permute-start.52 = (bf16[128,2048]{1,0:T(8,128)(2,1)}, bf16[128,2048]{1,0:T(8,128)(2,1)}, u32[]{:S(2)}, u32[]{:S(2)}) collective-permute-start(bf16[128,2048]{1,0:T(8,128)(2,1)} %get-tuple-element.569), channel_id=1, source_target_pairs={{0,4},{2,6},{4,0},{6,2},{8,12},{10,14},{12,8},{14,10},{16,20},{18,... | collective-permute-start | bytes 1572872 | tf_op jit(solution)/shard_map/ppermute | solution.py:625
  436.4 31.0 %collective-permute-start.57 = (bf16[1024,2048]{1,0:T(8,128)(2,1)}, bf16[1024,2048]{1,0:T(8,128)(2,1)}, u32[]{:S(2)}, u32[]{:S(2)}) collective-permute-start(bf16[1024,2048]{1,0:T(8,128)(2,1)} %get-tuple-element.405), channel_id=1, source_target_pairs={{0,1},{1,0},{2,3},{3,2},{4,5},{5,4},{6,7},{7,6},{8,9},{9,8},{10,11... | collective-permute-start | bytes 12582920 | tf_op jit(solution)/shard_map/ppermute | solution.py:607
  440.2 24.4 %collective-permute-start.55 = (bf16[256,2048]{1,0:T(8,128)(2,1)}, bf16[256,2048]{1,0:T(8,128)(2,1)}, u32[]{:S(2)}, u32[]{:S(2)}) collective-permute-start(bf16[256,2048]{1,0:T(8,128)(2,1)} %pad_maximum_fusion.6), channel_id=1, source_target_pairs={{0,2},{2,0},{4,6},{6,4},{8,10},{10,8},{12,14},{14,12},{16,18},{18,... | collective-permute-start | bytes 3145736 | tf_op jit(solution)/shard_map/ppermute | solution.py:625
  443.3 24.1 %collective-permute-start.56 = (bf16[256,2048]{1,0:T(8,128)(2,1)}, bf16[256,2048]{1,0:T(8,128)(2,1)}, u32[]{:S(2)}, u32[]{:S(2)}) collective-permute-start(bf16[256,2048]{1,0:T(8,128)(2,1)} %pad_maximum_fusion.7), channel_id=1, source_target_pairs={{0,4},{2,6},{4,0},{6,2},{8,12},{10,14},{12,8},{14,10},{16,20},{18,... | collective-permute-start | bytes 3145736 | tf_op jit(solution)/shard_map/ppermute | solution.py:625
  449.4 35.0 %collective-permute-start.58 = (bf16[512,1536]{1,0:T(8,128)(2,1)}, bf16[512,1536]{1,0:T(8,128)(2,1)}, u32[]{:S(2)}, u32[]{:S(2)}) collective-permute-start(bf16[512,1536]{1,0:T(8,128)(2,1)} %get-tuple-element.420), channel_id=1, source_target_pairs={{0,8},{2,10},{4,12},{6,14},{8,0},{10,2},{12,4},{14,6},{16,24},{18,... | collective-permute-start | bytes 4718600 | tf_op jit(solution)/shard_map/ppermute | solution.py:633
  449.4 35.8 %collective-permute-start.59 = (bf16[512,1536]{1,0:T(8,128)(2,1)S(1)}, bf16[512,1536]{1,0:T(8,128)(2,1)}, u32[]{:S(2)}, u32[]{:S(2)}) collective-permute-start(bf16[512,1536]{1,0:T(8,128)(2,1)S(1)} %get-tuple-element.421), channel_id=1, source_target_pairs={{8,16},{10,18},{12,20},{14,22},{16,8},{18,10},{20,12},{22,14},{9,1... | collective-permute-start | bytes 4718600 | tf_op jit(solution)/shard_map/ppermute | solution.py:633
  472.1 44.0 %collective-permute-start.66 = (bf16[512,1536]{1,0:T(8,128)(2,1)S(1)}, bf16[512,1536]{1,0:T(8,128)(2,1)S(1)}, u32[]{:S(2)}, u32[]{:S(2)}) collective-permute-start(bf16[512,1536]{1,0:T(8,128)(2,1)S(1)} %copy-done.16), channel_id=1, source_target_pairs={{0,8},{2,10},{4,12},{6,14},{1,9},{3,11},{5,13},{7,15}} | collective-permute-start | bytes 4718600 | tf_op jit(solution)/shard_map/ppermute | solution.py:633
  484.4 31.7 %collective-permute-start.67 = (bf16[512,1536]{1,0:T(8,128)(2,1)S(1)}, bf16[512,1536]{1,0:T(8,128)(2,1)S(1)}, u32[]{:S(2)}, u32[]{:S(2)}) collective-permute-start(bf16[512,1536]{1,0:T(8,128)(2,1)S(1)} %copy-done.14), channel_id=1, source_target_pairs={{24,16},{26,18},{28,20},{30,22},{25,17},{27,19},{29,21},{31,23}} | collective-permute-start | bytes 4718600 | tf_op jit(solution)/shard_map/ppermute | solution.py:633
  488.8 22.6 %collective-permute-start.62 = (bf16[256,2048]{1,0:T(8,128)(2,1)S(1)}, bf16[256,2048]{1,0:T(8,128)(2,1)S(1)}, u32[]{:S(2)}, u32[]{:S(2)}) collective-permute-start(bf16[256,2048]{1,0:T(8,128)(2,1)S(1)} %get-tuple-element.523), channel_id=1, source_target_pairs={{0,2},{2,0},{4,6},{6,4},{8,10},{10,8},{12,14},{14,12},{16,18},{18,... | collective-permute-start | bytes 3145736 | tf_op jit(solution)/shard_map/ppermute | solution.py:625
  489.3 23.1 %collective-permute-start.63 = (bf16[256,2048]{1,0:T(8,128)(2,1)S(1)}, bf16[256,2048]{1,0:T(8,128)(2,1)S(1)}, u32[]{:S(2)}, u32[]{:S(2)}) collective-permute-start(bf16[256,2048]{1,0:T(8,128)(2,1)S(1)} %get-tuple-element.523), channel_id=1, source_target_pairs={{0,4},{2,6},{4,0},{6,2},{8,12},{10,14},{12,8},{14,10},{16,20},{18,... | collective-permute-start | bytes 3145736 | tf_op jit(solution)/shard_map/ppermute | solution.py:625
  527.3 48.5 %collective-permute-start.71 = (bf16[512,1536]{1,0:T(8,128)(2,1)S(1)}, bf16[512,1536]{1,0:T(8,128)(2,1)}, u32[]{:S(2)}, u32[]{:S(2)}) collective-permute-start(bf16[512,1536]{1,0:T(8,128)(2,1)S(1)} %shard_map.247), channel_id=1, source_target_pairs={{8,16},{10,18},{12,20},{14,22},{16,8},{18,10},{20,12},{22,14},{9,1... | collective-permute-start | bytes 4718600 | tf_op jit(solution)/shard_map/ppermute | solution.py:633
  529.1 46.7 %collective-permute-start.72 = (bf16[512,1536]{1,0:T(8,128)(2,1)S(1)}, bf16[512,1536]{1,0:T(8,128)(2,1)}, u32[]{:S(2)}, u32[]{:S(2)}) collective-permute-start(bf16[512,1536]{1,0:T(8,128)(2,1)S(1)} %shard_map.247), channel_id=1, source_target_pairs={{0,8},{2,10},{4,12},{6,14},{24,16},{26,18},{28,20},{30,22},{1,9},{... | collective-permute-start | bytes 4718600 | tf_op jit(solution)/shard_map/ppermute | solution.py:633
  534.8 41.0 %collective-permute-start.69 = (bf16[256,2048]{1,0:T(8,128)(2,1)}, bf16[256,2048]{1,0:T(8,128)(2,1)}, u32[]{:S(2)}, u32[]{:S(2)}) collective-permute-start(bf16[256,2048]{1,0:T(8,128)(2,1)} %pad_maximum_fusion.8), channel_id=1, source_target_pairs={{0,2},{2,0},{4,6},{6,4},{8,10},{10,8},{12,14},{14,12},{16,18},{18,... | collective-permute-start | bytes 3145736 | tf_op jit(solution)/shard_map/ppermute | solution.py:625
  535.4 40.4 %collective-permute-start.70 = (bf16[256,2048]{1,0:T(8,128)(2,1)}, bf16[256,2048]{1,0:T(8,128)(2,1)}, u32[]{:S(2)}, u32[]{:S(2)}) collective-permute-start(bf16[256,2048]{1,0:T(8,128)(2,1)} %pad_maximum_fusion.9), channel_id=1, source_target_pairs={{0,4},{2,6},{4,0},{6,2},{8,12},{10,14},{12,8},{14,10},{16,20},{18,... | collective-permute-start | bytes 3145736 | tf_op jit(solution)/shard_map/ppermute | solution.py:625
  536.9 38.8 %collective-permute-start.73 = (bf16[256,1536]{1,0:T(8,128)(2,1)}, bf16[256,1536]{1,0:T(8,128)(2,1)S(1)}, u32[]{:S(2)}, u32[]{:S(2)}) collective-permute-start(bf16[256,1536]{1,0:T(8,128)(2,1)} %pad_maximum_fusion.14), channel_id=1, source_target_pairs={{0,2},{2,0},{4,6},{6,4},{8,10},{10,8},{12,14},{14,12},{16,18},{18,... | collective-permute-start | bytes 2359304 | tf_op jit(solution)/shard_map/ppermute | solution.py:625
  575.8 23.4 %collective-permute-start.74 = (bf16[1024,2048]{1,0:T(8,128)(2,1)}, bf16[1024,2048]{1,0:T(8,128)(2,1)}, u32[]{:S(2)}, u32[]{:S(2)}) collective-permute-start(bf16[1024,2048]{1,0:T(8,128)(2,1)} %get-tuple-element.451), channel_id=1, source_target_pairs={{0,1},{1,0},{2,3},{3,2},{4,5},{5,4},{6,7},{7,6},{8,9},{9,8},{10,11... | collective-permute-start | bytes 12582920 | tf_op jit(solution)/shard_map/ppermute | solution.py:607
  581.9 36.2 %collective-permute-start.77 = (bf16[512,1536]{1,0:T(8,128)(2,1)}, bf16[512,1536]{1,0:T(8,128)(2,1)}, u32[]{:S(2)}, u32[]{:S(2)}) collective-permute-start(bf16[512,1536]{1,0:T(8,128)(2,1)} %get-tuple-element.463), channel_id=1, source_target_pairs={{0,8},{2,10},{4,12},{6,14},{8,0},{10,2},{12,4},{14,6},{16,24},{18,... | collective-permute-start | bytes 4718600 | tf_op jit(solution)/shard_map/ppermute | solution.py:633
  582.0 37.1 %collective-permute-start.78 = (bf16[512,1536]{1,0:T(8,128)(2,1)}, bf16[512,1536]{1,0:T(8,128)(2,1)}, u32[]{:S(2)}, u32[]{:S(2)}) collective-permute-start(bf16[512,1536]{1,0:T(8,128)(2,1)} %get-tuple-element.464), channel_id=1, source_target_pairs={{8,16},{10,18},{12,20},{14,22},{16,8},{18,10},{20,12},{22,14},{9,1... | collective-permute-start | bytes 4718600 | tf_op jit(solution)/shard_map/ppermute | solution.py:633
  604.4 25.8 %collective-permute-start.82 = (bf16[512,640]{1,0:T(8,128)(2,1)S(1)}, bf16[512,640]{1,0:T(8,128)(2,1)S(1)}, u32[]{:S(2)}, u32[]{:S(2)}) collective-permute-start(bf16[512,640]{1,0:T(8,128)(2,1)S(1)} %copy-done.84), channel_id=1, source_target_pairs={{0,8},{2,10},{4,12},{6,14},{1,9},{3,11},{5,13},{7,15}} | collective-permute-start | bytes 1966088 | tf_op jit(solution)/shard_map/ppermute | solution.py:633
  620.3 35.0 %collective-permute-start.80 = (bf16[256,2048]{1,0:T(8,128)(2,1)}, bf16[256,2048]{1,0:T(8,128)(2,1)}, u32[]{:S(2)}, u32[]{:S(2)}) collective-permute-start(bf16[256,2048]{1,0:T(8,128)(2,1)} %pad_maximum_fusion.10), channel_id=1, source_target_pairs={{0,2},{2,0},{4,6},{6,4},{8,10},{10,8},{12,14},{14,12},{16,18},{18,... | collective-permute-start | bytes 3145736 | tf_op jit(solution)/shard_map/ppermute | solution.py:625
  622.1 33.2 %collective-permute-start.81 = (bf16[256,2048]{1,0:T(8,128)(2,1)}, bf16[256,2048]{1,0:T(8,128)(2,1)}, u32[]{:S(2)}, u32[]{:S(2)}) collective-permute-start(bf16[256,2048]{1,0:T(8,128)(2,1)} %pad_maximum_fusion.11), channel_id=1, source_target_pairs={{0,4},{2,6},{4,0},{6,2},{8,12},{10,14},{12,8},{14,10},{16,20},{18,... | collective-permute-start | bytes 3145736 | tf_op jit(solution)/shard_map/ppermute | solution.py:625
  626.4 26.2 %collective-permute-start.86 = (bf16[128,1536]{1,0:T(8,128)(2,1)}, bf16[128,1536]{1,0:T(8,128)(2,1)S(1)}, u32[]{:S(2)}, u32[]{:S(2)}) collective-permute-start(bf16[128,1536]{1,0:T(8,128)(2,1)} %get-tuple-element.555), channel_id=1, source_target_pairs={{0,2},{2,0},{4,6},{6,4},{8,10},{10,8},{12,14},{14,12},{16,18},{18,... | collective-permute-start | bytes 1179656 | tf_op jit(solution)/shard_map/ppermute | solution.py:625
  633.2 22.1 %collective-permute-start.85 = (bf16[512,640]{1,0:T(8,128)(2,1)S(1)}, bf16[512,640]{1,0:T(8,128)(2,1)S(1)}, u32[]{:S(2)}, u32[]{:S(2)}) collective-permute-start(bf16[512,640]{1,0:T(8,128)(2,1)S(1)} %shard_map.251), channel_id=1, source_target_pairs={{0,8},{2,10},{4,12},{6,14},{24,16},{26,18},{28,20},{30,22},{1,9},{... | collective-permute-start | bytes 1966088 | tf_op jit(solution)/shard_map/ppermute | solution.py:633
  662.7 23.5 %collective-permute-start.87 = (bf16[512,640]{1,0:T(8,128)(2,1)S(1)}, bf16[512,640]{1,0:T(8,128)(2,1)S(1)}, u32[]{:S(2)}, u32[]{:S(2)}) collective-permute-start(bf16[512,640]{1,0:T(8,128)(2,1)S(1)} %get-tuple-element.485), channel_id=1, source_target_pairs={{0,8},{2,10},{4,12},{6,14},{8,0},{10,2},{12,4},{14,6},{16,24},{18,... | collective-permute-start | bytes 1966088 | tf_op jit(solution)/shard_map/ppermute | solution.py:633
  (162 other events, 2163.6 us)
